TPU v7x, 32 devices: a whole 2x2x4 slice. The times are simulated.
32 devices in a mesh: tile: 4 (over y, x), date: 8 (over z, core).
Axes of the slice: x: 2, y: 2, z: 4, core: 2. Of those that a mesh axis runs over, the one named last changes fastest.
Arguments:
- layer_input: bfloat16 [32, 32, 1024], P('tile', 'date'), may hold values from -6 to 6
- head_input: bfloat16 [32, 32, 1024], P('tile', 'date'), may hold values from -6 to 6
- out_grad: bfloat16 [32, 32, 1024], P('tile', 'date'), may hold values from -6 to 6
- sensor_ids: int32 [32], P('date'), may hold values from 0 to 1
- valid_mask: int32 [32, 32], P('tile', 'date'), may hold values 0 or 1
- sensor_table: float32 [2, 1024], replicated, may hold values from -4 to 4
- proj_weight: bfloat16 [1024, 264], replicated, may hold values from -0.09375 to 0.09375
- step_bias: float32 [8], replicated, may hold values from -4 to -2
- decay_log: float32 [8], replicated, may hold values from -4 to 0
- skip_gain: float32 [8], replicated, may hold values from 0.5 to 1.5
Outputs:
- value_grad: bfloat16 [32, 32, 1024], P('tile', 'date')
- input_grad: bfloat16 [32, 32, 1024], P('tile', 'date')
- weight_grad: float32 [1024, 264], replicated
- table_grad: float32 [2, 1024], replicated
- head_grads: float32 [3, 8], replicated
All inputs are finite; a program needn't handle non-finite values. No bound on the sum of `valid_mask` on one device may be relied on, other than what follows from the above.
Results may differ from a plain program's by a relative error of at most 0.0088.
Values may be sent and summed in bfloat16 or wider, within the bound.
No kernel may reach another device: no remote copies, remote signals or barrier semaphores. Data moves between devices by JAX's collectives and lax.ppermute only.
A program may use at most 64 MiB of HBM per device.

v0:
```python
import math

import jax
import jax.numpy as jnp
from jax import lax
from jax.sharding import PartitionSpec as P

SPAN = 64


HIGHEST_PREC = lax.Precision.HIGHEST
NEG_FILL = -1e30


def span_scan(values_in, keys_in, reads_in, step_in, decay_in, skip_in, block_len):
    series, length, head_count, width_p = values_in.shape
    states_n = keys_in.shape[2]
    block_count = length // block_len
    decay_rate = -jnp.exp(decay_in)
    values_blk = values_in.reshape(series, block_count, block_len, head_count, width_p)
    keys_b = keys_in.reshape(series, block_count, block_len, states_n)
    reads_c = reads_in.reshape(series, block_count, block_len, states_n)
    step_blocks = step_in.reshape(series, block_count, block_len, head_count)
    weighted = values_blk * step_blocks[..., None]
    log_decay = jnp.cumsum(step_blocks * decay_rate, axis=2)
    log_heads = jnp.swapaxes(log_decay, 2, 3)
    row_ids = lax.broadcasted_iota(jnp.int32, (block_len, block_len), 0)
    col_ids = lax.broadcasted_iota(jnp.int32, (block_len, block_len), 1)
    causal = row_ids >= col_ids
    gap_logs = log_heads[..., :, None] - log_heads[..., None, :]
    kernel = jnp.exp(jnp.where(causal, gap_logs, NEG_FILL))
    scores = jnp.einsum("scin,scjn->scij", reads_c, keys_b, precision=HIGHEST_PREC)
    mixed_kernel = kernel * scores[:, :, None]
    within_block = jnp.einsum("schij,scjhp->scihp", mixed_kernel, weighted, precision=HIGHEST_PREC)
    to_block_end = jnp.exp(log_decay[:, :, -1:, :] - log_decay)
    block_states = jnp.einsum(
        "scjn,scjhp->schnp", keys_b, weighted * to_block_end[..., None], precision=HIGHEST_PREC
    )
    block_totals = jnp.exp(log_decay[:, :, -1, :])

    def advance(state_carry, block_item):
        block_total, block_state = block_item
        return (state_carry * block_total[:, :, None, None] + block_state, state_carry)

    zero_state = jnp.zeros((series, head_count, states_n, width_p), dtype=values_in.dtype)
    _, entering = lax.scan(
        advance, zero_state, (jnp.moveaxis(block_totals, 1, 0), jnp.moveaxis(block_states, 1, 0))
    )
    entering = jnp.moveaxis(entering, 0, 1)
    from_earlier = (
        jnp.einsum("scin,schnp->scihp", reads_c, entering, precision=HIGHEST_PREC)
        * jnp.exp(log_decay)[..., None]
    )
    result = within_block + from_earlier + skip_in[:, None] * values_blk
    return result.reshape(series, length, head_count, width_p)


def on_device(
    layer_input,
    head_input,
    out_grad,
    sensor_ids,
    valid_mask,
    sensor_table,
    proj_weight,
    step_bias,
    decay_log,
    skip_gain,
):
    pixel_dev, dates_dev, model_d = layer_input.shape
    head_count = step_bias.shape[0]
    width_hp = head_input.shape[2]
    width_p = width_hp // head_count
    states_n = (proj_weight.shape[1] - head_count) // 2
    is_second = (sensor_ids == 1)[None, :, None]
    sensor_embed = jnp.where(is_second, sensor_table[1], sensor_table[0])
    mixed_in = (layer_input.astype(jnp.float32) + sensor_embed).astype(jnp.bfloat16)
    flat_in = mixed_in.reshape(pixel_dev * dates_dev, model_d)
    projected = jnp.dot(flat_in, proj_weight, preferred_element_type=jnp.float32).reshape(
        pixel_dev, dates_dev, -1
    )
    pair_proj = projected[:, :, : 2 * states_n].astype(jnp.bfloat16)
    step_pre = projected[:, :, 2 * states_n :] + step_bias
    valid_gate = valid_mask.astype(jnp.float32)[:, :, None]
    step_sizes = (valid_gate * jax.nn.softplus(step_pre)).astype(jnp.bfloat16)

    def local_scan(values_in, keys_in, reads_in, step_in, decay_in, skip_in):
        return span_scan(
            values_in, keys_in, reads_in, step_in, decay_in, skip_in, min(SPAN, values_in.shape[1])
        )

    series_values, series_cot, series_pairs, series_steps = (
        lax.all_to_all(head_input, "date", split_axis=0, concat_axis=1, tiled=True),
        lax.all_to_all(out_grad, "date", split_axis=0, concat_axis=1, tiled=True),
        lax.all_to_all(pair_proj, "date", split_axis=0, concat_axis=1, tiled=True),
        lax.all_to_all(step_sizes, "date", split_axis=0, concat_axis=1, tiled=True),
    )
    series_count = series_values.shape[0]
    length = series_values.shape[1]
    _, pullback = jax.vjp(
        local_scan,
        series_values.astype(jnp.float32).reshape(series_count, length, head_count, width_p),
        series_pairs[..., :states_n].astype(jnp.float32),
        series_pairs[..., states_n:].astype(jnp.float32),
        series_steps.astype(jnp.float32),
        decay_log,
        skip_gain,
    )
    series_count = series_values.shape[0]
    length = series_values.shape[1]
    grad_values, grad_b, grad_c, grad_steps, grad_decay, grad_skip = pullback(
        series_cot.astype(jnp.float32).reshape(series_count, length, head_count, width_p)
    )
    value_series = grad_values.reshape(series_count, length, width_hp).astype(jnp.bfloat16)
    pair_series = jnp.concatenate([grad_b, grad_c], axis=-1).astype(jnp.bfloat16)
    step_series = grad_steps.astype(jnp.bfloat16)
    value_grad, pair_grad, step_grad = (
        lax.all_to_all(value_series, "date", split_axis=1, concat_axis=0, tiled=True),
        lax.all_to_all(pair_series, "date", split_axis=1, concat_axis=0, tiled=True),
        lax.all_to_all(step_series, "date", split_axis=1, concat_axis=0, tiled=True),
    )
    raw_grad = step_grad.astype(jnp.float32) * valid_gate * jax.nn.sigmoid(step_pre)
    proj_grad = jnp.concatenate([pair_grad, raw_grad.astype(jnp.bfloat16)], axis=-1).reshape(
        pixel_dev * dates_dev, -1
    )
    weight_part = lax.dot_general(
        flat_in, proj_grad, (((0,), (0,)), ((), ())), preferred_element_type=jnp.float32
    )
    flat_grad = lax.dot_general(
        proj_grad, proj_weight, (((1,), (1,)), ((), ())), preferred_element_type=jnp.float32
    )
    input_grad = flat_grad.astype(jnp.bfloat16).reshape(pixel_dev, dates_dev, model_d)
    flat_back = flat_grad.reshape(pixel_dev, dates_dev, model_d)
    second_sum = jnp.sum(jnp.where(is_second, flat_back, 0.0), axis=(0, 1))
    first_sum = jnp.sum(jnp.where(is_second, 0.0, flat_back), axis=(0, 1))
    table_part = jnp.stack([first_sum, second_sum])
    head_part = jnp.stack([grad_decay, jnp.sum(raw_grad, axis=(0, 1)), grad_skip])
    weight_sum, table_sum, head_sum = lax.psum(
        (weight_part, table_part, head_part), ("tile", "date")
    )
    total_tokens = pixel_dev * dates_dev * lax.axis_size("tile") * lax.axis_size("date")
    grad_scale = 1.0 / math.sqrt(total_tokens)
    return (
        value_grad,
        input_grad,
        weight_sum * grad_scale,
        table_sum * grad_scale,
        head_sum * grad_scale,
    )


def solution(mesh):
    in_specs = (
        P("tile", "date", None),
        P("tile", "date", None),
        P("tile", "date", None),
        P("date"),
        P("tile", "date"),
        P(),
        P(),
        P(),
        P(),
        P(),
    )
    out_specs = (P("tile", "date", None), P("tile", "date", None), P(), P(), P())
    return jax.shard_map(
        on_device, mesh=mesh, in_specs=in_specs, out_specs=out_specs, check_vma=False
    )
```

profile of v0, /device:TPU:0, one launch (start us, length us, event | category | flops | bytes accessed | tf_op | source)
XLA Modules:
  0.0 223.1 jit_solution(16304670032210417332)
XLA Ops:
  7.2 0.7 broadcast_compare_fusion
  7.9 0.7 convert_element_type.158
  8.6 0.8 fusion.67
  9.4 0.1 broadcast_select_fusion
  9.4 0.9 add_convert_fusion.1
  10.3 0.3 fusion.7
  10.6 0.7 fusion.37
  11.3 0.6 copy.183
  12.0 6.3 %all-to-all-start.2 = ((bf16[8,4,8]{2,1,0:T(4,128)(2,1)}), bf16[8,4,8]{2,1,0:T(4,128)(2,1)S(1)}, u32[]{:S(2)}, u32[]{:S(2)}) async-start(bf16[8,4,8]{2,1,0:T(4,128)(2,1)} %copy.183), calls=%async_computation.2 | async-start | bytes 16384 | tf_op jit(solution)/shard_map/all_to_all | solution.py:96
  18.3 0.7 exponential_negate_fusion
  19.0 0.1 broadcast_in_dim.97
  19.1 0.6 copy.182
  19.7 4.2 %all-to-all-done.2 = bf16[8,4,8]{2,1,0:T(4,128)(2,1)S(1)} async-done(((bf16[8,4,8]{2,1,0:T(4,128)(2,1)}), bf16[8,4,8]{2,1,0:T(4,128)(2,1)S(1)}, u32[]{:S(2)}, u32[]{:S(2)}) %all-to-all-start.2) | async-done | bytes 544 | tf_op jit(solution)/shard_map/all_to_all | solution.py:96
  23.9 3.3 %all-to-all-start.1 = ((bf16[8,4,256]{2,1,0:T(4,128)(2,1)}), bf16[8,4,256]{2,1,0:T(4,128)(2,1)S(1)}, u32[]{:S(2)}, u32[]{:S(2)}) async-start(bf16[8,4,256]{2,1,0:T(4,128)(2,1)} %copy.182), calls=%async_computation.1 | async-start | bytes 32768 | tf_op jit(solution)/shard_map/all_to_all | solution.py:95
  27.3 0.1 copy.184
  27.4 0.2 exponential_multiply_fusion
  27.8 0.1 mul.285
  27.9 0.1 mul.279
  28.1 0.1 mul.276.clone
  28.3 4.6 %all-to-all-done.1 = bf16[8,4,256]{2,1,0:T(4,128)(2,1)S(1)} async-done(((bf16[8,4,256]{2,1,0:T(4,128)(2,1)}), bf16[8,4,256]{2,1,0:T(4,128)(2,1)S(1)}, u32[]{:S(2)}, u32[]{:S(2)}) %all-to-all-start.1) | async-done | bytes 16416 | tf_op jit(solution)/shard_map/all_to_all | solution.py:95
  32.8 3.4 %all-to-all-start = ((bf16[8,4,1024]{2,1,0:T(4,128)(2,1)}), bf16[8,4,1024]{2,1,0:T(4,128)(2,1)S(1)}, u32[]{:S(2)}, u32[]{:S(2)}) async-start(bf16[8,4,1024]{2,1,0:T(4,128)(2,1)} %param.12), calls=%async_computation | async-start | bytes 131072 | tf_op jit(solution)/shard_map/all_to_all | solution.py:94
  36.2 0.1 fusion.42
  36.3 0.2 convolution_bitcast_fusion.1
  36.5 5.6 %all-to-all-done = bf16[8,4,1024]{2,1,0:T(4,128)(2,1)S(1)} async-done(((bf16[8,4,1024]{2,1,0:T(4,128)(2,1)}), bf16[8,4,1024]{2,1,0:T(4,128)(2,1)S(1)}, u32[]{:S(2)}, u32[]{:S(2)}) %all-to-all-start) | async-done | bytes 65568 | tf_op jit(solution)/shard_map/all_to_all | solution.py:94
  42.0 3.4 %all-to-all-start.4 = ((bf16[8,4,1024]{2,1,0:T(4,128)(2,1)}), bf16[8,4,1024]{2,1,0:T(4,128)(2,1)S(1)}, u32[]{:S(2)}, u32[]{:S(2)}) async-start(bf16[8,4,1024]{2,1,0:T(4,128)(2,1)} %param.11), calls=%async_computation.4 | async-start | bytes 131072 | tf_op jit(solution)/shard_map/all_to_all | solution.py:93
  45.4 0.2 fusion.1
  45.7 5.6 %all-to-all-done.4 = bf16[8,4,1024]{2,1,0:T(4,128)(2,1)S(1)} async-done(((bf16[8,4,1024]{2,1,0:T(4,128)(2,1)}), bf16[8,4,1024]{2,1,0:T(4,128)(2,1)S(1)}, u32[]{:S(2)}, u32[]{:S(2)}) %all-to-all-start.4) | async-done | bytes 65568 | tf_op jit(solution)/shard_map/all_to_all | solution.py:93
  51.2 0.1 multiply_reduce_fusion
  51.5 0.2 convolution_bitcast_fusion.4
  51.8 0.4 multiply_reduce_fusion.2
  52.2 0.1 copy.207
  52.3 0.1 copy.203
  52.4 0.1 copy.204
  52.5 0.4 fusion.17
  52.9 0.1 convolution_bitcast_fusion.5
  53.0 0.2 fusion.5
  53.2 0.1 bitcast_add_fusion.1
  53.3 0.1 copy.205
  53.4 0.1 reduce_window_sum.30
  53.5 0.6 copy.208
  54.1 3.3 %all-to-all-start.6 = ((bf16[1,32,8]{2,0,1:T(2,128)(2,1)}), bf16[1,32,8]{2,0,1:T(2,128)(2,1)S(1)}, u32[]{:S(2)}, u32[]{:S(2)}) async-start(bf16[1,32,8]{2,0,1:T(2,128)(2,1)} %copy.208), calls=%async_computation.6 | async-start | bytes 32768 | tf_op jit(solution)/shard_map/all_to_all | solution.py:120
  57.5 0.2 fusion.6
  57.8 0.1 bitcast_reduce_fusion
  57.9 0.5 broadcast.253
  58.5 1.0 reduce.27
  59.5 0.7 reshape.655
  60.2 0.7 reduce.28
  60.9 0.6 reshape.657
  61.5 1.5 all-to-all-done.6
  63.1 3.5 %all-to-all-start.5 = ((bf16[8,2,512]{2,1,0:T(2,128)(2,1)}), bf16[8,2,512]{2,1,0:T(2,128)(2,1)S(1)}, u32[]{:S(2)}, u32[]{:S(2)}) async-start(bf16[8,2,512]{2,1,0:T(2,128)(2,1)} %reshape.657), calls=%async_computation.5 | async-start | bytes 32768 | tf_op jit(solution)/shard_map/all_to_all | solution.py:119
  66.6 0.1 fusion.65
  66.7 5.5 %all-to-all-done.5 = bf16[8,2,512]{2,1,0:T(2,128)(2,1)S(1)} async-done(((bf16[8,2,512]{2,1,0:T(2,128)(2,1)}), bf16[8,2,512]{2,1,0:T(2,128)(2,1)S(1)}, u32[]{:S(2)}, u32[]{:S(2)}) %all-to-all-start.5) | async-done | bytes 16416 | tf_op jit(solution)/shard_map/all_to_all | solution.py:119
  72.2 3.4 %all-to-all-start.3 = ((bf16[8,2,2048]{2,1,0:T(2,128)(2,1)}), bf16[8,2,2048]{2,1,0:T(2,128)(2,1)S(1)}, u32[]{:S(2)}, u32[]{:S(2)}) async-start(bf16[8,2,2048]{2,1,0:T(2,128)(2,1)} %reshape.655), calls=%async_computation.3 | async-start | bytes 131072 | tf_op jit(solution)/shard_map/all_to_all | solution.py:118
  75.6 0.1 bitcast_reduce_fusion.2
  75.8 0.2 select_reduce_fusion.1
  76.0 0.7 reshape.639
  76.7 1.3 convolution_bitcast_fusion
  78.0 41.1 %all-reduce.2 = (f32[2,1024]{1,0:T(2,128)S(1)}, f32[3,8]{1,0:T(4,128)S(1)}) all-reduce(f32[2,1024]{1,0:T(2,128)S(1)} %pad_maximum_fusion.1, f32[3,8]{1,0:T(4,128)S(1)} %pad_maximum_fusion.2), channel_id=1, replica_groups=mesh['tile'=4,'date'=8] {'tile','date'}, use_global_device_ids=true, to_apply=%region_12.13 | all-reduce | flops 2072 | bytes 16576 | tf_op jit(solution)/shard_map/psum | solution.py:138
  119.2 0.6 broadcast_multiply_fusion.2
  119.8 0.6 broadcast_multiply_fusion.3
  120.4 0.4 bitcast_reduce_fusion.1
  120.8 0.7 all_to_all.28
  121.5 92.4 %all-reduce.5.cloned.1.call-done = f32[1024,264]{0,1:T(8,128)} async-done(((f32[1024,264]{0,1:T(8,128)}), f32[1024,264]{0,1:T(8,128)}) %all-reduce.5.cloned.1.call-update) | async-done | bytes 1081360 | tf_op jit(solution)/shard_map/psum | solution.py:138
  213.9 2.3 %broadcast_multiply_fusion = f32[1024,264]{0,1:T(8,128)} fusion(f32[1024,264]{0,1:T(8,128)} %all-reduce.5.cloned.1.call-done), kind=kLoop, calls=%fused_computation.18 | loop fusion | flops 270336 | bytes 2162688 | tf_op jit(solution)/shard_map/mul | solution.py:146
  (48 shorter events, 1.0 us)
Async XLA Ops:
  7.2 3.1 %copy-start = (bf16[1024,264]{0,1:T(8,128)(2,1)S(1)}, bf16[1024,264]{0,1:T(8,128)(2,1)}, u32[]{:S(2)}) copy-start(bf16[1024,264]{0,1:T(8,128)(2,1)} %param.16) | copy-start | bytes 1622020
  12.0 11.9 %all-to-all-start.2 = ((bf16[8,4,8]{2,1,0:T(4,128)(2,1)}), bf16[8,4,8]{2,1,0:T(4,128)(2,1)S(1)}, u32[]{:S(2)}, u32[]{:S(2)}) async-start(bf16[8,4,8]{2,1,0:T(4,128)(2,1)} %copy.183), calls=%async_computation.2 | async-start | bytes 16384 | tf_op jit(solution)/shard_map/all_to_all | solution.py:96
  23.9 8.9 %all-to-all-start.1 = ((bf16[8,4,256]{2,1,0:T(4,128)(2,1)}), bf16[8,4,256]{2,1,0:T(4,128)(2,1)S(1)}, u32[]{:S(2)}, u32[]{:S(2)}) async-start(bf16[8,4,256]{2,1,0:T(4,128)(2,1)} %copy.182), calls=%async_computation.1 | async-start | bytes 32768 | tf_op jit(solution)/shard_map/all_to_all | solution.py:95
  32.8 9.2 %all-to-all-start = ((bf16[8,4,1024]{2,1,0:T(4,128)(2,1)}), bf16[8,4,1024]{2,1,0:T(4,128)(2,1)S(1)}, u32[]{:S(2)}, u32[]{:S(2)}) async-start(bf16[8,4,1024]{2,1,0:T(4,128)(2,1)} %param.12), calls=%async_computation | async-start | bytes 131072 | tf_op jit(solution)/shard_map/all_to_all | solution.py:94
  42.0 9.2 %all-to-all-start.4 = ((bf16[8,4,1024]{2,1,0:T(4,128)(2,1)}), bf16[8,4,1024]{2,1,0:T(4,128)(2,1)S(1)}, u32[]{:S(2)}, u32[]{:S(2)}) async-start(bf16[8,4,1024]{2,1,0:T(4,128)(2,1)} %param.11), calls=%async_computation.4 | async-start | bytes 131072 | tf_op jit(solution)/shard_map/all_to_all | solution.py:93
  45.4 6.4 %copy-start.2 = (f32[8]{0:T(128)S(1)}, f32[8]{0:T(128)}, u32[]{:S(2)}) copy-start(f32[8]{0:T(128)} %param.19) | copy-start | bytes 100
  51.7 1.8 copy-start.3
  52.4 14.2 %copy-start.1 = (f32[8]{0:T(128)S(1)}, f32[8]{0:T(128)}, u32[]{:S(2)}) copy-start(f32[8]{0:T(128)} %param.17) | copy-start | bytes 100
  54.1 8.9 %all-to-all-start.6 = ((bf16[1,32,8]{2,0,1:T(2,128)(2,1)}), bf16[1,32,8]{2,0,1:T(2,128)(2,1)S(1)}, u32[]{:S(2)}, u32[]{:S(2)}) async-start(bf16[1,32,8]{2,0,1:T(2,128)(2,1)} %copy.208), calls=%async_computation.6 | async-start | bytes 32768 | tf_op jit(solution)/shard_map/all_to_all | solution.py:120
  63.1 9.1 %all-to-all-start.5 = ((bf16[8,2,512]{2,1,0:T(2,128)(2,1)}), bf16[8,2,512]{2,1,0:T(2,128)(2,1)S(1)}, u32[]{:S(2)}, u32[]{:S(2)}) async-start(bf16[8,2,512]{2,1,0:T(2,128)(2,1)} %reshape.657), calls=%async_computation.5 | async-start | bytes 32768 | tf_op jit(solution)/shard_map/all_to_all | solution.py:119
  72.2 48.2 %all-to-all-start.3 = ((bf16[8,2,2048]{2,1,0:T(2,128)(2,1)}), bf16[8,2,2048]{2,1,0:T(2,128)(2,1)S(1)}, u32[]{:S(2)}, u32[]{:S(2)}) async-start(bf16[8,2,2048]{2,1,0:T(2,128)(2,1)} %reshape.655), calls=%async_computation.3 | async-start | bytes 131072 | tf_op jit(solution)/shard_map/all_to_all | solution.py:118
  75.6 138.3 %all-reduce.5.cloned.1.call-start = ((), (), s32[]{:S(2)}) async-start(), calls=%async_computation.7 | async-start | bytes 2162688 | tf_op jit(solution)/shard_map/psum | solution.py:138
Sparse Core Ops, SparseCore 0:
  82.4 131.4 all-reduce.4
where the time goes:
time: 224 us; the launch traced here: 223 us
  waiting for transfers between devices  119 us (53%)
  blocking collectives  41.1 us (18%)
  starting transfers between devices  26.6 us (12%)
  between operations  14.4 us (6%)
  other arithmetic  9.87 us (4%)
  local copies, waits for them, and re-layouts  7.73 us (3%)
  matrix products  3.93 us (2%)
    psum x1, waiting for transfers between devices, on_device(): lax.psum((weight_part, table_part, head_part), ('tile', 'date'))  92.4 us
    psum x1, blocking collectives, on_device(): lax.psum((weight_part, table_part, head_part), ('tile', 'date'))  41.1 us
    all_to_all x1, starting transfers between devices, on_device(): lax.all_to_all(step_sizes, 'date', split_axis=0, concat_axis=1, tiled=True)  6.33 us
    all_to_all x1, waiting for transfers between devices, on_device(): lax.all_to_all(head_input, 'date', split_axis=0, concat_axis=1, tiled=True)  5.56 us
    all_to_all x1, waiting for transfers between devices, on_device(): lax.all_to_all(out_grad, 'date', split_axis=0, concat_axis=1, tiled=True)  5.55 us
    all_to_all x1, waiting for transfers between devices, on_device(): lax.all_to_all(pair_series, 'date', split_axis=1, concat_axis=0, tiled=True)  5.51 us
    all_to_all x1, waiting for transfers between devices, on_device(): lax.all_to_all(pair_proj, 'date', split_axis=0, concat_axis=1, tiled=True)  4.56 us
  transfers between devices with their start and end apart: 8, of which 7 were waited for; matrix products, arithmetic and copies ran while one was open for 5% of the time, Pallas kernels for 0%

commit v1 on v0

v1 whole, which is shorter than its diff:
```python
import functools
import math

import jax
import jax.numpy as jnp
from jax import lax
from jax.experimental import pallas as pl
from jax.experimental.pallas import tpu as pltpu
from jax.sharding import PartitionSpec as P

NEG_FILL = -1e30
HIGHEST_PREC = lax.Precision.HIGHEST
F32 = jnp.float32
BF16 = jnp.bfloat16
LANES = 128
EXT = 384
SLAB_ROWS = 320
WIDE = SLAB_ROWS // 8


def nt(a, b, precision=None):
    return lax.dot_general(
        a, b, (((1,), (1,)), ((), ())), preferred_element_type=F32, precision=precision
    )


def nn(a, b, precision=None):
    return lax.dot_general(
        a, b, (((1,), (0,)), ((), ())), preferred_element_type=F32, precision=precision
    )


def tn(a, b):
    return lax.dot_general(a, b, (((0,), (0,)), ((), ())), preferred_element_type=F32)


def split(x):
    high = x.astype(BF16)
    return high, (x - high.astype(F32)).astype(BF16)


def series_kernel(heads, model_d, tiles, slab, recv, w_t, params, send, back, sel):
    length = recv.shape[0]
    width_p = model_d // heads
    states = (w_t.shape[0] - heads) // 2
    mixed = recv[:, :model_d]
    aux = recv[:, 3 * model_d :].astype(F32)
    gate = aux[:, 0:1]
    ids = aux[:, 1:2]
    bias = params[0:1, :heads]
    rate = -jnp.exp(params[1:2, :heads])
    projected = nt(mixed, w_t[...])
    keys = projected[:, :states].astype(BF16)
    reads = projected[:, states : 2 * states].astype(BF16)
    step_pre = projected[:, 2 * states :] + bias
    softplus = jnp.maximum(step_pre, 0.0) + jnp.log1p(jnp.exp(-jnp.abs(step_pre)))
    steps_b = (gate * softplus).astype(BF16)
    steps = steps_b.astype(F32)

    row = lax.broadcasted_iota(jnp.int32, (length, length), 0)
    col = lax.broadcasted_iota(jnp.int32, (length, length), 1)
    upper = col >= row
    upper_f = upper.astype(F32)
    eye = (col == row).astype(F32)
    lower_b = (row >= col).astype(BF16)
    head_row = lax.broadcasted_iota(jnp.int32, (heads, heads), 0)
    head_col = lax.broadcasted_iota(jnp.int32, (heads, heads), 1)
    eye_h = (head_row == head_col).astype(F32)
    rate_col = jnp.sum(eye_h * rate, axis=1, keepdims=True)
    log_col = nn(lower_b, steps_b) * rate
    steps_t = nt(eye_h.astype(BF16), steps_b).astype(BF16)
    log_row = nn(steps_t, upper.astype(BF16)) * rate_col
    scores_t = nt(keys, reads)

    pair_t = jnp.zeros((length, length), F32)
    weighted_cols, read_rows, skip_cols = [], [], []
    for h in range(heads):
        lo = model_d + h * width_p
        x_h = recv[:, lo : lo + width_p]
        g_h = recv[:, lo + model_d : lo + model_d + width_p]
        dt_h = steps[:, h : h + 1]
        gap = log_row[h : h + 1, :] - log_col[:, h : h + 1]
        decay = jnp.exp(jnp.where(upper, gap, NEG_FILL))
        cross = nt(x_h, g_h)
        mix = decay * scores_t
        pair_t = pair_t + decay * cross * dt_h
        both = mix * cross
        weighted = jnp.sum(both, axis=1, keepdims=True)
        weighted_cols.append(weighted)
        read_rows.append(jnp.sum(both * dt_h, axis=0, keepdims=True))
        skip_cols.append(jnp.sum(cross * eye, axis=1, keepdims=True))
        value = nn(mix.astype(BF16), g_h) * dt_h + params[2 + h : 3 + h, :width_p] * g_h.astype(F32)
        back[:, h * width_p : (h + 1) * width_p] = value.astype(BF16)

    weighted = jnp.concatenate(weighted_cols, axis=1)
    read_sum = jnp.concatenate(read_rows, axis=0)
    skip_terms = jnp.concatenate(skip_cols, axis=1)
    later = nt(upper_f, read_sum, HIGHEST_PREC) - nn(upper_f, steps * weighted, HIGHEST_PREC)
    step_grad = (weighted + rate * later).astype(BF16).astype(F32)
    decay_terms = steps * later * rate
    pair_b = pair_t.astype(BF16)
    grad_keys = nn(pair_b, reads)
    grad_reads = tn(pair_b, keys)
    raw = step_grad * gate * jax.nn.sigmoid(step_pre)
    parts = []
    for term in (raw, decay_terms, skip_terms):
        high, low = split(term)
        parts += [high.astype(F32), low.astype(F32)]
    tail = jnp.concatenate(
        parts + [jnp.zeros((length, EXT - 2 * states - 6 * heads), F32)], axis=1
    )
    ext = jnp.concatenate([grad_keys, grad_reads, tail], axis=1).astype(BF16)
    back[:, model_d:] = ext
    for t in range(tiles):
        send[t, :, :EXT] = ext
        send[t, :, EXT:] = recv[:, t * slab : (t + 1) * slab]
    ids_row = jnp.sum(eye * ids, axis=0, keepdims=True)
    sel[...] = jnp.concatenate([1.0 - ids_row, ids_row, jnp.zeros((14, length), F32)], axis=0).astype(
        BF16
    )


def lane_pad(x, width):
    if x.shape[1] == width:
        return x
    return jnp.concatenate([x, jnp.zeros((x.shape[0], width - x.shape[1]), x.dtype)], axis=1)


def sum_rows(sums):
    high = sums.astype(BF16).astype(F32)
    low = (sums - high).astype(BF16).astype(F32)
    rows = jnp.concatenate([high, low, jnp.zeros((4, EXT), F32)], axis=0)
    return [rows[:, b * LANES : (b + 1) * LANES] for b in range(EXT // LANES)]


def rows_sum(block):
    rows = jnp.concatenate([block[8 * b : 8 * b + 8, :] for b in range(EXT // LANES)], axis=1)
    return rows[0:2] + rows[2:4]


def slab_kernel(cols, core, recv, sel, keep, keep_sums, give):
    tiles, length, width = recv.shape
    slab = width - EXT
    half = slab // 2
    ext = recv[:, :, :EXT].reshape(tiles * length, EXT)
    tokens = recv[:, :, EXT:].reshape(tiles * length, slab)
    part = tn(ext, tokens)[:cols]
    sums = jnp.zeros((16, EXT), F32)
    for t in range(tiles):
        sums = sums + nn(sel[...], recv[t, :, :EXT])
    sums = sums[0:2]
    mine = core[0] == 0
    first = lane_pad(part[:, :half], LANES)
    second = lane_pad(part[:, half:], LANES)
    keep[...] = jnp.where(mine, first, second)
    keep_sums[...] = sums
    other = jnp.where(mine, second, first)
    give[...] = jnp.concatenate(
        [other, jnp.zeros((24, LANES), F32)] + sum_rows(sums) + [jnp.zeros((8, LANES), F32)], axis=0
    ).astype(BF16)


def join_kernel(cols, keep, keep_sums, got, pair, send):
    levels = send.shape[0]
    model_d = send.shape[2]
    total = keep[...] + got[:cols, :].astype(F32)
    sums = keep_sums[...] + rows_sum(got[288:312, :].astype(F32))
    sums_r = sum_rows(sums)
    for z in range(levels):
        rows = pair[z].astype(F32)
        ext = [rows[:, model_d + b * LANES : model_d + (b + 1) * LANES] for b in range(EXT // LANES)]
        tall = jnp.concatenate([total] + ext + sums_r + [jnp.zeros((8, LANES), F32)], axis=0)
        wide = jnp.concatenate([tall[k * WIDE : (k + 1) * WIDE] for k in range(8)], axis=1)
        send[z] = jnp.concatenate([wide, rows[:, :model_d]], axis=0).astype(BF16)


def total_kernel(tiles, recv, send, rest):
    levels = recv.shape[0]
    total = recv[0, :WIDE, :].astype(F32)
    for z in range(1, levels):
        total = total + recv[z, :WIDE, :].astype(F32)
    tall = jnp.concatenate([total[:, k * LANES : (k + 1) * LANES] for k in range(8)], axis=0)
    slab = tall[:272].astype(BF16)
    for t in range(tiles):
        send[t] = slab
    rest[...] = tall[288:312]


def local_kernel(heads, scale, recv, sums_in, w_t, value, inputs, table, head):
    levels = recv.shape[0]
    model_d = w_t.shape[1]
    cols = w_t.shape[0]
    w = w_t[...]
    ext_rows, value_rows = [], []
    for z in range(levels):
        block = recv[z].astype(F32)
        tall = jnp.concatenate([block[:WIDE, k * LANES : (k + 1) * LANES] for k in range(8)], axis=0)
        ext_rows.append(
            jnp.concatenate([tall[264 + 8 * b : 272 + 8 * b] for b in range(EXT // LANES)], axis=1)
        )
        value_rows.append(block[WIDE:])
    ext = jnp.concatenate(ext_rows, axis=0).astype(BF16)[:, :cols]
    value[...] = jnp.concatenate(value_rows, axis=0).astype(BF16)
    inputs[...] = nn(ext, w).astype(BF16)
    sums = rows_sum(sums_in[...])
    high, low = split(sums[:, :cols])
    table[...] = (nn(high, w) + nn(low, w)) * scale
    both = sums[0:1] + sums[1:2]
    at = cols - heads
    rows = []
    for k in (2, 0, 4):
        lo = at + k * heads
        rows.append(both[:, lo : lo + heads] + both[:, lo + heads : lo + 2 * heads])
    head[...] = jnp.concatenate(rows, axis=0) * scale


def gather_kernel(cols, half, scale, core, own, other, out):
    tiles = own.shape[0]
    mine = core[0] == 0
    for t in range(tiles):
        a = own[t].astype(F32)
        b = other[t].astype(F32)
        first = jnp.where(mine, a, b)[:cols, :half]
        second = jnp.where(mine, b, a)[:cols, :half]
        out[:, 2 * half * t : 2 * half * (t + 1)] = jnp.concatenate([first, second], axis=1) * scale


VMEM = pl.BlockSpec(memory_space=pltpu.VMEM)
SMEM = pl.BlockSpec(memory_space=pltpu.SMEM)


def call(kernel, outs, ins, smem=0):
    return pl.pallas_call(
        kernel,
        out_shape=[jax.ShapeDtypeStruct(s, d) for s, d in outs],
        in_specs=[SMEM] * smem + [VMEM] * (len(ins) - smem),
        out_specs=[VMEM] * len(outs),
        compiler_params=pltpu.CompilerParams(vmem_limit_bytes=48 * 1024 * 1024),
    )(*ins)


def on_device(
    layer_input,
    head_input,
    out_grad,
    sensor_ids,
    valid_mask,
    sensor_table,
    proj_weight,
    step_bias,
    decay_log,
    skip_gain,
):
    pixel_dev, dates_dev, model_d = layer_input.shape
    heads = step_bias.shape[0]
    cols = proj_weight.shape[1]
    tiles = lax.axis_size("tile")
    dates = lax.axis_size("date")
    assert pixel_dev == dates and dates % 2 == 0
    levels = dates // 2
    length = dates * dates_dev
    slab = model_d // tiles
    half = slab // 2
    core = lax.axis_index("date") % 2
    core_s = core.astype(jnp.int32).reshape(1)
    w_t = proj_weight.T
    scale = 1.0 / math.sqrt(pixel_dev * dates_dev * tiles * dates)
    swap = [(i, i ^ 1) for i in range(dates)]
    planes = [[2 * z + c for z in range(levels)] for c in range(2)]

    is_second = (sensor_ids == 1)[None, :, None]
    sensor_embed = jnp.where(is_second, sensor_table[1], sensor_table[0])
    mixed_in = (layer_input.astype(F32) + sensor_embed).astype(BF16)
    mask_col = valid_mask.astype(BF16)[:, :, None]
    ids_col = jnp.broadcast_to(is_second.astype(BF16), mask_col.shape)
    aux = jnp.concatenate(
        [mask_col, ids_col, jnp.zeros((pixel_dev, dates_dev, LANES - 2), BF16)], axis=-1
    )
    packed = jnp.concatenate([mixed_in, head_input, out_grad, aux], axis=-1)
    series = lax.all_to_all(packed, "date", split_axis=0, concat_axis=0, tiled=True).reshape(
        length, 3 * model_d + LANES
    )

    width_p = model_d // heads
    params = jnp.zeros((16, LANES), F32)
    params = params.at[0, :heads].set(step_bias).at[1, :heads].set(decay_log)
    params = params.at[2 : 2 + heads, :].set(jnp.broadcast_to(skip_gain[:, None], (heads, LANES)))
    send_t, back, sel = call(
        functools.partial(series_kernel, heads, model_d, tiles, slab),
        [
            ((tiles, length, EXT + slab), BF16),
            ((length, model_d + EXT), BF16),
            ((16, length), BF16),
        ],
        [series, w_t, params],
    )
    recv_t = lax.all_to_all(send_t, "tile", split_axis=0, concat_axis=0, tiled=True)
    back = back.reshape(levels, 2, dates_dev, model_d + EXT)
    back_own = lax.dynamic_index_in_dim(back, core, 1, keepdims=False)
    back_give = lax.dynamic_index_in_dim(back, 1 - core, 1, keepdims=False)
    back_got = lax.ppermute(back_give, "date", swap)
    is_first = core == 0
    pair = jnp.concatenate(
        [jnp.where(is_first, back_own, back_got), jnp.where(is_first, back_got, back_own)], axis=1
    )

    keep, keep_sums, give = call(
        functools.partial(slab_kernel, cols),
        [((cols, LANES), F32), ((2, EXT), F32), ((SLAB_ROWS, LANES), BF16)],
        [core_s, recv_t, sel],
        1,
    )
    got = lax.ppermute(give, "date", swap)
    (send_z,) = call(
        functools.partial(join_kernel, cols),
        [((levels, WIDE + 2 * dates_dev, model_d), BF16)],
        [keep, keep_sums, got, pair],
    )
    recv_z = lax.all_to_all(
        send_z, "date", split_axis=0, concat_axis=0, tiled=True, axis_index_groups=planes
    )
    send_g, sums = call(
        functools.partial(total_kernel, tiles),
        [((tiles, 272, LANES), BF16), ((24, LANES), F32)],
        [recv_z],
    )
    recv_g = lax.all_to_all(send_g, "tile", split_axis=0, concat_axis=0, tiled=True)
    value, inputs, table, head = call(
        functools.partial(local_kernel, heads, scale),
        [
            ((length, model_d), BF16),
            ((length, model_d), BF16),
            ((2, model_d), F32),
            ((3, heads), F32),
        ],
        [recv_z, sums, w_t],
    )
    other_g = lax.ppermute(recv_g, "date", swap)
    (weight_t,) = call(
        functools.partial(gather_kernel, cols, half, scale),
        [((cols, model_d), F32)],
        [core_s, recv_g, other_g],
        1,
    )
    return (
        value.reshape(pixel_dev, dates_dev, model_d),
        inputs.reshape(pixel_dev, dates_dev, model_d),
        weight_t.T,
        table,
        head,
    )


def solution(mesh):
    in_specs = (
        P("tile", "date", None),
        P("tile", "date", None),
        P("tile", "date", None),
        P("date"),
        P("tile", "date"),
        P(),
        P(),
        P(),
        P(),
        P(),
    )
    out_specs = (P("tile", "date", None), P("tile", "date", None), P(), P(), P())
    return jax.shard_map(
        on_device, mesh=mesh, in_specs=in_specs, out_specs=out_specs, check_vma=False
    )
```

time: 224 us -> 60.3 us (0.27)
  waiting for transfers between devices: 119 us -> 14.5 us
  blocking collectives: 41.1 us -> 23.2 us
  starting transfers between devices: 26.6 us -> 10.2 us
  between operations: 14.4 us -> 0.8 us
  other arithmetic: 9.87 us -> 2.44 us
  Pallas kernels: 0 us -> 4.17 us
  matrix products: 3.93 us -> 0 us
  local copies, waits for them, and re-layouts: 7.73 us -> 4.48 us
    psum x1 -> x0, waiting for transfers between devices: 92.4 us -> none  [on_device(): lax.psum((weight_part, table_part, head_part), ('tile', 'date'))]
    psum x1 -> x0, blocking collectives: 41.1 us -> none  [on_device(): lax.psum((weight_part, table_part, head_part), ('tile', 'date'))]
    all_to_all x0 -> x2, blocking collectives: none -> 23.2 us  [the longest x1 14.7 us: on_device(): lax.all_to_all(send_z, 'date', split_axis=0, concat_axis=0, tiled=True, a...]
    all_to_all x7 -> x2, starting transfers between devices: 26.5 us -> 10.1 us  [the longest x1 6.33 us: on_device(): lax.all_to_all(packed, 'date', split_axis=0, concat_axis=0, tiled=True)]
    all_to_all x7 -> x2, waiting for transfers between devices: 26.9 us -> 13.3 us  [the longest x1 8.13 us: on_device(): lax.all_to_all(packed, 'date', split_axis=0, concat_axis=0, tiled=True)]
    pallas_call x0 -> x6, Pallas kernels: none -> 4.17 us  [call(): pl.pallas_call(kernel, out_shape=[jax.ShapeDtypeStruct(s, d) for s, d in...]
    dot_general x12 -> x0, matrix products: 3.93 us -> none  [the longest x1 1.33 us: on_device(): lax.dot_general(flat_in, proj_grad, (((0,), (0,)), ((), ())), preferred_e...]
    mul x5 -> x0, other arithmetic: 3.71 us -> none  [the longest x1 2.34 us: on_device(): weight_sum * grad_scale]
  transfers between devices with their start and end apart: 8 -> 5, of which waited for: 7 -> 3; matrix products, arithmetic and copies ran while one was open for 5% -> 3% of each run, Pallas kernels for 0% -> 2%
where the time goes in v1:
time: 60.3 us; the launch traced here: 59.7 us
  blocking collectives  23.2 us (38%)
  waiting for transfers between devices  14.5 us (24%)
  starting transfers between devices  10.2 us (17%)
  local copies, waits for them, and re-layouts  4.48 us (7%)
  Pallas kernels  4.17 us (7%)
  other arithmetic  2.44 us (4%)
  between operations  0.8 us (1%)
    all_to_all x1, blocking collectives, on_device(): lax.all_to_all(send_z, 'date', split_axis=0, concat_axis=0, tiled=True, a...  14.7 us
    all_to_all x1, blocking collectives, on_device(): lax.all_to_all(send_g, 'tile', split_axis=0, concat_axis=0, tiled=True)  8.48 us
    all_to_all x1, waiting for transfers between devices, on_device(): lax.all_to_all(packed, 'date', split_axis=0, concat_axis=0, tiled=True)  8.13 us
    all_to_all x1, starting transfers between devices, on_device(): lax.all_to_all(packed, 'date', split_axis=0, concat_axis=0, tiled=True)  6.33 us
    all_to_all x1, waiting for transfers between devices, on_device(): lax.all_to_all(send_t, 'tile', split_axis=0, concat_axis=0, tiled=True)  5.16 us
    pallas_call x6, Pallas kernels, call(): pl.pallas_call(kernel, out_shape=[jax.ShapeDtypeStruct(s, d) for s, d in...  4.17 us
    all_to_all x1, starting transfers between devices, on_device(): lax.all_to_all(send_t, 'tile', split_axis=0, concat_axis=0, tiled=True)  3.73 us
    concatenate x1, local copies, waits for them, and re-layouts, on_device(): packed = jnp.concatenate([mixed_in, head_input, out_grad, aux], axis=-1)  1.72 us
  transfers between devices with their start and end apart: 5, of which 3 were waited for; matrix products, arithmetic and copies ran while one was open for 3% of the time, Pallas kernels for 2%

profile of v1, /device:TPU:0, one launch (start us, length us, event | category | flops | bytes accessed | tf_op | source)
XLA Modules:
  0.0 59.7 jit_solution(10797434727880298246)
XLA Ops:
  0.6 0.0 copy-start.1
  0.6 0.0 copy-start.3
  0.7 0.0 copy-start.2
  0.7 0.0 copy-start
  0.7 0.7 %convert_bitcast_fusion = bf16[8,4,1]{0,1,2:T(4,128)(2,1)S(1)} fusion(s32[8,4]{0,1:T(4,128)} %param.20), kind=kLoop, calls=%fused_computation.6 | loop fusion | flops 32 | bytes 192 | tf_op jit(solution)/shard_map/broadcast_in_dim | solution.py:274
  1.4 0.7 %fusion = (bf16[4]{0:T(256)(128)(2,1)S(1)}, pred[4]{0:T(512)(128)(4,1)S(1)}) fusion(s32[4]{0:T(128)} %param.19), kind=kLoop, calls=%fused_computation.8 | loop fusion | flops 8 | bytes 28 | tf_op jit(solution)/shard_map/convert_element_type | solution.py:275
  2.1 0.1 copy.15
  2.2 0.8 %fusion.1 = (f32[1,1024]{1,0:T(1,128)S(1)}, f32[1,1024]{1,0:T(1,128)S(1)}) fusion(f32[2,1024]{1,0:T(2,128)} %param.21), kind=kLoop, calls=%fused_computation.9 | loop fusion | bytes 16384 | tf_op jit(solution)/shard_map/slice | solution.py:272
  3.0 0.1 broadcast_select_fusion
  3.1 0.9 %add_convert_fusion = bf16[8,4,1024]{2,1,0:T(4,128)(2,1)S(1)} fusion(bf16[8,4,1024]{2,1,0:T(4,128)(2,1)} %param.16, f32[4,1024]{1,0:T(4,128)S(1)} %broadcast_select_fusion), kind=kLoop, calls=%fused_computation | loop fusion | flops 98304 | bytes 147456 | tf_op jit(solution)/shard_map/convert_element_type | solution.py:273
  3.9 0.1 broadcast_in_dim.37
  4.0 1.7 %concatenate.12 = bf16[8,4,3200]{2,1,0:T(4,128)(2,1)} concatenate(bf16[8,4,1024]{2,1,0:T(4,128)(2,1)S(1)} %add_convert_fusion, bf16[8,4,1024]{2,1,0:T(4,128)(2,1)} %param.17, bf16[8,4,1024]{2,1,0:T(4,128)(2,1)} %param.18, bf16[8,4,1]{2,1,0:T(4,128)(2,1)S(1)} %copy.15, bf16[8,4,1]{2,1,0:T(4,128)(2,1)S(1)} %broadcast_in_dim.37, bf16[8,4,126]{2,1,0:T(4,128)(2,1)S(1)} %broadcast_in_dim.38), dimensions={2} | concatenate | bytes 409600 | tf_op jit(solution)/shard_map/concatenate | solution.py:279
  5.7 6.3 %all-to-all-start = ((bf16[8,4,3200]{2,1,0:T(4,128)(2,1)}), bf16[8,4,3200]{2,1,0:T(4,128)(2,1)S(1)}, u32[]{:S(2)}, u32[]{:S(2)}) async-start(bf16[8,4,3200]{2,1,0:T(4,128)(2,1)} %concatenate.12), calls=%async_computation | async-start | bytes 409600 | tf_op jit(solution)/shard_map/all_to_all | solution.py:280
  12.1 0.0 copy-done.1
  12.1 0.0 copy-done.3
  12.1 0.2 scatter.11
  12.3 0.0 copy-done.2
  12.3 0.1 broadcast.100
  12.4 0.1 scatter.14.params
  12.4 8.1 %all-to-all-done = bf16[8,4,3200]{2,1,0:T(4,128)(2,1)S(1)} async-done(((bf16[8,4,3200]{2,1,0:T(4,128)(2,1)}), bf16[8,4,3200]{2,1,0:T(4,128)(2,1)S(1)}, u32[]{:S(2)}, u32[]{:S(2)}) %all-to-all-start) | async-done | bytes 204832 | tf_op jit(solution)/shard_map/all_to_all | solution.py:280
  20.6 0.1 reshape.160.recv
  20.6 0.0 copy-done
  20.6 1.7 %shard_map.137 = (bf16[4,32,640]{2,1,0:T(8,128)(2,1)}, bf16[32,1408]{1,0:T(8,128)(2,1)S(1)}, bf16[16,32]{1,0:T(8,128)(2,1)S(1)}) custom-call(bf16[32,3200]{1,0:T(8,128)(2,1)S(1)} %reshape.160.recv, bf16[264,1024]{1,0:T(8,128)(2,1)S(1)} %bitcast.18, f32[16,128]{1,0:T(8,128)S(1)} %scatter.14.params), custom_call_target="tpu_custom_call" | custom-call | tf_op jit(solution)/shard_map/pallas_call | solution.py:233
  22.4 0.1 collective-permute-start.1
  22.5 3.7 %all-to-all-start.1 = ((bf16[4,32,640]{2,1,0:T(8,128)(2,1)}), bf16[4,32,640]{2,1,0:T(8,128)(2,1)S(1)}, u32[]{:S(2)}, u32[]{:S(2)}) async-start(bf16[4,32,640]{2,1,0:T(8,128)(2,1)} %get-tuple-element.53), calls=%async_computation.1 | async-start | bytes 327680 | tf_op jit(solution)/shard_map/all_to_all | solution.py:297
  26.2 0.0 collective-permute-done.1
  26.3 5.2 %all-to-all-done.1.recv = bf16[4,32,640]{2,1,0:T(8,128)(2,1)S(1)} async-done(((bf16[4,32,640]{2,1,0:T(8,128)(2,1)}), bf16[4,32,640]{2,1,0:T(8,128)(2,1)S(1)}, u32[]{:S(2)}, u32[]{:S(2)}) %all-to-all-start.1) | async-done | bytes 163872 | tf_op jit(solution)/shard_map/all_to_all | solution.py:297
  31.5 0.3 shard_map.138
  31.7 0.1 collective-permute-start
  31.8 0.1 pad_maximum_fusion.pair
  31.9 1.2 %collective-permute-done.got = bf16[320,128]{1,0:T(8,128)(2,1)S(1)} collective-permute-done((bf16[320,128]{1,0:T(8,128)(2,1)S(1)}, bf16[320,128]{1,0:T(8,128)(2,1)S(1)}, u32[]{:S(2)}, u32[]{:S(2)}) %collective-permute-start) | collective-permute-done | bytes 81952 | tf_op jit(solution)/shard_map/ppermute | solution.py:313
  33.1 14.7 %all_to_all.20.recv = bf16[4,48,1024]{2,1,0:T(8,128)(2,1)S(1)} all-to-all(bf16[4,48,1024]{2,1,0:T(8,128)(2,1)S(1)} %shard_map.139), channel_id=1, replica_groups={{0,2,4,6},{1,3,5,7},{8,10,12,14},{9,11,13,15},{16,18,20,22},{17,19,21,2..., dimensions={0} | all-to-all | bytes 786432 | tf_op jit(solution)/shard_map/all_to_all | solution.py:319
  47.8 8.5 %all_to_all.21.own = bf16[4,272,128]{2,1,0:T(8,128)(2,1)S(1)} all-to-all(bf16[4,272,128]{2,1,0:T(8,128)(2,1)S(1)} %get-tuple-element.62), channel_id=1, replica_groups=mesh['tile'=4,'date'=8] {'tile'}, dimensions={0} | all-to-all | bytes 557056 | tf_op jit(solution)/shard_map/all_to_all | solution.py:327
  56.3 0.0 collective-permute-start.2
  56.3 1.0 %shard_map.141 = (bf16[32,1024]{1,0:T(8,128)(2,1)S(1)}, bf16[32,1024]{1,0:T(8,128)(2,1)S(1)}, f32[2,1024]{1,0:T(2,128)}, f32[3,8]{1,0:T(4,128)}) custom-call(bf16[4,48,1024]{2,1,0:T(8,128)(2,1)S(1)} %all_to_all.20.recv, f32[24,128]{1,0:T(8,128)S(1)} %get-tuple-element.59.sums_in, bf16[264,1024]{1,0:T(8,128)(2,1)S(1)} %bitcast.19), custom_call_target="tpu_custom_call" | custom-call | tf_op jit(solution)/shard_map/pallas_call | solution.py:233
  57.3 0.7 %reshape.164 = bf16[8,4,1024]{2,1,0:T(4,128)(2,1)} reshape(bf16[32,1024]{1,0:T(8,128)(2,1)S(1)} %get-tuple-element.60) | data formatting | bytes 131072 | tf_op jit(solution)/shard_map/reshape | solution.py:346
  58.0 0.7 %reshape.165 = bf16[8,4,1024]{2,1,0:T(4,128)(2,1)} reshape(bf16[32,1024]{1,0:T(8,128)(2,1)S(1)} %get-tuple-element.61) | data formatting | bytes 131072 | tf_op jit(solution)/shard_map/reshape | solution.py:347
  58.6 0.0 collective-permute-done.2.other
  58.7 1.1 %shard_map.142 = f32[264,1024]{1,0:T(8,128)} custom-call(s32[1]{0:T(128)} %bitcast.core, bf16[4,272,128]{2,1,0:T(8,128)(2,1)S(1)} %all_to_all.21.own, bf16[4,272,128]{2,1,0:T(8,128)(2,1)S(1)} %collective-permute-done.2.other), custom_call_target="tpu_custom_call" | custom-call | tf_op jit(solution)/shard_map/pallas_call | solution.py:233
  (7 shorter events, 0.2 us)
Async XLA Ops:
  0.6 11.4 %copy-start.1 = (f32[8]{0:T(128)S(1)}, f32[8]{0:T(128)}, u32[]{:S(2)}) copy-start(f32[8]{0:T(128)} %param.23) | copy-start | bytes 100
  0.6 11.4 %copy-start.3 = (f32[8]{0:T(128)S(1)}, f32[8]{0:T(128)}, u32[]{:S(2)}) copy-start(f32[8]{0:T(128)} %param.24) | copy-start | bytes 100
  0.7 11.6 %copy-start.2 = (f32[8]{0:T(128)S(1)}, f32[8]{0:T(128)}, u32[]{:S(2)}) copy-start(f32[8]{0:T(128)} %param.25) | copy-start | bytes 100
  0.7 20.0 %copy-start = (bf16[1024,264]{0,1:T(8,128)(2,1)S(1)}, bf16[1024,264]{0,1:T(8,128)(2,1)}, u32[]{:S(2)}) copy-start(bf16[1024,264]{0,1:T(8,128)(2,1)} %param.22) | copy-start | bytes 1622020
  5.7 14.8 %all-to-all-start = ((bf16[8,4,3200]{2,1,0:T(4,128)(2,1)}), bf16[8,4,3200]{2,1,0:T(4,128)(2,1)S(1)}, u32[]{:S(2)}, u32[]{:S(2)}) async-start(bf16[8,4,3200]{2,1,0:T(4,128)(2,1)} %concatenate.12), calls=%async_computation | async-start | bytes 409600 | tf_op jit(solution)/shard_map/all_to_all | solution.py:280
  22.4 3.8 %collective-permute-start.1 = (bf16[4,4,1408]{2,1,0:T(4,128)(2,1)S(1)}, bf16[4,4,1408]{2,1,0:T(4,128)(2,1)S(1)}, u32[]{:S(2)}, u32[]{:S(2)}) collective-permute-start(bf16[4,4,1408]{2,1,0:T(4,128)(2,1)S(1)} %dynamic-slice_bitcast_fusion), channel_id=1, source_target_pairs={{0,1},{1,0},{2,3},{3,2},{4,5},{5,4},{6,7},{7,6},{8,9},{9,8},{10,11... | collective-permute-start | bytes 135176 | tf_op jit(solution)/shard_map/ppermute | solution.py:301
  22.5 8.9 %all-to-all-start.1 = ((bf16[4,32,640]{2,1,0:T(8,128)(2,1)}), bf16[4,32,640]{2,1,0:T(8,128)(2,1)S(1)}, u32[]{:S(2)}, u32[]{:S(2)}) async-start(bf16[4,32,640]{2,1,0:T(8,128)(2,1)} %get-tuple-element.53), calls=%async_computation.1 | async-start | bytes 327680 | tf_op jit(solution)/shard_map/all_to_all | solution.py:297
  31.7 1.3 %collective-permute-start = (bf16[320,128]{1,0:T(8,128)(2,1)S(1)}, bf16[320,128]{1,0:T(8,128)(2,1)S(1)}, u32[]{:S(2)}, u32[]{:S(2)}) collective-permute-start(bf16[320,128]{1,0:T(8,128)(2,1)S(1)} %get-tuple-element.57), channel_id=1, source_target_pairs={{0,1},{1,0},{2,3},{3,2},{4,5},{5,4},{6,7},{7,6},{8,9},{9,8},{10,11... | collective-permute-start | bytes 245768 | tf_op jit(solution)/shard_map/ppermute | solution.py:313
  56.3 2.4 %collective-permute-start.2 = (bf16[4,272,128]{2,1,0:T(8,128)(2,1)S(1)}, bf16[4,272,128]{2,1,0:T(8,128)(2,1)S(1)}, u32[]{:S(2)}, u32[]{:S(2)}) collective-permute-start(bf16[4,272,128]{2,1,0:T(8,128)(2,1)S(1)} %all_to_all.21.own), channel_id=1, source_target_pairs={{0,1},{1,0},{2,3},{3,2},{4,5},{5,4},{6,7},{7,6},{8,9},{9,8},{10,11... | collective-permute-start | bytes 835592 | tf_op jit(solution)/shard_map/ppermute | solution.py:338

commit v2 on v1

--- a/solution.py
+++ b/solution.py
@@ -14,8 +14,6 @@
 BF16 = jnp.bfloat16
 LANES = 128
 EXT = 384
-SLAB_ROWS = 320
-WIDE = SLAB_ROWS // 8
 
 
 def nt(a, b, precision=None):
@@ -39,16 +37,19 @@
     return high, (x - high.astype(F32)).astype(BF16)
 
 
-def series_kernel(heads, model_d, tiles, slab, recv, w_t, params, send, back, sel):
+def series_kernel(heads, model_d, dates, core, recv, w_t, params, send, own, give, sel):
     length = recv.shape[0]
+    tiles, _, width = send.shape
+    slab = width - EXT
     width_p = model_d // heads
     states = (w_t.shape[0] - heads) // 2
     mixed = recv[:, :model_d]
     aux = recv[:, 3 * model_d :].astype(F32)
     gate = aux[:, 0:1]
     ids = aux[:, 1:2]
-    bias = params[0:1, :heads]
-    rate = -jnp.exp(params[1:2, :heads])
+    bias = params[:, :heads]
+    rate = -jnp.exp(params[:, heads : 2 * heads])
+    skip = params[:, 2 * heads : 3 * heads]
     projected = nt(mixed, w_t[...])
     keys = projected[:, :states].astype(BF16)
     reads = projected[:, states : 2 * states].astype(BF16)
@@ -73,7 +74,7 @@
     scores_t = nt(keys, reads)
 
     pair_t = jnp.zeros((length, length), F32)
-    weighted_cols, read_rows, skip_cols = [], [], []
+    value_parts, weighted_cols, read_rows, skip_cols = [], [], [], []
     for h in range(heads):
         lo = model_d + h * width_p
         x_h = recv[:, lo : lo + width_p]
@@ -89,8 +90,7 @@
         weighted_cols.append(weighted)
         read_rows.append(jnp.sum(both * dt_h, axis=0, keepdims=True))
         skip_cols.append(jnp.sum(cross * eye, axis=1, keepdims=True))
-        value = nn(mix.astype(BF16), g_h) * dt_h + params[2 + h : 3 + h, :width_p] * g_h.astype(F32)
-        back[:, h * width_p : (h + 1) * width_p] = value.astype(BF16)
+        value_parts.append(nn(mix.astype(BF16), g_h) * dt_h + skip[:, h : h + 1] * g_h.astype(F32))
 
     weighted = jnp.concatenate(weighted_cols, axis=1)
     read_sum = jnp.concatenate(read_rows, axis=0)
@@ -109,8 +109,17 @@
     tail = jnp.concatenate(
         parts + [jnp.zeros((length, EXT - 2 * states - 6 * heads), F32)], axis=1
     )
-    ext = jnp.concatenate([grad_keys, grad_reads, tail], axis=1).astype(BF16)
-    back[:, model_d:] = ext
+    ext_f = jnp.concatenate([grad_keys, grad_reads, tail], axis=1)
+    ext = ext_f.astype(BF16)
+    back = jnp.concatenate(value_parts + [ext_f], axis=1)
+    first = core[0] == 0
+    own_rows, give_rows = [], []
+    for at in range(0, length, 2 * dates):
+        a, b = back[at : at + dates], back[at + dates : at + 2 * dates]
+        own_rows.append(jnp.where(first, a, b))
+        give_rows.append(jnp.where(first, b, a))
+    own[...] = jnp.concatenate(own_rows, axis=0).astype(BF16)
+    give[...] = jnp.concatenate(give_rows, axis=0).astype(BF16)
     for t in range(tiles):
         send[t, :, :EXT] = ext
         send[t, :, EXT:] = recv[:, t * slab : (t + 1) * slab]
@@ -118,6 +127,40 @@
     sel[...] = jnp.concatenate([1.0 - ids_row, ids_row, jnp.zeros((14, length), F32)], axis=0).astype(
         BF16
     )
+
+
+def pack_kernel(ids_in, mask_in, table_in, layer, values, cotangent, out, ids, mask_t, table, layer_v, packed, sems):
+    pixels, dates, model_d = layer.shape
+    small = [
+        pltpu.make_async_copy(ids_in, ids, sems.at[0]),
+        pltpu.make_async_copy(mask_in, mask_t, sems.at[1]),
+        pltpu.make_async_copy(table_in, table, sems.at[2]),
+        pltpu.make_async_copy(layer, layer_v, sems.at[3]),
+    ]
+    large = [
+        pltpu.make_async_copy(values, packed.at[:, :, model_d : 2 * model_d], sems.at[4]),
+        pltpu.make_async_copy(cotangent, packed.at[:, :, 2 * model_d : 3 * model_d], sems.at[5]),
+    ]
+    for copy in small + large:
+        copy.start()
+    for copy in small:
+        copy.wait()
+    rows = [jnp.where(ids[i] == 1, table[1:2, :], table[0:1, :]) for i in range(dates)]
+    embed = jnp.concatenate(rows, axis=0)
+    row = lax.broadcasted_iota(jnp.int32, (dates, LANES), 0)
+    lane = lax.broadcasted_iota(jnp.int32, (dates, LANES), 1)
+    second = jnp.zeros((dates, LANES), F32)
+    for i in range(dates):
+        second = jnp.where((row == i) & (lane == 1), (ids[i] == 1).astype(F32), second)
+    gate = mask_t[...].astype(F32)
+    for p in range(pixels):
+        packed[p, :, 3 * model_d :] = jnp.where(lane == 0, gate[:, p : p + 1], second).astype(BF16)
+        packed[p, :, :model_d] = (layer_v[p].astype(F32) + embed).astype(BF16)
+    for copy in large:
+        copy.wait()
+    store = pltpu.make_async_copy(packed, out, sems.at[0])
+    store.start()
+    store.wait()
 
 
 def lane_pad(x, width):
@@ -156,53 +199,62 @@
     keep_sums[...] = sums
     other = jnp.where(mine, second, first)
     give[...] = jnp.concatenate(
-        [other, jnp.zeros((24, LANES), F32)] + sum_rows(sums) + [jnp.zeros((8, LANES), F32)], axis=0
+        [other] + sum_rows(sums), axis=0
     ).astype(BF16)
 
 
-def join_kernel(cols, keep, keep_sums, got, pair, send):
+def join_kernel(cols, dates, core, keep, keep_sums, got, own, other, send):
     levels = send.shape[0]
-    model_d = send.shape[2]
+    first = core[0] == 0
+    model_d = own.shape[1] - EXT
     total = keep[...] + got[:cols, :].astype(F32)
-    sums = keep_sums[...] + rows_sum(got[288:312, :].astype(F32))
-    sums_r = sum_rows(sums)
+    sums = sum_rows(keep_sums[...] + rows_sum(got[cols : cols + 24, :].astype(F32)))
+    pair_sums = jnp.concatenate([sums[0][:4], sums[1][:4]], axis=0)
+    mine, theirs = own[...].astype(F32), other[...].astype(F32)
+    firsts, seconds = jnp.where(first, mine, theirs), jnp.where(first, theirs, mine)
+    lane = lax.broadcasted_iota(jnp.int32, (8, LANES), 1)
+    last = pltpu.roll(sums[2], 64, 1)
+    pad = [jnp.zeros((8, LANES), F32)] * ((send.shape[1] - cols - 32) // 8 - model_d // LANES)
     for z in range(levels):
-        rows = pair[z].astype(F32)
+        at = z * dates
+        rows = jnp.concatenate([firsts[at : at + dates], seconds[at : at + dates]], axis=0)
         ext = [rows[:, model_d + b * LANES : model_d + (b + 1) * LANES] for b in range(EXT // LANES)]
-        tall = jnp.concatenate([total] + ext + sums_r + [jnp.zeros((8, LANES), F32)], axis=0)
-        wide = jnp.concatenate([tall[k * WIDE : (k + 1) * WIDE] for k in range(8)], axis=1)
-        send[z] = jnp.concatenate([wide, rows[:, :model_d]], axis=0).astype(BF16)
-
-
-def total_kernel(tiles, recv, send, rest):
+        misc = jnp.where(lane < 64, ext[2], last)
+        value = [rows[:, b * LANES : (b + 1) * LANES] for b in range(model_d // LANES)]
+        send[z] = jnp.concatenate([total, ext[0], ext[1], misc, pair_sums] + value + pad, axis=0).astype(BF16)
+
+
+def total_kernel(cols, recv, send, rest):
     levels = recv.shape[0]
-    total = recv[0, :WIDE, :].astype(F32)
+    total = recv[0].astype(F32)
     for z in range(1, levels):
-        total = total + recv[z, :WIDE, :].astype(F32)
-    tall = jnp.concatenate([total[:, k * LANES : (k + 1) * LANES] for k in range(8)], axis=0)
-    slab = tall[:272].astype(BF16)
-    for t in range(tiles):
+        total = total + recv[z].astype(F32)
+    slab = total[:272].astype(BF16)
+    for t in range(send.shape[0]):
         send[t] = slab
-    rest[...] = tall[288:312]
-
-
-def local_kernel(heads, scale, recv, sums_in, w_t, value, inputs, table, head):
+    rest[...] = total[cols + 16 : cols + 32]
+
+
+def local_kernel(heads, scale, recv, rest, w_t, value, inputs, table, head):
     levels = recv.shape[0]
     model_d = w_t.shape[1]
     cols = w_t.shape[0]
+    dates = value.shape[1]
     w = w_t[...]
-    ext_rows, value_rows = [], []
+    ext_rows = []
     for z in range(levels):
-        block = recv[z].astype(F32)
-        tall = jnp.concatenate([block[:WIDE, k * LANES : (k + 1) * LANES] for k in range(8)], axis=0)
-        ext_rows.append(
-            jnp.concatenate([tall[264 + 8 * b : 272 + 8 * b] for b in range(EXT // LANES)], axis=1)
-        )
-        value_rows.append(block[WIDE:])
-    ext = jnp.concatenate(ext_rows, axis=0).astype(BF16)[:, :cols]
-    value[...] = jnp.concatenate(value_rows, axis=0).astype(BF16)
-    inputs[...] = nn(ext, w).astype(BF16)
-    sums = rows_sum(sums_in[...])
+        rows = recv[z].astype(F32)
+        ext_rows.append(jnp.concatenate([rows[cols + 8 * b : cols + 8 * b + 8] for b in range(3)], axis=1))
+        at = cols + 32
+        values = jnp.concatenate([rows[at + 8 * b : at + 8 * b + 8] for b in range(model_d // LANES)], axis=1)
+        for c in range(2):
+            value[2 * z + c] = values[c * dates : (c + 1) * dates].astype(BF16)
+    grads = nn(jnp.concatenate(ext_rows, axis=0).astype(BF16)[:, :cols], w)
+    for p in range(2 * levels):
+        inputs[p] = grads[p * dates : (p + 1) * dates].astype(BF16)
+    last = pltpu.roll(rest[0:8, :], 64, 1)
+    sums = jnp.concatenate([rest[8:12, :], rest[12:16, :], last[0:4]], axis=1)
+    sums = sums[0:2] + sums[2:4]
     high, low = split(sums[:, :cols])
     table[...] = (nn(high, w) + nn(low, w)) * scale
     both = sums[0:1] + sums[1:2]
@@ -227,6 +279,7 @@
 
 VMEM = pl.BlockSpec(memory_space=pltpu.VMEM)
 SMEM = pl.BlockSpec(memory_space=pltpu.SMEM)
+HBM = pl.BlockSpec(memory_space=pltpu.HBM)
 
 
 def call(kernel, outs, ins, smem=0):
@@ -268,72 +321,72 @@
     swap = [(i, i ^ 1) for i in range(dates)]
     planes = [[2 * z + c for z in range(levels)] for c in range(2)]
 
-    is_second = (sensor_ids == 1)[None, :, None]
-    sensor_embed = jnp.where(is_second, sensor_table[1], sensor_table[0])
-    mixed_in = (layer_input.astype(F32) + sensor_embed).astype(BF16)
-    mask_col = valid_mask.astype(BF16)[:, :, None]
-    ids_col = jnp.broadcast_to(is_second.astype(BF16), mask_col.shape)
-    aux = jnp.concatenate(
-        [mask_col, ids_col, jnp.zeros((pixel_dev, dates_dev, LANES - 2), BF16)], axis=-1
-    )
-    packed = jnp.concatenate([mixed_in, head_input, out_grad, aux], axis=-1)
+    packed = pl.pallas_call(
+        pack_kernel,
+        out_shape=jax.ShapeDtypeStruct((pixel_dev, dates_dev, 3 * model_d + LANES), BF16),
+        in_specs=[HBM] * 6,
+        out_specs=HBM,
+        scratch_shapes=[
+            pltpu.SMEM((dates_dev,), jnp.int32),
+            pltpu.VMEM((dates_dev, pixel_dev), jnp.int32),
+            pltpu.VMEM((2, model_d), F32),
+            pltpu.VMEM((pixel_dev, dates_dev, model_d), BF16),
+            pltpu.VMEM((pixel_dev, dates_dev, 3 * model_d + LANES), BF16),
+            pltpu.SemaphoreType.DMA((6,)),
+        ],
+        compiler_params=pltpu.CompilerParams(vmem_limit_bytes=64 * 1024 * 1024),
+    )(sensor_ids, valid_mask.T, sensor_table, layer_input, head_input, out_grad)
     series = lax.all_to_all(packed, "date", split_axis=0, concat_axis=0, tiled=True).reshape(
         length, 3 * model_d + LANES
     )
 
-    width_p = model_d // heads
-    params = jnp.zeros((16, LANES), F32)
-    params = params.at[0, :heads].set(step_bias).at[1, :heads].set(decay_log)
-    params = params.at[2 : 2 + heads, :].set(jnp.broadcast_to(skip_gain[:, None], (heads, LANES)))
-    send_t, back, sel = call(
-        functools.partial(series_kernel, heads, model_d, tiles, slab),
+    rows_core = length // 2
+    send_t, own, give_rows, sel = call(
+        functools.partial(series_kernel, heads, model_d, dates_dev),
         [
             ((tiles, length, EXT + slab), BF16),
-            ((length, model_d + EXT), BF16),
+            ((rows_core, model_d + EXT), BF16),
+            ((rows_core, model_d + EXT), BF16),
             ((16, length), BF16),
         ],
-        [series, w_t, params],
+        [core_s, series, w_t, jnp.concatenate([step_bias, decay_log, skip_gain])[None]],
+        1,
     )
     recv_t = lax.all_to_all(send_t, "tile", split_axis=0, concat_axis=0, tiled=True)
-    back = back.reshape(levels, 2, dates_dev, model_d + EXT)
-    back_own = lax.dynamic_index_in_dim(back, core, 1, keepdims=False)
-    back_give = lax.dynamic_index_in_dim(back, 1 - core, 1, keepdims=False)
-    back_got = lax.ppermute(back_give, "date", swap)
-    is_first = core == 0
-    pair = jnp.concatenate(
-        [jnp.where(is_first, back_own, back_got), jnp.where(is_first, back_got, back_own)], axis=1
-    )
-
+    give_rows, recv_t = lax.optimization_barrier((give_rows, recv_t))
+    other = lax.ppermute(give_rows, "date", swap)
     keep, keep_sums, give = call(
         functools.partial(slab_kernel, cols),
-        [((cols, LANES), F32), ((2, EXT), F32), ((SLAB_ROWS, LANES), BF16)],
+        [((cols, LANES), F32), ((2, EXT), F32), ((cols + 24, LANES), BF16)],
         [core_s, recv_t, sel],
         1,
     )
     got = lax.ppermute(give, "date", swap)
+    rows_z = -(-(cols + 32 + model_d // 16) // 16) * 16
     (send_z,) = call(
-        functools.partial(join_kernel, cols),
-        [((levels, WIDE + 2 * dates_dev, model_d), BF16)],
-        [keep, keep_sums, got, pair],
+        functools.partial(join_kernel, cols, dates_dev),
+        [((levels, rows_z, LANES), BF16)],
+        [core_s, keep, keep_sums, got, own, other],
+        1,
     )
     recv_z = lax.all_to_all(
         send_z, "date", split_axis=0, concat_axis=0, tiled=True, axis_index_groups=planes
     )
-    send_g, sums = call(
-        functools.partial(total_kernel, tiles),
-        [((tiles, 272, LANES), BF16), ((24, LANES), F32)],
+    send_g, rest = call(
+        functools.partial(total_kernel, cols),
+        [((tiles, 272, LANES), BF16), ((16, LANES), F32)],
         [recv_z],
     )
     recv_g = lax.all_to_all(send_g, "tile", split_axis=0, concat_axis=0, tiled=True)
     value, inputs, table, head = call(
         functools.partial(local_kernel, heads, scale),
         [
-            ((length, model_d), BF16),
-            ((length, model_d), BF16),
+            ((pixel_dev, dates_dev, model_d), BF16),
+            ((pixel_dev, dates_dev, model_d), BF16),
             ((2, model_d), F32),
             ((3, heads), F32),
         ],
-        [recv_z, sums, w_t],
+        [recv_z, rest, w_t],
     )
     other_g = lax.ppermute(recv_g, "date", swap)
     (weight_t,) = call(
@@ -343,8 +396,8 @@
         1,
     )
     return (
-        value.reshape(pixel_dev, dates_dev, model_d),
-        inputs.reshape(pixel_dev, dates_dev, model_d),
+        value,
+        inputs,
         weight_t.T,
         table,
         head,

time: 60.3 us -> 55.5 us (0.920)
  blocking collectives: 23.2 us -> 32 us
  waiting for transfers between devices: 14.5 us -> 9.16 us
  local copies, waits for them, and re-layouts: 4.48 us -> 0.06 us
  starting transfers between devices: 10.2 us -> 7.04 us
  other arithmetic: 2.44 us -> 0.76 us
  Pallas kernels: 4.17 us -> 5.48 us
    all_to_all x0 -> x1, blocking collectives: none -> 8.98 us  [on_device(): lax.all_to_all(send_t, 'tile', split_axis=0, concat_axis=0, tiled=True)]
    all_to_all x1 -> x0, waiting for transfers between devices: 5.16 us -> none  [on_device(): lax.all_to_all(send_t, 'tile', split_axis=0, concat_axis=0, tiled=True)]
    all_to_all x1 -> x0, starting transfers between devices: 3.73 us -> none  [on_device(): lax.all_to_all(send_t, 'tile', split_axis=0, concat_axis=0, tiled=True)]
    concatenate x1 -> x0, local copies, waits for them, and re-layouts: 1.72 us -> none  [on_device(): packed = jnp.concatenate([mixed_in, head_input, out_grad, aux], axis=-1)]
    pallas_call x0 -> x1, Pallas kernels: none -> 1.69 us  [on_device(): pl.pallas_call(pack_kernel, out_shape=jax.ShapeDtypeStruct((pixel_dev, da...]
    convert_element_type x2 -> x0, other arithmetic: 1.53 us -> none  [the longest x1 0.87 us: on_device(): mixed_in = (layer_input.astype(F32) + sensor_embed).astype(BF16)]
    reshape x3 -> x0, local copies, waits for them, and re-layouts: 1.35 us -> none  [the longest x1 0.66 us: on_device(): value.reshape(pixel_dev, dates_dev, model_d)]
    ppermute x1, waiting for transfers between devices: 1.21 us -> 0.01 us  [on_device(): got = lax.ppermute(give, 'date', swap)]
  transfers between devices with their start and end apart: 5 -> 4, of which waited for: 3 -> 3; matrix products, arithmetic and copies ran while one was open for 3% -> 1% of each run, Pallas kernels for 2% -> 2%
where the time goes in v2:
time: 55.5 us; the launch traced here: 55.1 us
  blocking collectives  32 us (58%)
  waiting for transfers between devices  9.16 us (17%)
  starting transfers between devices  7.04 us (13%)
  Pallas kernels  5.48 us (10%)
  other arithmetic  0.76 us (1%)
  between operations  0.69 us (1%)
    all_to_all x1, blocking collectives, on_device(): lax.all_to_all(send_z, 'date', split_axis=0, concat_axis=0, tiled=True, a...  14.5 us
    all_to_all x1, blocking collectives, on_device(): lax.all_to_all(send_t, 'tile', split_axis=0, concat_axis=0, tiled=True)  8.98 us
    all_to_all x1, blocking collectives, on_device(): lax.all_to_all(send_g, 'tile', split_axis=0, concat_axis=0, tiled=True)  8.48 us
    all_to_all x1, waiting for transfers between devices, on_device(): lax.all_to_all(packed, 'date', split_axis=0, concat_axis=0, tiled=True)  7.75 us
    all_to_all x1, starting transfers between devices, on_device(): lax.all_to_all(packed, 'date', split_axis=0, concat_axis=0, tiled=True)  6.47 us
    pallas_call x6, Pallas kernels, call(): pl.pallas_call(kernel, out_shape=[jax.ShapeDtypeStruct(s, d) for s, d in...  3.79 us
    pallas_call x1, Pallas kernels, on_device(): pl.pallas_call(pack_kernel, out_shape=jax.ShapeDtypeStruct((pixel_dev, da...  1.69 us
  transfers between devices with their start and end apart: 4, of which 3 were waited for; matrix products, arithmetic and copies ran while one was open for 1% of the time, Pallas kernels for 2%

profile of v2, /device:TPU:0, one launch (start us, length us, event | category | flops | bytes accessed | tf_op | source)
XLA Modules:
  0.0 55.1 jit_solution(14523898886368034957)
XLA Ops:
  0.6 1.7 %shard_map.137 = bf16[8,4,3200]{2,1,0:T(4,128)(2,1)} custom-call(s32[4]{0:T(128)} %ids_in.1, s32[4,8]{1,0:T(4,128)} %bitcast.9, f32[2,1024]{1,0:T(2,128)} %table_in.1, bf16[8,4,1024]{2,1,0:T(4,128)(2,1)} %layer.1, bf16[8,4,1024]{2,1,0:T(4,128)(2,1)} %values.1, bf16[8,4,1024]{2,1,0:T(4,128)(2,1)} %cotangent.1), custom_call_target="tpu_custom_call" | custom-call | tf_op jit(solution)/shard_map/pallas_call | solution.py:324
  2.3 0.0 copy-start
  2.3 6.5 %all-to-all-start = ((bf16[8,4,3200]{2,1,0:T(4,128)(2,1)}), bf16[8,4,3200]{2,1,0:T(4,128)(2,1)S(1)}, u32[]{:S(2)}, u32[]{:S(2)}) async-start(bf16[8,4,3200]{2,1,0:T(4,128)(2,1)} %shard_map.137), calls=%async_computation | async-start | bytes 409600 | tf_op jit(solution)/shard_map/all_to_all | solution.py:339
  8.8 0.8 %maximum_bitcast_fusion.params = f32[1,24]{1,0:T(1,128)S(1)} fusion(f32[8]{0:T(128)} %param.19, f32[8]{0:T(128)} %param.18, f32[8]{0:T(128)} %param.17), kind=kLoop, calls=%fused_computation | loop fusion | flops 48 | bytes 192 | tf_op jit(solution)/shard_map/broadcast_in_dim | solution.py:352
  9.6 7.8 %all-to-all-done = bf16[8,4,3200]{2,1,0:T(4,128)(2,1)S(1)} async-done(((bf16[8,4,3200]{2,1,0:T(4,128)(2,1)}), bf16[8,4,3200]{2,1,0:T(4,128)(2,1)S(1)}, u32[]{:S(2)}, u32[]{:S(2)}) %all-to-all-start) | async-done | bytes 204832 | tf_op jit(solution)/shard_map/all_to_all | solution.py:339
  17.3 0.1 reshape.17.recv
  17.4 0.0 copy-done
  17.4 1.3 %shard_map.138 = (bf16[4,32,640]{2,1,0:T(8,128)(2,1)S(1)}, bf16[16,1408]{1,0:T(8,128)(2,1)S(1)}, bf16[16,1408]{1,0:T(8,128)(2,1)S(1)}, bf16[16,32]{1,0:T(8,128)(2,1)S(1)}) custom-call(s32[1]{0:T(128)} %bitcast.core, bf16[32,3200]{1,0:T(8,128)(2,1)S(1)} %reshape.17.recv, bf16[264,1024]{1,0:T(8,128)(2,1)S(1)} %bitcast.6, f32[1,24]{1,0:T(1,128)S(1)} %maximum_bitcast_fusion.params), custom_call_target="tpu_custom_call" | custom-call | tf_op jit(solution)/shard_map/pallas_call | solution.py:286
  18.7 9.0 %all_to_all.20.recv = bf16[4,32,640]{2,1,0:T(8,128)(2,1)S(1)} all-to-all(bf16[4,32,640]{2,1,0:T(8,128)(2,1)S(1)} %get-tuple-element.21), channel_id=1, replica_groups=mesh['tile'=4,'date'=8] {'tile'}, dimensions={0} | all-to-all | bytes 327680 | tf_op jit(solution)/shard_map/all_to_all | solution.py:355
  27.7 0.3 shard_map.139
  27.9 0.1 collective-permute-start
  28.0 0.5 collective-permute-start.1
  28.5 0.9 %collective-permute-done.1.other = bf16[16,1408]{1,0:T(8,128)(2,1)S(1)} collective-permute-done((bf16[16,1408]{1,0:T(8,128)(2,1)S(1)}, bf16[16,1408]{1,0:T(8,128)(2,1)S(1)}, u32[]{:S(2)}, u32[]{:S(2)}) %collective-permute-start.1) | collective-permute-done | bytes 45088 | tf_op jit(solution)/shard_map/ppermute | solution.py:357
  29.4 0.0 collective-permute-done.got
  29.4 0.1 shard_map.140
  29.5 14.5 %all_to_all.21.recv = bf16[4,368,128]{2,1,0:T(8,128)(2,1)S(1)} all-to-all(bf16[4,368,128]{2,1,0:T(8,128)(2,1)S(1)} %shard_map.140), channel_id=1, replica_groups={{0,2,4,6},{1,3,5,7},{8,10,12,14},{9,11,13,15},{16,18,20,22},{17,19,21,2..., dimensions={0} | all-to-all | bytes 753664 | tf_op jit(solution)/shard_map/all_to_all | solution.py:372
  44.0 8.5 %all_to_all.22.own = bf16[4,272,128]{2,1,0:T(8,128)(2,1)S(1)} all-to-all(bf16[4,272,128]{2,1,0:T(8,128)(2,1)S(1)} %get-tuple-element.32), channel_id=1, replica_groups=mesh['tile'=4,'date'=8] {'tile'}, dimensions={0} | all-to-all | bytes 557056 | tf_op jit(solution)/shard_map/all_to_all | solution.py:380
  52.5 0.0 collective-permute-start.2
  52.5 1.0 %shard_map.142 = (bf16[8,4,1024]{2,1,0:T(4,128)(2,1)}, bf16[8,4,1024]{2,1,0:T(4,128)(2,1)}, f32[2,1024]{1,0:T(2,128)}, f32[3,8]{1,0:T(4,128)}) custom-call(bf16[4,368,128]{2,1,0:T(8,128)(2,1)S(1)} %all_to_all.21.recv, f32[16,128]{1,0:T(8,128)S(1)} %get-tuple-element.29.rest, bf16[264,1024]{1,0:T(8,128)(2,1)S(1)} %bitcast.7), custom_call_target="tpu_custom_call" | custom-call | tf_op jit(solution)/shard_map/pallas_call | solution.py:286
  53.5 0.5 collective-permute-done.2.other
  54.1 1.1 %shard_map.143 = f32[264,1024]{1,0:T(8,128)} custom-call(s32[1]{0:T(128)} %bitcast.core, bf16[4,272,128]{2,1,0:T(8,128)(2,1)S(1)} %all_to_all.22.own, bf16[4,272,128]{2,1,0:T(8,128)(2,1)S(1)} %collective-permute-done.2.other), custom_call_target="tpu_custom_call" | custom-call | tf_op jit(solution)/shard_map/pallas_call | solution.py:286
  (1 shorter events, 0.0 us)
Async XLA Ops:
  2.3 15.1 %copy-start = (bf16[1024,264]{0,1:T(8,128)(2,1)S(1)}, bf16[1024,264]{0,1:T(8,128)(2,1)}, u32[]{:S(2)}) copy-start(bf16[1024,264]{0,1:T(8,128)(2,1)} %param.16) | copy-start | bytes 1622020
  2.3 15.0 %all-to-all-start = ((bf16[8,4,3200]{2,1,0:T(4,128)(2,1)}), bf16[8,4,3200]{2,1,0:T(4,128)(2,1)S(1)}, u32[]{:S(2)}, u32[]{:S(2)}) async-start(bf16[8,4,3200]{2,1,0:T(4,128)(2,1)} %shard_map.137), calls=%async_computation | async-start | bytes 409600 | tf_op jit(solution)/shard_map/all_to_all | solution.py:339
  27.9 1.5 %collective-permute-start = (bf16[288,128]{1,0:T(8,128)(2,1)S(1)}, bf16[288,128]{1,0:T(8,128)(2,1)S(1)}, u32[]{:S(2)}, u32[]{:S(2)}) collective-permute-start(bf16[288,128]{1,0:T(8,128)(2,1)S(1)} %get-tuple-element.26), channel_id=1, source_target_pairs={{0,1},{1,0},{2,3},{3,2},{4,5},{5,4},{6,7},{7,6},{8,9},{9,8},{10,11... | collective-permute-start | bytes 221192 | tf_op jit(solution)/shard_map/ppermute | solution.py:364
  28.0 1.4 %collective-permute-start.1 = (bf16[16,1408]{1,0:T(8,128)(2,1)S(1)}, bf16[16,1408]{1,0:T(8,128)(2,1)S(1)}, u32[]{:S(2)}, u32[]{:S(2)}) collective-permute-start(bf16[16,1408]{1,0:T(8,128)(2,1)S(1)} %get-tuple-element.28), channel_id=1, source_target_pairs={{0,1},{1,0},{2,3},{3,2},{4,5},{5,4},{6,7},{7,6},{8,9},{9,8},{10,11... | collective-permute-start | bytes 135176 | tf_op jit(solution)/shard_map/ppermute | solution.py:357
  52.5 1.6 %collective-permute-start.2 = (bf16[4,272,128]{2,1,0:T(8,128)(2,1)S(1)}, bf16[4,272,128]{2,1,0:T(8,128)(2,1)S(1)}, u32[]{:S(2)}, u32[]{:S(2)}) collective-permute-start(bf16[4,272,128]{2,1,0:T(8,128)(2,1)S(1)} %all_to_all.22.own), channel_id=1, source_target_pairs={{0,1},{1,0},{2,3},{3,2},{4,5},{5,4},{6,7},{7,6},{8,9},{9,8},{10,11... | collective-permute-start | bytes 835592 | tf_op jit(solution)/shard_map/ppermute | solution.py:391

commit v3 on v2

--- a/solution.py
+++ b/solution.py
@@ -37,7 +37,7 @@
     return high, (x - high.astype(F32)).astype(BF16)
 
 
-def series_kernel(heads, model_d, dates, core, recv, w_t, params, send, own, give, sel):
+def series_kernel(heads, model_d, dates, core, recv, w_t, send, own, give, sel):
     length = recv.shape[0]
     tiles, _, width = send.shape
     slab = width - EXT
@@ -47,9 +47,10 @@
     aux = recv[:, 3 * model_d :].astype(F32)
     gate = aux[:, 0:1]
     ids = aux[:, 1:2]
-    bias = params[:, :heads]
-    rate = -jnp.exp(params[:, heads : 2 * heads])
-    skip = params[:, 2 * heads : 3 * heads]
+    params = []
+    for at in range(2, 2 + 9 * heads, 3 * heads):
+        params.append(sum(aux[0:1, at + k * heads : at + (k + 1) * heads] for k in range(3)))
+    bias, rate, skip = params[0], -jnp.exp(params[1]), params[2]
     projected = nt(mixed, w_t[...])
     keys = projected[:, :states].astype(BF16)
     reads = projected[:, states : 2 * states].astype(BF16)
@@ -129,17 +130,20 @@
     )
 
 
-def pack_kernel(ids_in, mask_in, table_in, layer, values, cotangent, out, ids, mask_t, table, layer_v, packed, sems):
+def pack_kernel(core, ids_in, mask_in, table_in, bias_in, decay_in, skip_in, layer, values, cotangent, out, ids, mask_t, table, params, layer_v, sems):
     pixels, dates, model_d = layer.shape
     small = [
         pltpu.make_async_copy(ids_in, ids, sems.at[0]),
         pltpu.make_async_copy(mask_in, mask_t, sems.at[1]),
         pltpu.make_async_copy(table_in, table, sems.at[2]),
         pltpu.make_async_copy(layer, layer_v, sems.at[3]),
+        pltpu.make_async_copy(bias_in, params.at[0:1], sems.at[6]),
+        pltpu.make_async_copy(decay_in, params.at[1:2], sems.at[7]),
+        pltpu.make_async_copy(skip_in, params.at[2:3], sems.at[8]),
     ]
     large = [
-        pltpu.make_async_copy(values, packed.at[:, :, model_d : 2 * model_d], sems.at[4]),
-        pltpu.make_async_copy(cotangent, packed.at[:, :, 2 * model_d : 3 * model_d], sems.at[5]),
+        pltpu.make_async_copy(values, out.at[:, :, model_d : 2 * model_d], sems.at[4]),
+        pltpu.make_async_copy(cotangent, out.at[:, :, 2 * model_d : 3 * model_d], sems.at[5]),
     ]
     for copy in small + large:
         copy.start()
@@ -153,14 +157,20 @@
     for i in range(dates):
         second = jnp.where((row == i) & (lane == 1), (ids[i] == 1).astype(F32), second)
     gate = mask_t[...].astype(F32)
+    at = 2
+    for k in range(3):
+        rest = params[k : k + 1, :]
+        for _ in range(3):
+            term = rest.astype(BF16).astype(F32)
+            rest = rest - term
+            term = jnp.concatenate([jnp.zeros((1, at), F32), term, jnp.zeros((1, LANES - at - term.shape[1]), F32)], axis=1)
+            second = second + term
+            at = at + params.shape[1]
     for p in range(pixels):
-        packed[p, :, 3 * model_d :] = jnp.where(lane == 0, gate[:, p : p + 1], second).astype(BF16)
-        packed[p, :, :model_d] = (layer_v[p].astype(F32) + embed).astype(BF16)
+        out[p, :, 3 * model_d :] = jnp.where(lane == 0, gate[:, p : p + 1], second).astype(BF16)
+        out[p, :, :model_d] = (layer_v[p].astype(F32) + embed).astype(BF16)
     for copy in large:
         copy.wait()
-    store = pltpu.make_async_copy(packed, out, sems.at[0])
-    store.start()
-    store.wait()
 
 
 def lane_pad(x, width):
@@ -181,7 +191,7 @@
     return rows[0:2] + rows[2:4]
 
 
-def slab_kernel(cols, core, recv, sel, keep, keep_sums, give):
+def slab_kernel(cols, core, recv, sel, rows, keep, keep_sums, give):
     tiles, length, width = recv.shape
     slab = width - EXT
     half = slab // 2
@@ -198,19 +208,20 @@
     keep[...] = jnp.where(mine, first, second)
     keep_sums[...] = sums
     other = jnp.where(mine, second, first)
-    give[...] = jnp.concatenate(
-        [other] + sum_rows(sums), axis=0
-    ).astype(BF16)
-
-
-def join_kernel(cols, dates, core, keep, keep_sums, got, own, other, send):
+    blocks = [rows[:, b * LANES : (b + 1) * LANES].astype(F32) for b in range(rows.shape[1] // LANES)]
+    give[...] = jnp.concatenate([other] + sum_rows(sums) + blocks, axis=0).astype(BF16)
+
+
+def join_kernel(cols, dates, core, keep, keep_sums, got, own, send):
     levels = send.shape[0]
     first = core[0] == 0
     model_d = own.shape[1] - EXT
     total = keep[...] + got[:cols, :].astype(F32)
     sums = sum_rows(keep_sums[...] + rows_sum(got[cols : cols + 24, :].astype(F32)))
     pair_sums = jnp.concatenate([sums[0][:4], sums[1][:4]], axis=0)
-    mine, theirs = own[...].astype(F32), other[...].astype(F32)
+    mine, count = own[...].astype(F32), own.shape[0]
+    tall = got[cols + 24 :, :].astype(F32)
+    theirs = jnp.concatenate([tall[k : k + count] for k in range(0, tall.shape[0], count)], axis=1)
     firsts, seconds = jnp.where(first, mine, theirs), jnp.where(first, theirs, mine)
     lane = lax.broadcasted_iota(jnp.int32, (8, LANES), 1)
     last = pltpu.roll(sums[2], 64, 1)
@@ -235,7 +246,32 @@
     rest[...] = total[cols + 16 : cols + 32]
 
 
-def local_kernel(heads, scale, recv, rest, w_t, value, inputs, table, head):
+def store_half(cols, scale, core, half, slabs, weight, held, sems):
+    copies = []
+    for t in range(slabs.shape[0]):
+        held[t] = slabs[t].astype(F32)[:cols] * scale
+        at = pl.multiple_of((2 * t + core) * half, half)
+        copies.append(pltpu.make_async_copy(held.at[t], weight.at[:, pl.ds(at, half)], sems.at[t]))
+        copies[-1].start()
+    return copies
+
+
+def half_kernel(cols, scale, half, core, slabs, weight_in, weight, held, sems):
+    for copy in store_half(cols, scale, 1 - core[0], half, slabs, weight, held, sems):
+        copy.wait()
+
+
+def local_weight_kernel(heads, scale, cols, half, core, slabs, recv, rest, w_t, *refs):
+    outs, held_outs = refs[:5], refs[5:10]
+    held, sems, out_sems = held_outs[4], refs[10], refs[11]
+    copies = store_half(cols, scale, core[0], half, slabs, outs[4], held, sems)
+    moves = [pltpu.make_async_copy(held_outs[k], outs[k], out_sems.at[k]) for k in range(4)]
+    local_kernel(heads, scale, recv, rest, w_t, *held_outs[:4], moves)
+    for copy in copies + moves:
+        copy.wait()
+
+
+def local_kernel(heads, scale, recv, rest, w_t, value, inputs, table, head, moves=()):
     levels = recv.shape[0]
     model_d = w_t.shape[1]
     cols = w_t.shape[0]
@@ -249,9 +285,13 @@
         values = jnp.concatenate([rows[at + 8 * b : at + 8 * b + 8] for b in range(model_d // LANES)], axis=1)
         for c in range(2):
             value[2 * z + c] = values[c * dates : (c + 1) * dates].astype(BF16)
+    for move in moves[:1]:
+        move.start()
     grads = nn(jnp.concatenate(ext_rows, axis=0).astype(BF16)[:, :cols], w)
     for p in range(2 * levels):
         inputs[p] = grads[p * dates : (p + 1) * dates].astype(BF16)
+    for move in moves[1:2]:
+        move.start()
     last = pltpu.roll(rest[0:8, :], 64, 1)
     sums = jnp.concatenate([rest[8:12, :], rest[12:16, :], last[0:4]], axis=1)
     sums = sums[0:2] + sums[2:4]
@@ -264,6 +304,8 @@
         lo = at + k * heads
         rows.append(both[:, lo : lo + heads] + both[:, lo + heads : lo + 2 * heads])
     head[...] = jnp.concatenate(rows, axis=0) * scale
+    for move in moves[2:]:
+        move.start()
 
 
 def gather_kernel(cols, half, scale, core, own, other, out):
@@ -321,21 +363,32 @@
     swap = [(i, i ^ 1) for i in range(dates)]
     planes = [[2 * z + c for z in range(levels)] for c in range(2)]
 
+    operands = [
+        sensor_ids,
+        valid_mask.T,
+        sensor_table,
+        step_bias[None],
+        decay_log[None],
+        skip_gain[None],
+        layer_input,
+        head_input,
+        out_grad,
+    ]
     packed = pl.pallas_call(
         pack_kernel,
         out_shape=jax.ShapeDtypeStruct((pixel_dev, dates_dev, 3 * model_d + LANES), BF16),
-        in_specs=[HBM] * 6,
-        out_specs=HBM,
+        in_specs=[SMEM] + [HBM] * 9,
+        out_specs=VMEM,
         scratch_shapes=[
             pltpu.SMEM((dates_dev,), jnp.int32),
             pltpu.VMEM((dates_dev, pixel_dev), jnp.int32),
             pltpu.VMEM((2, model_d), F32),
+            pltpu.VMEM((3, heads), F32),
             pltpu.VMEM((pixel_dev, dates_dev, model_d), BF16),
-            pltpu.VMEM((pixel_dev, dates_dev, 3 * model_d + LANES), BF16),
-            pltpu.SemaphoreType.DMA((6,)),
+            pltpu.SemaphoreType.DMA((9,)),
         ],
-        compiler_params=pltpu.CompilerParams(vmem_limit_bytes=64 * 1024 * 1024),
-    )(sensor_ids, valid_mask.T, sensor_table, layer_input, head_input, out_grad)
+        compiler_params=pltpu.CompilerParams(vmem_limit_bytes=16 * 1024 * 1024),
+    )(core_s, *[pltpu.with_memory_space_constraint(operand, pltpu.HBM) for operand in operands])
     series = lax.all_to_all(packed, "date", split_axis=0, concat_axis=0, tiled=True).reshape(
         length, 3 * model_d + LANES
     )
@@ -349,16 +402,15 @@
             ((rows_core, model_d + EXT), BF16),
             ((16, length), BF16),
         ],
-        [core_s, series, w_t, jnp.concatenate([step_bias, decay_log, skip_gain])[None]],
+        [core_s, series, w_t],
         1,
     )
     recv_t = lax.all_to_all(send_t, "tile", split_axis=0, concat_axis=0, tiled=True)
-    give_rows, recv_t = lax.optimization_barrier((give_rows, recv_t))
-    other = lax.ppermute(give_rows, "date", swap)
+    rows_give = cols + 24 + rows_core * (model_d + EXT) // LANES
     keep, keep_sums, give = call(
         functools.partial(slab_kernel, cols),
-        [((cols, LANES), F32), ((2, EXT), F32), ((cols + 24, LANES), BF16)],
-        [core_s, recv_t, sel],
+        [((cols, LANES), F32), ((2, EXT), F32), ((rows_give, LANES), BF16)],
+        [core_s, recv_t, sel, give_rows],
         1,
     )
     got = lax.ppermute(give, "date", swap)
@@ -366,7 +418,7 @@
     (send_z,) = call(
         functools.partial(join_kernel, cols, dates_dev),
         [((levels, rows_z, LANES), BF16)],
-        [core_s, keep, keep_sums, got, own, other],
+        [core_s, keep, keep_sums, got, own],
         1,
     )
     recv_z = lax.all_to_all(
@@ -378,23 +430,46 @@
         [recv_z],
     )
     recv_g = lax.all_to_all(send_g, "tile", split_axis=0, concat_axis=0, tiled=True)
-    value, inputs, table, head = call(
-        functools.partial(local_kernel, heads, scale),
-        [
-            ((pixel_dev, dates_dev, model_d), BF16),
-            ((pixel_dev, dates_dev, model_d), BF16),
-            ((2, model_d), F32),
-            ((3, heads), F32),
-        ],
-        [recv_z, rest, w_t],
-    )
+    local_outs = [
+        ((pixel_dev, dates_dev, model_d), BF16),
+        ((pixel_dev, dates_dev, model_d), BF16),
+        ((2, model_d), F32),
+        ((3, heads), F32),
+    ]
     other_g = lax.ppermute(recv_g, "date", swap)
-    (weight_t,) = call(
-        functools.partial(gather_kernel, cols, half, scale),
-        [((cols, model_d), F32)],
-        [core_s, recv_g, other_g],
-        1,
-    )
+    if half % LANES == 0:
+        weight_shape = jax.ShapeDtypeStruct((cols, model_d), F32)
+        held = [pltpu.VMEM((tiles, cols, half), F32), pltpu.SemaphoreType.DMA((tiles,))]
+        limit = pltpu.CompilerParams(vmem_limit_bytes=48 * 1024 * 1024)
+        value, inputs, table, head, weight_t = pl.pallas_call(
+            functools.partial(local_weight_kernel, heads, scale, cols, half),
+            out_shape=[jax.ShapeDtypeStruct(s, d) for s, d in local_outs] + [weight_shape],
+            in_specs=[SMEM] + [VMEM] * 4,
+            out_specs=[HBM] * 5,
+            scratch_shapes=[pltpu.VMEM(s, d) for s, d in local_outs]
+            + held
+            + [pltpu.SemaphoreType.DMA((4,))],
+            compiler_params=limit,
+        )(core_s, recv_g, recv_z, rest, w_t)
+        weight_t = pl.pallas_call(
+            functools.partial(half_kernel, cols, scale, half),
+            out_shape=weight_shape,
+            in_specs=[SMEM, VMEM, HBM],
+            out_specs=HBM,
+            scratch_shapes=held,
+            input_output_aliases={2: 0},
+            compiler_params=limit,
+        )(core_s, other_g, weight_t)
+    else:
+        value, inputs, table, head = call(
+            functools.partial(local_kernel, heads, scale), local_outs, [recv_z, rest, w_t]
+        )
+        (weight_t,) = call(
+            functools.partial(gather_kernel, cols, half, scale),
+            [((cols, model_d), F32)],
+            [core_s, recv_g, other_g],
+            1,
+        )
     return (
         value,
         inputs,

time: 55.5 us -> 54 us (0.973)
  blocking collectives: 32 us -> 46.4 us
  waiting for transfers between devices: 9.16 us -> 1.62 us
  starting transfers between devices: 7.04 us -> 0.07 us
  other arithmetic: 0.76 us -> 0 us
  Pallas kernels: 5.48 us -> 4.86 us
    all_to_all x0 -> x1, blocking collectives: none -> 14.6 us  [on_device(): lax.all_to_all(packed, 'date', split_axis=0, concat_axis=0, tiled=True)]
    all_to_all x1 -> x0, waiting for transfers between devices: 7.75 us -> none  [on_device(): lax.all_to_all(packed, 'date', split_axis=0, concat_axis=0, tiled=True)]
    all_to_all x1 -> x0, starting transfers between devices: 6.47 us -> none  [on_device(): lax.all_to_all(packed, 'date', split_axis=0, concat_axis=0, tiled=True)]
    pallas_call x6 -> x4, Pallas kernels: 3.79 us -> 1.67 us  [call(): pl.pallas_call(kernel, out_shape=[jax.ShapeDtypeStruct(s, d) for s, d in...]
    pallas_call x0 -> x2, Pallas kernels: none -> 2.08 us  [the longest x1 1.24 us: on_device(): pl.pallas_call(functools.partial(local_weight_kernel, heads, scale, cols,...]
    ppermute x1, waiting for transfers between devices: 0.01 us -> 1.32 us  [on_device(): got = lax.ppermute(give, 'date', swap)]
    ppermute x1 -> x0, waiting for transfers between devices: 0.88 us -> none  [on_device(): other = lax.ppermute(give_rows, 'date', swap)]
    broadcast_in_dim x1 -> x0, other arithmetic: 0.76 us -> none  [on_device(): jnp.concatenate([step_bias, decay_log, skip_gain])[None]]
  transfers between devices with their start and end apart: 4 -> 2, of which waited for: 3 -> 2; matrix products, arithmetic and copies ran while one was open for 1% -> 0% of each run, Pallas kernels for 2% -> 2%
where the time goes in v3:
time: 54 us; the launch traced here: 53.7 us
  blocking collectives  46.4 us (86%)
  Pallas kernels  4.86 us (9%)
  waiting for transfers between devices  1.62 us (3%)
  between operations  0.71 us (1%)
    all_to_all x1, blocking collectives, on_device(): lax.all_to_all(packed, 'date', split_axis=0, concat_axis=0, tiled=True)  14.6 us
    all_to_all x1, blocking collectives, on_device(): lax.all_to_all(send_z, 'date', split_axis=0, concat_axis=0, tiled=True, a...  14.3 us
    all_to_all x1, blocking collectives, on_device(): lax.all_to_all(send_t, 'tile', split_axis=0, concat_axis=0, tiled=True)  8.98 us
    all_to_all x1, blocking collectives, on_device(): lax.all_to_all(send_g, 'tile', split_axis=0, concat_axis=0, tiled=True)  8.48 us
    pallas_call x4, Pallas kernels, call(): pl.pallas_call(kernel, out_shape=[jax.ShapeDtypeStruct(s, d) for s, d in...  1.67 us
    ppermute x1, waiting for transfers between devices, on_device(): got = lax.ppermute(give, 'date', swap)  1.32 us
    pallas_call x1, Pallas kernels, on_device(): pl.pallas_call(functools.partial(local_weight_kernel, heads, scale, cols,...  1.24 us
    pallas_call x1, Pallas kernels, on_device(): pl.pallas_call(pack_kernel, out_shape=jax.ShapeDtypeStruct((pixel_dev, da...  1.12 us
  transfers between devices with their start and end apart: 2, of which 2 were waited for; matrix products, arithmetic and copies ran while one was open for 0% of the time, Pallas kernels for 2%

profile of v3, /device:TPU:0, one launch (start us, length us, event | category | flops | bytes accessed | tf_op | source)
XLA Modules:
  0.0 53.7 jit_solution(5957558986697157853)
XLA Ops:
  0.6 0.0 copy-start
  0.7 1.1 %shard_map.137 = bf16[8,4,3200]{2,1,0:T(4,128)(2,1)S(1)} custom-call(s32[1]{0:T(128)} %bitcast.core, s32[4]{0:T(128)} %ids_in.1, s32[4,8]{1,0:T(4,128)} %bitcast.10, f32[2,1024]{1,0:T(2,128)} %table_in.1, f32[1,8]{1,0:T(1,128)} %bitcast.11, f32[1,8]{1,0:T(1,128)} %bitcast.12, f32[1,8]{1,0:T(1,128)} %bitcast.13, bf16[8,4,1024]{2,1,0:T(4,128)(2,1)} %layer.1, ...), custom_call_target="tpu_custom_call" | custom-call | tf_op jit(solution)/shard_map/pallas_call | solution.py:377
  1.8 14.6 %all_to_all.20 = bf16[8,4,3200]{2,1,0:T(4,128)(2,1)S(1)} all-to-all(bf16[8,4,3200]{2,1,0:T(4,128)(2,1)S(1)} %shard_map.137), channel_id=1, replica_groups=mesh['tile'=4,'date'=8] {'date'}, dimensions={0} | all-to-all | bytes 409600 | tf_op jit(solution)/shard_map/all_to_all | solution.py:392
  16.4 0.1 reshape.17.recv
  16.5 0.0 copy-done
  16.5 1.3 %shard_map.138 = (bf16[4,32,640]{2,1,0:T(8,128)(2,1)S(1)}, bf16[16,1408]{1,0:T(8,128)(2,1)S(1)}, bf16[16,1408]{1,0:T(8,128)(2,1)S(1)}, bf16[16,32]{1,0:T(8,128)(2,1)S(1)}) custom-call(s32[1]{0:T(128)} %bitcast.core, bf16[32,3200]{1,0:T(8,128)(2,1)S(1)} %reshape.17.recv, bf16[264,1024]{1,0:T(8,128)(2,1)S(1)} %bitcast.7), custom_call_target="tpu_custom_call" | custom-call | tf_op jit(solution)/shard_map/pallas_call | solution.py:328
  17.8 9.0 %all_to_all.21.recv = bf16[4,32,640]{2,1,0:T(8,128)(2,1)S(1)} all-to-all(bf16[4,32,640]{2,1,0:T(8,128)(2,1)S(1)} %get-tuple-element.19), channel_id=1, replica_groups=mesh['tile'=4,'date'=8] {'tile'}, dimensions={0} | all-to-all | bytes 327680 | tf_op jit(solution)/shard_map/all_to_all | solution.py:408
  26.7 0.3 shard_map.139
  27.0 0.1 collective-permute-start
  27.1 1.3 %collective-permute-done.got = bf16[464,128]{1,0:T(8,128)(2,1)S(1)} collective-permute-done((bf16[464,128]{1,0:T(8,128)(2,1)S(1)}, bf16[464,128]{1,0:T(8,128)(2,1)S(1)}, u32[]{:S(2)}, u32[]{:S(2)}) %collective-permute-start) | collective-permute-done | bytes 118816 | tf_op jit(solution)/shard_map/ppermute | solution.py:416
  28.4 0.1 shard_map.140
  28.5 14.3 %all_to_all.22.recv = bf16[4,368,128]{2,1,0:T(8,128)(2,1)S(1)} all-to-all(bf16[4,368,128]{2,1,0:T(8,128)(2,1)S(1)} %shard_map.140), channel_id=1, replica_groups={{0,2,4,6},{1,3,5,7},{8,10,12,14},{9,11,13,15},{16,18,20,22},{17,19,21,2..., dimensions={0} | all-to-all | bytes 753664 | tf_op jit(solution)/shard_map/all_to_all | solution.py:424
  42.8 8.5 %all_to_all.23.slabs = bf16[4,272,128]{2,1,0:T(8,128)(2,1)S(1)} all-to-all(bf16[4,272,128]{2,1,0:T(8,128)(2,1)S(1)} %get-tuple-element.26), channel_id=1, replica_groups=mesh['tile'=4,'date'=8] {'tile'}, dimensions={0} | all-to-all | bytes 557056 | tf_op jit(solution)/shard_map/all_to_all | solution.py:432
  51.3 0.0 collective-permute-start.1
  51.3 1.2 %shard_map.142 = (bf16[8,4,1024]{2,1,0:T(4,128)(2,1)}, bf16[8,4,1024]{2,1,0:T(4,128)(2,1)}, f32[2,1024]{1,0:T(2,128)}, f32[3,8]{1,0:T(4,128)}, f32[264,1024]{1,0:T(8,128)}) custom-call(s32[1]{0:T(128)} %bitcast.core, bf16[4,272,128]{2,1,0:T(8,128)(2,1)S(1)} %all_to_all.23.slabs, bf16[4,368,128]{2,1,0:T(8,128)(2,1)S(1)} %all_to_all.22.recv, ...), custom_call_target="tpu_custom_call" | custom-call | tf_op jit(solution)/shard_map/pallas_call | solution.py:444
  52.6 0.3 collective-permute-done.1.slabs
  52.9 0.8 %shard_map.143 = f32[264,1024]{1,0:T(8,128)} custom-call(s32[1]{0:T(128)} %bitcast.core, bf16[4,272,128]{2,1,0:T(8,128)(2,1)S(1)} %collective-permute-done.1.slabs, f32[264,1024]{1,0:T(8,128)} %get-tuple-element.30.weight_in), custom_call_target="tpu_custom_call", output_to_operand_aliasing={{}: (2, {})} | custom-call | tf_op jit(solution)/shard_map/pallas_call | solution.py:454
  (1 shorter events, 0.0 us)
Async XLA Ops:
  0.6 15.8 %copy-start = (bf16[1024,264]{0,1:T(8,128)(2,1)S(1)}, bf16[1024,264]{0,1:T(8,128)(2,1)}, u32[]{:S(2)}) copy-start(bf16[1024,264]{0,1:T(8,128)(2,1)} %param.16) | copy-start | bytes 1622020
  27.0 1.4 %collective-permute-start = (bf16[464,128]{1,0:T(8,128)(2,1)S(1)}, bf16[464,128]{1,0:T(8,128)(2,1)S(1)}, u32[]{:S(2)}, u32[]{:S(2)}) collective-permute-start(bf16[464,128]{1,0:T(8,128)(2,1)S(1)} %get-tuple-element.24), channel_id=1, source_target_pairs={{0,1},{1,0},{2,3},{3,2},{4,5},{5,4},{6,7},{7,6},{8,9},{9,8},{10,11... | collective-permute-start | bytes 356360 | tf_op jit(solution)/shard_map/ppermute | solution.py:416
  51.3 1.6 %collective-permute-start.1 = (bf16[4,272,128]{2,1,0:T(8,128)(2,1)S(1)}, bf16[4,272,128]{2,1,0:T(8,128)(2,1)S(1)}, u32[]{:S(2)}, u32[]{:S(2)}) collective-permute-start(bf16[4,272,128]{2,1,0:T(8,128)(2,1)S(1)} %all_to_all.23.slabs), channel_id=1, source_target_pairs={{0,1},{1,0},{2,3},{3,2},{4,5},{5,4},{6,7},{7,6},{8,9},{9,8},{10,11... | collective-permute-start | bytes 835592 | tf_op jit(solution)/shard_map/ppermute | solution.py:439

commit v4 on v3

--- a/solution.py
+++ b/solution.py
@@ -405,7 +405,12 @@
         [core_s, series, w_t],
         1,
     )
-    recv_t = lax.all_to_all(send_t, "tile", split_axis=0, concat_axis=0, tiled=True)
+    mixed = [
+        [t * dates + 2 * z + (c + t) % 2 for t in range(tiles)] for z in range(levels) for c in range(2)
+    ]
+    recv_t = lax.all_to_all(
+        send_t, ("tile", "date"), split_axis=0, concat_axis=0, tiled=True, axis_index_groups=mixed
+    )
     rows_give = cols + 24 + rows_core * (model_d + EXT) // LANES
     keep, keep_sums, give = call(
         functools.partial(slab_kernel, cols),

time: 54 us -> 53.5 us (level)
  blocking collectives: 46.4 us -> 45.3 us
  starting transfers between devices: 0.07 us -> 0.98 us
    all_to_all x1, blocking collectives: 8.98 us -> 7.6 us  [on_device(): lax.all_to_all(send_t, ('tile', 'date'), split_axis=0, concat_axis=0, til...]
    ppermute x1, starting transfers between devices: 0.07 us -> 0.98 us  [on_device(): got = lax.ppermute(give, 'date', swap)]
where the time goes in v4:
time: 53.5 us; the launch traced here: 53.2 us
  blocking collectives  45.3 us (85%)
  Pallas kernels  4.87 us (9%)
  waiting for transfers between devices  1.28 us (2%)
  starting transfers between devices  0.98 us (2%)
  between operations  0.7 us (1%)
    all_to_all x1, blocking collectives, on_device(): lax.all_to_all(packed, 'date', split_axis=0, concat_axis=0, tiled=True)  14.6 us
    all_to_all x1, blocking collectives, on_device(): lax.all_to_all(send_z, 'date', split_axis=0, concat_axis=0, tiled=True, a...  14.5 us
    all_to_all x1, blocking collectives, on_device(): lax.all_to_all(send_g, 'tile', split_axis=0, concat_axis=0, tiled=True)  8.59 us
    all_to_all x1, blocking collectives, on_device(): lax.all_to_all(send_t, ('tile', 'date'), split_axis=0, concat_axis=0, til...  7.6 us
    pallas_call x4, Pallas kernels, call(): pl.pallas_call(kernel, out_shape=[jax.ShapeDtypeStruct(s, d) for s, d in...  1.67 us
    pallas_call x1, Pallas kernels, on_device(): pl.pallas_call(functools.partial(local_weight_kernel, heads, scale, cols,...  1.24 us
    pallas_call x1, Pallas kernels, on_device(): pl.pallas_call(pack_kernel, out_shape=jax.ShapeDtypeStruct((pixel_dev, da...  1.12 us
  transfers between devices with their start and end apart: 2, of which 2 were waited for; matrix products, arithmetic and copies ran while one was open for 0% of the time, Pallas kernels for 2%

profile of v4, /device:TPU:0, one launch (start us, length us, event | category | flops | bytes accessed | tf_op | source)
XLA Modules:
  0.0 53.2 jit_solution(7554005050249320919)
XLA Ops:
  0.6 0.0 copy-start
  0.7 1.1 %shard_map.137 = bf16[8,4,3200]{2,1,0:T(4,128)(2,1)S(1)} custom-call(s32[1]{0:T(128)} %bitcast.core, s32[4]{0:T(128)} %ids_in.1, s32[4,8]{1,0:T(4,128)} %bitcast.10, f32[2,1024]{1,0:T(2,128)} %table_in.1, f32[1,8]{1,0:T(1,128)} %bitcast.11, f32[1,8]{1,0:T(1,128)} %bitcast.12, f32[1,8]{1,0:T(1,128)} %bitcast.13, bf16[8,4,1024]{2,1,0:T(4,128)(2,1)} %layer.1, ...), custom_call_target="tpu_custom_call" | custom-call | tf_op jit(solution)/shard_map/pallas_call | solution.py:377
  1.8 14.6 %all_to_all.20 = bf16[8,4,3200]{2,1,0:T(4,128)(2,1)S(1)} all-to-all(bf16[8,4,3200]{2,1,0:T(4,128)(2,1)S(1)} %shard_map.137), channel_id=1, replica_groups=mesh['tile'=4,'date'=8] {'date'}, dimensions={0} | all-to-all | bytes 409600 | tf_op jit(solution)/shard_map/all_to_all | solution.py:392
  16.4 0.1 reshape.17.recv
  16.5 0.0 copy-done
  16.5 1.3 %shard_map.138 = (bf16[4,32,640]{2,1,0:T(8,128)(2,1)S(1)}, bf16[16,1408]{1,0:T(8,128)(2,1)S(1)}, bf16[16,1408]{1,0:T(8,128)(2,1)S(1)}, bf16[16,32]{1,0:T(8,128)(2,1)S(1)}) custom-call(s32[1]{0:T(128)} %bitcast.core, bf16[32,3200]{1,0:T(8,128)(2,1)S(1)} %reshape.17.recv, bf16[264,1024]{1,0:T(8,128)(2,1)S(1)} %bitcast.7), custom_call_target="tpu_custom_call" | custom-call | tf_op jit(solution)/shard_map/pallas_call | solution.py:328
  17.8 7.6 %all_to_all.21.recv = bf16[4,32,640]{2,1,0:T(8,128)(2,1)S(1)} all-to-all(bf16[4,32,640]{2,1,0:T(8,128)(2,1)S(1)} %get-tuple-element.19), channel_id=1, replica_groups={{0,9,16,25},{1,8,17,24},{2,11,18,27},{3,10,19,26},{4,13,20,29},{5,12,21..., dimensions={0} | all-to-all | bytes 327680 | tf_op jit(solution)/shard_map/all_to_all | solution.py:411
  25.4 0.3 shard_map.139
  25.6 1.0 %collective-permute-start = (bf16[464,128]{1,0:T(8,128)(2,1)S(1)}, bf16[464,128]{1,0:T(8,128)(2,1)S(1)}, u32[]{:S(2)}, u32[]{:S(2)}) collective-permute-start(bf16[464,128]{1,0:T(8,128)(2,1)S(1)} %get-tuple-element.24), channel_id=1, source_target_pairs={{0,1},{1,0},{2,3},{3,2},{4,5},{5,4},{6,7},{7,6},{8,9},{9,8},{10,11... | collective-permute-start | bytes 356360 | tf_op jit(solution)/shard_map/ppermute | solution.py:421
  26.6 1.0 %collective-permute-done.got = bf16[464,128]{1,0:T(8,128)(2,1)S(1)} collective-permute-done((bf16[464,128]{1,0:T(8,128)(2,1)S(1)}, bf16[464,128]{1,0:T(8,128)(2,1)S(1)}, u32[]{:S(2)}, u32[]{:S(2)}) %collective-permute-start) | collective-permute-done | bytes 118816 | tf_op jit(solution)/shard_map/ppermute | solution.py:421
  27.6 0.1 shard_map.140
  27.7 14.5 %all_to_all.22.recv = bf16[4,368,128]{2,1,0:T(8,128)(2,1)S(1)} all-to-all(bf16[4,368,128]{2,1,0:T(8,128)(2,1)S(1)} %shard_map.140), channel_id=1, replica_groups={{0,2,4,6},{1,3,5,7},{8,10,12,14},{9,11,13,15},{16,18,20,22},{17,19,21,2..., dimensions={0} | all-to-all | bytes 753664 | tf_op jit(solution)/shard_map/all_to_all | solution.py:429
  42.2 8.6 %all_to_all.23.slabs = bf16[4,272,128]{2,1,0:T(8,128)(2,1)S(1)} all-to-all(bf16[4,272,128]{2,1,0:T(8,128)(2,1)S(1)} %get-tuple-element.26), channel_id=1, replica_groups=mesh['tile'=4,'date'=8] {'tile'}, dimensions={0} | all-to-all | bytes 557056 | tf_op jit(solution)/shard_map/all_to_all | solution.py:437
  50.8 0.0 collective-permute-start.1
  50.8 1.2 %shard_map.142 = (bf16[8,4,1024]{2,1,0:T(4,128)(2,1)}, bf16[8,4,1024]{2,1,0:T(4,128)(2,1)}, f32[2,1024]{1,0:T(2,128)}, f32[3,8]{1,0:T(4,128)}, f32[264,1024]{1,0:T(8,128)}) custom-call(s32[1]{0:T(128)} %bitcast.core, bf16[4,272,128]{2,1,0:T(8,128)(2,1)S(1)} %all_to_all.23.slabs, bf16[4,368,128]{2,1,0:T(8,128)(2,1)S(1)} %all_to_all.22.recv, ...), custom_call_target="tpu_custom_call" | custom-call | tf_op jit(solution)/shard_map/pallas_call | solution.py:449
  52.1 0.3 collective-permute-done.1.slabs
  52.4 0.8 %shard_map.143 = f32[264,1024]{1,0:T(8,128)} custom-call(s32[1]{0:T(128)} %bitcast.core, bf16[4,272,128]{2,1,0:T(8,128)(2,1)S(1)} %collective-permute-done.1.slabs, f32[264,1024]{1,0:T(8,128)} %get-tuple-element.30.weight_in), custom_call_target="tpu_custom_call", output_to_operand_aliasing={{}: (2, {})} | custom-call | tf_op jit(solution)/shard_map/pallas_call | solution.py:459
  (1 shorter events, 0.0 us)
Async XLA Ops:
  0.6 15.8 %copy-start = (bf16[1024,264]{0,1:T(8,128)(2,1)S(1)}, bf16[1024,264]{0,1:T(8,128)(2,1)}, u32[]{:S(2)}) copy-start(bf16[1024,264]{0,1:T(8,128)(2,1)} %param.16) | copy-start | bytes 1622020
  25.6 1.9 %collective-permute-start = (bf16[464,128]{1,0:T(8,128)(2,1)S(1)}, bf16[464,128]{1,0:T(8,128)(2,1)S(1)}, u32[]{:S(2)}, u32[]{:S(2)}) collective-permute-start(bf16[464,128]{1,0:T(8,128)(2,1)S(1)} %get-tuple-element.24), channel_id=1, source_target_pairs={{0,1},{1,0},{2,3},{3,2},{4,5},{5,4},{6,7},{7,6},{8,9},{9,8},{10,11... | collective-permute-start | bytes 356360 | tf_op jit(solution)/shard_map/ppermute | solution.py:421
  50.8 1.6 %collective-permute-start.1 = (bf16[4,272,128]{2,1,0:T(8,128)(2,1)S(1)}, bf16[4,272,128]{2,1,0:T(8,128)(2,1)S(1)}, u32[]{:S(2)}, u32[]{:S(2)}) collective-permute-start(bf16[4,272,128]{2,1,0:T(8,128)(2,1)S(1)} %all_to_all.23.slabs), channel_id=1, source_target_pairs={{0,1},{1,0},{2,3},{3,2},{4,5},{5,4},{6,7},{7,6},{8,9},{9,8},{10,11... | collective-permute-start | bytes 835592 | tf_op jit(solution)/shard_map/ppermute | solution.py:444

commit v5 on v4

--- a/solution.py
+++ b/solution.py
@@ -103,13 +103,11 @@
     grad_keys = nn(pair_b, reads)
     grad_reads = tn(pair_b, keys)
     raw = step_grad * gate * jax.nn.sigmoid(step_pre)
-    parts = []
-    for term in (raw, decay_terms, skip_terms):
-        high, low = split(term)
-        parts += [high.astype(F32), low.astype(F32)]
-    tail = jnp.concatenate(
-        parts + [jnp.zeros((length, EXT - 2 * states - 6 * heads), F32)], axis=1
-    )
+    terms = jnp.concatenate(
+        [raw, decay_terms, skip_terms, jnp.zeros((length, LANES - 3 * heads), F32)], axis=1
+    )
+    high = terms.astype(BF16).astype(F32)
+    tail = high + pltpu.roll(terms - high, 3 * heads, 1)
     ext_f = jnp.concatenate([grad_keys, grad_reads, tail], axis=1)
     ext = ext_f.astype(BF16)
     back = jnp.concatenate(value_parts + [ext_f], axis=1)
@@ -145,7 +143,7 @@
         pltpu.make_async_copy(values, out.at[:, :, model_d : 2 * model_d], sems.at[4]),
         pltpu.make_async_copy(cotangent, out.at[:, :, 2 * model_d : 3 * model_d], sems.at[5]),
     ]
-    for copy in small + large:
+    for copy in small[3:4] + large + small[:3] + small[4:]:
         copy.start()
     for copy in small:
         copy.wait()
@@ -225,14 +223,13 @@
     firsts, seconds = jnp.where(first, mine, theirs), jnp.where(first, theirs, mine)
     lane = lax.broadcasted_iota(jnp.int32, (8, LANES), 1)
     last = pltpu.roll(sums[2], 64, 1)
-    pad = [jnp.zeros((8, LANES), F32)] * ((send.shape[1] - cols - 32) // 8 - model_d // LANES)
     for z in range(levels):
         at = z * dates
         rows = jnp.concatenate([firsts[at : at + dates], seconds[at : at + dates]], axis=0)
         ext = [rows[:, model_d + b * LANES : model_d + (b + 1) * LANES] for b in range(EXT // LANES)]
         misc = jnp.where(lane < 64, ext[2], last)
         value = [rows[:, b * LANES : (b + 1) * LANES] for b in range(model_d // LANES)]
-        send[z] = jnp.concatenate([total, ext[0], ext[1], misc, pair_sums] + value + pad, axis=0).astype(BF16)
+        send[z] = jnp.concatenate([total, ext[0], ext[1], misc, pair_sums] + value, axis=0).astype(BF16)
 
 
 def total_kernel(cols, recv, send, rest):
@@ -240,7 +237,7 @@
     total = recv[0].astype(F32)
     for z in range(1, levels):
         total = total + recv[z].astype(F32)
-    slab = total[:272].astype(BF16)
+    slab = total[:cols].astype(BF16)
     for t in range(send.shape[0]):
         send[t] = slab
     rest[...] = total[cols + 16 : cols + 32]
@@ -300,9 +297,9 @@
     both = sums[0:1] + sums[1:2]
     at = cols - heads
     rows = []
-    for k in (2, 0, 4):
+    for k in (1, 0, 2):
         lo = at + k * heads
-        rows.append(both[:, lo : lo + heads] + both[:, lo + heads : lo + 2 * heads])
+        rows.append(both[:, lo : lo + heads] + both[:, lo + 3 * heads : lo + 4 * heads])
     head[...] = jnp.concatenate(rows, axis=0) * scale
     for move in moves[2:]:
         move.start()
@@ -419,7 +416,7 @@
         1,
     )
     got = lax.ppermute(give, "date", swap)
-    rows_z = -(-(cols + 32 + model_d // 16) // 16) * 16
+    rows_z = cols + 32 + model_d // 16
     (send_z,) = call(
         functools.partial(join_kernel, cols, dates_dev),
         [((levels, rows_z, LANES), BF16)],
@@ -431,7 +428,7 @@
     )
     send_g, rest = call(
         functools.partial(total_kernel, cols),
-        [((tiles, 272, LANES), BF16), ((16, LANES), F32)],
+        [((tiles, cols, LANES), BF16), ((16, LANES), F32)],
         [recv_z],
     )
     recv_g = lax.all_to_all(send_g, "tile", split_axis=0, concat_axis=0, tiled=True)

time: 53.5 us -> 53.3 us (level)
  no operation moved by 1% of the time
where the time goes in v5:
time: 53.3 us; the launch traced here: 53 us
  blocking collectives  45.2 us (85%)
  Pallas kernels  4.82 us (9%)
  waiting for transfers between devices  1.27 us (2%)
  starting transfers between devices  0.98 us (2%)
  between operations  0.7 us (1%)
    all_to_all x1, blocking collectives, on_device(): lax.all_to_all(packed, 'date', split_axis=0, concat_axis=0, tiled=True)  14.6 us
    all_to_all x1, blocking collectives, on_device(): lax.all_to_all(send_z, 'date', split_axis=0, concat_axis=0, tiled=True, a...  14.3 us
    all_to_all x1, blocking collectives, on_device(): lax.all_to_all(send_g, 'tile', split_axis=0, concat_axis=0, tiled=True)  8.58 us
    all_to_all x1, blocking collectives, on_device(): lax.all_to_all(send_t, ('tile', 'date'), split_axis=0, concat_axis=0, til...  7.6 us
    pallas_call x4, Pallas kernels, call(): pl.pallas_call(kernel, out_shape=[jax.ShapeDtypeStruct(s, d) for s, d in...  1.67 us
    pallas_call x1, Pallas kernels, on_device(): pl.pallas_call(functools.partial(local_weight_kernel, heads, scale, cols,...  1.24 us
    pallas_call x1, Pallas kernels, on_device(): pl.pallas_call(pack_kernel, out_shape=jax.ShapeDtypeStruct((pixel_dev, da...  1.08 us
  transfers between devices with their start and end apart: 2, of which 2 were waited for; matrix products, arithmetic and copies ran while one was open for 0% of the time, Pallas kernels for 2%

profile of v5, /device:TPU:0, one launch (start us, length us, event | category | flops | bytes accessed | tf_op | source)
XLA Modules:
  0.0 53.0 jit_solution(8890660436341194242)
XLA Ops:
  0.6 0.0 copy-start
  0.7 1.1 %shard_map.137 = bf16[8,4,3200]{2,1,0:T(4,128)(2,1)S(1)} custom-call(s32[1]{0:T(128)} %bitcast.core, s32[4]{0:T(128)} %ids_in.1, s32[4,8]{1,0:T(4,128)} %bitcast.10, f32[2,1024]{1,0:T(2,128)} %table_in.1, f32[1,8]{1,0:T(1,128)} %bitcast.11, f32[1,8]{1,0:T(1,128)} %bitcast.12, f32[1,8]{1,0:T(1,128)} %bitcast.13, bf16[8,4,1024]{2,1,0:T(4,128)(2,1)} %layer.1, ...), custom_call_target="tpu_custom_call" | custom-call | tf_op jit(solution)/shard_map/pallas_call | solution.py:374
  1.7 14.6 %all_to_all.20 = bf16[8,4,3200]{2,1,0:T(4,128)(2,1)S(1)} all-to-all(bf16[8,4,3200]{2,1,0:T(4,128)(2,1)S(1)} %shard_map.137), channel_id=1, replica_groups=mesh['tile'=4,'date'=8] {'date'}, dimensions={0} | all-to-all | bytes 409600 | tf_op jit(solution)/shard_map/all_to_all | solution.py:389
  16.4 0.1 reshape.17.recv
  16.4 0.0 copy-done
  16.4 1.3 %shard_map.138 = (bf16[4,32,640]{2,1,0:T(8,128)(2,1)S(1)}, bf16[16,1408]{1,0:T(8,128)(2,1)S(1)}, bf16[16,1408]{1,0:T(8,128)(2,1)S(1)}, bf16[16,32]{1,0:T(8,128)(2,1)S(1)}) custom-call(s32[1]{0:T(128)} %bitcast.core, bf16[32,3200]{1,0:T(8,128)(2,1)S(1)} %reshape.17.recv, bf16[264,1024]{1,0:T(8,128)(2,1)S(1)} %bitcast.7), custom_call_target="tpu_custom_call" | custom-call | tf_op jit(solution)/shard_map/pallas_call | solution.py:325
  17.7 7.6 %all_to_all.21.recv = bf16[4,32,640]{2,1,0:T(8,128)(2,1)S(1)} all-to-all(bf16[4,32,640]{2,1,0:T(8,128)(2,1)S(1)} %get-tuple-element.19), channel_id=1, replica_groups={{0,9,16,25},{1,8,17,24},{2,11,18,27},{3,10,19,26},{4,13,20,29},{5,12,21..., dimensions={0} | all-to-all | bytes 327680 | tf_op jit(solution)/shard_map/all_to_all | solution.py:408
  25.3 0.3 shard_map.139
  25.6 1.0 %collective-permute-start = (bf16[464,128]{1,0:T(8,128)(2,1)S(1)}, bf16[464,128]{1,0:T(8,128)(2,1)S(1)}, u32[]{:S(2)}, u32[]{:S(2)}) collective-permute-start(bf16[464,128]{1,0:T(8,128)(2,1)S(1)} %get-tuple-element.24), channel_id=1, source_target_pairs={{0,1},{1,0},{2,3},{3,2},{4,5},{5,4},{6,7},{7,6},{8,9},{9,8},{10,11... | collective-permute-start | bytes 356360 | tf_op jit(solution)/shard_map/ppermute | solution.py:418
  26.6 1.0 %collective-permute-done.got = bf16[464,128]{1,0:T(8,128)(2,1)S(1)} collective-permute-done((bf16[464,128]{1,0:T(8,128)(2,1)S(1)}, bf16[464,128]{1,0:T(8,128)(2,1)S(1)}, u32[]{:S(2)}, u32[]{:S(2)}) %collective-permute-start) | collective-permute-done | bytes 118816 | tf_op jit(solution)/shard_map/ppermute | solution.py:418
  27.5 0.1 shard_map.140
  27.6 14.3 %all_to_all.22.recv = bf16[4,360,128]{2,1,0:T(8,128)(2,1)S(1)} all-to-all(bf16[4,360,128]{2,1,0:T(8,128)(2,1)S(1)} %shard_map.140), channel_id=1, replica_groups={{0,2,4,6},{1,3,5,7},{8,10,12,14},{9,11,13,15},{16,18,20,22},{17,19,21,2..., dimensions={0} | all-to-all | bytes 737280 | tf_op jit(solution)/shard_map/all_to_all | solution.py:426
  42.0 8.6 %all_to_all.23.slabs = bf16[4,264,128]{2,1,0:T(8,128)(2,1)S(1)} all-to-all(bf16[4,264,128]{2,1,0:T(8,128)(2,1)S(1)} %get-tuple-element.26), channel_id=1, replica_groups=mesh['tile'=4,'date'=8] {'tile'}, dimensions={0} | all-to-all | bytes 540672 | tf_op jit(solution)/shard_map/all_to_all | solution.py:434
  50.6 0.0 collective-permute-start.1
  50.6 1.2 %shard_map.142 = (bf16[8,4,1024]{2,1,0:T(4,128)(2,1)}, bf16[8,4,1024]{2,1,0:T(4,128)(2,1)}, f32[2,1024]{1,0:T(2,128)}, f32[3,8]{1,0:T(4,128)}, f32[264,1024]{1,0:T(8,128)}) custom-call(s32[1]{0:T(128)} %bitcast.core, bf16[4,264,128]{2,1,0:T(8,128)(2,1)S(1)} %all_to_all.23.slabs, bf16[4,360,128]{2,1,0:T(8,128)(2,1)S(1)} %all_to_all.22.recv, ...), custom_call_target="tpu_custom_call" | custom-call | tf_op jit(solution)/shard_map/pallas_call | solution.py:446
  51.8 0.3 collective-permute-done.1.slabs
  52.1 0.8 %shard_map.143 = f32[264,1024]{1,0:T(8,128)} custom-call(s32[1]{0:T(128)} %bitcast.core, bf16[4,264,128]{2,1,0:T(8,128)(2,1)S(1)} %collective-permute-done.1.slabs, f32[264,1024]{1,0:T(8,128)} %get-tuple-element.30.weight_in), custom_call_target="tpu_custom_call", output_to_operand_aliasing={{}: (2, {})} | custom-call | tf_op jit(solution)/shard_map/pallas_call | solution.py:456
  (1 shorter events, 0.0 us)
Async XLA Ops:
  0.6 15.8 %copy-start = (bf16[1024,264]{0,1:T(8,128)(2,1)S(1)}, bf16[1024,264]{0,1:T(8,128)(2,1)}, u32[]{:S(2)}) copy-start(bf16[1024,264]{0,1:T(8,128)(2,1)} %param.16) | copy-start | bytes 1622020
  25.6 1.9 %collective-permute-start = (bf16[464,128]{1,0:T(8,128)(2,1)S(1)}, bf16[464,128]{1,0:T(8,128)(2,1)S(1)}, u32[]{:S(2)}, u32[]{:S(2)}) collective-permute-start(bf16[464,128]{1,0:T(8,128)(2,1)S(1)} %get-tuple-element.24), channel_id=1, source_target_pairs={{0,1},{1,0},{2,3},{3,2},{4,5},{5,4},{6,7},{7,6},{8,9},{9,8},{10,11... | collective-permute-start | bytes 356360 | tf_op jit(solution)/shard_map/ppermute | solution.py:418
  50.6 1.5 %collective-permute-start.1 = (bf16[4,264,128]{2,1,0:T(8,128)(2,1)S(1)}, bf16[4,264,128]{2,1,0:T(8,128)(2,1)S(1)}, u32[]{:S(2)}, u32[]{:S(2)}) collective-permute-start(bf16[4,264,128]{2,1,0:T(8,128)(2,1)S(1)} %all_to_all.23.slabs), channel_id=1, source_target_pairs={{0,1},{1,0},{2,3},{3,2},{4,5},{5,4},{6,7},{7,6},{8,9},{9,8},{10,11... | collective-permute-start | bytes 811016 | tf_op jit(solution)/shard_map/ppermute | solution.py:441

commit v6 on v5

--- a/solution.py
+++ b/solution.py
@@ -37,7 +37,21 @@
     return high, (x - high.astype(F32)).astype(BF16)
 
 
-def series_kernel(heads, model_d, dates, core, recv, w_t, send, own, give, sel):
+def bit_of(pos, bit):
+    return lax.rem(lax.div(pos[0], 2**bit), 2)
+
+
+def halves(arrays, span, first):
+    kept, given = [], []
+    for array in arrays:
+        for at in range(0, array.shape[0], 2 * span):
+            a, b = array[at : at + span], array[at + span : at + 2 * span]
+            kept.append(jnp.where(first, a, b))
+            given.append(jnp.where(first, b, a))
+    return jnp.concatenate(kept, axis=0), jnp.concatenate(given, axis=0)
+
+
+def series_kernel(heads, model_d, bit, span, pos, recv, w_t, send, own, give, sel):
     length = recv.shape[0]
     tiles, _, width = send.shape
     slab = width - EXT
@@ -111,14 +125,9 @@
     ext_f = jnp.concatenate([grad_keys, grad_reads, tail], axis=1)
     ext = ext_f.astype(BF16)
     back = jnp.concatenate(value_parts + [ext_f], axis=1)
-    first = core[0] == 0
-    own_rows, give_rows = [], []
-    for at in range(0, length, 2 * dates):
-        a, b = back[at : at + dates], back[at + dates : at + 2 * dates]
-        own_rows.append(jnp.where(first, a, b))
-        give_rows.append(jnp.where(first, b, a))
-    own[...] = jnp.concatenate(own_rows, axis=0).astype(BF16)
-    give[...] = jnp.concatenate(give_rows, axis=0).astype(BF16)
+    kept, given = halves([back], span, bit_of(pos, bit) == 0)
+    own[...] = kept.astype(BF16)
+    give[...] = given.astype(BF16)
     for t in range(tiles):
         send[t, :, :EXT] = ext
         send[t, :, EXT:] = recv[:, t * slab : (t + 1) * slab]
@@ -189,7 +198,7 @@
     return rows[0:2] + rows[2:4]
 
 
-def slab_kernel(cols, core, recv, sel, rows, keep, keep_sums, give):
+def slab_kernel(cols, pos, recv, sel, rows, keep, keep_sums, give):
     tiles, length, width = recv.shape
     slab = width - EXT
     half = slab // 2
@@ -200,7 +209,7 @@
     for t in range(tiles):
         sums = sums + nn(sel[...], recv[t, :, :EXT])
     sums = sums[0:2]
-    mine = core[0] == 0
+    mine = bit_of(pos, 0) == 0
     first = lane_pad(part[:, :half], LANES)
     second = lane_pad(part[:, half:], LANES)
     keep[...] = jnp.where(mine, first, second)
@@ -210,9 +219,9 @@
     give[...] = jnp.concatenate([other] + sum_rows(sums) + blocks, axis=0).astype(BF16)
 
 
-def join_kernel(cols, dates, core, keep, keep_sums, got, own, send):
+def join_kernel(cols, dates, pos, keep, keep_sums, got, own, send):
     levels = send.shape[0]
-    first = core[0] == 0
+    first = bit_of(pos, 0) == 0
     model_d = own.shape[1] - EXT
     total = keep[...] + got[:cols, :].astype(F32)
     sums = sum_rows(keep_sums[...] + rows_sum(got[cols : cols + 24, :].astype(F32)))
@@ -253,19 +262,32 @@
     return copies
 
 
-def half_kernel(cols, scale, half, core, slabs, weight_in, weight, held, sems):
-    for copy in store_half(cols, scale, 1 - core[0], half, slabs, weight, held, sems):
+def half_kernel(cols, scale, half, pos, slabs, weight_in, weight, held, sems):
+    for copy in store_half(cols, scale, 1 - bit_of(pos, 0), half, slabs, weight, held, sems):
         copy.wait()
 
 
-def local_weight_kernel(heads, scale, cols, half, core, slabs, recv, rest, w_t, *refs):
+def local_weight_kernel(heads, scale, cols, half, pos, slabs, recv, rest, w_t, *refs):
     outs, held_outs = refs[:5], refs[5:10]
     held, sems, out_sems = held_outs[4], refs[10], refs[11]
-    copies = store_half(cols, scale, core[0], half, slabs, outs[4], held, sems)
+    copies = store_half(cols, scale, bit_of(pos, 0), half, slabs, outs[4], held, sems)
     moves = [pltpu.make_async_copy(held_outs[k], outs[k], out_sems.at[k]) for k in range(4)]
     local_kernel(heads, scale, recv, rest, w_t, *held_outs[:4], moves)
     for copy in copies + moves:
         copy.wait()
+
+
+def write_sums(heads, scale, sums, w, table, head):
+    cols = w.shape[0]
+    high, low = split(sums[:, :cols])
+    table[...] = (nn(high, w) + nn(low, w)) * scale
+    both = sums[0:1] + sums[1:2]
+    at = cols - heads
+    rows = []
+    for k in (1, 0, 2):
+        lo = at + k * heads
+        rows.append(both[:, lo : lo + heads] + both[:, lo + 3 * heads : lo + 4 * heads])
+    head[...] = jnp.concatenate(rows, axis=0) * scale
 
 
 def local_kernel(heads, scale, recv, rest, w_t, value, inputs, table, head, moves=()):
@@ -292,22 +314,14 @@
     last = pltpu.roll(rest[0:8, :], 64, 1)
     sums = jnp.concatenate([rest[8:12, :], rest[12:16, :], last[0:4]], axis=1)
     sums = sums[0:2] + sums[2:4]
-    high, low = split(sums[:, :cols])
-    table[...] = (nn(high, w) + nn(low, w)) * scale
-    both = sums[0:1] + sums[1:2]
-    at = cols - heads
-    rows = []
-    for k in (1, 0, 2):
-        lo = at + k * heads
-        rows.append(both[:, lo : lo + heads] + both[:, lo + 3 * heads : lo + 4 * heads])
-    head[...] = jnp.concatenate(rows, axis=0) * scale
+    write_sums(heads, scale, sums, w, table, head)
     for move in moves[2:]:
         move.start()
 
 
-def gather_kernel(cols, half, scale, core, own, other, out):
+def gather_kernel(cols, half, scale, pos, own, other, out):
     tiles = own.shape[0]
-    mine = core[0] == 0
+    mine = bit_of(pos, 0) == 0
     for t in range(tiles):
         a = own[t].astype(F32)
         b = other[t].astype(F32)
@@ -329,6 +343,302 @@
         out_specs=[VMEM] * len(outs),
         compiler_params=pltpu.CompilerParams(vmem_limit_bytes=48 * 1024 * 1024),
     )(*ins)
+
+
+def rows_block(rows):
+    return [rows[:, b * LANES : (b + 1) * LANES] for b in range(rows.shape[1] // LANES)]
+
+
+def block_rows(block, count):
+    return jnp.concatenate([block[k : k + count] for k in range(0, block.shape[0], count)], axis=1)
+
+
+def group_slab_kernel(cols, dates, pos, recv, sel, rows_own, rows_got, keep, keep_sums, rows_keep, give):
+    peers, length, _ = recv.shape
+    count = keep.shape[0]
+    first = bit_of(pos, 0) == 0
+    ext = recv[:, :, :EXT].reshape(peers * length, EXT)
+    tokens = recv[:, :, EXT:].reshape(peers * length, LANES)
+    part = tn(ext, tokens)[:cols]
+    sums = jnp.zeros((16, EXT), F32)
+    for t in range(peers):
+        sums = sums + nn(sel[...], recv[t, :, :EXT])
+    sums = sums[0:2]
+    upper, lower = part[:count], part[cols - count :]
+    keep[...] = jnp.where(first, upper, lower)
+    keep_sums[...] = sums
+    kept, given = halves([rows_own[...].astype(F32), rows_got[...].astype(F32)], dates, first)
+    rows_keep[...] = kept.astype(BF16)
+    give[...] = jnp.concatenate(
+        [jnp.where(first, lower, upper)] + sum_rows(sums) + rows_block(given), axis=0
+    ).astype(BF16)
+
+
+def group_join_kernel(dates, pos, keep, keep_sums, rows_own, got, rows_keep, give):
+    count = keep.shape[0]
+    first = bit_of(pos, 2) == 0
+    total = keep[...] + got[:count, :].astype(F32)
+    sums = keep_sums[...] + rows_sum(got[count : count + 24, :].astype(F32))
+    rows_got = block_rows(got[count + 24 :, :].astype(F32), rows_own.shape[0])
+    kept, given = halves([rows_own[...].astype(F32), rows_got], dates, first)
+    rows_keep[...] = kept.astype(BF16)
+    give[...] = jnp.concatenate([total] + sum_rows(sums) + rows_block(given), axis=0).astype(BF16)
+
+
+def group_total_kernel(own, got, send, rest):
+    count = send.shape[1]
+    total = own[: count + 24, :].astype(F32) + got[: count + 24, :].astype(F32)
+    slab = total[:count].astype(BF16)
+    for t in range(send.shape[0]):
+        send[t] = slab
+    rest[...] = total[count:]
+
+
+def store_rows(cols, scale, core, slabs, weight, held, sems):
+    count = slabs.shape[1]
+    base = cols - count
+    for t in range(slabs.shape[0]):
+        held[:, t * LANES : (t + 1) * LANES] = slabs[t].astype(F32) * scale
+    at = pl.multiple_of(core * base, 8)
+    main = pltpu.make_async_copy(held.at[:base], weight.at[pl.ds(at, base)], sems.at[0])
+    last = pltpu.make_async_copy(held.at[base:], weight.at[2 * base :], sems.at[1])
+    main.start()
+
+    @pl.when(core == 1)
+    def _():
+        last.start()
+
+    def wait():
+        main.wait()
+
+        @pl.when(core == 1)
+        def _():
+            last.wait()
+
+    return wait
+
+
+def other_rows_kernel(cols, scale, pos, slabs, weight_in, weight, held, sems):
+    store_rows(cols, scale, 1 - bit_of(pos, 0), slabs, weight, held, sems)()
+
+
+def final_kernel(heads, scale, pos, slabs, rows_own, got, rest, w_t, *refs):
+    outs, (value, inputs, table, head), (held, sems, out_sems) = refs[:5], refs[5:9], refs[9:]
+    model_d, cols, dates = w_t.shape[1], w_t.shape[0], value.shape[1]
+    wait = store_rows(cols, scale, bit_of(pos, 0), slabs, outs[4], held, sems)
+    moves = [
+        pltpu.make_async_copy(source, outs[k], out_sems.at[k])
+        for k, source in enumerate((value, inputs, table, head))
+    ]
+    w = w_t[...]
+    rows_got = block_rows(got[slabs.shape[1] + 24 :, :].astype(F32), rows_own.shape[0])
+    rows = jnp.concatenate([rows_own[...].astype(F32), rows_got], axis=0)
+    masks = [4 * high + core + 2 * low for high in range(2) for core in range(2) for low in range(2)]
+    where_to = []
+    for mask in masks:
+        index = 0
+        for bit in range(3):
+            here = bit_of(pos, bit)
+            index = index + 2**bit * (1 - here if mask >> bit & 1 else here)
+        where_to.append(index)
+    for k, pixel in enumerate(where_to):
+        value[pixel] = rows[k * dates : (k + 1) * dates, :model_d].astype(BF16)
+    moves[0].start()
+    grads = nn(rows[:, model_d : model_d + EXT].astype(BF16)[:, :cols], w)
+    for k, pixel in enumerate(where_to):
+        inputs[pixel] = grads[k * dates : (k + 1) * dates].astype(BF16)
+    moves[1].start()
+    write_sums(heads, scale, rows_sum(rest[...]), w, table, head)
+    for move in moves[2:]:
+        move.start()
+    wait()
+    for move in moves:
+        move.wait()
+
+
+def finish_four_levels(series, w_t, date_s, heads, scale, pixel_dev, dates_dev, tiles, dates):
+    length = series.shape[0]
+    cols, model_d = w_t.shape
+    peers = 2 * tiles
+    wide = model_d + EXT
+    count = (cols + 8) // 2
+    half_rows = length // 2
+    payload = count + 24 + half_rows * wide // LANES
+
+    def groups(alternate):
+        return [
+            [t * dates + 4 * high + 2 * low + (c + alternate * t) % 2 for t in range(tiles) for low in range(2)]
+            for high in range(2)
+            for c in range(2)
+        ]
+
+    def across(bit):
+        return [(i, i ^ 2**bit) for i in range(dates)]
+
+    send_t, rows_own, rows_give, sel = call(
+        functools.partial(series_kernel, heads, model_d, 1, 2 * dates_dev),
+        [
+            ((peers, length, EXT + LANES), BF16),
+            ((half_rows, wide), BF16),
+            ((half_rows, wide), BF16),
+            ((16, length), BF16),
+        ],
+        [date_s, series, w_t],
+        1,
+    )
+    recv_t = lax.all_to_all(
+        send_t, ("tile", "date"), split_axis=0, concat_axis=0, tiled=True, axis_index_groups=groups(1)
+    )
+    rows_got = lax.ppermute(rows_give, "date", across(1))
+    keep, keep_sums, rows_own, give = call(
+        functools.partial(group_slab_kernel, cols, dates_dev),
+        [((count, LANES), F32), ((2, EXT), F32), ((half_rows, wide), BF16), ((payload, LANES), BF16)],
+        [date_s, recv_t, sel, rows_own, rows_got],
+        1,
+    )
+    got = lax.ppermute(give, "date", across(0))
+    rows_own, give = call(
+        functools.partial(group_join_kernel, dates_dev),
+        [((half_rows, wide), BF16), ((payload, LANES), BF16)],
+        [date_s, keep, keep_sums, rows_own, got],
+        1,
+    )
+    got = lax.ppermute(give, "date", across(2))
+    send_g, rest = call(
+        group_total_kernel, [((peers, count, LANES), BF16), ((24, LANES), F32)], [give, got]
+    )
+    recv_g = lax.all_to_all(
+        send_g, ("tile", "date"), split_axis=0, concat_axis=0, tiled=True, axis_index_groups=groups(0)
+    )
+    other_g = lax.ppermute(recv_g, "date", across(0))
+    outs = [
+        jax.ShapeDtypeStruct((pixel_dev, dates_dev, model_d), BF16),
+        jax.ShapeDtypeStruct((pixel_dev, dates_dev, model_d), BF16),
+        jax.ShapeDtypeStruct((2, model_d), F32),
+        jax.ShapeDtypeStruct((3, heads), F32),
+        jax.ShapeDtypeStruct((cols, model_d), F32),
+    ]
+    held = [pltpu.VMEM((count, model_d), F32), pltpu.SemaphoreType.DMA((2,))]
+    limit = pltpu.CompilerParams(vmem_limit_bytes=48 * 1024 * 1024)
+    value, inputs, table, head, weight_t = pl.pallas_call(
+        functools.partial(final_kernel, heads, scale),
+        out_shape=outs,
+        in_specs=[SMEM] + [VMEM] * 5,
+        out_specs=[HBM] * 5,
+        scratch_shapes=[pltpu.VMEM(o.shape, o.dtype) for o in outs[:4]]
+        + held
+        + [pltpu.SemaphoreType.DMA((4,))],
+        compiler_params=limit,
+    )(date_s, recv_g, rows_own, got, rest, w_t)
+    weight_t = pl.pallas_call(
+        functools.partial(other_rows_kernel, cols, scale),
+        out_shape=outs[4],
+        in_specs=[SMEM, VMEM, HBM],
+        out_specs=HBM,
+        scratch_shapes=held,
+        input_output_aliases={2: 0},
+        compiler_params=limit,
+    )(date_s, other_g, weight_t)
+    return value, inputs, weight_t.T, table, head
+
+
+def finish_any(series, w_t, date_s, heads, scale, pixel_dev, dates_dev, tiles, dates):
+    length = series.shape[0]
+    cols, model_d = w_t.shape
+    levels = dates // 2
+    slab = model_d // tiles
+    half = slab // 2
+    swap = [(i, i ^ 1) for i in range(dates)]
+    planes = [[2 * z + c for z in range(levels)] for c in range(2)]
+    rows_core = length // 2
+    send_t, own, give_rows, sel = call(
+        functools.partial(series_kernel, heads, model_d, 0, dates_dev),
+        [
+            ((tiles, length, EXT + slab), BF16),
+            ((rows_core, model_d + EXT), BF16),
+            ((rows_core, model_d + EXT), BF16),
+            ((16, length), BF16),
+        ],
+        [date_s, series, w_t],
+        1,
+    )
+    mixed = [
+        [t * dates + 2 * z + (c + t) % 2 for t in range(tiles)] for z in range(levels) for c in range(2)
+    ]
+    recv_t = lax.all_to_all(
+        send_t, ("tile", "date"), split_axis=0, concat_axis=0, tiled=True, axis_index_groups=mixed
+    )
+    rows_give = cols + 24 + rows_core * (model_d + EXT) // LANES
+    keep, keep_sums, give = call(
+        functools.partial(slab_kernel, cols),
+        [((cols, LANES), F32), ((2, EXT), F32), ((rows_give, LANES), BF16)],
+        [date_s, recv_t, sel, give_rows],
+        1,
+    )
+    got = lax.ppermute(give, "date", swap)
+    rows_z = cols + 32 + model_d // 16
+    (send_z,) = call(
+        functools.partial(join_kernel, cols, dates_dev),
+        [((levels, rows_z, LANES), BF16)],
+        [date_s, keep, keep_sums, got, own],
+        1,
+    )
+    recv_z = lax.all_to_all(
+        send_z, "date", split_axis=0, concat_axis=0, tiled=True, axis_index_groups=planes
+    )
+    send_g, rest = call(
+        functools.partial(total_kernel, cols),
+        [((tiles, cols, LANES), BF16), ((16, LANES), F32)],
+        [recv_z],
+    )
+    recv_g = lax.all_to_all(send_g, "tile", split_axis=0, concat_axis=0, tiled=True)
+    local_outs = [
+        ((pixel_dev, dates_dev, model_d), BF16),
+        ((pixel_dev, dates_dev, model_d), BF16),
+        ((2, model_d), F32),
+        ((3, heads), F32),
+    ]
+    other_g = lax.ppermute(recv_g, "date", swap)
+    if half % LANES == 0:
+        weight_shape = jax.ShapeDtypeStruct((cols, model_d), F32)
+        held = [pltpu.VMEM((tiles, cols, half), F32), pltpu.SemaphoreType.DMA((tiles,))]
+        limit = pltpu.CompilerParams(vmem_limit_bytes=48 * 1024 * 1024)
+        value, inputs, table, head, weight_t = pl.pallas_call(
+            functools.partial(local_weight_kernel, heads, scale, cols, half),
+            out_shape=[jax.ShapeDtypeStruct(s, d) for s, d in local_outs] + [weight_shape],
+            in_specs=[SMEM] + [VMEM] * 4,
+            out_specs=[HBM] * 5,
+            scratch_shapes=[pltpu.VMEM(s, d) for s, d in local_outs]
+            + held
+            + [pltpu.SemaphoreType.DMA((4,))],
+            compiler_params=limit,
+        )(date_s, recv_g, recv_z, rest, w_t)
+        weight_t = pl.pallas_call(
+            functools.partial(half_kernel, cols, scale, half),
+            out_shape=weight_shape,
+            in_specs=[SMEM, VMEM, HBM],
+            out_specs=HBM,
+            scratch_shapes=held,
+            input_output_aliases={2: 0},
+            compiler_params=limit,
+        )(date_s, other_g, weight_t)
+    else:
+        value, inputs, table, head = call(
+            functools.partial(local_kernel, heads, scale), local_outs, [recv_z, rest, w_t]
+        )
+        (weight_t,) = call(
+            functools.partial(gather_kernel, cols, half, scale),
+            [((cols, model_d), F32)],
+            [date_s, recv_g, other_g],
+            1,
+        )
+    return (
+        value,
+        inputs,
+        weight_t.T,
+        table,
+        head,
+    )
 
 
 def on_device(
@@ -345,7 +655,6 @@
 ):
     pixel_dev, dates_dev, model_d = layer_input.shape
     heads = step_bias.shape[0]
-    cols = proj_weight.shape[1]
     tiles = lax.axis_size("tile")
     dates = lax.axis_size("date")
     assert pixel_dev == dates and dates % 2 == 0
@@ -353,12 +662,9 @@
     length = dates * dates_dev
     slab = model_d // tiles
     half = slab // 2
-    core = lax.axis_index("date") % 2
-    core_s = core.astype(jnp.int32).reshape(1)
+    date_s = lax.axis_index("date").astype(jnp.int32).reshape(1)
     w_t = proj_weight.T
     scale = 1.0 / math.sqrt(pixel_dev * dates_dev * tiles * dates)
-    swap = [(i, i ^ 1) for i in range(dates)]
-    planes = [[2 * z + c for z in range(levels)] for c in range(2)]
 
     operands = [
         sensor_ids,
@@ -385,100 +691,16 @@
             pltpu.SemaphoreType.DMA((9,)),
         ],
         compiler_params=pltpu.CompilerParams(vmem_limit_bytes=16 * 1024 * 1024),
-    )(core_s, *[pltpu.with_memory_space_constraint(operand, pltpu.HBM) for operand in operands])
+    )(date_s, *[pltpu.with_memory_space_constraint(operand, pltpu.HBM) for operand in operands])
     series = lax.all_to_all(packed, "date", split_axis=0, concat_axis=0, tiled=True).reshape(
         length, 3 * model_d + LANES
     )
 
-    rows_core = length // 2
-    send_t, own, give_rows, sel = call(
-        functools.partial(series_kernel, heads, model_d, dates_dev),
-        [
-            ((tiles, length, EXT + slab), BF16),
-            ((rows_core, model_d + EXT), BF16),
-            ((rows_core, model_d + EXT), BF16),
-            ((16, length), BF16),
-        ],
-        [core_s, series, w_t],
-        1,
-    )
-    mixed = [
-        [t * dates + 2 * z + (c + t) % 2 for t in range(tiles)] for z in range(levels) for c in range(2)
-    ]
-    recv_t = lax.all_to_all(
-        send_t, ("tile", "date"), split_axis=0, concat_axis=0, tiled=True, axis_index_groups=mixed
-    )
-    rows_give = cols + 24 + rows_core * (model_d + EXT) // LANES
-    keep, keep_sums, give = call(
-        functools.partial(slab_kernel, cols),
-        [((cols, LANES), F32), ((2, EXT), F32), ((rows_give, LANES), BF16)],
-        [core_s, recv_t, sel, give_rows],
-        1,
-    )
-    got = lax.ppermute(give, "date", swap)
-    rows_z = cols + 32 + model_d // 16
-    (send_z,) = call(
-        functools.partial(join_kernel, cols, dates_dev),
-        [((levels, rows_z, LANES), BF16)],
-        [core_s, keep, keep_sums, got, own],
-        1,
-    )
-    recv_z = lax.all_to_all(
-        send_z, "date", split_axis=0, concat_axis=0, tiled=True, axis_index_groups=planes
-    )
-    send_g, rest = call(
-        functools.partial(total_kernel, cols),
-        [((tiles, cols, LANES), BF16), ((16, LANES), F32)],
-        [recv_z],
-    )
-    recv_g = lax.all_to_all(send_g, "tile", split_axis=0, concat_axis=0, tiled=True)
-    local_outs = [
-        ((pixel_dev, dates_dev, model_d), BF16),
-        ((pixel_dev, dates_dev, model_d), BF16),
-        ((2, model_d), F32),
-        ((3, heads), F32),
-    ]
-    other_g = lax.ppermute(recv_g, "date", swap)
-    if half % LANES == 0:
-        weight_shape = jax.ShapeDtypeStruct((cols, model_d), F32)
-        held = [pltpu.VMEM((tiles, cols, half), F32), pltpu.SemaphoreType.DMA((tiles,))]
-        limit = pltpu.CompilerParams(vmem_limit_bytes=48 * 1024 * 1024)
-        value, inputs, table, head, weight_t = pl.pallas_call(
-            functools.partial(local_weight_kernel, heads, scale, cols, half),
-            out_shape=[jax.ShapeDtypeStruct(s, d) for s, d in local_outs] + [weight_shape],
-            in_specs=[SMEM] + [VMEM] * 4,
-            out_specs=[HBM] * 5,
-            scratch_shapes=[pltpu.VMEM(s, d) for s, d in local_outs]
-            + held
-            + [pltpu.SemaphoreType.DMA((4,))],
-            compiler_params=limit,
-        )(core_s, recv_g, recv_z, rest, w_t)
-        weight_t = pl.pallas_call(
-            functools.partial(half_kernel, cols, scale, half),
-            out_shape=weight_shape,
-            in_specs=[SMEM, VMEM, HBM],
-            out_specs=HBM,
-            scratch_shapes=held,
-            input_output_aliases={2: 0},
-            compiler_params=limit,
-        )(core_s, other_g, weight_t)
+    if levels == 4 and model_d == 2 * LANES * tiles:
+        finish = finish_four_levels
     else:
-        value, inputs, table, head = call(
-            functools.partial(local_kernel, heads, scale), local_outs, [recv_z, rest, w_t]
-        )
-        (weight_t,) = call(
-            functools.partial(gather_kernel, cols, half, scale),
-            [((cols, model_d), F32)],
-            [core_s, recv_g, other_g],
-            1,
-        )
-    return (
-        value,
-        inputs,
-        weight_t.T,
-        table,
-        head,
-    )
+        finish = finish_any
+    return finish(series, w_t, date_s, heads, scale, pixel_dev, dates_dev, tiles, dates)
 
 
 def solution(mesh):

time: 53.3 us -> 51.4 us (0.964)
  blocking collectives: 45.2 us -> 24.7 us
  waiting for transfers between devices: 1.27 us -> 12.5 us
  starting transfers between devices: 0.98 us -> 7.68 us
  Pallas kernels: 4.82 us -> 5.51 us
    all_to_all x3 -> x1, blocking collectives: 30.5 us -> 10.1 us  [finish_four_levels(): lax.all_to_all(send_g, ('tile', 'date'), split_axis=0, concat_axis=0, til...]
    ppermute x2 -> x4, waiting for transfers between devices: 1.27 us -> 12.3 us  [the longest x1 6.02 us: finish_four_levels(): got = lax.ppermute(give, 'date', across(2))]
    all_to_all x0 -> x1, starting transfers between devices: none -> 3.41 us  [finish_four_levels(): lax.all_to_all(send_t, ('tile', 'date'), split_axis=0, concat_axis=0, til...]
    ppermute x2 -> x4, starting transfers between devices: 0.98 us -> 4.26 us  [the longest x1 1.92 us: finish_four_levels(): rows_got = lax.ppermute(rows_give, 'date', across(1))]
    pallas_call x4, Pallas kernels: 1.67 us -> 2.33 us  [call(): pl.pallas_call(kernel, out_shape=[jax.ShapeDtypeStruct(s, d) for s, d in...]
  transfers between devices with their start and end apart: 2 -> 5, of which waited for: 2 -> 5; matrix products, arithmetic and copies ran while one was open for 0% -> 0% of each run, Pallas kernels for 2% -> 2%
where the time goes in v6:
time: 51.4 us; the launch traced here: 51.1 us
  blocking collectives  24.7 us (48%)
  waiting for transfers between devices  12.5 us (24%)
  starting transfers between devices  7.68 us (15%)
  Pallas kernels  5.51 us (11%)
  between operations  0.7 us (1%)
    all_to_all x1, blocking collectives, on_device(): lax.all_to_all(packed, 'date', split_axis=0, concat_axis=0, tiled=True)  14.6 us
    all_to_all x1, blocking collectives, finish_four_levels(): lax.all_to_all(send_g, ('tile', 'date'), split_axis=0, concat_axis=0, til...  10.1 us
    ppermute x1, waiting for transfers between devices, finish_four_levels(): got = lax.ppermute(give, 'date', across(2))  6.02 us
    ppermute x1, waiting for transfers between devices, finish_four_levels(): rows_got = lax.ppermute(rows_give, 'date', across(1))  5.07 us
    all_to_all x1, starting transfers between devices, finish_four_levels(): lax.all_to_all(send_t, ('tile', 'date'), split_axis=0, concat_axis=0, til...  3.41 us
    pallas_call x4, Pallas kernels, call(): pl.pallas_call(kernel, out_shape=[jax.ShapeDtypeStruct(s, d) for s, d in...  2.33 us
    ppermute x1, starting transfers between devices, finish_four_levels(): rows_got = lax.ppermute(rows_give, 'date', across(1))  1.92 us
    ppermute x1, starting transfers between devices, finish_four_levels(): got = lax.ppermute(give, 'date', across(2))  1.36 us
  transfers between devices with their start and end apart: 5, of which 5 were waited for; matrix products, arithmetic and copies ran while one was open for 0% of the time, Pallas kernels for 2%

profile of v6, /device:TPU:0, one launch (start us, length us, event | category | flops | bytes accessed | tf_op | source)
XLA Modules:
  0.0 51.1 jit_solution(11736053986542088696)
XLA Ops:
  0.6 0.0 copy-start
  0.6 1.1 %shard_map.137 = bf16[8,4,3200]{2,1,0:T(4,128)(2,1)S(1)} custom-call(s32[1]{0:T(128)} %bitcast.core.pos, s32[4]{0:T(128)} %ids_in.1, s32[4,8]{1,0:T(4,128)} %bitcast.10, f32[2,1024]{1,0:T(2,128)} %table_in.1, f32[1,8]{1,0:T(1,128)} %bitcast.11, f32[1,8]{1,0:T(1,128)} %bitcast.12, f32[1,8]{1,0:T(1,128)} %bitcast.13, bf16[8,4,1024]{2,1,0:T(4,128)(2,1)} %layer.1, ...), custom_call_target="tpu_custom_call" | custom-call | tf_op jit(solution)/shard_map/pallas_call | solution.py:680
  1.7 14.6 %all_to_all.15 = bf16[8,4,3200]{2,1,0:T(4,128)(2,1)S(1)} all-to-all(bf16[8,4,3200]{2,1,0:T(4,128)(2,1)S(1)} %shard_map.137), channel_id=1, replica_groups=mesh['tile'=4,'date'=8] {'date'}, dimensions={0} | all-to-all | bytes 409600 | tf_op jit(solution)/shard_map/all_to_all | solution.py:695
  16.4 0.1 reshape.17.recv
  16.4 0.0 copy-done
  16.4 2.0 %shard_map.138 = (bf16[8,32,512]{2,1,0:T(8,128)(2,1)}, bf16[16,1408]{1,0:T(8,128)(2,1)S(1)}, bf16[16,1408]{1,0:T(8,128)(2,1)S(1)}, bf16[16,32]{1,0:T(8,128)(2,1)S(1)}) custom-call(s32[1]{0:T(128)} %bitcast.core.pos, bf16[32,3200]{1,0:T(8,128)(2,1)S(1)} %reshape.17.recv, bf16[264,1024]{1,0:T(8,128)(2,1)S(1)} %bitcast.7), custom_call_target="tpu_custom_call" | custom-call | tf_op jit(solution)/shard_map/pallas_call | solution.py:339
  18.4 3.4 %all-to-all-start.1 = ((bf16[8,32,512]{2,1,0:T(8,128)(2,1)}), bf16[8,32,512]{2,1,0:T(8,128)(2,1)S(1)}, u32[]{:S(2)}, u32[]{:S(2)}) async-start(bf16[8,32,512]{2,1,0:T(8,128)(2,1)} %get-tuple-element.22), calls=%async_computation.1 | async-start | bytes 524288 | tf_op jit(solution)/shard_map/all_to_all | solution.py:489
  21.8 1.9 %collective-permute-start = (bf16[16,1408]{1,0:T(8,128)(2,1)S(1)}, bf16[16,1408]{1,0:T(8,128)(2,1)S(1)}, u32[]{:S(2)}, u32[]{:S(2)}) collective-permute-start(bf16[16,1408]{1,0:T(8,128)(2,1)S(1)} %get-tuple-element.25), channel_id=1, source_target_pairs={{0,2},{1,3},{2,0},{3,1},{4,6},{5,7},{6,4},{7,5},{8,10},{9,11},{10,... | collective-permute-start | bytes 135176 | tf_op jit(solution)/shard_map/ppermute | solution.py:492
  23.7 5.1 %collective-permute-done.rows_got = bf16[16,1408]{1,0:T(8,128)(2,1)S(1)} collective-permute-done((bf16[16,1408]{1,0:T(8,128)(2,1)S(1)}, bf16[16,1408]{1,0:T(8,128)(2,1)S(1)}, u32[]{:S(2)}, u32[]{:S(2)}) %collective-permute-start) | collective-permute-done | bytes 45088 | tf_op jit(solution)/shard_map/ppermute | solution.py:492
  28.8 0.1 all-to-all-done.1.recv
  28.9 0.3 shard_map.139
  29.2 1.0 %collective-permute-start.1 = (bf16[336,128]{1,0:T(8,128)(2,1)S(1)}, bf16[336,128]{1,0:T(8,128)(2,1)S(1)}, u32[]{:S(2)}, u32[]{:S(2)}) collective-permute-start(bf16[336,128]{1,0:T(8,128)(2,1)S(1)} %get-tuple-element.29), channel_id=1, source_target_pairs={{0,1},{1,0},{2,3},{3,2},{4,5},{5,4},{6,7},{7,6},{8,9},{9,8},{10,11... | collective-permute-start | bytes 258056 | tf_op jit(solution)/shard_map/ppermute | solution.py:499
  30.2 0.9 %collective-permute-done.1.got = bf16[336,128]{1,0:T(8,128)(2,1)S(1)} collective-permute-done((bf16[336,128]{1,0:T(8,128)(2,1)S(1)}, bf16[336,128]{1,0:T(8,128)(2,1)S(1)}, u32[]{:S(2)}, u32[]{:S(2)}) %collective-permute-start.1) | collective-permute-done | bytes 86048 | tf_op jit(solution)/shard_map/ppermute | solution.py:499
  31.1 0.1 shard_map.140
  31.2 1.4 %collective-permute-start.2 = (bf16[336,128]{1,0:T(8,128)(2,1)S(1)}, bf16[336,128]{1,0:T(8,128)(2,1)S(1)}, u32[]{:S(2)}, u32[]{:S(2)}) collective-permute-start(bf16[336,128]{1,0:T(8,128)(2,1)S(1)} %get-tuple-element.30.own), channel_id=1, source_target_pairs={{0,4},{1,5},{2,6},{3,7},{4,0},{5,1},{6,2},{7,3},{8,12},{9,13},{10,... | collective-permute-start | bytes 258056 | tf_op jit(solution)/shard_map/ppermute | solution.py:506
  32.6 6.0 %collective-permute-done.2.got = bf16[336,128]{1,0:T(8,128)(2,1)S(1)} collective-permute-done((bf16[336,128]{1,0:T(8,128)(2,1)S(1)}, bf16[336,128]{1,0:T(8,128)(2,1)S(1)}, u32[]{:S(2)}, u32[]{:S(2)}) %collective-permute-start.2) | collective-permute-done | bytes 86048 | tf_op jit(solution)/shard_map/ppermute | solution.py:506
  38.6 10.1 %all_to_all.16.slabs = bf16[8,136,128]{2,1,0:T(8,128)(2,1)S(1)} all-to-all(bf16[8,136,128]{2,1,0:T(8,128)(2,1)S(1)} %get-tuple-element.31), channel_id=1, replica_groups={{0,2,8,10,16,18,24,26},{1,3,9,11,17,19,25,27},{4,6,12,14,20,22,28,30},{..., dimensions={0} | all-to-all | bytes 557056 | tf_op jit(solution)/shard_map/all_to_all | solution.py:510
  48.7 0.0 collective-permute-start.3
  48.7 1.2 %shard_map.142 = (bf16[8,4,1024]{2,1,0:T(4,128)(2,1)}, bf16[8,4,1024]{2,1,0:T(4,128)(2,1)}, f32[2,1024]{1,0:T(2,128)}, f32[3,8]{1,0:T(4,128)}, f32[264,1024]{1,0:T(8,128)}) custom-call(s32[1]{0:T(128)} %bitcast.core.pos, bf16[8,136,128]{2,1,0:T(8,128)(2,1)S(1)} %all_to_all.16.slabs, bf16[16,1408]{1,0:T(8,128)(2,1)S(1)} %get-tuple-element.32.rows_own, ...), custom_call_target="tpu_custom_call" | custom-call | tf_op jit(solution)/shard_map/pallas_call | solution.py:523
  49.9 0.3 collective-permute-done.3.slabs
  50.2 0.9 %shard_map.143 = f32[264,1024]{1,0:T(8,128)} custom-call(s32[1]{0:T(128)} %bitcast.core.pos, bf16[8,136,128]{2,1,0:T(8,128)(2,1)S(1)} %collective-permute-done.3.slabs, f32[264,1024]{1,0:T(8,128)} %get-tuple-element.36.weight_in), custom_call_target="tpu_custom_call", output_to_operand_aliasing={{}: (2, {})} | custom-call | tf_op jit(solution)/shard_map/pallas_call | solution.py:533
  (1 shorter events, 0.0 us)
Async XLA Ops:
  0.6 15.8 %copy-start = (bf16[1024,264]{0,1:T(8,128)(2,1)S(1)}, bf16[1024,264]{0,1:T(8,128)(2,1)}, u32[]{:S(2)}) copy-start(bf16[1024,264]{0,1:T(8,128)(2,1)} %param.16) | copy-start | bytes 1622020
  18.4 10.5 %all-to-all-start.1 = ((bf16[8,32,512]{2,1,0:T(8,128)(2,1)}), bf16[8,32,512]{2,1,0:T(8,128)(2,1)S(1)}, u32[]{:S(2)}, u32[]{:S(2)}) async-start(bf16[8,32,512]{2,1,0:T(8,128)(2,1)} %get-tuple-element.22), calls=%async_computation.1 | async-start | bytes 524288 | tf_op jit(solution)/shard_map/all_to_all | solution.py:489
  21.8 7.0 %collective-permute-start = (bf16[16,1408]{1,0:T(8,128)(2,1)S(1)}, bf16[16,1408]{1,0:T(8,128)(2,1)S(1)}, u32[]{:S(2)}, u32[]{:S(2)}) collective-permute-start(bf16[16,1408]{1,0:T(8,128)(2,1)S(1)} %get-tuple-element.25), channel_id=1, source_target_pairs={{0,2},{1,3},{2,0},{3,1},{4,6},{5,7},{6,4},{7,5},{8,10},{9,11},{10,... | collective-permute-start | bytes 135176 | tf_op jit(solution)/shard_map/ppermute | solution.py:492
  29.2 1.9 %collective-permute-start.1 = (bf16[336,128]{1,0:T(8,128)(2,1)S(1)}, bf16[336,128]{1,0:T(8,128)(2,1)S(1)}, u32[]{:S(2)}, u32[]{:S(2)}) collective-permute-start(bf16[336,128]{1,0:T(8,128)(2,1)S(1)} %get-tuple-element.29), channel_id=1, source_target_pairs={{0,1},{1,0},{2,3},{3,2},{4,5},{5,4},{6,7},{7,6},{8,9},{9,8},{10,11... | collective-permute-start | bytes 258056 | tf_op jit(solution)/shard_map/ppermute | solution.py:499
  31.2 7.4 %collective-permute-start.2 = (bf16[336,128]{1,0:T(8,128)(2,1)S(1)}, bf16[336,128]{1,0:T(8,128)(2,1)S(1)}, u32[]{:S(2)}, u32[]{:S(2)}) collective-permute-start(bf16[336,128]{1,0:T(8,128)(2,1)S(1)} %get-tuple-element.30.own), channel_id=1, source_target_pairs={{0,4},{1,5},{2,6},{3,7},{4,0},{5,1},{6,2},{7,3},{8,12},{9,13},{10,... | collective-permute-start | bytes 258056 | tf_op jit(solution)/shard_map/ppermute | solution.py:506
  48.7 1.6 %collective-permute-start.3 = (bf16[8,136,128]{2,1,0:T(8,128)(2,1)S(1)}, bf16[8,136,128]{2,1,0:T(8,128)(2,1)S(1)}, u32[]{:S(2)}, u32[]{:S(2)}) collective-permute-start(bf16[8,136,128]{2,1,0:T(8,128)(2,1)S(1)} %all_to_all.16.slabs), channel_id=1, source_target_pairs={{0,1},{1,0},{2,3},{3,2},{4,5},{5,4},{6,7},{7,6},{8,9},{9,8},{10,11... | collective-permute-start | bytes 835592 | tf_op jit(solution)/shard_map/ppermute | solution.py:513

commit v7 on v6

--- a/solution.py
+++ b/solution.py
@@ -51,10 +51,8 @@
     return jnp.concatenate(kept, axis=0), jnp.concatenate(given, axis=0)
 
 
-def series_kernel(heads, model_d, bit, span, pos, recv, w_t, send, own, give, sel):
+def series_terms(heads, model_d, recv, w_t):
     length = recv.shape[0]
-    tiles, _, width = send.shape
-    slab = width - EXT
     width_p = model_d // heads
     states = (w_t.shape[0] - heads) // 2
     mixed = recv[:, :model_d]
@@ -89,7 +87,7 @@
     scores_t = nt(keys, reads)
 
     pair_t = jnp.zeros((length, length), F32)
-    value_parts, weighted_cols, read_rows, skip_cols = [], [], [], []
+    mixes, weighted_cols, read_rows, skip_cols = [], [], [], []
     for h in range(heads):
         lo = model_d + h * width_p
         x_h = recv[:, lo : lo + width_p]
@@ -105,7 +103,7 @@
         weighted_cols.append(weighted)
         read_rows.append(jnp.sum(both * dt_h, axis=0, keepdims=True))
         skip_cols.append(jnp.sum(cross * eye, axis=1, keepdims=True))
-        value_parts.append(nn(mix.astype(BF16), g_h) * dt_h + skip[:, h : h + 1] * g_h.astype(F32))
+        mixes.append((mix.astype(BF16), g_h, dt_h, skip[:, h : h + 1]))
 
     weighted = jnp.concatenate(weighted_cols, axis=1)
     read_sum = jnp.concatenate(read_rows, axis=0)
@@ -120,21 +118,66 @@
     terms = jnp.concatenate(
         [raw, decay_terms, skip_terms, jnp.zeros((length, LANES - 3 * heads), F32)], axis=1
     )
+    ids_row = jnp.sum(eye * ids, axis=0, keepdims=True)
+    return mixes, grad_keys, grad_reads, raw, terms, ids_row, eye_h
+
+
+def value_columns(mixes):
+    return [nn(mix, g_h) * dt_h + skip_h * g_h.astype(F32) for mix, g_h, dt_h, skip_h in mixes]
+
+
+def sensor_rows(ids_row):
+    zeros = jnp.zeros((14, ids_row.shape[1]), F32)
+    return jnp.concatenate([1.0 - ids_row, ids_row, zeros], axis=0).astype(BF16)
+
+
+def series_kernel(heads, model_d, bit, span, pos, recv, w_t, send, own, give, sel):
+    tiles, _, width = send.shape
+    slab = width - EXT
+    mixes, grad_keys, grad_reads, _, terms, ids_row, _ = series_terms(heads, model_d, recv, w_t)
     high = terms.astype(BF16).astype(F32)
     tail = high + pltpu.roll(terms - high, 3 * heads, 1)
     ext_f = jnp.concatenate([grad_keys, grad_reads, tail], axis=1)
     ext = ext_f.astype(BF16)
-    back = jnp.concatenate(value_parts + [ext_f], axis=1)
+    back = jnp.concatenate(value_columns(mixes) + [ext_f], axis=1)
     kept, given = halves([back], span, bit_of(pos, bit) == 0)
     own[...] = kept.astype(BF16)
     give[...] = given.astype(BF16)
     for t in range(tiles):
         send[t, :, :EXT] = ext
         send[t, :, EXT:] = recv[:, t * slab : (t + 1) * slab]
-    ids_row = jnp.sum(eye * ids, axis=0, keepdims=True)
-    sel[...] = jnp.concatenate([1.0 - ids_row, ids_row, jnp.zeros((14, length), F32)], axis=0).astype(
-        BF16
-    )
+    sel[...] = sensor_rows(ids_row)
+
+
+def group_series_kernel(heads, model_d, bit, span, pos, recv, w_t, send, own, give, sel, grads, sems):
+    peers, length = send.shape[0], recv.shape[0]
+    copies = []
+    for t in range(peers):
+        copies.append(
+            pltpu.make_async_copy(
+                recv.at[:, t * LANES : (t + 1) * LANES], send.at[t, :length], sems.at[0, t]
+            )
+        )
+        copies[-1].start()
+    mixes, grad_keys, grad_reads, raw, terms, ids_row, eye_h = series_terms(heads, model_d, recv, w_t)
+    raw_b = raw.astype(BF16)
+    raw_t = nt(eye_h.astype(BF16), raw_b)
+    total = jnp.sum(terms, axis=0, keepdims=True)
+    high = total.astype(BF16).astype(F32)
+    misc = jnp.concatenate(
+        [lane_pad(raw_t, LANES), high, total - high, jnp.zeros((6, LANES), F32)], axis=0
+    )
+    grads[...] = jnp.concatenate([grad_keys, grad_reads, misc], axis=0).astype(BF16)
+    for t in range(peers):
+        copies.append(pltpu.make_async_copy(grads, send.at[t, length:], sems.at[1, t]))
+        copies[-1].start()
+    back = jnp.concatenate(value_columns(mixes) + [grad_keys, grad_reads, lane_pad(raw, LANES)], axis=1)
+    kept, given = halves([back], span, bit_of(pos, bit) == 0)
+    own[...] = kept.astype(BF16)
+    give[...] = given.astype(BF16)
+    sel[...] = jnp.concatenate([sensor_rows(ids_row)] * peers, axis=1)
+    for copy in copies:
+        copy.wait()
 
 
 def pack_kernel(core, ids_in, mask_in, table_in, bias_in, decay_in, skip_in, layer, values, cotangent, out, ids, mask_t, table, params, layer_v, sems):
@@ -353,45 +396,67 @@
     return jnp.concatenate([block[k : k + count] for k in range(0, block.shape[0], count)], axis=1)
 
 
-def group_slab_kernel(cols, dates, pos, recv, sel, rows_own, rows_got, keep, keep_sums, rows_keep, give):
-    peers, length, _ = recv.shape
+def pack_sums(sums):
+    high = sums.astype(BF16).astype(F32)
+    return jnp.concatenate([high, sums - high], axis=0)
+
+
+def unpack_sums(rows):
+    return rows[:8] + rows[8:16]
+
+
+def group_slab_kernel(dates, pos, recv, sel, rows_own, rows_got, keep, keep_sums, rows_keep, give):
+    peers = recv.shape[0]
+    length = sel.shape[1] // peers
     count = keep.shape[0]
     first = bit_of(pos, 0) == 0
-    ext = recv[:, :, :EXT].reshape(peers * length, EXT)
-    tokens = recv[:, :, EXT:].reshape(peers * length, LANES)
-    part = tn(ext, tokens)[:cols]
-    sums = jnp.zeros((16, EXT), F32)
-    for t in range(peers):
-        sums = sums + nn(sel[...], recv[t, :, :EXT])
-    sums = sums[0:2]
-    upper, lower = part[:count], part[cols - count :]
+    tokens = recv[:, :length, :].reshape(peers * length, LANES)
+    keys = recv[:, length : 2 * length, :].reshape(peers * length, LANES)
+    reads = recv[:, 2 * length : 3 * length, :].reshape(peers * length, LANES)
+    misc = [recv[t, 3 * length :, :] for t in range(peers)]
+    raw_t = jnp.concatenate([m[:, :length] for m in misc], axis=1)
+    part = jnp.concatenate([tn(keys, tokens), tn(reads, tokens), nn(raw_t, tokens)[: count - LANES]], axis=0)
+    chosen = sel[...]
+    head = sum(m.astype(F32) for m in misc)[8:10]
+    sums = jnp.concatenate(
+        [
+            nn(chosen, keys)[0:2],
+            nn(chosen, reads)[0:2],
+            lane_pad(nt(chosen, raw_t)[0:2], LANES),
+            head[0:1] + head[1:2],
+            jnp.zeros((1, LANES), F32),
+        ],
+        axis=0,
+    )
+    upper, lower = part[:count], part[part.shape[0] - count :]
     keep[...] = jnp.where(first, upper, lower)
     keep_sums[...] = sums
     kept, given = halves([rows_own[...].astype(F32), rows_got[...].astype(F32)], dates, first)
     rows_keep[...] = kept.astype(BF16)
     give[...] = jnp.concatenate(
-        [jnp.where(first, lower, upper)] + sum_rows(sums) + rows_block(given), axis=0
+        [jnp.where(first, lower, upper), pack_sums(sums)] + rows_block(given), axis=0
     ).astype(BF16)
 
 
 def group_join_kernel(dates, pos, keep, keep_sums, rows_own, got, rows_keep, give):
     count = keep.shape[0]
     first = bit_of(pos, 2) == 0
-    total = keep[...] + got[:count, :].astype(F32)
-    sums = keep_sums[...] + rows_sum(got[count : count + 24, :].astype(F32))
-    rows_got = block_rows(got[count + 24 :, :].astype(F32), rows_own.shape[0])
+    there = got[...].astype(F32)
+    total = keep[...] + there[:count]
+    sums = keep_sums[...] + unpack_sums(there[count : count + 16])
+    rows_got = block_rows(there[count + 16 :], rows_own.shape[0])
     kept, given = halves([rows_own[...].astype(F32), rows_got], dates, first)
     rows_keep[...] = kept.astype(BF16)
-    give[...] = jnp.concatenate([total] + sum_rows(sums) + rows_block(given), axis=0).astype(BF16)
+    give[...] = jnp.concatenate([total, pack_sums(sums)] + rows_block(given), axis=0).astype(BF16)
 
 
 def group_total_kernel(own, got, send, rest):
     count = send.shape[1]
-    total = own[: count + 24, :].astype(F32) + got[: count + 24, :].astype(F32)
+    total = (own[...].astype(F32) + got[...].astype(F32))[: count + 16]
     slab = total[:count].astype(BF16)
     for t in range(send.shape[0]):
         send[t] = slab
-    rest[...] = total[count:]
+    rest[...] = unpack_sums(total[count:])
 
 
 def store_rows(cols, scale, core, slabs, weight, held, sems):
@@ -431,7 +496,7 @@
         for k, source in enumerate((value, inputs, table, head))
     ]
     w = w_t[...]
-    rows_got = block_rows(got[slabs.shape[1] + 24 :, :].astype(F32), rows_own.shape[0])
+    rows_got = block_rows(got[...].astype(F32)[slabs.shape[1] + 16 :], rows_own.shape[0])
     rows = jnp.concatenate([rows_own[...].astype(F32), rows_got], axis=0)
     masks = [4 * high + core + 2 * low for high in range(2) for core in range(2) for low in range(2)]
     where_to = []
@@ -448,7 +513,11 @@
     for k, pixel in enumerate(where_to):
         inputs[pixel] = grads[k * dates : (k + 1) * dates].astype(BF16)
     moves[1].start()
-    write_sums(heads, scale, rows_sum(rest[...]), w, table, head)
+    sums = jnp.concatenate([rest[0:2, :], rest[2:4, :], rest[4:6, :]], axis=1)[:, :cols]
+    high, low = split(sums)
+    table[...] = (nn(high, w) + nn(low, w)) * scale
+    total = rest[6:7, :]
+    head[...] = jnp.concatenate([total[:, k * heads : (k + 1) * heads] for k in (1, 0, 2)], axis=0) * scale
     for move in moves[2:]:
         move.start()
     wait()
@@ -463,7 +532,7 @@
     wide = model_d + EXT
     count = (cols + 8) // 2
     half_rows = length // 2
-    payload = count + 24 + half_rows * wide // LANES
+    payload = count + 16 + half_rows * wide // LANES
 
     def groups(alternate):
         return [
@@ -475,24 +544,29 @@
     def across(bit):
         return [(i, i ^ 2**bit) for i in range(dates)]
 
-    send_t, rows_own, rows_give, sel = call(
-        functools.partial(series_kernel, heads, model_d, 1, 2 * dates_dev),
-        [
-            ((peers, length, EXT + LANES), BF16),
-            ((half_rows, wide), BF16),
-            ((half_rows, wide), BF16),
-            ((16, length), BF16),
+    send_t, rows_own, rows_give, sel = pl.pallas_call(
+        functools.partial(group_series_kernel, heads, model_d, 1, 2 * dates_dev),
+        out_shape=[
+            jax.ShapeDtypeStruct((peers, 3 * length + 16, LANES), BF16),
+            jax.ShapeDtypeStruct((half_rows, wide), BF16),
+            jax.ShapeDtypeStruct((half_rows, wide), BF16),
+            jax.ShapeDtypeStruct((16, peers * length), BF16),
         ],
-        [date_s, series, w_t],
-        1,
-    )
+        in_specs=[SMEM, VMEM, VMEM],
+        out_specs=[HBM, VMEM, VMEM, VMEM],
+        scratch_shapes=[
+            pltpu.VMEM((2 * length + 16, LANES), BF16),
+            pltpu.SemaphoreType.DMA((2, peers)),
+        ],
+        compiler_params=pltpu.CompilerParams(vmem_limit_bytes=48 * 1024 * 1024),
+    )(date_s, series, w_t)
     recv_t = lax.all_to_all(
         send_t, ("tile", "date"), split_axis=0, concat_axis=0, tiled=True, axis_index_groups=groups(1)
     )
     rows_got = lax.ppermute(rows_give, "date", across(1))
     keep, keep_sums, rows_own, give = call(
-        functools.partial(group_slab_kernel, cols, dates_dev),
-        [((count, LANES), F32), ((2, EXT), F32), ((half_rows, wide), BF16), ((payload, LANES), BF16)],
+        functools.partial(group_slab_kernel, dates_dev),
+        [((count, LANES), F32), ((8, LANES), F32), ((half_rows, wide), BF16), ((payload, LANES), BF16)],
         [date_s, recv_t, sel, rows_own, rows_got],
         1,
     )
@@ -505,7 +579,7 @@
     )
     got = lax.ppermute(give, "date", across(2))
     send_g, rest = call(
-        group_total_kernel, [((peers, count, LANES), BF16), ((24, LANES), F32)], [give, got]
+        group_total_kernel, [((peers, count, LANES), BF16), ((8, LANES), F32)], [give, got]
     )
     recv_g = lax.all_to_all(
         send_g, ("tile", "date"), split_axis=0, concat_axis=0, tiled=True, axis_index_groups=groups(0)

time: 51.4 us -> 50.9 us (level)
    pallas_call x4 -> x3, Pallas kernels: 2.33 us -> 0.32 us  [call(): pl.pallas_call(kernel, out_shape=[jax.ShapeDtypeStruct(s, d) for s, d in...]
    pallas_call x0 -> x1, Pallas kernels: none -> 1.93 us  [finish_four_levels(): pl.pallas_call(functools.partial(group_series_kernel, heads, model_d, 1,...]
where the time goes in v7:
time: 50.9 us; the launch traced here: 50.6 us
  blocking collectives  24.7 us (49%)
  waiting for transfers between devices  12 us (24%)
  starting transfers between devices  7.7 us (15%)
  Pallas kernels  5.43 us (11%)
  between operations  0.71 us (1%)
    all_to_all x1, blocking collectives, on_device(): lax.all_to_all(packed, 'date', split_axis=0, concat_axis=0, tiled=True)  14.6 us
    all_to_all x1, blocking collectives, finish_four_levels(): lax.all_to_all(send_g, ('tile', 'date'), split_axis=0, concat_axis=0, til...  10.1 us
    ppermute x1, waiting for transfers between devices, finish_four_levels(): got = lax.ppermute(give, 'date', across(2))  5.92 us
    ppermute x1, waiting for transfers between devices, finish_four_levels(): rows_got = lax.ppermute(rows_give, 'date', across(1))  4.73 us
    all_to_all x1, starting transfers between devices, finish_four_levels(): lax.all_to_all(send_t, ('tile', 'date'), split_axis=0, concat_axis=0, til...  3.41 us
    pallas_call x1, Pallas kernels, finish_four_levels(): pl.pallas_call(functools.partial(group_series_kernel, heads, model_d, 1,...  1.93 us
    ppermute x1, starting transfers between devices, finish_four_levels(): rows_got = lax.ppermute(rows_give, 'date', across(1))  1.92 us
    ppermute x1, starting transfers between devices, finish_four_levels(): got = lax.ppermute(give, 'date', across(2))  1.37 us
  transfers between devices with their start and end apart: 5, of which 5 were waited for; matrix products, arithmetic and copies ran while one was open for 0% of the time, Pallas kernels for 2%

profile of v7, /device:TPU:0, one launch (start us, length us, event | category | flops | bytes accessed | tf_op | source)
XLA Modules:
  0.0 50.6 jit_solution(13757399010126010388)
XLA Ops:
  0.6 0.0 copy-start
  0.6 1.1 %shard_map.137 = bf16[8,4,3200]{2,1,0:T(4,128)(2,1)S(1)} custom-call(s32[1]{0:T(128)} %bitcast.core.pos, s32[4]{0:T(128)} %ids_in.1, s32[4,8]{1,0:T(4,128)} %bitcast.10, f32[2,1024]{1,0:T(2,128)} %table_in.1, f32[1,8]{1,0:T(1,128)} %bitcast.11, f32[1,8]{1,0:T(1,128)} %bitcast.12, f32[1,8]{1,0:T(1,128)} %bitcast.13, bf16[8,4,1024]{2,1,0:T(4,128)(2,1)} %layer.1, ...), custom_call_target="tpu_custom_call" | custom-call | tf_op jit(solution)/shard_map/pallas_call | solution.py:754
  1.7 14.6 %all_to_all.15 = bf16[8,4,3200]{2,1,0:T(4,128)(2,1)S(1)} all-to-all(bf16[8,4,3200]{2,1,0:T(4,128)(2,1)S(1)} %shard_map.137), channel_id=1, replica_groups=mesh['tile'=4,'date'=8] {'date'}, dimensions={0} | all-to-all | bytes 409600 | tf_op jit(solution)/shard_map/all_to_all | solution.py:769
  16.4 0.1 reshape.17.recv
  16.4 0.0 copy-done
  16.4 1.9 %shard_map.138 = (bf16[8,112,128]{2,1,0:T(8,128)(2,1)}, bf16[16,1408]{1,0:T(8,128)(2,1)S(1)}, bf16[16,1408]{1,0:T(8,128)(2,1)S(1)}, bf16[16,256]{1,0:T(8,128)(2,1)S(1)}) custom-call(s32[1]{0:T(128)} %bitcast.core.pos, bf16[32,3200]{1,0:T(8,128)(2,1)S(1)} %reshape.17.recv, bf16[264,1024]{1,0:T(8,128)(2,1)S(1)} %bitcast.7), custom_call_target="tpu_custom_call" | custom-call | tf_op jit(solution)/shard_map/pallas_call | solution.py:547
  18.4 3.4 %all-to-all-start.1 = ((bf16[8,112,128]{2,1,0:T(8,128)(2,1)}), bf16[8,112,128]{2,1,0:T(8,128)(2,1)S(1)}, u32[]{:S(2)}, u32[]{:S(2)}) async-start(bf16[8,112,128]{2,1,0:T(8,128)(2,1)} %get-tuple-element.22), calls=%async_computation.1 | async-start | bytes 458752 | tf_op jit(solution)/shard_map/all_to_all | solution.py:563
  21.8 1.9 %collective-permute-start = (bf16[16,1408]{1,0:T(8,128)(2,1)S(1)}, bf16[16,1408]{1,0:T(8,128)(2,1)S(1)}, u32[]{:S(2)}, u32[]{:S(2)}) collective-permute-start(bf16[16,1408]{1,0:T(8,128)(2,1)S(1)} %get-tuple-element.25), channel_id=1, source_target_pairs={{0,2},{1,3},{2,0},{3,1},{4,6},{5,7},{6,4},{7,5},{8,10},{9,11},{10,... | collective-permute-start | bytes 135176 | tf_op jit(solution)/shard_map/ppermute | solution.py:566
  23.7 4.7 %collective-permute-done.rows_got = bf16[16,1408]{1,0:T(8,128)(2,1)S(1)} collective-permute-done((bf16[16,1408]{1,0:T(8,128)(2,1)S(1)}, bf16[16,1408]{1,0:T(8,128)(2,1)S(1)}, u32[]{:S(2)}, u32[]{:S(2)}) %collective-permute-start) | collective-permute-done | bytes 45088 | tf_op jit(solution)/shard_map/ppermute | solution.py:566
  28.5 0.1 all-to-all-done.1.recv
  28.6 0.3 shard_map.139
  28.8 1.0 %collective-permute-start.1 = (bf16[328,128]{1,0:T(8,128)(2,1)S(1)}, bf16[328,128]{1,0:T(8,128)(2,1)S(1)}, u32[]{:S(2)}, u32[]{:S(2)}) collective-permute-start(bf16[328,128]{1,0:T(8,128)(2,1)S(1)} %get-tuple-element.29), channel_id=1, source_target_pairs={{0,1},{1,0},{2,3},{3,2},{4,5},{5,4},{6,7},{7,6},{8,9},{9,8},{10,11... | collective-permute-start | bytes 251912 | tf_op jit(solution)/shard_map/ppermute | solution.py:573
  29.8 0.9 %collective-permute-done.1.got = bf16[328,128]{1,0:T(8,128)(2,1)S(1)} collective-permute-done((bf16[328,128]{1,0:T(8,128)(2,1)S(1)}, bf16[328,128]{1,0:T(8,128)(2,1)S(1)}, u32[]{:S(2)}, u32[]{:S(2)}) %collective-permute-start.1) | collective-permute-done | bytes 84000 | tf_op jit(solution)/shard_map/ppermute | solution.py:573
  30.8 1.4 %collective-permute-start.2 = (bf16[328,128]{1,0:T(8,128)(2,1)S(1)}, bf16[328,128]{1,0:T(8,128)(2,1)S(1)}, u32[]{:S(2)}, u32[]{:S(2)}) collective-permute-start(bf16[328,128]{1,0:T(8,128)(2,1)S(1)} %get-tuple-element.30.own), channel_id=1, source_target_pairs={{0,4},{1,5},{2,6},{3,7},{4,0},{5,1},{6,2},{7,3},{8,12},{9,13},{10,... | collective-permute-start | bytes 251912 | tf_op jit(solution)/shard_map/ppermute | solution.py:580
  32.2 5.9 %collective-permute-done.2.got = bf16[328,128]{1,0:T(8,128)(2,1)S(1)} collective-permute-done((bf16[328,128]{1,0:T(8,128)(2,1)S(1)}, bf16[328,128]{1,0:T(8,128)(2,1)S(1)}, u32[]{:S(2)}, u32[]{:S(2)}) %collective-permute-start.2) | collective-permute-done | bytes 84000 | tf_op jit(solution)/shard_map/ppermute | solution.py:580
  38.1 10.1 %all_to_all.16.slabs = bf16[8,136,128]{2,1,0:T(8,128)(2,1)S(1)} all-to-all(bf16[8,136,128]{2,1,0:T(8,128)(2,1)S(1)} %get-tuple-element.31), channel_id=1, replica_groups={{0,2,8,10,16,18,24,26},{1,3,9,11,17,19,25,27},{4,6,12,14,20,22,28,30},{..., dimensions={0} | all-to-all | bytes 557056 | tf_op jit(solution)/shard_map/all_to_all | solution.py:584
  48.2 0.0 collective-permute-start.3
  48.2 1.2 %shard_map.142 = (bf16[8,4,1024]{2,1,0:T(4,128)(2,1)}, bf16[8,4,1024]{2,1,0:T(4,128)(2,1)}, f32[2,1024]{1,0:T(2,128)}, f32[3,8]{1,0:T(4,128)}, f32[264,1024]{1,0:T(8,128)}) custom-call(s32[1]{0:T(128)} %bitcast.core.pos, bf16[8,136,128]{2,1,0:T(8,128)(2,1)S(1)} %all_to_all.16.slabs, bf16[16,1408]{1,0:T(8,128)(2,1)S(1)} %get-tuple-element.32.rows_own, ...), custom_call_target="tpu_custom_call" | custom-call | tf_op jit(solution)/shard_map/pallas_call | solution.py:597
  49.4 0.3 collective-permute-done.3.slabs
  49.7 0.9 %shard_map.143 = f32[264,1024]{1,0:T(8,128)} custom-call(s32[1]{0:T(128)} %bitcast.core.pos, bf16[8,136,128]{2,1,0:T(8,128)(2,1)S(1)} %collective-permute-done.3.slabs, f32[264,1024]{1,0:T(8,128)} %get-tuple-element.36.weight_in), custom_call_target="tpu_custom_call", output_to_operand_aliasing={{}: (2, {})} | custom-call | tf_op jit(solution)/shard_map/pallas_call | solution.py:607
  (2 shorter events, 0.1 us)
Async XLA Ops:
  0.6 15.8 %copy-start = (bf16[1024,264]{0,1:T(8,128)(2,1)S(1)}, bf16[1024,264]{0,1:T(8,128)(2,1)}, u32[]{:S(2)}) copy-start(bf16[1024,264]{0,1:T(8,128)(2,1)} %param.16) | copy-start | bytes 1622020
  18.4 10.2 %all-to-all-start.1 = ((bf16[8,112,128]{2,1,0:T(8,128)(2,1)}), bf16[8,112,128]{2,1,0:T(8,128)(2,1)S(1)}, u32[]{:S(2)}, u32[]{:S(2)}) async-start(bf16[8,112,128]{2,1,0:T(8,128)(2,1)} %get-tuple-element.22), calls=%async_computation.1 | async-start | bytes 458752 | tf_op jit(solution)/shard_map/all_to_all | solution.py:563
  21.8 6.6 %collective-permute-start = (bf16[16,1408]{1,0:T(8,128)(2,1)S(1)}, bf16[16,1408]{1,0:T(8,128)(2,1)S(1)}, u32[]{:S(2)}, u32[]{:S(2)}) collective-permute-start(bf16[16,1408]{1,0:T(8,128)(2,1)S(1)} %get-tuple-element.25), channel_id=1, source_target_pairs={{0,2},{1,3},{2,0},{3,1},{4,6},{5,7},{6,4},{7,5},{8,10},{9,11},{10,... | collective-permute-start | bytes 135176 | tf_op jit(solution)/shard_map/ppermute | solution.py:566
  28.8 1.9 %collective-permute-start.1 = (bf16[328,128]{1,0:T(8,128)(2,1)S(1)}, bf16[328,128]{1,0:T(8,128)(2,1)S(1)}, u32[]{:S(2)}, u32[]{:S(2)}) collective-permute-start(bf16[328,128]{1,0:T(8,128)(2,1)S(1)} %get-tuple-element.29), channel_id=1, source_target_pairs={{0,1},{1,0},{2,3},{3,2},{4,5},{5,4},{6,7},{7,6},{8,9},{9,8},{10,11... | collective-permute-start | bytes 251912 | tf_op jit(solution)/shard_map/ppermute | solution.py:573
  30.8 7.3 %collective-permute-start.2 = (bf16[328,128]{1,0:T(8,128)(2,1)S(1)}, bf16[328,128]{1,0:T(8,128)(2,1)S(1)}, u32[]{:S(2)}, u32[]{:S(2)}) collective-permute-start(bf16[328,128]{1,0:T(8,128)(2,1)S(1)} %get-tuple-element.30.own), channel_id=1, source_target_pairs={{0,4},{1,5},{2,6},{3,7},{4,0},{5,1},{6,2},{7,3},{8,12},{9,13},{10,... | collective-permute-start | bytes 251912 | tf_op jit(solution)/shard_map/ppermute | solution.py:580
  48.2 1.6 %collective-permute-start.3 = (bf16[8,136,128]{2,1,0:T(8,128)(2,1)S(1)}, bf16[8,136,128]{2,1,0:T(8,128)(2,1)S(1)}, u32[]{:S(2)}, u32[]{:S(2)}) collective-permute-start(bf16[8,136,128]{2,1,0:T(8,128)(2,1)S(1)} %all_to_all.16.slabs), channel_id=1, source_target_pairs={{0,1},{1,0},{2,3},{3,2},{4,5},{5,4},{6,7},{7,6},{8,9},{9,8},{10,11... | collective-permute-start | bytes 835592 | tf_op jit(solution)/shard_map/ppermute | solution.py:587

commit v8 on v7

--- a/solution.py
+++ b/solution.py
@@ -149,7 +149,7 @@
     sel[...] = sensor_rows(ids_row)
 
 
-def group_series_kernel(heads, model_d, bit, span, pos, recv, w_t, send, own, give, sel, grads, sems):
+def group_series_kernel(heads, model_d, span, pos, recv, w_t, send, own, give_low, give_high, sel, grads, sems):
     peers, length = send.shape[0], recv.shape[0]
     copies = []
     for t in range(peers):
@@ -172,9 +172,12 @@
         copies.append(pltpu.make_async_copy(grads, send.at[t, length:], sems.at[1, t]))
         copies[-1].start()
     back = jnp.concatenate(value_columns(mixes) + [grad_keys, grad_reads, lane_pad(raw, LANES)], axis=1)
-    kept, given = halves([back], span, bit_of(pos, bit) == 0)
-    own[...] = kept.astype(BF16)
-    give[...] = given.astype(BF16)
+    kept, given = halves([back], span, bit_of(pos, 1) == 0)
+    here, high_only = halves([kept], span, bit_of(pos, 2) == 0)
+    low_only, both = halves([given], span, bit_of(pos, 2) == 0)
+    own[...] = here.astype(BF16)
+    give_high[...] = high_only.astype(BF16)
+    give_low[...] = jnp.concatenate([low_only, both], axis=0).astype(BF16)
     sel[...] = jnp.concatenate([sensor_rows(ids_row)] * peers, axis=1)
     for copy in copies:
         copy.wait()
@@ -405,7 +408,7 @@
     return rows[:8] + rows[8:16]
 
 
-def group_slab_kernel(dates, pos, recv, sel, rows_own, rows_got, keep, keep_sums, rows_keep, give):
+def group_slab_kernel(dates, pos, recv, sel, rows_own, rows_high, rows_low, keep, keep_sums, rows_keep, give):
     peers = recv.shape[0]
     length = sel.shape[1] // peers
     count = keep.shape[0]
@@ -431,22 +434,24 @@
     upper, lower = part[:count], part[part.shape[0] - count :]
     keep[...] = jnp.where(first, upper, lower)
     keep_sums[...] = sums
-    kept, given = halves([rows_own[...].astype(F32), rows_got[...].astype(F32)], dates, first)
+    arrived = [rows[...].astype(F32) for rows in (rows_own, rows_high, rows_low)]
+    kept, given = halves(arrived, dates, first)
     rows_keep[...] = kept.astype(BF16)
     give[...] = jnp.concatenate(
         [jnp.where(first, lower, upper), pack_sums(sums)] + rows_block(given), axis=0
     ).astype(BF16)
 
 
-def group_join_kernel(dates, pos, keep, keep_sums, rows_own, got, rows_keep, give):
+def group_join_kernel(dates, keep, keep_sums, rows_own, got, rows_keep, give):
     count = keep.shape[0]
-    first = bit_of(pos, 2) == 0
     there = got[...].astype(F32)
     total = keep[...] + there[:count]
     sums = keep_sums[...] + unpack_sums(there[count : count + 16])
-    rows_got = block_rows(there[count + 16 :], rows_own.shape[0])
-    kept, given = halves([rows_own[...].astype(F32), rows_got], dates, first)
-    rows_keep[...] = kept.astype(BF16)
+    mine = rows_own[...].astype(F32)
+    theirs = block_rows(there[count + 16 :], mine.shape[0])
+    stay = mine.shape[0] - dates
+    rows_keep[...] = jnp.concatenate([mine[:stay], theirs[:stay]], axis=0).astype(BF16)
+    given = jnp.concatenate([mine[stay:], theirs[stay:]], axis=0)
     give[...] = jnp.concatenate([total, pack_sums(sums)] + rows_block(given), axis=0).astype(BF16)
 
 
@@ -496,9 +501,9 @@
         for k, source in enumerate((value, inputs, table, head))
     ]
     w = w_t[...]
-    rows_got = block_rows(got[...].astype(F32)[slabs.shape[1] + 16 :], rows_own.shape[0])
+    rows_got = block_rows(got[...].astype(F32)[slabs.shape[1] + 16 :], 2 * dates)
     rows = jnp.concatenate([rows_own[...].astype(F32), rows_got], axis=0)
-    masks = [4 * high + core + 2 * low for high in range(2) for core in range(2) for low in range(2)]
+    masks = [0, 4, 2, 1, 5, 3, 6, 7]
     where_to = []
     for mask in masks:
         index = 0
@@ -533,6 +538,7 @@
     count = (cols + 8) // 2
     half_rows = length // 2
     payload = count + 16 + half_rows * wide // LANES
+    payload_high = count + 16 + half_rows // 2 * wide // LANES
 
     def groups(alternate):
         return [
@@ -544,16 +550,17 @@
     def across(bit):
         return [(i, i ^ 2**bit) for i in range(dates)]
 
-    send_t, rows_own, rows_give, sel = pl.pallas_call(
-        functools.partial(group_series_kernel, heads, model_d, 1, 2 * dates_dev),
+    send_t, rows_own, give_low, give_high, sel = pl.pallas_call(
+        functools.partial(group_series_kernel, heads, model_d, 2 * dates_dev),
         out_shape=[
             jax.ShapeDtypeStruct((peers, 3 * length + 16, LANES), BF16),
+            jax.ShapeDtypeStruct((half_rows // 2, wide), BF16),
             jax.ShapeDtypeStruct((half_rows, wide), BF16),
-            jax.ShapeDtypeStruct((half_rows, wide), BF16),
+            jax.ShapeDtypeStruct((half_rows // 2, wide), BF16),
             jax.ShapeDtypeStruct((16, peers * length), BF16),
         ],
         in_specs=[SMEM, VMEM, VMEM],
-        out_specs=[HBM, VMEM, VMEM, VMEM],
+        out_specs=[HBM, VMEM, VMEM, VMEM, VMEM],
         scratch_shapes=[
             pltpu.VMEM((2 * length + 16, LANES), BF16),
             pltpu.SemaphoreType.DMA((2, peers)),
@@ -563,19 +570,19 @@
     recv_t = lax.all_to_all(
         send_t, ("tile", "date"), split_axis=0, concat_axis=0, tiled=True, axis_index_groups=groups(1)
     )
-    rows_got = lax.ppermute(rows_give, "date", across(1))
+    rows_low = lax.ppermute(give_low, "date", across(1))
+    rows_high = lax.ppermute(give_high, "date", across(2))
     keep, keep_sums, rows_own, give = call(
         functools.partial(group_slab_kernel, dates_dev),
         [((count, LANES), F32), ((8, LANES), F32), ((half_rows, wide), BF16), ((payload, LANES), BF16)],
-        [date_s, recv_t, sel, rows_own, rows_got],
+        [date_s, recv_t, sel, rows_own, rows_high, rows_low],
         1,
     )
     got = lax.ppermute(give, "date", across(0))
     rows_own, give = call(
         functools.partial(group_join_kernel, dates_dev),
-        [((half_rows, wide), BF16), ((payload, LANES), BF16)],
-        [date_s, keep, keep_sums, rows_own, got],
-        1,
+        [((half_rows * 3 // 2, wide), BF16), ((payload_high, LANES), BF16)],
+        [keep, keep_sums, rows_own, got],
     )
     got = lax.ppermute(give, "date", across(2))
     send_g, rest = call(

time: 50.9 us -> 50.3 us (0.988)
  waiting for transfers between devices: 12 us -> 10.4 us
  starting transfers between devices: 7.7 us -> 8.75 us
    ppermute x1 -> x2, starting transfers between devices: 1.92 us -> 3.26 us  [the longest x1 1.92 us: finish_four_levels(): rows_low = lax.ppermute(give_low, 'date', across(1))]
    ppermute x1 -> x2, waiting for transfers between devices: 4.73 us -> 3.87 us  [the longest x1 3.47 us: finish_four_levels(): rows_high = lax.ppermute(give_high, 'date', across(2))]
    ppermute x1, waiting for transfers between devices: 5.92 us -> 5.33 us  [finish_four_levels(): got = lax.ppermute(give, 'date', across(2))]
  transfers between devices with their start and end apart: 5 -> 6, of which waited for: 5 -> 5; matrix products, arithmetic and copies ran while one was open for 0% -> 0% of each run, Pallas kernels for 2% -> 2%
where the time goes in v8:
time: 50.3 us; the launch traced here: 49.9 us
  blocking collectives  24.6 us (49%)
  waiting for transfers between devices  10.4 us (21%)
  starting transfers between devices  8.75 us (17%)
  Pallas kernels  5.41 us (11%)
  between operations  0.71 us (1%)
    all_to_all x1, blocking collectives, on_device(): lax.all_to_all(packed, 'date', split_axis=0, concat_axis=0, tiled=True)  14.6 us
    all_to_all x1, blocking collectives, finish_four_levels(): lax.all_to_all(send_g, ('tile', 'date'), split_axis=0, concat_axis=0, til...  9.94 us
    ppermute x1, waiting for transfers between devices, finish_four_levels(): got = lax.ppermute(give, 'date', across(2))  5.33 us
    ppermute x1, waiting for transfers between devices, finish_four_levels(): rows_high = lax.ppermute(give_high, 'date', across(2))  3.47 us
    all_to_all x1, starting transfers between devices, finish_four_levels(): lax.all_to_all(send_t, ('tile', 'date'), split_axis=0, concat_axis=0, til...  3.41 us
    pallas_call x1, Pallas kernels, finish_four_levels(): pl.pallas_call(functools.partial(group_series_kernel, heads, model_d, 2 *...  1.93 us
    ppermute x1, starting transfers between devices, finish_four_levels(): rows_low = lax.ppermute(give_low, 'date', across(1))  1.92 us
    ppermute x1, starting transfers between devices, finish_four_levels(): rows_high = lax.ppermute(give_high, 'date', across(2))  1.34 us
  transfers between devices with their start and end apart: 6, of which 5 were waited for; matrix products, arithmetic and copies ran while one was open for 0% of the time, Pallas kernels for 2%

profile of v8, /device:TPU:0, one launch (start us, length us, event | category | flops | bytes accessed | tf_op | source)
XLA Modules:
  0.0 49.9 jit_solution(2738763526413669213)
XLA Ops:
  0.6 0.0 copy-start
  0.6 1.1 %shard_map.137 = bf16[8,4,3200]{2,1,0:T(4,128)(2,1)S(1)} custom-call(s32[1]{0:T(128)} %bitcast.core.pos, s32[4]{0:T(128)} %ids_in.1, s32[4,8]{1,0:T(4,128)} %bitcast.10, f32[2,1024]{1,0:T(2,128)} %table_in.1, f32[1,8]{1,0:T(1,128)} %bitcast.11, f32[1,8]{1,0:T(1,128)} %bitcast.12, f32[1,8]{1,0:T(1,128)} %bitcast.13, bf16[8,4,1024]{2,1,0:T(4,128)(2,1)} %layer.1, ...), custom_call_target="tpu_custom_call" | custom-call | tf_op jit(solution)/shard_map/pallas_call | solution.py:761
  1.7 14.6 %all_to_all.15 = bf16[8,4,3200]{2,1,0:T(4,128)(2,1)S(1)} all-to-all(bf16[8,4,3200]{2,1,0:T(4,128)(2,1)S(1)} %shard_map.137), channel_id=1, replica_groups=mesh['tile'=4,'date'=8] {'date'}, dimensions={0} | all-to-all | bytes 409600 | tf_op jit(solution)/shard_map/all_to_all | solution.py:776
  16.4 0.1 reshape.17.recv
  16.4 0.0 copy-done
  16.4 1.9 %shard_map.138 = (bf16[8,112,128]{2,1,0:T(8,128)(2,1)}, bf16[8,1408]{1,0:T(8,128)(2,1)S(1)}, bf16[16,1408]{1,0:T(8,128)(2,1)S(1)}, bf16[8,1408]{1,0:T(8,128)(2,1)S(1)}, bf16[16,256]{1,0:T(8,128)(2,1)S(1)}) custom-call(s32[1]{0:T(128)} %bitcast.core.pos, bf16[32,3200]{1,0:T(8,128)(2,1)S(1)} %reshape.17.recv, bf16[264,1024]{1,0:T(8,128)(2,1)S(1)} %bitcast.7), custom_call_target="tpu_custom_call" | custom-call | tf_op jit(solution)/shard_map/pallas_call | solution.py:553
  18.4 3.4 %all-to-all-start.1 = ((bf16[8,112,128]{2,1,0:T(8,128)(2,1)}), bf16[8,112,128]{2,1,0:T(8,128)(2,1)S(1)}, u32[]{:S(2)}, u32[]{:S(2)}) async-start(bf16[8,112,128]{2,1,0:T(8,128)(2,1)} %get-tuple-element.23), calls=%async_computation.1 | async-start | bytes 458752 | tf_op jit(solution)/shard_map/all_to_all | solution.py:570
  21.8 1.9 %collective-permute-start.1 = (bf16[16,1408]{1,0:T(8,128)(2,1)S(1)}, bf16[16,1408]{1,0:T(8,128)(2,1)S(1)}, u32[]{:S(2)}, u32[]{:S(2)}) collective-permute-start(bf16[16,1408]{1,0:T(8,128)(2,1)S(1)} %get-tuple-element.27), channel_id=1, source_target_pairs={{0,2},{1,3},{2,0},{3,1},{4,6},{5,7},{6,4},{7,5},{8,10},{9,11},{10,... | collective-permute-start | bytes 135176 | tf_op jit(solution)/shard_map/ppermute | solution.py:573
  23.7 1.3 %collective-permute-start = (bf16[8,1408]{1,0:T(8,128)(2,1)S(1)}, bf16[8,1408]{1,0:T(8,128)(2,1)S(1)}, u32[]{:S(2)}, u32[]{:S(2)}) collective-permute-start(bf16[8,1408]{1,0:T(8,128)(2,1)S(1)} %get-tuple-element.26), channel_id=1, source_target_pairs={{0,4},{1,5},{2,6},{3,7},{4,0},{5,1},{6,2},{7,3},{8,12},{9,13},{10,... | collective-permute-start | bytes 67592 | tf_op jit(solution)/shard_map/ppermute | solution.py:574
  25.1 3.5 %collective-permute-done.rows_high = bf16[8,1408]{1,0:T(8,128)(2,1)S(1)} collective-permute-done((bf16[8,1408]{1,0:T(8,128)(2,1)S(1)}, bf16[8,1408]{1,0:T(8,128)(2,1)S(1)}, u32[]{:S(2)}, u32[]{:S(2)}) %collective-permute-start) | collective-permute-done | bytes 22560 | tf_op jit(solution)/shard_map/ppermute | solution.py:574
  28.5 0.4 collective-permute-done.1.rows_low
  28.9 0.0 all-to-all-done.1.recv
  28.9 0.3 shard_map.139
  29.2 0.9 %collective-permute-start.2 = (bf16[328,128]{1,0:T(8,128)(2,1)S(1)}, bf16[328,128]{1,0:T(8,128)(2,1)S(1)}, u32[]{:S(2)}, u32[]{:S(2)}) collective-permute-start(bf16[328,128]{1,0:T(8,128)(2,1)S(1)} %get-tuple-element.31), channel_id=1, source_target_pairs={{0,1},{1,0},{2,3},{3,2},{4,5},{5,4},{6,7},{7,6},{8,9},{9,8},{10,11... | collective-permute-start | bytes 251912 | tf_op jit(solution)/shard_map/ppermute | solution.py:581
  30.1 0.9 %collective-permute-done.2.got = bf16[328,128]{1,0:T(8,128)(2,1)S(1)} collective-permute-done((bf16[328,128]{1,0:T(8,128)(2,1)S(1)}, bf16[328,128]{1,0:T(8,128)(2,1)S(1)}, u32[]{:S(2)}, u32[]{:S(2)}) %collective-permute-start.2) | collective-permute-done | bytes 84000 | tf_op jit(solution)/shard_map/ppermute | solution.py:581
  31.0 1.2 %collective-permute-start.3 = (bf16[240,128]{1,0:T(8,128)(2,1)S(1)}, bf16[240,128]{1,0:T(8,128)(2,1)S(1)}, u32[]{:S(2)}, u32[]{:S(2)}) collective-permute-start(bf16[240,128]{1,0:T(8,128)(2,1)S(1)} %get-tuple-element.32.own), channel_id=1, source_target_pairs={{0,4},{1,5},{2,6},{3,7},{4,0},{5,1},{6,2},{7,3},{8,12},{9,13},{10,... | collective-permute-start | bytes 184328 | tf_op jit(solution)/shard_map/ppermute | solution.py:587
  32.2 5.3 %collective-permute-done.3.got = bf16[240,128]{1,0:T(8,128)(2,1)S(1)} collective-permute-done((bf16[240,128]{1,0:T(8,128)(2,1)S(1)}, bf16[240,128]{1,0:T(8,128)(2,1)S(1)}, u32[]{:S(2)}, u32[]{:S(2)}) %collective-permute-start.3) | collective-permute-done | bytes 61472 | tf_op jit(solution)/shard_map/ppermute | solution.py:587
  37.6 9.9 %all_to_all.16.slabs = bf16[8,136,128]{2,1,0:T(8,128)(2,1)S(1)} all-to-all(bf16[8,136,128]{2,1,0:T(8,128)(2,1)S(1)} %get-tuple-element.33), channel_id=1, replica_groups={{0,2,8,10,16,18,24,26},{1,3,9,11,17,19,25,27},{4,6,12,14,20,22,28,30},{..., dimensions={0} | all-to-all | bytes 557056 | tf_op jit(solution)/shard_map/all_to_all | solution.py:591
  47.5 0.0 collective-permute-start.4
  47.5 1.2 %shard_map.142 = (bf16[8,4,1024]{2,1,0:T(4,128)(2,1)}, bf16[8,4,1024]{2,1,0:T(4,128)(2,1)}, f32[2,1024]{1,0:T(2,128)}, f32[3,8]{1,0:T(4,128)}, f32[264,1024]{1,0:T(8,128)}) custom-call(s32[1]{0:T(128)} %bitcast.core.pos, bf16[8,136,128]{2,1,0:T(8,128)(2,1)S(1)} %all_to_all.16.slabs, bf16[24,1408]{1,0:T(8,128)(2,1)S(1)} %get-tuple-element.34.rows_own, ...), custom_call_target="tpu_custom_call" | custom-call | tf_op jit(solution)/shard_map/pallas_call | solution.py:604
  48.8 0.3 collective-permute-done.4.slabs
  49.1 0.9 %shard_map.143 = f32[264,1024]{1,0:T(8,128)} custom-call(s32[1]{0:T(128)} %bitcast.core.pos, bf16[8,136,128]{2,1,0:T(8,128)(2,1)S(1)} %collective-permute-done.4.slabs, f32[264,1024]{1,0:T(8,128)} %get-tuple-element.38.weight_in), custom_call_target="tpu_custom_call", output_to_operand_aliasing={{}: (2, {})} | custom-call | tf_op jit(solution)/shard_map/pallas_call | solution.py:614
  (2 shorter events, 0.1 us)
Async XLA Ops:
  0.6 15.8 %copy-start = (bf16[1024,264]{0,1:T(8,128)(2,1)S(1)}, bf16[1024,264]{0,1:T(8,128)(2,1)}, u32[]{:S(2)}) copy-start(bf16[1024,264]{0,1:T(8,128)(2,1)} %param.16) | copy-start | bytes 1622020
  18.4 10.6 %all-to-all-start.1 = ((bf16[8,112,128]{2,1,0:T(8,128)(2,1)}), bf16[8,112,128]{2,1,0:T(8,128)(2,1)S(1)}, u32[]{:S(2)}, u32[]{:S(2)}) async-start(bf16[8,112,128]{2,1,0:T(8,128)(2,1)} %get-tuple-element.23), calls=%async_computation.1 | async-start | bytes 458752 | tf_op jit(solution)/shard_map/all_to_all | solution.py:570
  21.8 7.1 %collective-permute-start.1 = (bf16[16,1408]{1,0:T(8,128)(2,1)S(1)}, bf16[16,1408]{1,0:T(8,128)(2,1)S(1)}, u32[]{:S(2)}, u32[]{:S(2)}) collective-permute-start(bf16[16,1408]{1,0:T(8,128)(2,1)S(1)} %get-tuple-element.27), channel_id=1, source_target_pairs={{0,2},{1,3},{2,0},{3,1},{4,6},{5,7},{6,4},{7,5},{8,10},{9,11},{10,... | collective-permute-start | bytes 135176 | tf_op jit(solution)/shard_map/ppermute | solution.py:573
  23.7 4.8 %collective-permute-start = (bf16[8,1408]{1,0:T(8,128)(2,1)S(1)}, bf16[8,1408]{1,0:T(8,128)(2,1)S(1)}, u32[]{:S(2)}, u32[]{:S(2)}) collective-permute-start(bf16[8,1408]{1,0:T(8,128)(2,1)S(1)} %get-tuple-element.26), channel_id=1, source_target_pairs={{0,4},{1,5},{2,6},{3,7},{4,0},{5,1},{6,2},{7,3},{8,12},{9,13},{10,... | collective-permute-start | bytes 67592 | tf_op jit(solution)/shard_map/ppermute | solution.py:574
  29.2 1.8 %collective-permute-start.2 = (bf16[328,128]{1,0:T(8,128)(2,1)S(1)}, bf16[328,128]{1,0:T(8,128)(2,1)S(1)}, u32[]{:S(2)}, u32[]{:S(2)}) collective-permute-start(bf16[328,128]{1,0:T(8,128)(2,1)S(1)} %get-tuple-element.31), channel_id=1, source_target_pairs={{0,1},{1,0},{2,3},{3,2},{4,5},{5,4},{6,7},{7,6},{8,9},{9,8},{10,11... | collective-permute-start | bytes 251912 | tf_op jit(solution)/shard_map/ppermute | solution.py:581
  31.0 6.5 %collective-permute-start.3 = (bf16[240,128]{1,0:T(8,128)(2,1)S(1)}, bf16[240,128]{1,0:T(8,128)(2,1)S(1)}, u32[]{:S(2)}, u32[]{:S(2)}) collective-permute-start(bf16[240,128]{1,0:T(8,128)(2,1)S(1)} %get-tuple-element.32.own), channel_id=1, source_target_pairs={{0,4},{1,5},{2,6},{3,7},{4,0},{5,1},{6,2},{7,3},{8,12},{9,13},{10,... | collective-permute-start | bytes 184328 | tf_op jit(solution)/shard_map/ppermute | solution.py:587
  47.5 1.6 %collective-permute-start.4 = (bf16[8,136,128]{2,1,0:T(8,128)(2,1)S(1)}, bf16[8,136,128]{2,1,0:T(8,128)(2,1)S(1)}, u32[]{:S(2)}, u32[]{:S(2)}) collective-permute-start(bf16[8,136,128]{2,1,0:T(8,128)(2,1)S(1)} %all_to_all.16.slabs), channel_id=1, source_target_pairs={{0,1},{1,0},{2,3},{3,2},{4,5},{5,4},{6,7},{7,6},{8,9},{9,8},{10,11... | collective-permute-start | bytes 835592 | tf_op jit(solution)/shard_map/ppermute | solution.py:594

commit v9 on v7

--- a/solution.py
+++ b/solution.py
@@ -149,35 +149,24 @@
     sel[...] = sensor_rows(ids_row)
 
 
-def group_series_kernel(heads, model_d, bit, span, pos, recv, w_t, send, own, give, sel, grads, sems):
+def group_series_kernel(heads, model_d, dates, pos, recv, w_t, send, own, give, sel):
     peers, length = send.shape[0], recv.shape[0]
-    copies = []
-    for t in range(peers):
-        copies.append(
-            pltpu.make_async_copy(
-                recv.at[:, t * LANES : (t + 1) * LANES], send.at[t, :length], sems.at[0, t]
-            )
-        )
-        copies[-1].start()
     mixes, grad_keys, grad_reads, raw, terms, ids_row, eye_h = series_terms(heads, model_d, recv, w_t)
-    raw_b = raw.astype(BF16)
-    raw_t = nt(eye_h.astype(BF16), raw_b)
+    raw_t = nt(eye_h.astype(BF16), raw.astype(BF16))
     total = jnp.sum(terms, axis=0, keepdims=True)
     high = total.astype(BF16).astype(F32)
     misc = jnp.concatenate(
         [lane_pad(raw_t, LANES), high, total - high, jnp.zeros((6, LANES), F32)], axis=0
     )
-    grads[...] = jnp.concatenate([grad_keys, grad_reads, misc], axis=0).astype(BF16)
+    grads = jnp.concatenate([grad_keys, grad_reads, misc], axis=0).astype(BF16)
     for t in range(peers):
-        copies.append(pltpu.make_async_copy(grads, send.at[t, length:], sems.at[1, t]))
-        copies[-1].start()
+        send[t, :length] = recv[:, t * LANES : (t + 1) * LANES]
+        send[t, length:] = grads
     back = jnp.concatenate(value_columns(mixes) + [grad_keys, grad_reads, lane_pad(raw, LANES)], axis=1)
-    kept, given = halves([back], span, bit_of(pos, bit) == 0)
+    kept, given = halves([back], dates, bit_of(pos, 0) == 0)
     own[...] = kept.astype(BF16)
     give[...] = given.astype(BF16)
     sel[...] = jnp.concatenate([sensor_rows(ids_row)] * peers, axis=1)
-    for copy in copies:
-        copy.wait()
 
 
 def pack_kernel(core, ids_in, mask_in, table_in, bias_in, decay_in, skip_in, layer, values, cotangent, out, ids, mask_t, table, params, layer_v, sems):
@@ -405,7 +394,7 @@
     return rows[:8] + rows[8:16]
 
 
-def group_slab_kernel(dates, pos, recv, sel, rows_own, rows_got, keep, keep_sums, rows_keep, give):
+def group_slab_kernel(pos, recv, sel, rows, keep, keep_sums, give):
     peers = recv.shape[0]
     length = sel.shape[1] // peers
     count = keep.shape[0]
@@ -431,23 +420,24 @@
     upper, lower = part[:count], part[part.shape[0] - count :]
     keep[...] = jnp.where(first, upper, lower)
     keep_sums[...] = sums
-    kept, given = halves([rows_own[...].astype(F32), rows_got[...].astype(F32)], dates, first)
-    rows_keep[...] = kept.astype(BF16)
     give[...] = jnp.concatenate(
-        [jnp.where(first, lower, upper), pack_sums(sums)] + rows_block(given), axis=0
+        [jnp.where(first, lower, upper), pack_sums(sums)] + rows_block(rows[...].astype(F32)), axis=0
     ).astype(BF16)
 
 
-def group_join_kernel(dates, pos, keep, keep_sums, rows_own, got, rows_keep, give):
+def group_join_kernel(dates, pos, keep, keep_sums, rows_own, got, rows_keep, give, give_low, give_both):
     count = keep.shape[0]
-    first = bit_of(pos, 2) == 0
     there = got[...].astype(F32)
     total = keep[...] + there[:count]
     sums = keep_sums[...] + unpack_sums(there[count : count + 16])
-    rows_got = block_rows(there[count + 16 :], rows_own.shape[0])
-    kept, given = halves([rows_own[...].astype(F32), rows_got], dates, first)
-    rows_keep[...] = kept.astype(BF16)
-    give[...] = jnp.concatenate([total, pack_sums(sums)] + rows_block(given), axis=0).astype(BF16)
+    rows = [rows_own[...].astype(F32), block_rows(there[count + 16 :], rows_own.shape[0])]
+    same_low, other_low = halves(rows, dates, bit_of(pos, 1) == 0)
+    here, high = halves([same_low], dates, bit_of(pos, 2) == 0)
+    low, both = halves([other_low], dates, bit_of(pos, 2) == 0)
+    rows_keep[...] = here.astype(BF16)
+    give_low[...] = low.astype(BF16)
+    give_both[...] = both.astype(BF16)
+    give[...] = jnp.concatenate([total, pack_sums(sums)] + rows_block(high), axis=0).astype(BF16)
 
 
 def group_total_kernel(own, got, send, rest):
@@ -487,7 +477,7 @@
     store_rows(cols, scale, 1 - bit_of(pos, 0), slabs, weight, held, sems)()
 
 
-def final_kernel(heads, scale, pos, slabs, rows_own, got, rest, w_t, *refs):
+def final_kernel(heads, scale, pos, slabs, rows_own, got, low, both, rest, w_t, *refs):
     outs, (value, inputs, table, head), (held, sems, out_sems) = refs[:5], refs[5:9], refs[9:]
     model_d, cols, dates = w_t.shape[1], w_t.shape[0], value.shape[1]
     wait = store_rows(cols, scale, bit_of(pos, 0), slabs, outs[4], held, sems)
@@ -496,9 +486,11 @@
         for k, source in enumerate((value, inputs, table, head))
     ]
     w = w_t[...]
-    rows_got = block_rows(got[...].astype(F32)[slabs.shape[1] + 16 :], rows_own.shape[0])
-    rows = jnp.concatenate([rows_own[...].astype(F32), rows_got], axis=0)
-    masks = [4 * high + core + 2 * low for high in range(2) for core in range(2) for low in range(2)]
+    rows_got = block_rows(got[...].astype(F32)[slabs.shape[1] + 16 :], 2 * dates)
+    rows = jnp.concatenate(
+        [rows_own[...].astype(F32), rows_got, low[...].astype(F32), both[...].astype(F32)], axis=0
+    )
+    masks = [0, 1, 4, 5, 2, 3, 6, 7]
     where_to = []
     for mask in masks:
         index = 0
@@ -533,6 +525,7 @@
     count = (cols + 8) // 2
     half_rows = length // 2
     payload = count + 16 + half_rows * wide // LANES
+    payload_high = count + 16 + 2 * dates_dev * wide // LANES
 
     def groups(alternate):
         return [
@@ -544,40 +537,42 @@
     def across(bit):
         return [(i, i ^ 2**bit) for i in range(dates)]
 
-    send_t, rows_own, rows_give, sel = pl.pallas_call(
-        functools.partial(group_series_kernel, heads, model_d, 1, 2 * dates_dev),
-        out_shape=[
-            jax.ShapeDtypeStruct((peers, 3 * length + 16, LANES), BF16),
-            jax.ShapeDtypeStruct((half_rows, wide), BF16),
-            jax.ShapeDtypeStruct((half_rows, wide), BF16),
-            jax.ShapeDtypeStruct((16, peers * length), BF16),
+    send_t, rows_own, rows_give, sel = call(
+        functools.partial(group_series_kernel, heads, model_d, dates_dev),
+        [
+            ((peers, 3 * length + 16, LANES), BF16),
+            ((half_rows, wide), BF16),
+            ((half_rows, wide), BF16),
+            ((16, peers * length), BF16),
         ],
-        in_specs=[SMEM, VMEM, VMEM],
-        out_specs=[HBM, VMEM, VMEM, VMEM],
-        scratch_shapes=[
-            pltpu.VMEM((2 * length + 16, LANES), BF16),
-            pltpu.SemaphoreType.DMA((2, peers)),
-        ],
-        compiler_params=pltpu.CompilerParams(vmem_limit_bytes=48 * 1024 * 1024),
-    )(date_s, series, w_t)
+        [date_s, series, w_t],
+        1,
+    )
     recv_t = lax.all_to_all(
         send_t, ("tile", "date"), split_axis=0, concat_axis=0, tiled=True, axis_index_groups=groups(1)
     )
-    rows_got = lax.ppermute(rows_give, "date", across(1))
-    keep, keep_sums, rows_own, give = call(
-        functools.partial(group_slab_kernel, dates_dev),
-        [((count, LANES), F32), ((8, LANES), F32), ((half_rows, wide), BF16), ((payload, LANES), BF16)],
-        [date_s, recv_t, sel, rows_own, rows_got],
+    keep, keep_sums, give = call(
+        group_slab_kernel,
+        [((count, LANES), F32), ((8, LANES), F32), ((payload, LANES), BF16)],
+        [date_s, recv_t, sel, rows_give],
         1,
     )
     got = lax.ppermute(give, "date", across(0))
-    rows_own, give = call(
+    rows_own, give, give_low, give_both = call(
         functools.partial(group_join_kernel, dates_dev),
-        [((half_rows, wide), BF16), ((payload, LANES), BF16)],
+        [
+            ((2 * dates_dev, wide), BF16),
+            ((payload_high, LANES), BF16),
+            ((2 * dates_dev, wide), BF16),
+            ((2 * dates_dev, wide), BF16),
+        ],
         [date_s, keep, keep_sums, rows_own, got],
         1,
     )
     got = lax.ppermute(give, "date", across(2))
+    rows_both = lax.ppermute(give_both, "date", [(i, i ^ 6) for i in range(dates)])
+    rows_low = lax.ppermute(give_low, "date", across(1))
+    got, rows_both, rows_low = lax.optimization_barrier((got, rows_both, rows_low))
     send_g, rest = call(
         group_total_kernel, [((peers, count, LANES), BF16), ((8, LANES), F32)], [give, got]
     )
@@ -597,13 +592,13 @@
     value, inputs, table, head, weight_t = pl.pallas_call(
         functools.partial(final_kernel, heads, scale),
         out_shape=outs,
-        in_specs=[SMEM] + [VMEM] * 5,
+        in_specs=[SMEM] + [VMEM] * 7,
         out_specs=[HBM] * 5,
         scratch_shapes=[pltpu.VMEM(o.shape, o.dtype) for o in outs[:4]]
         + held
         + [pltpu.SemaphoreType.DMA((4,))],
         compiler_params=limit,
-    )(date_s, recv_g, rows_own, got, rest, w_t)
+    )(date_s, recv_g, rows_own, got, rows_low, rows_both, rest, w_t)
     weight_t = pl.pallas_call(
         functools.partial(other_rows_kernel, cols, scale),
         out_shape=outs[4],

time: 50.9 us -> 48.9 us (0.961)
  blocking collectives: 24.7 us -> 33.4 us
  waiting for transfers between devices: 12 us -> 5.22 us
  starting transfers between devices: 7.7 us -> 4.57 us
  Pallas kernels: 5.43 us -> 4.73 us
    all_to_all x0 -> x1, blocking collectives: none -> 8.91 us  [finish_four_levels(): lax.all_to_all(send_t, ('tile', 'date'), split_axis=0, concat_axis=0, til...]
    ppermute x1, waiting for transfers between devices: 5.92 us -> 0.01 us  [finish_four_levels(): got = lax.ppermute(give, 'date', across(2))]
    all_to_all x1 -> x0, starting transfers between devices: 3.41 us -> none  [finish_four_levels(): lax.all_to_all(send_t, ('tile', 'date'), split_axis=0, concat_axis=0, til...]
    pallas_call x1 -> x0, Pallas kernels: 1.93 us -> none  [finish_four_levels(): pl.pallas_call(functools.partial(group_series_kernel, heads, model_d, 1,...]
    pallas_call x3 -> x4, Pallas kernels: 0.32 us -> 1.55 us  [call(): pl.pallas_call(kernel, out_shape=[jax.ShapeDtypeStruct(s, d) for s, d in...]
    ppermute x1 -> x2, waiting for transfers between devices: 4.73 us -> 3.97 us  [the longest x1 3.97 us: finish_four_levels(): lax.ppermute(give_both, 'date', [(i, i ^ 6) for i in range(dates)])]
    ppermute x1, starting transfers between devices: 1.37 us -> 1.92 us  [finish_four_levels(): got = lax.ppermute(give, 'date', across(2))]
    ppermute x1 -> x2, starting transfers between devices: 1.92 us -> 1.63 us  [the longest x1 1.07 us: finish_four_levels(): lax.ppermute(give_both, 'date', [(i, i ^ 6) for i in range(dates)])]
  transfers between devices with their start and end apart: 5 -> 5, of which waited for: 5 -> 3; matrix products, arithmetic and copies ran while one was open for 0% -> 0% of each run, Pallas kernels for 2% -> 3%
where the time goes in v9:
time: 48.9 us; the launch traced here: 48.6 us
  blocking collectives  33.4 us (68%)
  waiting for transfers between devices  5.22 us (11%)
  Pallas kernels  4.73 us (10%)
  starting transfers between devices  4.57 us (9%)
  between operations  0.69 us (1%)
    all_to_all x1, blocking collectives, on_device(): lax.all_to_all(packed, 'date', split_axis=0, concat_axis=0, tiled=True)  14.6 us
    all_to_all x1, blocking collectives, finish_four_levels(): lax.all_to_all(send_g, ('tile', 'date'), split_axis=0, concat_axis=0, til...  9.83 us
    all_to_all x1, blocking collectives, finish_four_levels(): lax.all_to_all(send_t, ('tile', 'date'), split_axis=0, concat_axis=0, til...  8.91 us
    ppermute x1, waiting for transfers between devices, finish_four_levels(): lax.ppermute(give_both, 'date', [(i, i ^ 6) for i in range(dates)])  3.97 us
    ppermute x1, starting transfers between devices, finish_four_levels(): got = lax.ppermute(give, 'date', across(2))  1.92 us
    pallas_call x4, Pallas kernels, call(): pl.pallas_call(kernel, out_shape=[jax.ShapeDtypeStruct(s, d) for s, d in...  1.55 us
    pallas_call x1, Pallas kernels, finish_four_levels(): pl.pallas_call(functools.partial(final_kernel, heads, scale), out_shape=o...  1.23 us
    pallas_call x1, Pallas kernels, on_device(): pl.pallas_call(pack_kernel, out_shape=jax.ShapeDtypeStruct((pixel_dev, da...  1.08 us
  transfers between devices with their start and end apart: 5, of which 3 were waited for; matrix products, arithmetic and copies ran while one was open for 0% of the time, Pallas kernels for 3%

profile of v9, /device:TPU:0, one launch (start us, length us, event | category | flops | bytes accessed | tf_op | source)
XLA Modules:
  0.0 48.6 jit_solution(8339028380356974464)
XLA Ops:
  0.6 0.0 copy-start
  0.6 1.1 %shard_map.137 = bf16[8,4,3200]{2,1,0:T(4,128)(2,1)S(1)} custom-call(s32[1]{0:T(128)} %bitcast.core.pos, s32[4]{0:T(128)} %ids_in.1, s32[4,8]{1,0:T(4,128)} %bitcast.10, f32[2,1024]{1,0:T(2,128)} %table_in.1, f32[1,8]{1,0:T(1,128)} %bitcast.11, f32[1,8]{1,0:T(1,128)} %bitcast.12, f32[1,8]{1,0:T(1,128)} %bitcast.13, bf16[8,4,1024]{2,1,0:T(4,128)(2,1)} %layer.1, ...), custom_call_target="tpu_custom_call" | custom-call | tf_op jit(solution)/shard_map/pallas_call | solution.py:749
  1.7 14.6 %all_to_all.15 = bf16[8,4,3200]{2,1,0:T(4,128)(2,1)S(1)} all-to-all(bf16[8,4,3200]{2,1,0:T(4,128)(2,1)S(1)} %shard_map.137), channel_id=1, replica_groups=mesh['tile'=4,'date'=8] {'date'}, dimensions={0} | all-to-all | bytes 409600 | tf_op jit(solution)/shard_map/all_to_all | solution.py:764
  16.4 0.1 reshape.17.recv
  16.4 0.0 copy-done
  16.4 1.2 %shard_map.138 = (bf16[8,112,128]{2,1,0:T(8,128)(2,1)S(1)}, bf16[16,1408]{1,0:T(8,128)(2,1)S(1)}, bf16[16,1408]{1,0:T(8,128)(2,1)S(1)}, bf16[16,256]{1,0:T(8,128)(2,1)S(1)}) custom-call(s32[1]{0:T(128)} %bitcast.core.pos, bf16[32,3200]{1,0:T(8,128)(2,1)S(1)} %reshape.17.recv, bf16[264,1024]{1,0:T(8,128)(2,1)S(1)} %bitcast.7), custom_call_target="tpu_custom_call" | custom-call | tf_op jit(solution)/shard_map/pallas_call | solution.py:371
  17.6 8.9 %all_to_all.16.recv = bf16[8,112,128]{2,1,0:T(8,128)(2,1)S(1)} all-to-all(bf16[8,112,128]{2,1,0:T(8,128)(2,1)S(1)} %get-tuple-element.26), channel_id=1, replica_groups={{0,2,9,11,16,18,25,27},{1,3,8,10,17,19,24,26},{4,6,13,15,20,22,29,31},{..., dimensions={0} | all-to-all | bytes 458752 | tf_op jit(solution)/shard_map/all_to_all | solution.py:551
  26.6 0.3 shard_map.139
  26.8 1.0 %collective-permute-start = (bf16[328,128]{1,0:T(8,128)(2,1)S(1)}, bf16[328,128]{1,0:T(8,128)(2,1)S(1)}, u32[]{:S(2)}, u32[]{:S(2)}) collective-permute-start(bf16[328,128]{1,0:T(8,128)(2,1)S(1)} %get-tuple-element.32), channel_id=1, source_target_pairs={{0,1},{1,0},{2,3},{3,2},{4,5},{5,4},{6,7},{7,6},{8,9},{9,8},{10,11... | collective-permute-start | bytes 251912 | tf_op jit(solution)/shard_map/ppermute | solution.py:560
  27.8 0.9 %collective-permute-done.got = bf16[328,128]{1,0:T(8,128)(2,1)S(1)} collective-permute-done((bf16[328,128]{1,0:T(8,128)(2,1)S(1)}, bf16[328,128]{1,0:T(8,128)(2,1)S(1)}, u32[]{:S(2)}, u32[]{:S(2)}) %collective-permute-start) | collective-permute-done | bytes 84000 | tf_op jit(solution)/shard_map/ppermute | solution.py:560
  28.7 0.1 shard_map.140
  28.8 1.9 %collective-permute-start.1 = (bf16[240,128]{1,0:T(8,128)(2,1)S(1)}, bf16[240,128]{1,0:T(8,128)(2,1)S(1)}, u32[]{:S(2)}, u32[]{:S(2)}) collective-permute-start(bf16[240,128]{1,0:T(8,128)(2,1)S(1)} %get-tuple-element.33.own), channel_id=1, source_target_pairs={{0,4},{1,5},{2,6},{3,7},{4,0},{5,1},{6,2},{7,3},{8,12},{9,13},{10,... | collective-permute-start | bytes 184328 | tf_op jit(solution)/shard_map/ppermute | solution.py:572
  30.7 1.1 %collective-permute-start.2 = (bf16[8,1408]{1,0:T(8,128)(2,1)S(1)}, bf16[8,1408]{1,0:T(8,128)(2,1)S(1)}, u32[]{:S(2)}, u32[]{:S(2)}) collective-permute-start(bf16[8,1408]{1,0:T(8,128)(2,1)S(1)} %get-tuple-element.34), channel_id=1, source_target_pairs={{0,6},{1,7},{2,4},{3,5},{4,2},{5,3},{6,0},{7,1},{8,14},{9,15},{10,... | collective-permute-start | bytes 67592 | tf_op jit(solution)/shard_map/ppermute | solution.py:573
  31.8 0.6 %collective-permute-start.3 = (bf16[8,1408]{1,0:T(8,128)(2,1)S(1)}, bf16[8,1408]{1,0:T(8,128)(2,1)S(1)}, u32[]{:S(2)}, u32[]{:S(2)}) collective-permute-start(bf16[8,1408]{1,0:T(8,128)(2,1)S(1)} %get-tuple-element.35), channel_id=1, source_target_pairs={{0,2},{1,3},{2,0},{3,1},{4,6},{5,7},{6,4},{7,5},{8,10},{9,11},{10,... | collective-permute-start | bytes 67592 | tf_op jit(solution)/shard_map/ppermute | solution.py:574
  32.4 4.0 %collective-permute-done.2.both = bf16[8,1408]{1,0:T(8,128)(2,1)S(1)} collective-permute-done((bf16[8,1408]{1,0:T(8,128)(2,1)S(1)}, bf16[8,1408]{1,0:T(8,128)(2,1)S(1)}, u32[]{:S(2)}, u32[]{:S(2)}) %collective-permute-start.2) | collective-permute-done | bytes 22560 | tf_op jit(solution)/shard_map/ppermute | solution.py:573
  36.3 0.0 collective-permute-done.3.low
  36.3 0.0 collective-permute-done.1.got
  36.4 9.8 %all_to_all.17.slabs = bf16[8,136,128]{2,1,0:T(8,128)(2,1)S(1)} all-to-all(bf16[8,136,128]{2,1,0:T(8,128)(2,1)S(1)} %get-tuple-element.37), channel_id=1, replica_groups={{0,2,8,10,16,18,24,26},{1,3,9,11,17,19,25,27},{4,6,12,14,20,22,28,30},{..., dimensions={0} | all-to-all | bytes 557056 | tf_op jit(solution)/shard_map/all_to_all | solution.py:579
  46.2 0.0 collective-permute-start.4
  46.2 1.2 %shard_map.142 = (bf16[8,4,1024]{2,1,0:T(4,128)(2,1)}, bf16[8,4,1024]{2,1,0:T(4,128)(2,1)}, f32[2,1024]{1,0:T(2,128)}, f32[3,8]{1,0:T(4,128)}, f32[264,1024]{1,0:T(8,128)}) custom-call(s32[1]{0:T(128)} %bitcast.core.pos, bf16[8,136,128]{2,1,0:T(8,128)(2,1)S(1)} %all_to_all.17.slabs, bf16[8,1408]{1,0:T(8,128)(2,1)S(1)} %get-tuple-element.38.rows_own, ...), custom_call_target="tpu_custom_call" | custom-call | tf_op jit(solution)/shard_map/pallas_call | solution.py:592
  47.5 0.3 collective-permute-done.4.slabs
  47.8 0.9 %shard_map.143 = f32[264,1024]{1,0:T(8,128)} custom-call(s32[1]{0:T(128)} %bitcast.core.pos, bf16[8,136,128]{2,1,0:T(8,128)(2,1)S(1)} %collective-permute-done.4.slabs, f32[264,1024]{1,0:T(8,128)} %get-tuple-element.44.weight_in), custom_call_target="tpu_custom_call", output_to_operand_aliasing={{}: (2, {})} | custom-call | tf_op jit(solution)/shard_map/pallas_call | solution.py:602
  (1 shorter events, 0.0 us)
Async XLA Ops:
  0.6 15.8 %copy-start = (bf16[1024,264]{0,1:T(8,128)(2,1)S(1)}, bf16[1024,264]{0,1:T(8,128)(2,1)}, u32[]{:S(2)}) copy-start(bf16[1024,264]{0,1:T(8,128)(2,1)} %param.16) | copy-start | bytes 1622020
  26.8 1.9 %collective-permute-start = (bf16[328,128]{1,0:T(8,128)(2,1)S(1)}, bf16[328,128]{1,0:T(8,128)(2,1)S(1)}, u32[]{:S(2)}, u32[]{:S(2)}) collective-permute-start(bf16[328,128]{1,0:T(8,128)(2,1)S(1)} %get-tuple-element.32), channel_id=1, source_target_pairs={{0,1},{1,0},{2,3},{3,2},{4,5},{5,4},{6,7},{7,6},{8,9},{9,8},{10,11... | collective-permute-start | bytes 251912 | tf_op jit(solution)/shard_map/ppermute | solution.py:560
  28.8 7.5 %collective-permute-start.1 = (bf16[240,128]{1,0:T(8,128)(2,1)S(1)}, bf16[240,128]{1,0:T(8,128)(2,1)S(1)}, u32[]{:S(2)}, u32[]{:S(2)}) collective-permute-start(bf16[240,128]{1,0:T(8,128)(2,1)S(1)} %get-tuple-element.33.own), channel_id=1, source_target_pairs={{0,4},{1,5},{2,6},{3,7},{4,0},{5,1},{6,2},{7,3},{8,12},{9,13},{10,... | collective-permute-start | bytes 184328 | tf_op jit(solution)/shard_map/ppermute | solution.py:572
  30.7 5.6 %collective-permute-start.2 = (bf16[8,1408]{1,0:T(8,128)(2,1)S(1)}, bf16[8,1408]{1,0:T(8,128)(2,1)S(1)}, u32[]{:S(2)}, u32[]{:S(2)}) collective-permute-start(bf16[8,1408]{1,0:T(8,128)(2,1)S(1)} %get-tuple-element.34), channel_id=1, source_target_pairs={{0,6},{1,7},{2,4},{3,5},{4,2},{5,3},{6,0},{7,1},{8,14},{9,15},{10,... | collective-permute-start | bytes 67592 | tf_op jit(solution)/shard_map/ppermute | solution.py:573
  31.8 4.5 %collective-permute-start.3 = (bf16[8,1408]{1,0:T(8,128)(2,1)S(1)}, bf16[8,1408]{1,0:T(8,128)(2,1)S(1)}, u32[]{:S(2)}, u32[]{:S(2)}) collective-permute-start(bf16[8,1408]{1,0:T(8,128)(2,1)S(1)} %get-tuple-element.35), channel_id=1, source_target_pairs={{0,2},{1,3},{2,0},{3,1},{4,6},{5,7},{6,4},{7,5},{8,10},{9,11},{10,... | collective-permute-start | bytes 67592 | tf_op jit(solution)/shard_map/ppermute | solution.py:574
  46.2 1.6 %collective-permute-start.4 = (bf16[8,136,128]{2,1,0:T(8,128)(2,1)S(1)}, bf16[8,136,128]{2,1,0:T(8,128)(2,1)S(1)}, u32[]{:S(2)}, u32[]{:S(2)}) collective-permute-start(bf16[8,136,128]{2,1,0:T(8,128)(2,1)S(1)} %all_to_all.17.slabs), channel_id=1, source_target_pairs={{0,1},{1,0},{2,3},{3,2},{4,5},{5,4},{6,7},{7,6},{8,9},{9,8},{10,11... | collective-permute-start | bytes 835592 | tf_op jit(solution)/shard_map/ppermute | solution.py:582

commit v10 on v9

--- a/solution.py
+++ b/solution.py
@@ -149,8 +149,10 @@
     sel[...] = sensor_rows(ids_row)
 
 
-def group_series_kernel(heads, model_d, dates, pos, recv, w_t, send, own, give, sel):
-    peers, length = send.shape[0], recv.shape[0]
+def direct_series_kernel(heads, model_d, dates, pos, tile, recv, w_t, *refs):
+    sends, (own, give, sel) = refs[:-3], refs[-3:]
+    length = recv.shape[0]
+    slab = 2 * LANES
     mixes, grad_keys, grad_reads, raw, terms, ids_row, eye_h = series_terms(heads, model_d, recv, w_t)
     raw_t = nt(eye_h.astype(BF16), raw.astype(BF16))
     total = jnp.sum(terms, axis=0, keepdims=True)
@@ -159,17 +161,19 @@
         [lane_pad(raw_t, LANES), high, total - high, jnp.zeros((6, LANES), F32)], axis=0
     )
     grads = jnp.concatenate([grad_keys, grad_reads, misc], axis=0).astype(BF16)
-    for t in range(peers):
-        send[t, :length] = recv[:, t * LANES : (t + 1) * LANES]
-        send[t, length:] = grads
+    for k, send in enumerate(sends):
+        for block in range(2):
+            at = pl.multiple_of((tile[0] ^ k) * slab + block * LANES, LANES)
+            send[block * length : (block + 1) * length] = recv[:, pl.ds(at, LANES)]
+        send[2 * length :] = grads
     back = jnp.concatenate(value_columns(mixes) + [grad_keys, grad_reads, lane_pad(raw, LANES)], axis=1)
     kept, given = halves([back], dates, bit_of(pos, 0) == 0)
     own[...] = kept.astype(BF16)
     give[...] = given.astype(BF16)
-    sel[...] = jnp.concatenate([sensor_rows(ids_row)] * peers, axis=1)
-
-
-def pack_kernel(core, ids_in, mask_in, table_in, bias_in, decay_in, skip_in, layer, values, cotangent, out, ids, mask_t, table, params, layer_v, sems):
+    sel[...] = sensor_rows(ids_row)
+
+
+def pack_kernel(pos, tile, ids_in, mask_in, table_in, bias_in, decay_in, skip_in, layer, values, cotangent, out, ids, mask_t, table, params, layer_v, sems):
     pixels, dates, model_d = layer.shape
     small = [
         pltpu.make_async_copy(ids_in, ids, sems.at[0]),
@@ -394,192 +398,167 @@
     return rows[:8] + rows[8:16]
 
 
-def group_slab_kernel(pos, recv, sel, rows, keep, keep_sums, give):
-    peers = recv.shape[0]
-    length = sel.shape[1] // peers
-    count = keep.shape[0]
+def pair_sum(parts):
+    return (parts[0] + parts[1]) + (parts[2] + parts[3])
+
+
+def direct_slab_kernel(pos, *refs):
+    parts, (sel, rows, keep, keep_sums, give) = refs[:4], refs[4:]
+    cols = keep.shape[0]
+    length = sel.shape[1]
     first = bit_of(pos, 0) == 0
-    tokens = recv[:, :length, :].reshape(peers * length, LANES)
-    keys = recv[:, length : 2 * length, :].reshape(peers * length, LANES)
-    reads = recv[:, 2 * length : 3 * length, :].reshape(peers * length, LANES)
-    misc = [recv[t, 3 * length :, :] for t in range(peers)]
-    raw_t = jnp.concatenate([m[:, :length] for m in misc], axis=1)
-    part = jnp.concatenate([tn(keys, tokens), tn(reads, tokens), nn(raw_t, tokens)[: count - LANES]], axis=0)
     chosen = sel[...]
-    head = sum(m.astype(F32) for m in misc)[8:10]
-    sums = jnp.concatenate(
+    tokens, keys, reads, raw_t, sums = [], [], [], [], []
+    for part in parts:
+        tokens.append(jnp.concatenate([part[:length], part[length : 2 * length]], axis=1))
+        keys.append(part[2 * length : 3 * length])
+        reads.append(part[3 * length : 4 * length])
+        misc = part[4 * length :]
+        raw_t.append(misc[:, :length])
+        head = misc.astype(F32)[8:10]
+        sums.append(
+            jnp.concatenate(
+                [
+                    nn(chosen, keys[-1])[0:2],
+                    nn(chosen, reads[-1])[0:2],
+                    lane_pad(nt(chosen, raw_t[-1])[0:2], LANES),
+                    head[0:1] + head[1:2],
+                    jnp.zeros((1, LANES), F32),
+                ],
+                axis=0,
+            )
+        )
+    tokens = jnp.concatenate(tokens, axis=0)
+    slab = jnp.concatenate(
         [
-            nn(chosen, keys)[0:2],
-            nn(chosen, reads)[0:2],
-            lane_pad(nt(chosen, raw_t)[0:2], LANES),
-            head[0:1] + head[1:2],
-            jnp.zeros((1, LANES), F32),
+            tn(jnp.concatenate(keys, axis=0), tokens),
+            tn(jnp.concatenate(reads, axis=0), tokens),
+            nn(jnp.concatenate(raw_t, axis=1), tokens)[: cols - 2 * LANES],
         ],
         axis=0,
     )
-    upper, lower = part[:count], part[part.shape[0] - count :]
-    keep[...] = jnp.where(first, upper, lower)
-    keep_sums[...] = sums
+    left, right = slab[:, :LANES], slab[:, LANES:]
+    keep[...] = jnp.where(first, left, right)
+    packed = pack_sums(pair_sum(sums))
+    keep_sums[...] = unpack_sums(packed)
     give[...] = jnp.concatenate(
-        [jnp.where(first, lower, upper), pack_sums(sums)] + rows_block(rows[...].astype(F32)), axis=0
+        [jnp.where(first, right, left), packed] + rows_block(rows[...].astype(F32)), axis=0
     ).astype(BF16)
 
 
-def group_join_kernel(dates, pos, keep, keep_sums, rows_own, got, rows_keep, give, give_low, give_both):
-    count = keep.shape[0]
+def direct_join_kernel(dates, pos, keep, keep_sums, rows_own, got, rows_keep, own, low, high, both):
+    cols = keep.shape[0]
     there = got[...].astype(F32)
-    total = keep[...] + there[:count]
-    sums = keep_sums[...] + unpack_sums(there[count : count + 16])
-    rows = [rows_own[...].astype(F32), block_rows(there[count + 16 :], rows_own.shape[0])]
+    total = keep[...] + there[:cols]
+    sums = keep_sums[...] + unpack_sums(there[cols : cols + 16])
+    rows = [rows_own[...].astype(F32), block_rows(there[cols + 16 :], rows_own.shape[0])]
     same_low, other_low = halves(rows, dates, bit_of(pos, 1) == 0)
-    here, high = halves([same_low], dates, bit_of(pos, 2) == 0)
-    low, both = halves([other_low], dates, bit_of(pos, 2) == 0)
+    here, high_rows = halves([same_low], dates, bit_of(pos, 2) == 0)
+    low_rows, both_rows = halves([other_low], dates, bit_of(pos, 2) == 0)
     rows_keep[...] = here.astype(BF16)
-    give_low[...] = low.astype(BF16)
-    give_both[...] = both.astype(BF16)
-    give[...] = jnp.concatenate([total, pack_sums(sums)] + rows_block(high), axis=0).astype(BF16)
-
-
-def group_total_kernel(own, got, send, rest):
-    count = send.shape[1]
-    total = (own[...].astype(F32) + got[...].astype(F32))[: count + 16]
-    slab = total[:count].astype(BF16)
-    for t in range(send.shape[0]):
-        send[t] = slab
-    rest[...] = unpack_sums(total[count:])
-
-
-def store_rows(cols, scale, core, slabs, weight, held, sems):
-    count = slabs.shape[1]
-    base = cols - count
-    for t in range(slabs.shape[0]):
-        held[:, t * LANES : (t + 1) * LANES] = slabs[t].astype(F32) * scale
-    at = pl.multiple_of(core * base, 8)
-    main = pltpu.make_async_copy(held.at[:base], weight.at[pl.ds(at, base)], sems.at[0])
-    last = pltpu.make_async_copy(held.at[base:], weight.at[2 * base :], sems.at[1])
-    main.start()
-
-    @pl.when(core == 1)
-    def _():
-        last.start()
-
-    def wait():
-        main.wait()
-
-        @pl.when(core == 1)
-        def _():
-            last.wait()
-
-    return wait
-
-
-def other_rows_kernel(cols, scale, pos, slabs, weight_in, weight, held, sems):
-    store_rows(cols, scale, 1 - bit_of(pos, 0), slabs, weight, held, sems)()
-
-
-def final_kernel(heads, scale, pos, slabs, rows_own, got, low, both, rest, w_t, *refs):
+    common = jnp.concatenate([total, pack_sums(sums)], axis=0).astype(BF16)
+    own[...] = common
+    for send, part in ((low, low_rows), (high, high_rows), (both, both_rows)):
+        send[...] = jnp.concatenate([common] + rows_block(part.astype(BF16)), axis=0)
+
+
+def direct_total_kernel(own, low, high, both, send, rest):
+    cols = send.shape[0]
+    total = pair_sum([part[...].astype(F32)[: cols + 16] for part in (own, low, high, both)])
+    send[...] = total[:cols].astype(BF16)
+    rest[...] = unpack_sums(total[cols:])
+
+
+def store_slabs(scale, tile, core, slabs, weight, held, sems):
+    copies = []
+    for k, slab in enumerate(slabs):
+        held[k] = slab.astype(F32) * scale
+        at = pl.multiple_of((2 * (tile ^ k) + core) * LANES, LANES)
+        copies.append(pltpu.make_async_copy(held.at[k], weight.at[:, pl.ds(at, LANES)], sems.at[k]))
+        copies[-1].start()
+    return copies
+
+
+def other_slabs_kernel(scale, pos, tile, slabs, weight_in, weight, held, sems):
+    parts = [slabs[k] for k in range(slabs.shape[0])]
+    for copy in store_slabs(scale, tile[0], 1 - bit_of(pos, 0), parts, weight, held, sems):
+        copy.wait()
+
+
+def final_kernel(heads, scale, pos, tile, slabs, rows_own, low, high, both, rest, w_t, *refs):
     outs, (value, inputs, table, head), (held, sems, out_sems) = refs[:5], refs[5:9], refs[9:]
     model_d, cols, dates = w_t.shape[1], w_t.shape[0], value.shape[1]
-    wait = store_rows(cols, scale, bit_of(pos, 0), slabs, outs[4], held, sems)
+    parts = [slabs[k] for k in range(slabs.shape[0])]
+    copies = store_slabs(scale, tile[0], bit_of(pos, 0), parts, outs[4], held, sems)
     moves = [
         pltpu.make_async_copy(source, outs[k], out_sems.at[k])
         for k, source in enumerate((value, inputs, table, head))
     ]
     w = w_t[...]
-    rows_got = block_rows(got[...].astype(F32)[slabs.shape[1] + 16 :], 2 * dates)
-    rows = jnp.concatenate(
-        [rows_own[...].astype(F32), rows_got, low[...].astype(F32), both[...].astype(F32)], axis=0
-    )
-    masks = [0, 1, 4, 5, 2, 3, 6, 7]
-    where_to = []
-    for mask in masks:
-        index = 0
-        for bit in range(3):
-            here = bit_of(pos, bit)
-            index = index + 2**bit * (1 - here if mask >> bit & 1 else here)
-        where_to.append(index)
-    for k, pixel in enumerate(where_to):
-        value[pixel] = rows[k * dates : (k + 1) * dates, :model_d].astype(BF16)
+    rows = [rows_own[...].astype(F32)]
+    for part in (low, high, both):
+        rows.append(block_rows(part[...].astype(F32)[cols + 16 :], 2 * dates))
+    rows = jnp.concatenate(rows, axis=0)
+    masks = [0, 1, 2, 3, 4, 5, 6, 7]
+    for k, mask in enumerate(masks):
+        value[pos[0] ^ mask] = rows[k * dates : (k + 1) * dates, :model_d].astype(BF16)
     moves[0].start()
     grads = nn(rows[:, model_d : model_d + EXT].astype(BF16)[:, :cols], w)
-    for k, pixel in enumerate(where_to):
-        inputs[pixel] = grads[k * dates : (k + 1) * dates].astype(BF16)
+    for k, mask in enumerate(masks):
+        inputs[pos[0] ^ mask] = grads[k * dates : (k + 1) * dates].astype(BF16)
     moves[1].start()
     sums = jnp.concatenate([rest[0:2, :], rest[2:4, :], rest[4:6, :]], axis=1)[:, :cols]
-    high, low = split(sums)
-    table[...] = (nn(high, w) + nn(low, w)) * scale
+    parts_high, parts_low = split(sums)
+    table[...] = (nn(parts_high, w) + nn(parts_low, w)) * scale
     total = rest[6:7, :]
     head[...] = jnp.concatenate([total[:, k * heads : (k + 1) * heads] for k in (1, 0, 2)], axis=0) * scale
     for move in moves[2:]:
         move.start()
-    wait()
-    for move in moves:
-        move.wait()
-
-
-def finish_four_levels(series, w_t, date_s, heads, scale, pixel_dev, dates_dev, tiles, dates):
+    for copy in copies + moves:
+        copy.wait()
+
+
+def finish_direct(series, w_t, date_s, tile_s, heads, scale, pixel_dev, dates_dev, tiles, dates):
     length = series.shape[0]
     cols, model_d = w_t.shape
-    peers = 2 * tiles
     wide = model_d + EXT
-    count = (cols + 8) // 2
     half_rows = length // 2
-    payload = count + 16 + half_rows * wide // LANES
-    payload_high = count + 16 + 2 * dates_dev * wide // LANES
-
-    def groups(alternate):
-        return [
-            [t * dates + 4 * high + 2 * low + (c + alternate * t) % 2 for t in range(tiles) for low in range(2)]
-            for high in range(2)
-            for c in range(2)
-        ]
-
-    def across(bit):
-        return [(i, i ^ 2**bit) for i in range(dates)]
-
-    send_t, rows_own, rows_give, sel = call(
-        functools.partial(group_series_kernel, heads, model_d, dates_dev),
-        [
-            ((peers, 3 * length + 16, LANES), BF16),
-            ((half_rows, wide), BF16),
-            ((half_rows, wide), BF16),
-            ((16, peers * length), BF16),
-        ],
-        [date_s, series, w_t],
+    payload = cols + 16 + half_rows * wide // LANES
+    payload_z = cols + 16 + 2 * dates_dev * wide // LANES
+    axes = ("tile", "date")
+
+    def across(mask):
+        return [(i, i ^ mask) for i in range(tiles * dates)]
+
+    *sends, rows_own, rows_give, sel = call(
+        functools.partial(direct_series_kernel, heads, model_d, dates_dev),
+        [((4 * length + 16, LANES), BF16)] * tiles
+        + [((half_rows, wide), BF16), ((half_rows, wide), BF16), ((16, length), BF16)],
+        [date_s, tile_s, series, w_t],
+        2,
+    )
+    parts = {k: lax.ppermute(sends[k], axes, across(dates * k + k % 2)) for k in (3, 2, 1)}
+    keep, keep_sums, give = call(
+        direct_slab_kernel,
+        [((cols, LANES), F32), ((8, LANES), F32), ((payload, LANES), BF16)],
+        [date_s, sends[0], parts[1], parts[2], parts[3], sel, rows_give],
         1,
     )
-    recv_t = lax.all_to_all(
-        send_t, ("tile", "date"), split_axis=0, concat_axis=0, tiled=True, axis_index_groups=groups(1)
-    )
-    keep, keep_sums, give = call(
-        group_slab_kernel,
-        [((count, LANES), F32), ((8, LANES), F32), ((payload, LANES), BF16)],
-        [date_s, recv_t, sel, rows_give],
-        1,
-    )
-    got = lax.ppermute(give, "date", across(0))
-    rows_own, give, give_low, give_both = call(
-        functools.partial(group_join_kernel, dates_dev),
-        [
-            ((2 * dates_dev, wide), BF16),
-            ((payload_high, LANES), BF16),
-            ((2 * dates_dev, wide), BF16),
-            ((2 * dates_dev, wide), BF16),
-        ],
+    got = lax.ppermute(give, axes, across(1))
+    rows_own, own, *levels = call(
+        functools.partial(direct_join_kernel, dates_dev),
+        [((2 * dates_dev, wide), BF16), ((cols + 16, LANES), BF16)] + [((payload_z, LANES), BF16)] * 3,
         [date_s, keep, keep_sums, rows_own, got],
         1,
     )
-    got = lax.ppermute(give, "date", across(2))
-    rows_both = lax.ppermute(give_both, "date", [(i, i ^ 6) for i in range(dates)])
-    rows_low = lax.ppermute(give_low, "date", across(1))
-    got, rows_both, rows_low = lax.optimization_barrier((got, rows_both, rows_low))
-    send_g, rest = call(
-        group_total_kernel, [((peers, count, LANES), BF16), ((8, LANES), F32)], [give, got]
-    )
-    recv_g = lax.all_to_all(
-        send_g, ("tile", "date"), split_axis=0, concat_axis=0, tiled=True, axis_index_groups=groups(0)
-    )
-    other_g = lax.ppermute(recv_g, "date", across(0))
+    arrived = {k: lax.ppermute(levels[k - 1], axes, across(2 * k)) for k in (3, 2, 1)}
+    low, high, both = (arrived[k] for k in (1, 2, 3))
+    slab, rest = call(
+        direct_total_kernel, [((cols, LANES), BF16), ((8, LANES), F32)], [own, low, high, both]
+    )
+    gathered = {k: lax.ppermute(slab, axes, across(dates * k)) for k in (3, 2, 1)}
+    slabs = jnp.stack([slab] + [gathered[k] for k in (1, 2, 3)])
+    other_slabs = lax.ppermute(slabs, axes, across(1))
     outs = [
         jax.ShapeDtypeStruct((pixel_dev, dates_dev, model_d), BF16),
         jax.ShapeDtypeStruct((pixel_dev, dates_dev, model_d), BF16),
@@ -587,31 +566,31 @@
         jax.ShapeDtypeStruct((3, heads), F32),
         jax.ShapeDtypeStruct((cols, model_d), F32),
     ]
-    held = [pltpu.VMEM((count, model_d), F32), pltpu.SemaphoreType.DMA((2,))]
+    held = [pltpu.VMEM((tiles, cols, LANES), F32), pltpu.SemaphoreType.DMA((tiles,))]
     limit = pltpu.CompilerParams(vmem_limit_bytes=48 * 1024 * 1024)
     value, inputs, table, head, weight_t = pl.pallas_call(
         functools.partial(final_kernel, heads, scale),
         out_shape=outs,
-        in_specs=[SMEM] + [VMEM] * 7,
+        in_specs=[SMEM] * 2 + [VMEM] * 7,
         out_specs=[HBM] * 5,
         scratch_shapes=[pltpu.VMEM(o.shape, o.dtype) for o in outs[:4]]
         + held
         + [pltpu.SemaphoreType.DMA((4,))],
         compiler_params=limit,
-    )(date_s, recv_g, rows_own, got, rows_low, rows_both, rest, w_t)
+    )(date_s, tile_s, slabs, rows_own, low, high, both, rest, w_t)
     weight_t = pl.pallas_call(
-        functools.partial(other_rows_kernel, cols, scale),
+        functools.partial(other_slabs_kernel, scale),
         out_shape=outs[4],
-        in_specs=[SMEM, VMEM, HBM],
+        in_specs=[SMEM, SMEM, VMEM, HBM],
         out_specs=HBM,
         scratch_shapes=held,
-        input_output_aliases={2: 0},
+        input_output_aliases={3: 0},
         compiler_params=limit,
-    )(date_s, other_g, weight_t)
+    )(date_s, tile_s, other_slabs, weight_t)
     return value, inputs, weight_t.T, table, head
 
 
-def finish_any(series, w_t, date_s, heads, scale, pixel_dev, dates_dev, tiles, dates):
+def finish_any(series, w_t, date_s, tile_s, heads, scale, pixel_dev, dates_dev, tiles, dates):
     length = series.shape[0]
     cols, model_d = w_t.shape
     levels = dates // 2
@@ -732,6 +711,7 @@
     slab = model_d // tiles
     half = slab // 2
     date_s = lax.axis_index("date").astype(jnp.int32).reshape(1)
+    tile_s = lax.axis_index("tile").astype(jnp.int32).reshape(1)
     w_t = proj_weight.T
     scale = 1.0 / math.sqrt(pixel_dev * dates_dev * tiles * dates)
 
@@ -749,7 +729,7 @@
     packed = pl.pallas_call(
         pack_kernel,
         out_shape=jax.ShapeDtypeStruct((pixel_dev, dates_dev, 3 * model_d + LANES), BF16),
-        in_specs=[SMEM] + [HBM] * 9,
+        in_specs=[SMEM] * 2 + [HBM] * 9,
         out_specs=VMEM,
         scratch_shapes=[
             pltpu.SMEM((dates_dev,), jnp.int32),
@@ -760,16 +740,16 @@
             pltpu.SemaphoreType.DMA((9,)),
         ],
         compiler_params=pltpu.CompilerParams(vmem_limit_bytes=16 * 1024 * 1024),
-    )(date_s, *[pltpu.with_memory_space_constraint(operand, pltpu.HBM) for operand in operands])
+    )(date_s, tile_s, *[pltpu.with_memory_space_constraint(operand, pltpu.HBM) for operand in operands])
     series = lax.all_to_all(packed, "date", split_axis=0, concat_axis=0, tiled=True).reshape(
         length, 3 * model_d + LANES
     )
 
-    if levels == 4 and model_d == 2 * LANES * tiles:
-        finish = finish_four_levels
+    if levels == 4 and tiles == 4 and model_d == 2 * LANES * tiles:
+        finish = finish_direct
     else:
         finish = finish_any
-    return finish(series, w_t, date_s, heads, scale, pixel_dev, dates_dev, tiles, dates)
+    return finish(series, w_t, date_s, tile_s, heads, scale, pixel_dev, dates_dev, tiles, dates)
 
 
 def solution(mesh):

time: 48.9 us -> 46.3 us (0.947)
  blocking collectives: 33.4 us -> 14.6 us
  waiting for transfers between devices: 5.22 us -> 13.7 us
  starting transfers between devices: 4.57 us -> 12.4 us
    all_to_all x2 -> x0, blocking collectives: 18.7 us -> none  [the longest x1 9.83 us: finish_four_levels(): lax.all_to_all(send_g, ('tile', 'date'), split_axis=0, concat_axis=0, til...]
    ppermute x5 -> x11, waiting for transfers between devices: 5.22 us -> 13.7 us  [the longest x3 6.53 us: finish_direct(): lax.ppermute(levels[k - 1], axes, across(2 * k))]
    ppermute x5 -> x11, starting transfers between devices: 4.57 us -> 12.4 us  [the longest x3 4.47 us: finish_direct(): lax.ppermute(levels[k - 1], axes, across(2 * k))]
  transfers between devices with their start and end apart: 5 -> 11, of which waited for: 3 -> 10; matrix products, arithmetic and copies ran while one was open for 0% -> 0% of each run, Pallas kernels for 3% -> 3%
where the time goes in v10:
time: 46.3 us; the launch traced here: 46.1 us
  blocking collectives  14.6 us (32%)
  waiting for transfers between devices  13.7 us (30%)
  starting transfers between devices  12.4 us (27%)
  Pallas kernels  4.62 us (10%)
  between operations  0.73 us (2%)
    all_to_all x1, blocking collectives, on_device(): lax.all_to_all(packed, 'date', split_axis=0, concat_axis=0, tiled=True)  14.6 us
    ppermute x3, waiting for transfers between devices, finish_direct(): lax.ppermute(levels[k - 1], axes, across(2 * k))  6.53 us
    ppermute x3, starting transfers between devices, finish_direct(): lax.ppermute(levels[k - 1], axes, across(2 * k))  4.47 us
    ppermute x3, starting transfers between devices, finish_direct(): lax.ppermute(slab, axes, across(dates * k))  3.55 us
    ppermute x3, starting transfers between devices, finish_direct(): lax.ppermute(sends[k], axes, across(dates * k + k % 2))  2.99 us
    ppermute x3, waiting for transfers between devices, finish_direct(): lax.ppermute(sends[k], axes, across(dates * k + k % 2))  2.95 us
    ppermute x3, waiting for transfers between devices, finish_direct(): lax.ppermute(slab, axes, across(dates * k))  2.85 us
    pallas_call x4, Pallas kernels, call(): pl.pallas_call(kernel, out_shape=[jax.ShapeDtypeStruct(s, d) for s, d in...  1.53 us
  transfers between devices with their start and end apart: 11, of which 10 were waited for; matrix products, arithmetic and copies ran while one was open for 0% of the time, Pallas kernels for 3%

profile of v10, /device:TPU:0, one launch (start us, length us, event | category | flops | bytes accessed | tf_op | source)
XLA Modules:
  0.0 46.1 jit_solution(12791546080823019505)
XLA Ops:
  0.6 0.0 copy-start
  0.7 1.1 %shard_map.137 = bf16[8,4,3200]{2,1,0:T(4,128)(2,1)S(1)} custom-call(s32[1]{0:T(128)} %bitcast.pos, s32[1]{0:T(128)} %bitcast.1.tile, s32[4]{0:T(128)} %ids_in.1, s32[4,8]{1,0:T(4,128)} %bitcast.19, f32[2,1024]{1,0:T(2,128)} %table_in.1, f32[1,8]{1,0:T(1,128)} %bitcast.20, f32[1,8]{1,0:T(1,128)} %bitcast.21, f32[1,8]{1,0:T(1,128)} %bitcast.22, ...), custom_call_target="tpu_custom_call" | custom-call | tf_op jit(solution)/shard_map/pallas_call | solution.py:729
  1.7 14.6 %all_to_all.5 = bf16[8,4,3200]{2,1,0:T(4,128)(2,1)S(1)} all-to-all(bf16[8,4,3200]{2,1,0:T(4,128)(2,1)S(1)} %shard_map.137), channel_id=1, replica_groups=mesh['tile'=4,'date'=8] {'date'}, dimensions={0} | all-to-all | bytes 409600 | tf_op jit(solution)/shard_map/all_to_all | solution.py:744
  16.4 0.1 reshape.21.recv
  16.4 0.0 copy-done
  16.4 1.2 %shard_map.138 = (bf16[144,128]{1,0:T(8,128)(2,1)S(1)}, bf16[144,128]{1,0:T(8,128)(2,1)S(1)}, bf16[144,128]{1,0:T(8,128)(2,1)S(1)}, bf16[144,128]{1,0:T(8,128)(2...) custom-call(s32[1]{0:T(128)} %bitcast.pos, s32[1]{0:T(128)} %bitcast.1.tile, ...), custom_call_target="tpu_custom_call" | custom-call | tf_op jit(solution)/shard_map/pallas_call | solution.py:375
  17.6 0.1 collective-permute-start
  17.7 1.6 %collective-permute-start.1 = (bf16[144,128]{1,0:T(8,128)(2,1)S(1)}, bf16[144,128]{1,0:T(8,128)(2,1)S(1)}, u32[]{:S(2)}, u32[]{:S(2)}) collective-permute-start(bf16[144,128]{1,0:T(8,128)(2,1)S(1)} %get-tuple-element.29), channel_id=1, source_target_pairs={{0,16},{1,17},{2,18},{3,19},{4,20},{5,21},{6,22},{7,23},{8,24},{9,... | collective-permute-start | bytes 110600 | tf_op jit(solution)/shard_map/ppermute | solution.py:540
  19.3 1.3 %collective-permute-start.2 = (bf16[144,128]{1,0:T(8,128)(2,1)S(1)}, bf16[144,128]{1,0:T(8,128)(2,1)S(1)}, u32[]{:S(2)}, u32[]{:S(2)}) collective-permute-start(bf16[144,128]{1,0:T(8,128)(2,1)S(1)} %get-tuple-element.30), channel_id=1, source_target_pairs={{0,25},{1,24},{2,27},{3,26},{4,29},{5,28},{6,31},{7,30},{8,17},{9,... | collective-permute-start | bytes 110600 | tf_op jit(solution)/shard_map/ppermute | solution.py:540
  20.6 0.8 %collective-permute-done.refs_1_ = bf16[144,128]{1,0:T(8,128)(2,1)S(1)} collective-permute-done((bf16[144,128]{1,0:T(8,128)(2,1)S(1)}, bf16[144,128]{1,0:T(8,128)(2,1)S(1)}, u32[]{:S(2)}, u32[]{:S(2)}) %collective-permute-start) | collective-permute-done | bytes 36896 | tf_op jit(solution)/shard_map/ppermute | solution.py:540
  21.4 0.3 collective-permute-done.1.refs_2_
  21.7 1.8 %collective-permute-done.2.refs_3_ = bf16[144,128]{1,0:T(8,128)(2,1)S(1)} collective-permute-done((bf16[144,128]{1,0:T(8,128)(2,1)S(1)}, bf16[144,128]{1,0:T(8,128)(2,1)S(1)}, u32[]{:S(2)}, u32[]{:S(2)}) %collective-permute-start.2) | collective-permute-done | bytes 36896 | tf_op jit(solution)/shard_map/ppermute | solution.py:540
  23.6 0.2 shard_map.139
  23.8 1.3 %collective-permute-start.3 = (bf16[456,128]{1,0:T(8,128)(2,1)S(1)}, bf16[456,128]{1,0:T(8,128)(2,1)S(1)}, u32[]{:S(2)}, u32[]{:S(2)}) collective-permute-start(bf16[456,128]{1,0:T(8,128)(2,1)S(1)} %get-tuple-element.36), channel_id=1, source_target_pairs={{0,1},{1,0},{2,3},{3,2},{4,5},{5,4},{6,7},{7,6},{8,9},{9,8},{10,11... | collective-permute-start | bytes 350216 | tf_op jit(solution)/shard_map/ppermute | solution.py:547
  25.1 1.0 %collective-permute-done.3.got = bf16[456,128]{1,0:T(8,128)(2,1)S(1)} collective-permute-done((bf16[456,128]{1,0:T(8,128)(2,1)S(1)}, bf16[456,128]{1,0:T(8,128)(2,1)S(1)}, u32[]{:S(2)}, u32[]{:S(2)}) %collective-permute-start.3) | collective-permute-done | bytes 116768 | tf_op jit(solution)/shard_map/ppermute | solution.py:547
  26.1 0.1 shard_map.140
  26.2 0.5 collective-permute-start.4
  26.6 1.7 %collective-permute-start.5 = (bf16[368,128]{1,0:T(8,128)(2,1)S(1)}, bf16[368,128]{1,0:T(8,128)(2,1)S(1)}, u32[]{:S(2)}, u32[]{:S(2)}) collective-permute-start(bf16[368,128]{1,0:T(8,128)(2,1)S(1)} %get-tuple-element.39), channel_id=1, source_target_pairs={{0,4},{1,5},{2,6},{3,7},{4,0},{5,1},{6,2},{7,3},{8,12},{9,13},{10,... | collective-permute-start | bytes 282632 | tf_op jit(solution)/shard_map/ppermute | solution.py:554
  28.3 2.3 %collective-permute-start.6 = (bf16[368,128]{1,0:T(8,128)(2,1)S(1)}, bf16[368,128]{1,0:T(8,128)(2,1)S(1)}, u32[]{:S(2)}, u32[]{:S(2)}) collective-permute-start(bf16[368,128]{1,0:T(8,128)(2,1)S(1)} %get-tuple-element.40), channel_id=1, source_target_pairs={{0,6},{1,7},{2,4},{3,5},{4,2},{5,3},{6,0},{7,1},{8,14},{9,15},{10,... | collective-permute-start | bytes 282632 | tf_op jit(solution)/shard_map/ppermute | solution.py:554
  30.7 1.7 %collective-permute-done.4.low = bf16[368,128]{1,0:T(8,128)(2,1)S(1)} collective-permute-done((bf16[368,128]{1,0:T(8,128)(2,1)S(1)}, bf16[368,128]{1,0:T(8,128)(2,1)S(1)}, u32[]{:S(2)}, u32[]{:S(2)}) %collective-permute-start.4) | collective-permute-done | bytes 94240 | tf_op jit(solution)/shard_map/ppermute | solution.py:554
  32.4 4.8 %collective-permute-done.5.high = bf16[368,128]{1,0:T(8,128)(2,1)S(1)} collective-permute-done((bf16[368,128]{1,0:T(8,128)(2,1)S(1)}, bf16[368,128]{1,0:T(8,128)(2,1)S(1)}, u32[]{:S(2)}, u32[]{:S(2)}) %collective-permute-start.5) | collective-permute-done | bytes 94240 | tf_op jit(solution)/shard_map/ppermute | solution.py:554
  37.2 0.0 collective-permute-done.6.both
  37.2 0.6 %collective-permute-start.9 = (bf16[264,128]{1,0:T(8,128)(2,1)S(1)}, bf16[264,128]{1,0:T(8,128)(2,1)S(1)}, u32[]{:S(2)}, u32[]{:S(2)}) collective-permute-start(bf16[264,128]{1,0:T(8,128)(2,1)S(1)} %get-tuple-element.41), channel_id=1, source_target_pairs={{0,24},{1,25},{2,26},{3,27},{4,28},{5,29},{6,30},{7,31},{8,16},{9,... | collective-permute-start | bytes 202760 | tf_op jit(solution)/shard_map/ppermute | solution.py:559
  37.8 1.5 %collective-permute-start.8 = (bf16[264,128]{1,0:T(8,128)(2,1)S(1)}, bf16[264,128]{1,0:T(8,128)(2,1)S(1)}, u32[]{:S(2)}, u32[]{:S(2)}) collective-permute-start(bf16[264,128]{1,0:T(8,128)(2,1)S(1)} %get-tuple-element.41), channel_id=1, source_target_pairs={{0,16},{1,17},{2,18},{3,19},{4,20},{5,21},{6,22},{7,23},{8,24},{9,... | collective-permute-start | bytes 202760 | tf_op jit(solution)/shard_map/ppermute | solution.py:559
  39.4 1.4 %collective-permute-start.7 = (bf16[264,128]{1,0:T(8,128)(2,1)S(1)}, bf16[264,128]{1,0:T(8,128)(2,1)S(1)}, u32[]{:S(2)}, u32[]{:S(2)}) collective-permute-start(bf16[264,128]{1,0:T(8,128)(2,1)S(1)} %get-tuple-element.41), channel_id=1, source_target_pairs={{0,8},{1,9},{2,10},{3,11},{4,12},{5,13},{6,14},{7,15},{8,0},{9,1},... | collective-permute-start | bytes 202760 | tf_op jit(solution)/shard_map/ppermute | solution.py:559
  40.8 1.8 %collective-permute-done.9 = bf16[264,128]{1,0:T(8,128)(2,1)S(1)} collective-permute-done((bf16[264,128]{1,0:T(8,128)(2,1)S(1)}, bf16[264,128]{1,0:T(8,128)(2,1)S(1)}, u32[]{:S(2)}, u32[]{:S(2)}) %collective-permute-start.9) | collective-permute-done | bytes 67616 | tf_op jit(solution)/shard_map/ppermute | solution.py:559
  42.6 0.3 collective-permute-done.8
  42.8 0.8 %collective-permute-done.7 = bf16[264,128]{1,0:T(8,128)(2,1)S(1)} collective-permute-done((bf16[264,128]{1,0:T(8,128)(2,1)S(1)}, bf16[264,128]{1,0:T(8,128)(2,1)S(1)}, u32[]{:S(2)}, u32[]{:S(2)}) %collective-permute-start.7) | collective-permute-done | bytes 67616 | tf_op jit(solution)/shard_map/ppermute | solution.py:559
  43.7 0.1 collective-permute-start.10
  43.8 1.2 %shard_map.142 = (bf16[8,4,1024]{2,1,0:T(4,128)(2,1)}, bf16[8,4,1024]{2,1,0:T(4,128)(2,1)}, f32[2,1024]{1,0:T(2,128)}, f32[3,8]{1,0:T(4,128)}, f32[264,1024]{1,0:T(8,128)}) custom-call(s32[1]{0:T(128)} %bitcast.pos, s32[1]{0:T(128)} %bitcast.1.tile, bf16[4,264,128]{2,1,0:T(8,128)(2,1)S(1)} %pad_maximum_fusion.slabs, ...), custom_call_target="tpu_custom_call" | custom-call | tf_op jit(solution)/shard_map/pallas_call | solution.py:571
  44.9 0.3 collective-permute-done.10.slabs
  45.3 0.8 %shard_map.143 = f32[264,1024]{1,0:T(8,128)} custom-call(s32[1]{0:T(128)} %bitcast.pos, s32[1]{0:T(128)} %bitcast.1.tile, bf16[4,264,128]{2,1,0:T(8,128)(2,1)S(1)} %collective-permute-done.10.slabs, f32[264,1024]{1,0:T(8,128)} %get-tuple-element.46.weight_in), custom_call_target="tpu_custom_call", output_to_operand_aliasing={{}: (3, {})} | custom-call | tf_op jit(solution)/shard_map/pallas_call | solution.py:581
  (2 shorter events, 0.1 us)
Async XLA Ops:
  0.6 15.8 %copy-start = (bf16[1024,264]{0,1:T(8,128)(2,1)S(1)}, bf16[1024,264]{0,1:T(8,128)(2,1)}, u32[]{:S(2)}) copy-start(bf16[1024,264]{0,1:T(8,128)(2,1)} %param.16) | copy-start | bytes 1622020
  17.6 3.8 %collective-permute-start = (bf16[144,128]{1,0:T(8,128)(2,1)S(1)}, bf16[144,128]{1,0:T(8,128)(2,1)S(1)}, u32[]{:S(2)}, u32[]{:S(2)}) collective-permute-start(bf16[144,128]{1,0:T(8,128)(2,1)S(1)} %get-tuple-element.28), channel_id=1, source_target_pairs={{0,9},{1,8},{2,11},{3,10},{4,13},{5,12},{6,15},{7,14},{8,1},{9,0},... | collective-permute-start | bytes 110600 | tf_op jit(solution)/shard_map/ppermute | solution.py:540
  17.7 4.0 %collective-permute-start.1 = (bf16[144,128]{1,0:T(8,128)(2,1)S(1)}, bf16[144,128]{1,0:T(8,128)(2,1)S(1)}, u32[]{:S(2)}, u32[]{:S(2)}) collective-permute-start(bf16[144,128]{1,0:T(8,128)(2,1)S(1)} %get-tuple-element.29), channel_id=1, source_target_pairs={{0,16},{1,17},{2,18},{3,19},{4,20},{5,21},{6,22},{7,23},{8,24},{9,... | collective-permute-start | bytes 110600 | tf_op jit(solution)/shard_map/ppermute | solution.py:540
  19.3 4.3 %collective-permute-start.2 = (bf16[144,128]{1,0:T(8,128)(2,1)S(1)}, bf16[144,128]{1,0:T(8,128)(2,1)S(1)}, u32[]{:S(2)}, u32[]{:S(2)}) collective-permute-start(bf16[144,128]{1,0:T(8,128)(2,1)S(1)} %get-tuple-element.30), channel_id=1, source_target_pairs={{0,25},{1,24},{2,27},{3,26},{4,29},{5,28},{6,31},{7,30},{8,17},{9,... | collective-permute-start | bytes 110600 | tf_op jit(solution)/shard_map/ppermute | solution.py:540
  23.8 2.3 %collective-permute-start.3 = (bf16[456,128]{1,0:T(8,128)(2,1)S(1)}, bf16[456,128]{1,0:T(8,128)(2,1)S(1)}, u32[]{:S(2)}, u32[]{:S(2)}) collective-permute-start(bf16[456,128]{1,0:T(8,128)(2,1)S(1)} %get-tuple-element.36), channel_id=1, source_target_pairs={{0,1},{1,0},{2,3},{3,2},{4,5},{5,4},{6,7},{7,6},{8,9},{9,8},{10,11... | collective-permute-start | bytes 350216 | tf_op jit(solution)/shard_map/ppermute | solution.py:547
  26.2 6.2 %collective-permute-start.4 = (bf16[368,128]{1,0:T(8,128)(2,1)S(1)}, bf16[368,128]{1,0:T(8,128)(2,1)S(1)}, u32[]{:S(2)}, u32[]{:S(2)}) collective-permute-start(bf16[368,128]{1,0:T(8,128)(2,1)S(1)} %get-tuple-element.38), channel_id=1, source_target_pairs={{0,2},{1,3},{2,0},{3,1},{4,6},{5,7},{6,4},{7,5},{8,10},{9,11},{10,... | collective-permute-start | bytes 282632 | tf_op jit(solution)/shard_map/ppermute | solution.py:554
  26.6 10.5 %collective-permute-start.5 = (bf16[368,128]{1,0:T(8,128)(2,1)S(1)}, bf16[368,128]{1,0:T(8,128)(2,1)S(1)}, u32[]{:S(2)}, u32[]{:S(2)}) collective-permute-start(bf16[368,128]{1,0:T(8,128)(2,1)S(1)} %get-tuple-element.39), channel_id=1, source_target_pairs={{0,4},{1,5},{2,6},{3,7},{4,0},{5,1},{6,2},{7,3},{8,12},{9,13},{10,... | collective-permute-start | bytes 282632 | tf_op jit(solution)/shard_map/ppermute | solution.py:554
  28.3 8.9 %collective-permute-start.6 = (bf16[368,128]{1,0:T(8,128)(2,1)S(1)}, bf16[368,128]{1,0:T(8,128)(2,1)S(1)}, u32[]{:S(2)}, u32[]{:S(2)}) collective-permute-start(bf16[368,128]{1,0:T(8,128)(2,1)S(1)} %get-tuple-element.40), channel_id=1, source_target_pairs={{0,6},{1,7},{2,4},{3,5},{4,2},{5,3},{6,0},{7,1},{8,14},{9,15},{10,... | collective-permute-start | bytes 282632 | tf_op jit(solution)/shard_map/ppermute | solution.py:554
  37.2 5.4 %collective-permute-start.9 = (bf16[264,128]{1,0:T(8,128)(2,1)S(1)}, bf16[264,128]{1,0:T(8,128)(2,1)S(1)}, u32[]{:S(2)}, u32[]{:S(2)}) collective-permute-start(bf16[264,128]{1,0:T(8,128)(2,1)S(1)} %get-tuple-element.41), channel_id=1, source_target_pairs={{0,24},{1,25},{2,26},{3,27},{4,28},{5,29},{6,30},{7,31},{8,16},{9,... | collective-permute-start | bytes 202760 | tf_op jit(solution)/shard_map/ppermute | solution.py:559
  37.8 5.0 %collective-permute-start.8 = (bf16[264,128]{1,0:T(8,128)(2,1)S(1)}, bf16[264,128]{1,0:T(8,128)(2,1)S(1)}, u32[]{:S(2)}, u32[]{:S(2)}) collective-permute-start(bf16[264,128]{1,0:T(8,128)(2,1)S(1)} %get-tuple-element.41), channel_id=1, source_target_pairs={{0,16},{1,17},{2,18},{3,19},{4,20},{5,21},{6,22},{7,23},{8,24},{9,... | collective-permute-start | bytes 202760 | tf_op jit(solution)/shard_map/ppermute | solution.py:559
  39.4 4.3 %collective-permute-start.7 = (bf16[264,128]{1,0:T(8,128)(2,1)S(1)}, bf16[264,128]{1,0:T(8,128)(2,1)S(1)}, u32[]{:S(2)}, u32[]{:S(2)}) collective-permute-start(bf16[264,128]{1,0:T(8,128)(2,1)S(1)} %get-tuple-element.41), channel_id=1, source_target_pairs={{0,8},{1,9},{2,10},{3,11},{4,12},{5,13},{6,14},{7,15},{8,0},{9,1},... | collective-permute-start | bytes 202760 | tf_op jit(solution)/shard_map/ppermute | solution.py:559
  43.7 1.6 %collective-permute-start.10 = (bf16[4,264,128]{2,1,0:T(8,128)(2,1)S(1)}, bf16[4,264,128]{2,1,0:T(8,128)(2,1)S(1)}, u32[]{:S(2)}, u32[]{:S(2)}) collective-permute-start(bf16[4,264,128]{2,1,0:T(8,128)(2,1)S(1)} %pad_maximum_fusion.slabs), channel_id=1, source_target_pairs={{0,1},{1,0},{2,3},{3,2},{4,5},{5,4},{6,7},{7,6},{8,9},{9,8},{10,11... | collective-permute-start | bytes 811016 | tf_op jit(solution)/shard_map/ppermute | solution.py:561

commit v11 on v10

--- a/solution.py
+++ b/solution.py
@@ -51,7 +51,7 @@
     return jnp.concatenate(kept, axis=0), jnp.concatenate(given, axis=0)
 
 
-def series_terms(heads, model_d, recv, w_t):
+def series_terms(heads, model_d, recv, w_t, order=0):
     length = recv.shape[0]
     width_p = model_d // heads
     states = (w_t.shape[0] - heads) // 2
@@ -73,10 +73,10 @@
 
     row = lax.broadcasted_iota(jnp.int32, (length, length), 0)
     col = lax.broadcasted_iota(jnp.int32, (length, length), 1)
-    upper = col >= row
+    upper = (col ^ order) >= (row ^ order)
     upper_f = upper.astype(F32)
     eye = (col == row).astype(F32)
-    lower_b = (row >= col).astype(BF16)
+    lower_b = ((row ^ order) >= (col ^ order)).astype(BF16)
     head_row = lax.broadcasted_iota(jnp.int32, (heads, heads), 0)
     head_col = lax.broadcasted_iota(jnp.int32, (heads, heads), 1)
     eye_h = (head_row == head_col).astype(F32)
@@ -149,11 +149,13 @@
     sel[...] = sensor_rows(ids_row)
 
 
-def direct_series_kernel(heads, model_d, dates, pos, tile, recv, w_t, *refs):
-    sends, (own, give, sel) = refs[:-3], refs[-3:]
+def direct_series_kernel(heads, model_d, dates, pos, tile, *refs):
+    levels, w_t, sends, (own, give, sel, recv) = refs[:4], refs[4], refs[5:-4], refs[-4:]
     length = recv.shape[0]
     slab = 2 * LANES
-    mixes, grad_keys, grad_reads, raw, terms, ids_row, eye_h = series_terms(heads, model_d, recv, w_t)
+    recv[...] = jnp.concatenate([level[...].astype(F32) for level in levels], axis=0).astype(BF16)
+    order = lax.div(pos[0], 2) * (2 * dates)
+    mixes, grad_keys, grad_reads, raw, terms, ids_row, eye_h = series_terms(heads, model_d, recv, w_t, order)
     raw_t = nt(eye_h.astype(BF16), raw.astype(BF16))
     total = jnp.sum(terms, axis=0, keepdims=True)
     high = total.astype(BF16).astype(F32)
@@ -171,6 +173,26 @@
     own[...] = kept.astype(BF16)
     give[...] = given.astype(BF16)
     sel[...] = sensor_rows(ids_row)
+
+
+def shared_rows(dates, ids, table, params):
+    rows = [jnp.where(ids[i] == 1, table[1:2, :], table[0:1, :]) for i in range(dates)]
+    embed = jnp.concatenate(rows, axis=0)
+    row = lax.broadcasted_iota(jnp.int32, (dates, LANES), 0)
+    lane = lax.broadcasted_iota(jnp.int32, (dates, LANES), 1)
+    second = jnp.zeros((dates, LANES), F32)
+    for i in range(dates):
+        second = jnp.where((row == i) & (lane == 1), (ids[i] == 1).astype(F32), second)
+    at = 2
+    for k in range(3):
+        rest = params[k : k + 1, :]
+        for _ in range(3):
+            term = rest.astype(BF16).astype(F32)
+            rest = rest - term
+            term = jnp.concatenate([jnp.zeros((1, at), F32), term, jnp.zeros((1, LANES - at - term.shape[1]), F32)], axis=1)
+            second = second + term
+            at = at + params.shape[1]
+    return embed, second
 
 
 def pack_kernel(pos, tile, ids_in, mask_in, table_in, bias_in, decay_in, skip_in, layer, values, cotangent, out, ids, mask_t, table, params, layer_v, sems):
@@ -192,28 +214,63 @@
         copy.start()
     for copy in small:
         copy.wait()
-    rows = [jnp.where(ids[i] == 1, table[1:2, :], table[0:1, :]) for i in range(dates)]
-    embed = jnp.concatenate(rows, axis=0)
-    row = lax.broadcasted_iota(jnp.int32, (dates, LANES), 0)
+    embed, second = shared_rows(dates, ids, table, params)
     lane = lax.broadcasted_iota(jnp.int32, (dates, LANES), 1)
-    second = jnp.zeros((dates, LANES), F32)
-    for i in range(dates):
-        second = jnp.where((row == i) & (lane == 1), (ids[i] == 1).astype(F32), second)
     gate = mask_t[...].astype(F32)
-    at = 2
-    for k in range(3):
-        rest = params[k : k + 1, :]
-        for _ in range(3):
-            term = rest.astype(BF16).astype(F32)
-            rest = rest - term
-            term = jnp.concatenate([jnp.zeros((1, at), F32), term, jnp.zeros((1, LANES - at - term.shape[1]), F32)], axis=1)
-            second = second + term
-            at = at + params.shape[1]
     for p in range(pixels):
         out[p, :, 3 * model_d :] = jnp.where(lane == 0, gate[:, p : p + 1], second).astype(BF16)
         out[p, :, :model_d] = (layer_v[p].astype(F32) + embed).astype(BF16)
     for copy in large:
         copy.wait()
+
+
+def direct_pack_kernel(
+    pos, w_in, ids_in, mask_in, table_in, bias_in, decay_in, skip_in, layer, values, cotangent, keep, give, w_t, *scratch
+):
+    ids, mask_t, table, params, layer_v, sems = scratch
+    levels, _, dates, model_d = layer.shape
+    core = bit_of(pos, 0)
+    small = [
+        pltpu.make_async_copy(ids_in, ids, sems.at[0]),
+        pltpu.make_async_copy(mask_in, mask_t, sems.at[1]),
+        pltpu.make_async_copy(table_in, table, sems.at[2]),
+        pltpu.make_async_copy(bias_in, params.at[0:1], sems.at[3]),
+        pltpu.make_async_copy(decay_in, params.at[1:2], sems.at[4]),
+        pltpu.make_async_copy(skip_in, params.at[2:3], sems.at[5]),
+        pltpu.make_async_copy(layer, layer_v, sems.at[6]),
+    ]
+    large = [pltpu.make_async_copy(w_in, w_t, sems.at[11])]
+    for k, array in enumerate((values, cotangent)):
+        to = slice((k + 1) * model_d, (k + 2) * model_d)
+        large.append(pltpu.make_async_copy(array.at[:, core], keep.at[:, :, to], sems.at[7 + k]))
+        large.append(pltpu.make_async_copy(array.at[:, 1 - core], give.at[:, :, to], sems.at[9 + k]))
+    for copy in small[-1:] + large[1:] + small[:-1] + large[:1]:
+        copy.start()
+    for copy in small:
+        copy.wait()
+    embed, extra = shared_rows(dates, ids, table, params)
+    lane = lax.broadcasted_iota(jnp.int32, (dates, LANES), 1)
+    gate = mask_t[...].astype(F32)
+    first = core == 0
+    for level in range(levels):
+        gates = [gate[:, 2 * level + c : 2 * level + c + 1] for c in range(2)]
+        mixed = [layer_v[level, c].astype(F32) + embed for c in range(2)]
+        for out, mine in ((keep, first), (give, jnp.logical_not(first))):
+            chosen = jnp.where(mine, gates[0], gates[1])
+            out[level, :, 3 * model_d :] = jnp.where(lane == 0, chosen, extra).astype(BF16)
+            out[level, :, :model_d] = jnp.where(mine, mixed[0], mixed[1]).astype(BF16)
+    for copy in large:
+        copy.wait()
+
+
+def level_rows_kernel(pos, keep, got, *outs):
+    first = bit_of(pos, 0) == 0
+    level = lax.div(pos[0], 2)
+    for k, out in enumerate(outs):
+        mine, theirs = keep[level ^ k].astype(F32), got[level ^ k].astype(F32)
+        out[...] = jnp.concatenate(
+            [jnp.where(first, mine, theirs), jnp.where(first, theirs, mine)], axis=0
+        ).astype(BF16)
 
 
 def lane_pad(x, width):
@@ -371,12 +428,13 @@
 HBM = pl.BlockSpec(memory_space=pltpu.HBM)
 
 
-def call(kernel, outs, ins, smem=0):
+def call(kernel, outs, ins, smem=0, scratch=()):
     return pl.pallas_call(
         kernel,
         out_shape=[jax.ShapeDtypeStruct(s, d) for s, d in outs],
         in_specs=[SMEM] * smem + [VMEM] * (len(ins) - smem),
         out_specs=[VMEM] * len(outs),
+        scratch_shapes=list(scratch),
         compiler_params=pltpu.CompilerParams(vmem_limit_bytes=48 * 1024 * 1024),
     )(*ins)
 
@@ -446,15 +504,15 @@
     ).astype(BF16)
 
 
-def direct_join_kernel(dates, pos, keep, keep_sums, rows_own, got, rows_keep, own, low, high, both):
+def direct_join_kernel(dates, keep, keep_sums, rows_own, got, rows_keep, own, low, high, both):
     cols = keep.shape[0]
     there = got[...].astype(F32)
     total = keep[...] + there[:cols]
     sums = keep_sums[...] + unpack_sums(there[cols : cols + 16])
     rows = [rows_own[...].astype(F32), block_rows(there[cols + 16 :], rows_own.shape[0])]
-    same_low, other_low = halves(rows, dates, bit_of(pos, 1) == 0)
-    here, high_rows = halves([same_low], dates, bit_of(pos, 2) == 0)
-    low_rows, both_rows = halves([other_low], dates, bit_of(pos, 2) == 0)
+    here, low_rows, high_rows, both_rows = (
+        jnp.concatenate([part[k * dates : (k + 1) * dates] for part in rows], axis=0) for k in range(4)
+    )
     rows_keep[...] = here.astype(BF16)
     common = jnp.concatenate([total, pack_sums(sums)], axis=0).astype(BF16)
     own[...] = common
@@ -518,8 +576,36 @@
         copy.wait()
 
 
-def finish_direct(series, w_t, date_s, tile_s, heads, scale, pixel_dev, dates_dev, tiles, dates):
-    length = series.shape[0]
+def direct_series(operands, w_t, date_s, dates_dev, model_d, axes, across):
+    *small, layer, values, cotangent = operands
+    arrays = [a.reshape(4, 2, dates_dev, model_d) for a in (layer, values, cotangent)]
+    packed = jax.ShapeDtypeStruct((4, dates_dev, 3 * model_d + LANES), BF16)
+    heads = small[-1].shape[1]
+    keep, give, w_t = pl.pallas_call(
+        direct_pack_kernel,
+        out_shape=[packed, packed, jax.ShapeDtypeStruct(w_t.shape, w_t.dtype)],
+        in_specs=[SMEM] + [HBM] * 10,
+        out_specs=[VMEM] * 3,
+        scratch_shapes=[
+            pltpu.SMEM((dates_dev,), jnp.int32),
+            pltpu.VMEM((dates_dev, 8), jnp.int32),
+            pltpu.VMEM((2, model_d), F32),
+            pltpu.VMEM((3, heads), F32),
+            pltpu.VMEM((4, 2, dates_dev, model_d), BF16),
+            pltpu.SemaphoreType.DMA((12,)),
+        ],
+        compiler_params=pltpu.CompilerParams(vmem_limit_bytes=16 * 1024 * 1024),
+    )(date_s, *[pltpu.with_memory_space_constraint(operand, pltpu.HBM) for operand in [w_t] + small + arrays])
+    got = lax.ppermute(give, axes, across(1))
+    levels = call(
+        level_rows_kernel, [((2 * dates_dev, 3 * model_d + LANES), BF16)] * 4, [date_s, keep, got], 1
+    )
+    arrived = {k: lax.ppermute(levels[k], axes, across(2 * k)) for k in (3, 2, 1)}
+    return [levels[0]] + [arrived[k] for k in (1, 2, 3)], w_t
+
+
+def finish_direct(operands, w_t, date_s, tile_s, heads, scale, pixel_dev, dates_dev, tiles, dates):
+    length = dates * dates_dev
     cols, model_d = w_t.shape
     wide = model_d + EXT
     half_rows = length // 2
@@ -530,12 +616,14 @@
     def across(mask):
         return [(i, i ^ mask) for i in range(tiles * dates)]
 
+    series, w_t = direct_series(operands, w_t, date_s, dates_dev, model_d, axes, across)
     *sends, rows_own, rows_give, sel = call(
         functools.partial(direct_series_kernel, heads, model_d, dates_dev),
         [((4 * length + 16, LANES), BF16)] * tiles
         + [((half_rows, wide), BF16), ((half_rows, wide), BF16), ((16, length), BF16)],
-        [date_s, tile_s, series, w_t],
+        [date_s, tile_s, *series, w_t],
         2,
+        [pltpu.VMEM((length, 3 * model_d + LANES), BF16)],
     )
     parts = {k: lax.ppermute(sends[k], axes, across(dates * k + k % 2)) for k in (3, 2, 1)}
     keep, keep_sums, give = call(
@@ -548,8 +636,7 @@
     rows_own, own, *levels = call(
         functools.partial(direct_join_kernel, dates_dev),
         [((2 * dates_dev, wide), BF16), ((cols + 16, LANES), BF16)] + [((payload_z, LANES), BF16)] * 3,
-        [date_s, keep, keep_sums, rows_own, got],
-        1,
+        [keep, keep_sums, rows_own, got],
     )
     arrived = {k: lax.ppermute(levels[k - 1], axes, across(2 * k)) for k in (3, 2, 1)}
     low, high, both = (arrived[k] for k in (1, 2, 3))
@@ -726,6 +813,8 @@
         head_input,
         out_grad,
     ]
+    if levels == 4 and tiles == 4 and model_d == 2 * LANES * tiles:
+        return finish_direct(operands, w_t, date_s, tile_s, heads, scale, pixel_dev, dates_dev, tiles, dates)
     packed = pl.pallas_call(
         pack_kernel,
         out_shape=jax.ShapeDtypeStruct((pixel_dev, dates_dev, 3 * model_d + LANES), BF16),
@@ -745,11 +834,7 @@
         length, 3 * model_d + LANES
     )
 
-    if levels == 4 and tiles == 4 and model_d == 2 * LANES * tiles:
-        finish = finish_direct
-    else:
-        finish = finish_any
-    return finish(series, w_t, date_s, tile_s, heads, scale, pixel_dev, dates_dev, tiles, dates)
+    return finish_any(series, w_t, date_s, tile_s, heads, scale, pixel_dev, dates_dev, tiles, dates)
 
 
 def solution(mesh):

time: 46.3 us -> 43.7 us (0.944)
  blocking collectives: 14.6 us -> 0 us
  starting transfers between devices: 12.4 us -> 18.5 us
  waiting for transfers between devices: 13.7 us -> 19.4 us
    all_to_all x1 -> x0, blocking collectives: 14.6 us -> none  [on_device(): lax.all_to_all(packed, 'date', split_axis=0, concat_axis=0, tiled=True)]
    ppermute x0 -> x4, waiting for transfers between devices: none -> 6.86 us  [the longest x3 5.91 us: direct_series(): lax.ppermute(levels[k], axes, across(2 * k))]
    ppermute x0 -> x4, starting transfers between devices: none -> 6.1 us  [the longest x3 5.59 us: direct_series(): lax.ppermute(levels[k], axes, across(2 * k))]
    ppermute x3, waiting for transfers between devices: 6.53 us -> 5.52 us  [finish_direct(): lax.ppermute(levels[k - 1], axes, across(2 * k))]
    pallas_call x4 -> x5, Pallas kernels: 1.53 us -> 1.56 us  [call(): pl.pallas_call(kernel, out_shape=[jax.ShapeDtypeStruct(s, d) for s, d in...]
  transfers between devices with their start and end apart: 11 -> 15, of which waited for: 10 -> 13; matrix products, arithmetic and copies ran while one was open for 0% -> 0% of each run, Pallas kernels for 3% -> 3%
where the time goes in v11:
time: 43.7 us; the launch traced here: 43.5 us
  waiting for transfers between devices  19.4 us (44%)
  starting transfers between devices  18.5 us (42%)
  Pallas kernels  4.91 us (11%)
  between operations  0.71 us (2%)
    ppermute x3, waiting for transfers between devices, direct_series(): lax.ppermute(levels[k], axes, across(2 * k))  5.91 us
    ppermute x3, starting transfers between devices, direct_series(): lax.ppermute(levels[k], axes, across(2 * k))  5.59 us
    ppermute x3, waiting for transfers between devices, finish_direct(): lax.ppermute(levels[k - 1], axes, across(2 * k))  5.52 us
    ppermute x3, starting transfers between devices, finish_direct(): lax.ppermute(levels[k - 1], axes, across(2 * k))  4.47 us
    ppermute x3, starting transfers between devices, finish_direct(): lax.ppermute(slab, axes, across(dates * k))  3.55 us
    ppermute x3, starting transfers between devices, finish_direct(): lax.ppermute(sends[k], axes, across(dates * k + k % 2))  2.99 us
    ppermute x3, waiting for transfers between devices, finish_direct(): lax.ppermute(sends[k], axes, across(dates * k + k % 2))  2.95 us
    ppermute x3, waiting for transfers between devices, finish_direct(): lax.ppermute(slab, axes, across(dates * k))  2.74 us
  transfers between devices with their start and end apart: 15, of which 13 were waited for; matrix products, arithmetic and copies ran while one was open for 0% of the time, Pallas kernels for 3%

profile of v11, /device:TPU:0, one launch (start us, length us, event | category | flops | bytes accessed | tf_op | source)
XLA Modules:
  0.0 43.5 jit_solution(10662534061909057042)
XLA Ops:
  0.6 1.3 %shard_map.137 = (bf16[4,4,3200]{2,1,0:T(4,128)(2,1)S(1)}, bf16[4,4,3200]{2,1,0:T(4,128)(2,1)S(1)}, bf16[264,1024]{1,0:T(8,128)(2,1)S(1)}) custom-call(s32[1]{0:T(128)} %bitcast.pos, bf16[264,1024]{1,0:T(8,128)(2,1)} %bitcast.17, s32[4]{0:T(128)} %ids_in.1, s32[4,8]{1,0:T(4,128)} %bitcast.24, f32[2,1024]{1,0:T(2,128)} %table_in.1, f32[1,8]{1,0:T(1,128)} %bitcast.25, ...), custom_call_target="tpu_custom_call" | custom-call | tf_op jit(solution)/shard_map/pallas_call | solution.py:584
  2.0 0.5 %collective-permute-start = (bf16[4,4,3200]{2,1,0:T(4,128)(2,1)S(1)}, bf16[4,4,3200]{2,1,0:T(4,128)(2,1)S(1)}, u32[]{:S(2)}, u32[]{:S(2)}) collective-permute-start(bf16[4,4,3200]{2,1,0:T(4,128)(2,1)S(1)} %get-tuple-element.35), channel_id=1, source_target_pairs={{0,1},{1,0},{2,3},{3,2},{4,5},{5,4},{6,7},{7,6},{8,9},{9,8},{10,11... | collective-permute-start | bytes 307208 | tf_op jit(solution)/shard_map/ppermute | solution.py:599
  2.5 0.9 %collective-permute-done.got = bf16[4,4,3200]{2,1,0:T(4,128)(2,1)S(1)} collective-permute-done((bf16[4,4,3200]{2,1,0:T(4,128)(2,1)S(1)}, bf16[4,4,3200]{2,1,0:T(4,128)(2,1)S(1)}, u32[]{:S(2)}, u32[]{:S(2)}) %collective-permute-start) | collective-permute-done | bytes 102432 | tf_op jit(solution)/shard_map/ppermute | solution.py:599
  3.5 0.1 shard_map.138
  3.5 3.0 %collective-permute-start.1 = (bf16[8,3200]{1,0:T(8,128)(2,1)S(1)}, bf16[8,3200]{1,0:T(8,128)(2,1)S(1)}, u32[]{:S(2)}, u32[]{:S(2)}) collective-permute-start(bf16[8,3200]{1,0:T(8,128)(2,1)S(1)} %get-tuple-element.37), channel_id=1, source_target_pairs={{0,2},{1,3},{2,0},{3,1},{4,6},{5,7},{6,4},{7,5},{8,10},{9,11},{10,... | collective-permute-start | bytes 153608 | tf_op jit(solution)/shard_map/ppermute | solution.py:603
  6.5 2.6 %collective-permute-start.2 = (bf16[8,3200]{1,0:T(8,128)(2,1)S(1)}, bf16[8,3200]{1,0:T(8,128)(2,1)S(1)}, u32[]{:S(2)}, u32[]{:S(2)}) collective-permute-start(bf16[8,3200]{1,0:T(8,128)(2,1)S(1)} %get-tuple-element.38), channel_id=1, source_target_pairs={{0,4},{1,5},{2,6},{3,7},{4,0},{5,1},{6,2},{7,3},{8,12},{9,13},{10,... | collective-permute-start | bytes 153608 | tf_op jit(solution)/shard_map/ppermute | solution.py:603
  9.1 0.0 collective-permute-start.3
  9.1 0.0 collective-permute-done.1.refs_1_
  9.1 3.4 %collective-permute-done.2.refs_2_ = bf16[8,3200]{1,0:T(8,128)(2,1)S(1)} collective-permute-done((bf16[8,3200]{1,0:T(8,128)(2,1)S(1)}, bf16[8,3200]{1,0:T(8,128)(2,1)S(1)}, u32[]{:S(2)}, u32[]{:S(2)}) %collective-permute-start.2) | collective-permute-done | bytes 51232 | tf_op jit(solution)/shard_map/ppermute | solution.py:603
  12.6 2.5 %collective-permute-done.3.refs_3_ = bf16[8,3200]{1,0:T(8,128)(2,1)S(1)} collective-permute-done((bf16[8,3200]{1,0:T(8,128)(2,1)S(1)}, bf16[8,3200]{1,0:T(8,128)(2,1)S(1)}, u32[]{:S(2)}, u32[]{:S(2)}) %collective-permute-start.3) | collective-permute-done | bytes 51232 | tf_op jit(solution)/shard_map/ppermute | solution.py:603
  15.0 1.2 %shard_map.139 = (bf16[144,128]{1,0:T(8,128)(2,1)S(1)}, bf16[144,128]{1,0:T(8,128)(2,1)S(1)}, bf16[144,128]{1,0:T(8,128)(2,1)S(1)}, bf16[144,128]{1,0:T(8,128)(2...) custom-call(s32[1]{0:T(128)} %bitcast.pos, s32[1]{0:T(128)} %bitcast.1.tile, ...), custom_call_target="tpu_custom_call" | custom-call | tf_op jit(solution)/shard_map/pallas_call | solution.py:432
  16.2 0.1 collective-permute-start.4
  16.3 1.6 %collective-permute-start.5 = (bf16[144,128]{1,0:T(8,128)(2,1)S(1)}, bf16[144,128]{1,0:T(8,128)(2,1)S(1)}, u32[]{:S(2)}, u32[]{:S(2)}) collective-permute-start(bf16[144,128]{1,0:T(8,128)(2,1)S(1)} %get-tuple-element.43), channel_id=1, source_target_pairs={{0,16},{1,17},{2,18},{3,19},{4,20},{5,21},{6,22},{7,23},{8,24},{9,... | collective-permute-start | bytes 110600 | tf_op jit(solution)/shard_map/ppermute | solution.py:628
  17.9 1.3 %collective-permute-start.6 = (bf16[144,128]{1,0:T(8,128)(2,1)S(1)}, bf16[144,128]{1,0:T(8,128)(2,1)S(1)}, u32[]{:S(2)}, u32[]{:S(2)}) collective-permute-start(bf16[144,128]{1,0:T(8,128)(2,1)S(1)} %get-tuple-element.44), channel_id=1, source_target_pairs={{0,25},{1,24},{2,27},{3,26},{4,29},{5,28},{6,31},{7,30},{8,17},{9,... | collective-permute-start | bytes 110600 | tf_op jit(solution)/shard_map/ppermute | solution.py:628
  19.2 0.8 %collective-permute-done.4.refs_1_ = bf16[144,128]{1,0:T(8,128)(2,1)S(1)} collective-permute-done((bf16[144,128]{1,0:T(8,128)(2,1)S(1)}, bf16[144,128]{1,0:T(8,128)(2,1)S(1)}, u32[]{:S(2)}, u32[]{:S(2)}) %collective-permute-start.4) | collective-permute-done | bytes 36896 | tf_op jit(solution)/shard_map/ppermute | solution.py:628
  20.0 0.3 collective-permute-done.5.refs_2_
  20.3 1.8 %collective-permute-done.6.refs_3_ = bf16[144,128]{1,0:T(8,128)(2,1)S(1)} collective-permute-done((bf16[144,128]{1,0:T(8,128)(2,1)S(1)}, bf16[144,128]{1,0:T(8,128)(2,1)S(1)}, u32[]{:S(2)}, u32[]{:S(2)}) %collective-permute-start.6) | collective-permute-done | bytes 36896 | tf_op jit(solution)/shard_map/ppermute | solution.py:628
  22.2 0.2 shard_map.140
  22.4 1.3 %collective-permute-start.7 = (bf16[456,128]{1,0:T(8,128)(2,1)S(1)}, bf16[456,128]{1,0:T(8,128)(2,1)S(1)}, u32[]{:S(2)}, u32[]{:S(2)}) collective-permute-start(bf16[456,128]{1,0:T(8,128)(2,1)S(1)} %get-tuple-element.50), channel_id=1, source_target_pairs={{0,1},{1,0},{2,3},{3,2},{4,5},{5,4},{6,7},{7,6},{8,9},{9,8},{10,11... | collective-permute-start | bytes 350216 | tf_op jit(solution)/shard_map/ppermute | solution.py:635
  23.7 1.0 %collective-permute-done.7.got = bf16[456,128]{1,0:T(8,128)(2,1)S(1)} collective-permute-done((bf16[456,128]{1,0:T(8,128)(2,1)S(1)}, bf16[456,128]{1,0:T(8,128)(2,1)S(1)}, u32[]{:S(2)}, u32[]{:S(2)}) %collective-permute-start.7) | collective-permute-done | bytes 116768 | tf_op jit(solution)/shard_map/ppermute | solution.py:635
  24.7 0.1 shard_map.141
  24.7 1.3 %collective-permute-start.10 = (bf16[368,128]{1,0:T(8,128)(2,1)S(1)}, bf16[368,128]{1,0:T(8,128)(2,1)S(1)}, u32[]{:S(2)}, u32[]{:S(2)}) collective-permute-start(bf16[368,128]{1,0:T(8,128)(2,1)S(1)} %get-tuple-element.54), channel_id=1, source_target_pairs={{0,6},{1,7},{2,4},{3,5},{4,2},{5,3},{6,0},{7,1},{8,14},{9,15},{10,... | collective-permute-start | bytes 282632 | tf_op jit(solution)/shard_map/ppermute | solution.py:641
  26.0 0.2 collective-permute-start.8
  26.2 3.0 %collective-permute-start.9 = (bf16[368,128]{1,0:T(8,128)(2,1)S(1)}, bf16[368,128]{1,0:T(8,128)(2,1)S(1)}, u32[]{:S(2)}, u32[]{:S(2)}) collective-permute-start(bf16[368,128]{1,0:T(8,128)(2,1)S(1)} %get-tuple-element.53), channel_id=1, source_target_pairs={{0,4},{1,5},{2,6},{3,7},{4,0},{5,1},{6,2},{7,3},{8,12},{9,13},{10,... | collective-permute-start | bytes 282632 | tf_op jit(solution)/shard_map/ppermute | solution.py:641
  29.2 3.0 %collective-permute-done.10.both = bf16[368,128]{1,0:T(8,128)(2,1)S(1)} collective-permute-done((bf16[368,128]{1,0:T(8,128)(2,1)S(1)}, bf16[368,128]{1,0:T(8,128)(2,1)S(1)}, u32[]{:S(2)}, u32[]{:S(2)}) %collective-permute-start.10) | collective-permute-done | bytes 94240 | tf_op jit(solution)/shard_map/ppermute | solution.py:641
  32.2 2.5 %collective-permute-done.8.low = bf16[368,128]{1,0:T(8,128)(2,1)S(1)} collective-permute-done((bf16[368,128]{1,0:T(8,128)(2,1)S(1)}, bf16[368,128]{1,0:T(8,128)(2,1)S(1)}, u32[]{:S(2)}, u32[]{:S(2)}) %collective-permute-start.8) | collective-permute-done | bytes 94240 | tf_op jit(solution)/shard_map/ppermute | solution.py:641
  34.7 0.0 collective-permute-done.9.high
  34.7 0.6 %collective-permute-start.11 = (bf16[264,128]{1,0:T(8,128)(2,1)S(1)}, bf16[264,128]{1,0:T(8,128)(2,1)S(1)}, u32[]{:S(2)}, u32[]{:S(2)}) collective-permute-start(bf16[264,128]{1,0:T(8,128)(2,1)S(1)} %get-tuple-element.55), channel_id=1, source_target_pairs={{0,8},{1,9},{2,10},{3,11},{4,12},{5,13},{6,14},{7,15},{8,0},{9,1},... | collective-permute-start | bytes 202760 | tf_op jit(solution)/shard_map/ppermute | solution.py:646
  35.3 0.5 %collective-permute-start.12 = (bf16[264,128]{1,0:T(8,128)(2,1)S(1)}, bf16[264,128]{1,0:T(8,128)(2,1)S(1)}, u32[]{:S(2)}, u32[]{:S(2)}) collective-permute-start(bf16[264,128]{1,0:T(8,128)(2,1)S(1)} %get-tuple-element.55), channel_id=1, source_target_pairs={{0,16},{1,17},{2,18},{3,19},{4,20},{5,21},{6,22},{7,23},{8,24},{9,... | collective-permute-start | bytes 202760 | tf_op jit(solution)/shard_map/ppermute | solution.py:646
  35.8 2.4 %collective-permute-start.13 = (bf16[264,128]{1,0:T(8,128)(2,1)S(1)}, bf16[264,128]{1,0:T(8,128)(2,1)S(1)}, u32[]{:S(2)}, u32[]{:S(2)}) collective-permute-start(bf16[264,128]{1,0:T(8,128)(2,1)S(1)} %get-tuple-element.55), channel_id=1, source_target_pairs={{0,24},{1,25},{2,26},{3,27},{4,28},{5,29},{6,30},{7,31},{8,16},{9,... | collective-permute-start | bytes 202760 | tf_op jit(solution)/shard_map/ppermute | solution.py:646
  38.3 1.5 %collective-permute-done.11 = bf16[264,128]{1,0:T(8,128)(2,1)S(1)} collective-permute-done((bf16[264,128]{1,0:T(8,128)(2,1)S(1)}, bf16[264,128]{1,0:T(8,128)(2,1)S(1)}, u32[]{:S(2)}, u32[]{:S(2)}) %collective-permute-start.11) | collective-permute-done | bytes 67616 | tf_op jit(solution)/shard_map/ppermute | solution.py:646
  39.8 0.2 collective-permute-done.12
  40.1 1.0 %collective-permute-done.13 = bf16[264,128]{1,0:T(8,128)(2,1)S(1)} collective-permute-done((bf16[264,128]{1,0:T(8,128)(2,1)S(1)}, bf16[264,128]{1,0:T(8,128)(2,1)S(1)}, u32[]{:S(2)}, u32[]{:S(2)}) %collective-permute-start.13) | collective-permute-done | bytes 67616 | tf_op jit(solution)/shard_map/ppermute | solution.py:646
  41.1 0.1 collective-permute-start.14
  41.2 1.2 %shard_map.143 = (bf16[8,4,1024]{2,1,0:T(4,128)(2,1)}, bf16[8,4,1024]{2,1,0:T(4,128)(2,1)}, f32[2,1024]{1,0:T(2,128)}, f32[3,8]{1,0:T(4,128)}, f32[264,1024]{1,0:T(8,128)}) custom-call(s32[1]{0:T(128)} %bitcast.pos, s32[1]{0:T(128)} %bitcast.1.tile, bf16[4,264,128]{2,1,0:T(8,128)(2,1)S(1)} %pad_maximum_fusion.slabs, ...), custom_call_target="tpu_custom_call" | custom-call | tf_op jit(solution)/shard_map/pallas_call | solution.py:658
  42.3 0.3 collective-permute-done.14.slabs
  42.7 0.8 %shard_map.144 = f32[264,1024]{1,0:T(8,128)} custom-call(s32[1]{0:T(128)} %bitcast.pos, s32[1]{0:T(128)} %bitcast.1.tile, bf16[4,264,128]{2,1,0:T(8,128)(2,1)S(1)} %collective-permute-done.14.slabs, f32[264,1024]{1,0:T(8,128)} %get-tuple-element.60.weight_in), custom_call_target="tpu_custom_call", output_to_operand_aliasing={{}: (3, {})} | custom-call | tf_op jit(solution)/shard_map/pallas_call | solution.py:668
  (2 shorter events, 0.1 us)
Async XLA Ops:
  2.0 1.5 %collective-permute-start = (bf16[4,4,3200]{2,1,0:T(4,128)(2,1)S(1)}, bf16[4,4,3200]{2,1,0:T(4,128)(2,1)S(1)}, u32[]{:S(2)}, u32[]{:S(2)}) collective-permute-start(bf16[4,4,3200]{2,1,0:T(4,128)(2,1)S(1)} %get-tuple-element.35), channel_id=1, source_target_pairs={{0,1},{1,0},{2,3},{3,2},{4,5},{5,4},{6,7},{7,6},{8,9},{9,8},{10,11... | collective-permute-start | bytes 307208 | tf_op jit(solution)/shard_map/ppermute | solution.py:599
  3.5 5.6 %collective-permute-start.1 = (bf16[8,3200]{1,0:T(8,128)(2,1)S(1)}, bf16[8,3200]{1,0:T(8,128)(2,1)S(1)}, u32[]{:S(2)}, u32[]{:S(2)}) collective-permute-start(bf16[8,3200]{1,0:T(8,128)(2,1)S(1)} %get-tuple-element.37), channel_id=1, source_target_pairs={{0,2},{1,3},{2,0},{3,1},{4,6},{5,7},{6,4},{7,5},{8,10},{9,11},{10,... | collective-permute-start | bytes 153608 | tf_op jit(solution)/shard_map/ppermute | solution.py:603
  6.5 6.0 %collective-permute-start.2 = (bf16[8,3200]{1,0:T(8,128)(2,1)S(1)}, bf16[8,3200]{1,0:T(8,128)(2,1)S(1)}, u32[]{:S(2)}, u32[]{:S(2)}) collective-permute-start(bf16[8,3200]{1,0:T(8,128)(2,1)S(1)} %get-tuple-element.38), channel_id=1, source_target_pairs={{0,4},{1,5},{2,6},{3,7},{4,0},{5,1},{6,2},{7,3},{8,12},{9,13},{10,... | collective-permute-start | bytes 153608 | tf_op jit(solution)/shard_map/ppermute | solution.py:603
  9.1 5.9 %collective-permute-start.3 = (bf16[8,3200]{1,0:T(8,128)(2,1)S(1)}, bf16[8,3200]{1,0:T(8,128)(2,1)S(1)}, u32[]{:S(2)}, u32[]{:S(2)}) collective-permute-start(bf16[8,3200]{1,0:T(8,128)(2,1)S(1)} %get-tuple-element.39), channel_id=1, source_target_pairs={{0,6},{1,7},{2,4},{3,5},{4,2},{5,3},{6,0},{7,1},{8,14},{9,15},{10,... | collective-permute-start | bytes 153608 | tf_op jit(solution)/shard_map/ppermute | solution.py:603
  16.2 3.8 %collective-permute-start.4 = (bf16[144,128]{1,0:T(8,128)(2,1)S(1)}, bf16[144,128]{1,0:T(8,128)(2,1)S(1)}, u32[]{:S(2)}, u32[]{:S(2)}) collective-permute-start(bf16[144,128]{1,0:T(8,128)(2,1)S(1)} %get-tuple-element.42), channel_id=1, source_target_pairs={{0,9},{1,8},{2,11},{3,10},{4,13},{5,12},{6,15},{7,14},{8,1},{9,0},... | collective-permute-start | bytes 110600 | tf_op jit(solution)/shard_map/ppermute | solution.py:628
  16.3 4.0 %collective-permute-start.5 = (bf16[144,128]{1,0:T(8,128)(2,1)S(1)}, bf16[144,128]{1,0:T(8,128)(2,1)S(1)}, u32[]{:S(2)}, u32[]{:S(2)}) collective-permute-start(bf16[144,128]{1,0:T(8,128)(2,1)S(1)} %get-tuple-element.43), channel_id=1, source_target_pairs={{0,16},{1,17},{2,18},{3,19},{4,20},{5,21},{6,22},{7,23},{8,24},{9,... | collective-permute-start | bytes 110600 | tf_op jit(solution)/shard_map/ppermute | solution.py:628
  17.9 4.3 %collective-permute-start.6 = (bf16[144,128]{1,0:T(8,128)(2,1)S(1)}, bf16[144,128]{1,0:T(8,128)(2,1)S(1)}, u32[]{:S(2)}, u32[]{:S(2)}) collective-permute-start(bf16[144,128]{1,0:T(8,128)(2,1)S(1)} %get-tuple-element.44), channel_id=1, source_target_pairs={{0,25},{1,24},{2,27},{3,26},{4,29},{5,28},{6,31},{7,30},{8,17},{9,... | collective-permute-start | bytes 110600 | tf_op jit(solution)/shard_map/ppermute | solution.py:628
  22.4 2.3 %collective-permute-start.7 = (bf16[456,128]{1,0:T(8,128)(2,1)S(1)}, bf16[456,128]{1,0:T(8,128)(2,1)S(1)}, u32[]{:S(2)}, u32[]{:S(2)}) collective-permute-start(bf16[456,128]{1,0:T(8,128)(2,1)S(1)} %get-tuple-element.50), channel_id=1, source_target_pairs={{0,1},{1,0},{2,3},{3,2},{4,5},{5,4},{6,7},{7,6},{8,9},{9,8},{10,11... | collective-permute-start | bytes 350216 | tf_op jit(solution)/shard_map/ppermute | solution.py:635
  24.7 7.5 %collective-permute-start.10 = (bf16[368,128]{1,0:T(8,128)(2,1)S(1)}, bf16[368,128]{1,0:T(8,128)(2,1)S(1)}, u32[]{:S(2)}, u32[]{:S(2)}) collective-permute-start(bf16[368,128]{1,0:T(8,128)(2,1)S(1)} %get-tuple-element.54), channel_id=1, source_target_pairs={{0,6},{1,7},{2,4},{3,5},{4,2},{5,3},{6,0},{7,1},{8,14},{9,15},{10,... | collective-permute-start | bytes 282632 | tf_op jit(solution)/shard_map/ppermute | solution.py:641
  26.0 8.7 %collective-permute-start.8 = (bf16[368,128]{1,0:T(8,128)(2,1)S(1)}, bf16[368,128]{1,0:T(8,128)(2,1)S(1)}, u32[]{:S(2)}, u32[]{:S(2)}) collective-permute-start(bf16[368,128]{1,0:T(8,128)(2,1)S(1)} %get-tuple-element.52), channel_id=1, source_target_pairs={{0,2},{1,3},{2,0},{3,1},{4,6},{5,7},{6,4},{7,5},{8,10},{9,11},{10,... | collective-permute-start | bytes 282632 | tf_op jit(solution)/shard_map/ppermute | solution.py:641
  26.2 8.5 %collective-permute-start.9 = (bf16[368,128]{1,0:T(8,128)(2,1)S(1)}, bf16[368,128]{1,0:T(8,128)(2,1)S(1)}, u32[]{:S(2)}, u32[]{:S(2)}) collective-permute-start(bf16[368,128]{1,0:T(8,128)(2,1)S(1)} %get-tuple-element.53), channel_id=1, source_target_pairs={{0,4},{1,5},{2,6},{3,7},{4,0},{5,1},{6,2},{7,3},{8,12},{9,13},{10,... | collective-permute-start | bytes 282632 | tf_op jit(solution)/shard_map/ppermute | solution.py:641
  34.7 5.1 %collective-permute-start.11 = (bf16[264,128]{1,0:T(8,128)(2,1)S(1)}, bf16[264,128]{1,0:T(8,128)(2,1)S(1)}, u32[]{:S(2)}, u32[]{:S(2)}) collective-permute-start(bf16[264,128]{1,0:T(8,128)(2,1)S(1)} %get-tuple-element.55), channel_id=1, source_target_pairs={{0,8},{1,9},{2,10},{3,11},{4,12},{5,13},{6,14},{7,15},{8,0},{9,1},... | collective-permute-start | bytes 202760 | tf_op jit(solution)/shard_map/ppermute | solution.py:646
  35.3 4.7 %collective-permute-start.12 = (bf16[264,128]{1,0:T(8,128)(2,1)S(1)}, bf16[264,128]{1,0:T(8,128)(2,1)S(1)}, u32[]{:S(2)}, u32[]{:S(2)}) collective-permute-start(bf16[264,128]{1,0:T(8,128)(2,1)S(1)} %get-tuple-element.55), channel_id=1, source_target_pairs={{0,16},{1,17},{2,18},{3,19},{4,20},{5,21},{6,22},{7,23},{8,24},{9,... | collective-permute-start | bytes 202760 | tf_op jit(solution)/shard_map/ppermute | solution.py:646
  35.8 5.2 %collective-permute-start.13 = (bf16[264,128]{1,0:T(8,128)(2,1)S(1)}, bf16[264,128]{1,0:T(8,128)(2,1)S(1)}, u32[]{:S(2)}, u32[]{:S(2)}) collective-permute-start(bf16[264,128]{1,0:T(8,128)(2,1)S(1)} %get-tuple-element.55), channel_id=1, source_target_pairs={{0,24},{1,25},{2,26},{3,27},{4,28},{5,29},{6,30},{7,31},{8,16},{9,... | collective-permute-start | bytes 202760 | tf_op jit(solution)/shard_map/ppermute | solution.py:646
  41.1 1.6 %collective-permute-start.14 = (bf16[4,264,128]{2,1,0:T(8,128)(2,1)S(1)}, bf16[4,264,128]{2,1,0:T(8,128)(2,1)S(1)}, u32[]{:S(2)}, u32[]{:S(2)}) collective-permute-start(bf16[4,264,128]{2,1,0:T(8,128)(2,1)S(1)} %pad_maximum_fusion.slabs), channel_id=1, source_target_pairs={{0,1},{1,0},{2,3},{3,2},{4,5},{5,4},{6,7},{7,6},{8,9},{9,8},{10,11... | collective-permute-start | bytes 811016 | tf_op jit(solution)/shard_map/ppermute | solution.py:648

commit v12 on v11

--- a/solution.py
+++ b/solution.py
@@ -151,6 +151,7 @@
 
 def direct_series_kernel(heads, model_d, dates, pos, tile, *refs):
     levels, w_t, sends, (own, give, sel, recv) = refs[:4], refs[4], refs[5:-4], refs[-4:]
+    levels = tuple(levels[k] for k in (0, 2, 1, 3))
     length = recv.shape[0]
     slab = 2 * LANES
     recv[...] = jnp.concatenate([level[...].astype(F32) for level in levels], axis=0).astype(BF16)
@@ -462,6 +463,7 @@
 
 def direct_slab_kernel(pos, *refs):
     parts, (sel, rows, keep, keep_sums, give) = refs[:4], refs[4:]
+    parts = (parts[0], parts[3], parts[2], parts[1])
     cols = keep.shape[0]
     length = sel.shape[1]
     first = bit_of(pos, 0) == 0
@@ -520,7 +522,7 @@
         send[...] = jnp.concatenate([common] + rows_block(part.astype(BF16)), axis=0)
 
 
-def direct_total_kernel(own, low, high, both, send, rest):
+def direct_total_kernel(own, low, both, high, send, rest):
     cols = send.shape[0]
     total = pair_sum([part[...].astype(F32)[: cols + 16] for part in (own, low, high, both)])
     send[...] = total[:cols].astype(BF16)
@@ -601,7 +603,7 @@
         level_rows_kernel, [((2 * dates_dev, 3 * model_d + LANES), BF16)] * 4, [date_s, keep, got], 1
     )
     arrived = {k: lax.ppermute(levels[k], axes, across(2 * k)) for k in (3, 2, 1)}
-    return [levels[0]] + [arrived[k] for k in (1, 2, 3)], w_t
+    return [levels[0]] + [arrived[k] for k in (2, 1, 3)], w_t
 
 
 def finish_direct(operands, w_t, date_s, tile_s, heads, scale, pixel_dev, dates_dev, tiles, dates):
@@ -629,7 +631,7 @@
     keep, keep_sums, give = call(
         direct_slab_kernel,
         [((cols, LANES), F32), ((8, LANES), F32), ((payload, LANES), BF16)],
-        [date_s, sends[0], parts[1], parts[2], parts[3], sel, rows_give],
+        [date_s, sends[0], parts[3], parts[2], parts[1], sel, rows_give],
         1,
     )
     got = lax.ppermute(give, axes, across(1))
@@ -641,7 +643,7 @@
     arrived = {k: lax.ppermute(levels[k - 1], axes, across(2 * k)) for k in (3, 2, 1)}
     low, high, both = (arrived[k] for k in (1, 2, 3))
     slab, rest = call(
-        direct_total_kernel, [((cols, LANES), BF16), ((8, LANES), F32)], [own, low, high, both]
+        direct_total_kernel, [((cols, LANES), BF16), ((8, LANES), F32)], [own, low, both, high]
     )
     gathered = {k: lax.ppermute(slab, axes, across(dates * k)) for k in (3, 2, 1)}
     slabs = jnp.stack([slab] + [gathered[k] for k in (1, 2, 3)])

time: 43.7 us -> 43.1 us (0.986)
  waiting for transfers between devices: 19.4 us -> 18.9 us
    ppermute x3, waiting for transfers between devices: 2.74 us -> 3.75 us  [finish_direct(): lax.ppermute(slab, axes, across(dates * k))]
    ppermute x3, waiting for transfers between devices: 2.95 us -> 2.14 us  [finish_direct(): lax.ppermute(sends[k], axes, across(dates * k + k % 2))]
    ppermute x3, waiting for transfers between devices: 5.52 us -> 4.88 us  [finish_direct(): lax.ppermute(levels[k - 1], axes, across(2 * k))]
where the time goes in v12:
time: 43.1 us; the launch traced here: 42.9 us
  waiting for transfers between devices  18.9 us (44%)
  starting transfers between devices  18.4 us (43%)
  Pallas kernels  4.91 us (11%)
  between operations  0.71 us (2%)
    ppermute x3, waiting for transfers between devices, direct_series(): lax.ppermute(levels[k], axes, across(2 * k))  5.91 us
    ppermute x3, starting transfers between devices, direct_series(): lax.ppermute(levels[k], axes, across(2 * k))  5.59 us
    ppermute x3, waiting for transfers between devices, finish_direct(): lax.ppermute(levels[k - 1], axes, across(2 * k))  4.88 us
    ppermute x3, starting transfers between devices, finish_direct(): lax.ppermute(levels[k - 1], axes, across(2 * k))  4.47 us
    ppermute x3, waiting for transfers between devices, finish_direct(): lax.ppermute(slab, axes, across(dates * k))  3.75 us
    ppermute x3, starting transfers between devices, finish_direct(): lax.ppermute(slab, axes, across(dates * k))  3.55 us
    ppermute x3, starting transfers between devices, finish_direct(): lax.ppermute(sends[k], axes, across(dates * k + k % 2))  2.99 us
    ppermute x3, waiting for transfers between devices, finish_direct(): lax.ppermute(sends[k], axes, across(dates * k + k % 2))  2.14 us
  transfers between devices with their start and end apart: 15, of which 13 were waited for; matrix products, arithmetic and copies ran while one was open for 0% of the time, Pallas kernels for 3%

profile of v12, /device:TPU:0, one launch (start us, length us, event | category | flops | bytes accessed | tf_op | source)
XLA Modules:
  0.0 42.9 jit_solution(17647030555221987034)
XLA Ops:
  0.6 1.3 %shard_map.137 = (bf16[4,4,3200]{2,1,0:T(4,128)(2,1)S(1)}, bf16[4,4,3200]{2,1,0:T(4,128)(2,1)S(1)}, bf16[264,1024]{1,0:T(8,128)(2,1)S(1)}) custom-call(s32[1]{0:T(128)} %bitcast.pos, bf16[264,1024]{1,0:T(8,128)(2,1)} %bitcast.17, s32[4]{0:T(128)} %ids_in.1, s32[4,8]{1,0:T(4,128)} %bitcast.24, f32[2,1024]{1,0:T(2,128)} %table_in.1, f32[1,8]{1,0:T(1,128)} %bitcast.25, ...), custom_call_target="tpu_custom_call" | custom-call | tf_op jit(solution)/shard_map/pallas_call | solution.py:586
  2.0 0.5 %collective-permute-start = (bf16[4,4,3200]{2,1,0:T(4,128)(2,1)S(1)}, bf16[4,4,3200]{2,1,0:T(4,128)(2,1)S(1)}, u32[]{:S(2)}, u32[]{:S(2)}) collective-permute-start(bf16[4,4,3200]{2,1,0:T(4,128)(2,1)S(1)} %get-tuple-element.35), channel_id=1, source_target_pairs={{0,1},{1,0},{2,3},{3,2},{4,5},{5,4},{6,7},{7,6},{8,9},{9,8},{10,11... | collective-permute-start | bytes 307208 | tf_op jit(solution)/shard_map/ppermute | solution.py:601
  2.5 0.9 %collective-permute-done.got = bf16[4,4,3200]{2,1,0:T(4,128)(2,1)S(1)} collective-permute-done((bf16[4,4,3200]{2,1,0:T(4,128)(2,1)S(1)}, bf16[4,4,3200]{2,1,0:T(4,128)(2,1)S(1)}, u32[]{:S(2)}, u32[]{:S(2)}) %collective-permute-start) | collective-permute-done | bytes 102432 | tf_op jit(solution)/shard_map/ppermute | solution.py:601
  3.5 0.1 shard_map.138
  3.5 4.0 %collective-permute-start.1 = (bf16[8,3200]{1,0:T(8,128)(2,1)S(1)}, bf16[8,3200]{1,0:T(8,128)(2,1)S(1)}, u32[]{:S(2)}, u32[]{:S(2)}) collective-permute-start(bf16[8,3200]{1,0:T(8,128)(2,1)S(1)} %get-tuple-element.37), channel_id=1, source_target_pairs={{0,4},{1,5},{2,6},{3,7},{4,0},{5,1},{6,2},{7,3},{8,12},{9,13},{10,... | collective-permute-start | bytes 153608 | tf_op jit(solution)/shard_map/ppermute | solution.py:605
  7.5 1.6 %collective-permute-start.2 = (bf16[8,3200]{1,0:T(8,128)(2,1)S(1)}, bf16[8,3200]{1,0:T(8,128)(2,1)S(1)}, u32[]{:S(2)}, u32[]{:S(2)}) collective-permute-start(bf16[8,3200]{1,0:T(8,128)(2,1)S(1)} %get-tuple-element.38), channel_id=1, source_target_pairs={{0,2},{1,3},{2,0},{3,1},{4,6},{5,7},{6,4},{7,5},{8,10},{9,11},{10,... | collective-permute-start | bytes 153608 | tf_op jit(solution)/shard_map/ppermute | solution.py:605
  9.1 0.0 collective-permute-start.3
  9.1 0.5 %collective-permute-done.1.refs_1_ = bf16[8,3200]{1,0:T(8,128)(2,1)S(1)} collective-permute-done((bf16[8,3200]{1,0:T(8,128)(2,1)S(1)}, bf16[8,3200]{1,0:T(8,128)(2,1)S(1)}, u32[]{:S(2)}, u32[]{:S(2)}) %collective-permute-start.1) | collective-permute-done | bytes 51232 | tf_op jit(solution)/shard_map/ppermute | solution.py:605
  9.6 2.0 %collective-permute-done.2.refs_2_ = bf16[8,3200]{1,0:T(8,128)(2,1)S(1)} collective-permute-done((bf16[8,3200]{1,0:T(8,128)(2,1)S(1)}, bf16[8,3200]{1,0:T(8,128)(2,1)S(1)}, u32[]{:S(2)}, u32[]{:S(2)}) %collective-permute-start.2) | collective-permute-done | bytes 51232 | tf_op jit(solution)/shard_map/ppermute | solution.py:605
  11.6 3.4 %collective-permute-done.3.refs_3_ = bf16[8,3200]{1,0:T(8,128)(2,1)S(1)} collective-permute-done((bf16[8,3200]{1,0:T(8,128)(2,1)S(1)}, bf16[8,3200]{1,0:T(8,128)(2,1)S(1)}, u32[]{:S(2)}, u32[]{:S(2)}) %collective-permute-start.3) | collective-permute-done | bytes 51232 | tf_op jit(solution)/shard_map/ppermute | solution.py:605
  15.0 1.2 %shard_map.139 = (bf16[144,128]{1,0:T(8,128)(2,1)S(1)}, bf16[144,128]{1,0:T(8,128)(2,1)S(1)}, bf16[144,128]{1,0:T(8,128)(2,1)S(1)}, bf16[144,128]{1,0:T(8,128)(2...) custom-call(s32[1]{0:T(128)} %bitcast.pos, s32[1]{0:T(128)} %bitcast.1.tile, ...), custom_call_target="tpu_custom_call" | custom-call | tf_op jit(solution)/shard_map/pallas_call | solution.py:433
  16.2 0.6 %collective-permute-start.4 = (bf16[144,128]{1,0:T(8,128)(2,1)S(1)}, bf16[144,128]{1,0:T(8,128)(2,1)S(1)}, u32[]{:S(2)}, u32[]{:S(2)}) collective-permute-start(bf16[144,128]{1,0:T(8,128)(2,1)S(1)} %get-tuple-element.42), channel_id=1, source_target_pairs={{0,25},{1,24},{2,27},{3,26},{4,29},{5,28},{6,31},{7,30},{8,17},{9,... | collective-permute-start | bytes 110600 | tf_op jit(solution)/shard_map/ppermute | solution.py:630
  16.8 1.1 %collective-permute-start.5 = (bf16[144,128]{1,0:T(8,128)(2,1)S(1)}, bf16[144,128]{1,0:T(8,128)(2,1)S(1)}, u32[]{:S(2)}, u32[]{:S(2)}) collective-permute-start(bf16[144,128]{1,0:T(8,128)(2,1)S(1)} %get-tuple-element.43), channel_id=1, source_target_pairs={{0,16},{1,17},{2,18},{3,19},{4,20},{5,21},{6,22},{7,23},{8,24},{9,... | collective-permute-start | bytes 110600 | tf_op jit(solution)/shard_map/ppermute | solution.py:630
  17.9 1.3 %collective-permute-start.6 = (bf16[144,128]{1,0:T(8,128)(2,1)S(1)}, bf16[144,128]{1,0:T(8,128)(2,1)S(1)}, u32[]{:S(2)}, u32[]{:S(2)}) collective-permute-start(bf16[144,128]{1,0:T(8,128)(2,1)S(1)} %get-tuple-element.44), channel_id=1, source_target_pairs={{0,9},{1,8},{2,11},{3,10},{4,13},{5,12},{6,15},{7,14},{8,1},{9,0},... | collective-permute-start | bytes 110600 | tf_op jit(solution)/shard_map/ppermute | solution.py:630
  19.2 1.7 %collective-permute-done.4.refs_1_ = bf16[144,128]{1,0:T(8,128)(2,1)S(1)} collective-permute-done((bf16[144,128]{1,0:T(8,128)(2,1)S(1)}, bf16[144,128]{1,0:T(8,128)(2,1)S(1)}, u32[]{:S(2)}, u32[]{:S(2)}) %collective-permute-start.4) | collective-permute-done | bytes 36896 | tf_op jit(solution)/shard_map/ppermute | solution.py:630
  20.9 0.4 %collective-permute-done.5.refs_2_ = bf16[144,128]{1,0:T(8,128)(2,1)S(1)} collective-permute-done((bf16[144,128]{1,0:T(8,128)(2,1)S(1)}, bf16[144,128]{1,0:T(8,128)(2,1)S(1)}, u32[]{:S(2)}, u32[]{:S(2)}) %collective-permute-start.5) | collective-permute-done | bytes 36896 | tf_op jit(solution)/shard_map/ppermute | solution.py:630
  21.3 0.0 collective-permute-done.6.refs_3_
  21.3 0.2 shard_map.140
  21.6 1.2 %collective-permute-start.7 = (bf16[456,128]{1,0:T(8,128)(2,1)S(1)}, bf16[456,128]{1,0:T(8,128)(2,1)S(1)}, u32[]{:S(2)}, u32[]{:S(2)}) collective-permute-start(bf16[456,128]{1,0:T(8,128)(2,1)S(1)} %get-tuple-element.50), channel_id=1, source_target_pairs={{0,1},{1,0},{2,3},{3,2},{4,5},{5,4},{6,7},{7,6},{8,9},{9,8},{10,11... | collective-permute-start | bytes 350216 | tf_op jit(solution)/shard_map/ppermute | solution.py:637
  22.7 1.0 %collective-permute-done.7.got = bf16[456,128]{1,0:T(8,128)(2,1)S(1)} collective-permute-done((bf16[456,128]{1,0:T(8,128)(2,1)S(1)}, bf16[456,128]{1,0:T(8,128)(2,1)S(1)}, u32[]{:S(2)}, u32[]{:S(2)}) %collective-permute-start.7) | collective-permute-done | bytes 116768 | tf_op jit(solution)/shard_map/ppermute | solution.py:637
  23.7 0.1 shard_map.141
  23.8 0.7 %collective-permute-start.10 = (bf16[368,128]{1,0:T(8,128)(2,1)S(1)}, bf16[368,128]{1,0:T(8,128)(2,1)S(1)}, u32[]{:S(2)}, u32[]{:S(2)}) collective-permute-start(bf16[368,128]{1,0:T(8,128)(2,1)S(1)} %get-tuple-element.54), channel_id=1, source_target_pairs={{0,4},{1,5},{2,6},{3,7},{4,0},{5,1},{6,2},{7,3},{8,12},{9,13},{10,... | collective-permute-start | bytes 282632 | tf_op jit(solution)/shard_map/ppermute | solution.py:643
  24.5 0.6 %collective-permute-start.8 = (bf16[368,128]{1,0:T(8,128)(2,1)S(1)}, bf16[368,128]{1,0:T(8,128)(2,1)S(1)}, u32[]{:S(2)}, u32[]{:S(2)}) collective-permute-start(bf16[368,128]{1,0:T(8,128)(2,1)S(1)} %get-tuple-element.52), channel_id=1, source_target_pairs={{0,2},{1,3},{2,0},{3,1},{4,6},{5,7},{6,4},{7,5},{8,10},{9,11},{10,... | collective-permute-start | bytes 282632 | tf_op jit(solution)/shard_map/ppermute | solution.py:643
  25.1 3.1 %collective-permute-start.9 = (bf16[368,128]{1,0:T(8,128)(2,1)S(1)}, bf16[368,128]{1,0:T(8,128)(2,1)S(1)}, u32[]{:S(2)}, u32[]{:S(2)}) collective-permute-start(bf16[368,128]{1,0:T(8,128)(2,1)S(1)} %get-tuple-element.53), channel_id=1, source_target_pairs={{0,6},{1,7},{2,4},{3,5},{4,2},{5,3},{6,0},{7,1},{8,14},{9,15},{10,... | collective-permute-start | bytes 282632 | tf_op jit(solution)/shard_map/ppermute | solution.py:643
  28.2 2.4 %collective-permute-done.10.high = bf16[368,128]{1,0:T(8,128)(2,1)S(1)} collective-permute-done((bf16[368,128]{1,0:T(8,128)(2,1)S(1)}, bf16[368,128]{1,0:T(8,128)(2,1)S(1)}, u32[]{:S(2)}, u32[]{:S(2)}) %collective-permute-start.10) | collective-permute-done | bytes 94240 | tf_op jit(solution)/shard_map/ppermute | solution.py:643
  30.6 2.5 %collective-permute-done.8.low = bf16[368,128]{1,0:T(8,128)(2,1)S(1)} collective-permute-done((bf16[368,128]{1,0:T(8,128)(2,1)S(1)}, bf16[368,128]{1,0:T(8,128)(2,1)S(1)}, u32[]{:S(2)}, u32[]{:S(2)}) %collective-permute-start.8) | collective-permute-done | bytes 94240 | tf_op jit(solution)/shard_map/ppermute | solution.py:643
  33.1 0.0 collective-permute-done.9.both
  33.1 1.0 %collective-permute-start.11 = (bf16[264,128]{1,0:T(8,128)(2,1)S(1)}, bf16[264,128]{1,0:T(8,128)(2,1)S(1)}, u32[]{:S(2)}, u32[]{:S(2)}) collective-permute-start(bf16[264,128]{1,0:T(8,128)(2,1)S(1)} %get-tuple-element.55), channel_id=1, source_target_pairs={{0,8},{1,9},{2,10},{3,11},{4,12},{5,13},{6,14},{7,15},{8,0},{9,1},... | collective-permute-start | bytes 202760 | tf_op jit(solution)/shard_map/ppermute | solution.py:648
  34.2 1.1 %collective-permute-start.12 = (bf16[264,128]{1,0:T(8,128)(2,1)S(1)}, bf16[264,128]{1,0:T(8,128)(2,1)S(1)}, u32[]{:S(2)}, u32[]{:S(2)}) collective-permute-start(bf16[264,128]{1,0:T(8,128)(2,1)S(1)} %get-tuple-element.55), channel_id=1, source_target_pairs={{0,16},{1,17},{2,18},{3,19},{4,20},{5,21},{6,22},{7,23},{8,24},{9,... | collective-permute-start | bytes 202760 | tf_op jit(solution)/shard_map/ppermute | solution.py:648
  35.3 1.4 %collective-permute-start.13 = (bf16[264,128]{1,0:T(8,128)(2,1)S(1)}, bf16[264,128]{1,0:T(8,128)(2,1)S(1)}, u32[]{:S(2)}, u32[]{:S(2)}) collective-permute-start(bf16[264,128]{1,0:T(8,128)(2,1)S(1)} %get-tuple-element.55), channel_id=1, source_target_pairs={{0,24},{1,25},{2,26},{3,27},{4,28},{5,29},{6,30},{7,31},{8,16},{9,... | collective-permute-start | bytes 202760 | tf_op jit(solution)/shard_map/ppermute | solution.py:648
  36.7 0.8 %collective-permute-done.11 = bf16[264,128]{1,0:T(8,128)(2,1)S(1)} collective-permute-done((bf16[264,128]{1,0:T(8,128)(2,1)S(1)}, bf16[264,128]{1,0:T(8,128)(2,1)S(1)}, u32[]{:S(2)}, u32[]{:S(2)}) %collective-permute-start.11) | collective-permute-done | bytes 67616 | tf_op jit(solution)/shard_map/ppermute | solution.py:648
  37.5 1.1 %collective-permute-done.12 = bf16[264,128]{1,0:T(8,128)(2,1)S(1)} collective-permute-done((bf16[264,128]{1,0:T(8,128)(2,1)S(1)}, bf16[264,128]{1,0:T(8,128)(2,1)S(1)}, u32[]{:S(2)}, u32[]{:S(2)}) %collective-permute-start.12) | collective-permute-done | bytes 67616 | tf_op jit(solution)/shard_map/ppermute | solution.py:648
  38.7 1.8 %collective-permute-done.13 = bf16[264,128]{1,0:T(8,128)(2,1)S(1)} collective-permute-done((bf16[264,128]{1,0:T(8,128)(2,1)S(1)}, bf16[264,128]{1,0:T(8,128)(2,1)S(1)}, u32[]{:S(2)}, u32[]{:S(2)}) %collective-permute-start.13) | collective-permute-done | bytes 67616 | tf_op jit(solution)/shard_map/ppermute | solution.py:648
  40.5 0.1 collective-permute-start.14
  40.6 1.2 %shard_map.143 = (bf16[8,4,1024]{2,1,0:T(4,128)(2,1)}, bf16[8,4,1024]{2,1,0:T(4,128)(2,1)}, f32[2,1024]{1,0:T(2,128)}, f32[3,8]{1,0:T(4,128)}, f32[264,1024]{1,0:T(8,128)}) custom-call(s32[1]{0:T(128)} %bitcast.pos, s32[1]{0:T(128)} %bitcast.1.tile, bf16[4,264,128]{2,1,0:T(8,128)(2,1)S(1)} %pad_maximum_fusion.slabs, ...), custom_call_target="tpu_custom_call" | custom-call | tf_op jit(solution)/shard_map/pallas_call | solution.py:660
  41.8 0.4 collective-permute-done.14.slabs
  42.1 0.8 %shard_map.144 = f32[264,1024]{1,0:T(8,128)} custom-call(s32[1]{0:T(128)} %bitcast.pos, s32[1]{0:T(128)} %bitcast.1.tile, bf16[4,264,128]{2,1,0:T(8,128)(2,1)S(1)} %collective-permute-done.14.slabs, f32[264,1024]{1,0:T(8,128)} %get-tuple-element.60.weight_in), custom_call_target="tpu_custom_call", output_to_operand_aliasing={{}: (3, {})} | custom-call | tf_op jit(solution)/shard_map/pallas_call | solution.py:670
  (2 shorter events, 0.1 us)
Async XLA Ops:
  2.0 1.5 %collective-permute-start = (bf16[4,4,3200]{2,1,0:T(4,128)(2,1)S(1)}, bf16[4,4,3200]{2,1,0:T(4,128)(2,1)S(1)}, u32[]{:S(2)}, u32[]{:S(2)}) collective-permute-start(bf16[4,4,3200]{2,1,0:T(4,128)(2,1)S(1)} %get-tuple-element.35), channel_id=1, source_target_pairs={{0,1},{1,0},{2,3},{3,2},{4,5},{5,4},{6,7},{7,6},{8,9},{9,8},{10,11... | collective-permute-start | bytes 307208 | tf_op jit(solution)/shard_map/ppermute | solution.py:601
  3.5 6.1 %collective-permute-start.1 = (bf16[8,3200]{1,0:T(8,128)(2,1)S(1)}, bf16[8,3200]{1,0:T(8,128)(2,1)S(1)}, u32[]{:S(2)}, u32[]{:S(2)}) collective-permute-start(bf16[8,3200]{1,0:T(8,128)(2,1)S(1)} %get-tuple-element.37), channel_id=1, source_target_pairs={{0,4},{1,5},{2,6},{3,7},{4,0},{5,1},{6,2},{7,3},{8,12},{9,13},{10,... | collective-permute-start | bytes 153608 | tf_op jit(solution)/shard_map/ppermute | solution.py:605
  7.5 4.1 %collective-permute-start.2 = (bf16[8,3200]{1,0:T(8,128)(2,1)S(1)}, bf16[8,3200]{1,0:T(8,128)(2,1)S(1)}, u32[]{:S(2)}, u32[]{:S(2)}) collective-permute-start(bf16[8,3200]{1,0:T(8,128)(2,1)S(1)} %get-tuple-element.38), channel_id=1, source_target_pairs={{0,2},{1,3},{2,0},{3,1},{4,6},{5,7},{6,4},{7,5},{8,10},{9,11},{10,... | collective-permute-start | bytes 153608 | tf_op jit(solution)/shard_map/ppermute | solution.py:605
  9.1 5.9 %collective-permute-start.3 = (bf16[8,3200]{1,0:T(8,128)(2,1)S(1)}, bf16[8,3200]{1,0:T(8,128)(2,1)S(1)}, u32[]{:S(2)}, u32[]{:S(2)}) collective-permute-start(bf16[8,3200]{1,0:T(8,128)(2,1)S(1)} %get-tuple-element.39), channel_id=1, source_target_pairs={{0,6},{1,7},{2,4},{3,5},{4,2},{5,3},{6,0},{7,1},{8,14},{9,15},{10,... | collective-permute-start | bytes 153608 | tf_op jit(solution)/shard_map/ppermute | solution.py:605
  16.2 4.7 %collective-permute-start.4 = (bf16[144,128]{1,0:T(8,128)(2,1)S(1)}, bf16[144,128]{1,0:T(8,128)(2,1)S(1)}, u32[]{:S(2)}, u32[]{:S(2)}) collective-permute-start(bf16[144,128]{1,0:T(8,128)(2,1)S(1)} %get-tuple-element.42), channel_id=1, source_target_pairs={{0,25},{1,24},{2,27},{3,26},{4,29},{5,28},{6,31},{7,30},{8,17},{9,... | collective-permute-start | bytes 110600 | tf_op jit(solution)/shard_map/ppermute | solution.py:630
  16.8 4.6 %collective-permute-start.5 = (bf16[144,128]{1,0:T(8,128)(2,1)S(1)}, bf16[144,128]{1,0:T(8,128)(2,1)S(1)}, u32[]{:S(2)}, u32[]{:S(2)}) collective-permute-start(bf16[144,128]{1,0:T(8,128)(2,1)S(1)} %get-tuple-element.43), channel_id=1, source_target_pairs={{0,16},{1,17},{2,18},{3,19},{4,20},{5,21},{6,22},{7,23},{8,24},{9,... | collective-permute-start | bytes 110600 | tf_op jit(solution)/shard_map/ppermute | solution.py:630
  17.9 3.5 %collective-permute-start.6 = (bf16[144,128]{1,0:T(8,128)(2,1)S(1)}, bf16[144,128]{1,0:T(8,128)(2,1)S(1)}, u32[]{:S(2)}, u32[]{:S(2)}) collective-permute-start(bf16[144,128]{1,0:T(8,128)(2,1)S(1)} %get-tuple-element.44), channel_id=1, source_target_pairs={{0,9},{1,8},{2,11},{3,10},{4,13},{5,12},{6,15},{7,14},{8,1},{9,0},... | collective-permute-start | bytes 110600 | tf_op jit(solution)/shard_map/ppermute | solution.py:630
  21.6 2.1 %collective-permute-start.7 = (bf16[456,128]{1,0:T(8,128)(2,1)S(1)}, bf16[456,128]{1,0:T(8,128)(2,1)S(1)}, u32[]{:S(2)}, u32[]{:S(2)}) collective-permute-start(bf16[456,128]{1,0:T(8,128)(2,1)S(1)} %get-tuple-element.50), channel_id=1, source_target_pairs={{0,1},{1,0},{2,3},{3,2},{4,5},{5,4},{6,7},{7,6},{8,9},{9,8},{10,11... | collective-permute-start | bytes 350216 | tf_op jit(solution)/shard_map/ppermute | solution.py:637
  23.8 6.9 %collective-permute-start.10 = (bf16[368,128]{1,0:T(8,128)(2,1)S(1)}, bf16[368,128]{1,0:T(8,128)(2,1)S(1)}, u32[]{:S(2)}, u32[]{:S(2)}) collective-permute-start(bf16[368,128]{1,0:T(8,128)(2,1)S(1)} %get-tuple-element.54), channel_id=1, source_target_pairs={{0,4},{1,5},{2,6},{3,7},{4,0},{5,1},{6,2},{7,3},{8,12},{9,13},{10,... | collective-permute-start | bytes 282632 | tf_op jit(solution)/shard_map/ppermute | solution.py:643
  24.5 8.6 %collective-permute-start.8 = (bf16[368,128]{1,0:T(8,128)(2,1)S(1)}, bf16[368,128]{1,0:T(8,128)(2,1)S(1)}, u32[]{:S(2)}, u32[]{:S(2)}) collective-permute-start(bf16[368,128]{1,0:T(8,128)(2,1)S(1)} %get-tuple-element.52), channel_id=1, source_target_pairs={{0,2},{1,3},{2,0},{3,1},{4,6},{5,7},{6,4},{7,5},{8,10},{9,11},{10,... | collective-permute-start | bytes 282632 | tf_op jit(solution)/shard_map/ppermute | solution.py:643
  25.1 8.0 %collective-permute-start.9 = (bf16[368,128]{1,0:T(8,128)(2,1)S(1)}, bf16[368,128]{1,0:T(8,128)(2,1)S(1)}, u32[]{:S(2)}, u32[]{:S(2)}) collective-permute-start(bf16[368,128]{1,0:T(8,128)(2,1)S(1)} %get-tuple-element.53), channel_id=1, source_target_pairs={{0,6},{1,7},{2,4},{3,5},{4,2},{5,3},{6,0},{7,1},{8,14},{9,15},{10,... | collective-permute-start | bytes 282632 | tf_op jit(solution)/shard_map/ppermute | solution.py:643
  33.1 4.4 %collective-permute-start.11 = (bf16[264,128]{1,0:T(8,128)(2,1)S(1)}, bf16[264,128]{1,0:T(8,128)(2,1)S(1)}, u32[]{:S(2)}, u32[]{:S(2)}) collective-permute-start(bf16[264,128]{1,0:T(8,128)(2,1)S(1)} %get-tuple-element.55), channel_id=1, source_target_pairs={{0,8},{1,9},{2,10},{3,11},{4,12},{5,13},{6,14},{7,15},{8,0},{9,1},... | collective-permute-start | bytes 202760 | tf_op jit(solution)/shard_map/ppermute | solution.py:648
  34.2 4.5 %collective-permute-start.12 = (bf16[264,128]{1,0:T(8,128)(2,1)S(1)}, bf16[264,128]{1,0:T(8,128)(2,1)S(1)}, u32[]{:S(2)}, u32[]{:S(2)}) collective-permute-start(bf16[264,128]{1,0:T(8,128)(2,1)S(1)} %get-tuple-element.55), channel_id=1, source_target_pairs={{0,16},{1,17},{2,18},{3,19},{4,20},{5,21},{6,22},{7,23},{8,24},{9,... | collective-permute-start | bytes 202760 | tf_op jit(solution)/shard_map/ppermute | solution.py:648
  35.3 5.2 %collective-permute-start.13 = (bf16[264,128]{1,0:T(8,128)(2,1)S(1)}, bf16[264,128]{1,0:T(8,128)(2,1)S(1)}, u32[]{:S(2)}, u32[]{:S(2)}) collective-permute-start(bf16[264,128]{1,0:T(8,128)(2,1)S(1)} %get-tuple-element.55), channel_id=1, source_target_pairs={{0,24},{1,25},{2,26},{3,27},{4,28},{5,29},{6,30},{7,31},{8,16},{9,... | collective-permute-start | bytes 202760 | tf_op jit(solution)/shard_map/ppermute | solution.py:648
  40.5 1.6 %collective-permute-start.14 = (bf16[4,264,128]{2,1,0:T(8,128)(2,1)S(1)}, bf16[4,264,128]{2,1,0:T(8,128)(2,1)S(1)}, u32[]{:S(2)}, u32[]{:S(2)}) collective-permute-start(bf16[4,264,128]{2,1,0:T(8,128)(2,1)S(1)} %pad_maximum_fusion.slabs), channel_id=1, source_target_pairs={{0,1},{1,0},{2,3},{3,2},{4,5},{5,4},{6,7},{7,6},{8,9},{9,8},{10,11... | collective-permute-start | bytes 811016 | tf_op jit(solution)/shard_map/ppermute | solution.py:650

commit v13 on v12

--- a/solution.py
+++ b/solution.py
@@ -13,6 +13,7 @@
 F32 = jnp.float32
 BF16 = jnp.bfloat16
 LANES = 128
+TILE_ORDER = (0, 3, 2, 1)
 EXT = 384
 
 
@@ -533,7 +534,7 @@
     copies = []
     for k, slab in enumerate(slabs):
         held[k] = slab.astype(F32) * scale
-        at = pl.multiple_of((2 * (tile ^ k) + core) * LANES, LANES)
+        at = pl.multiple_of((2 * (tile ^ TILE_ORDER[k]) + core) * LANES, LANES)
         copies.append(pltpu.make_async_copy(held.at[k], weight.at[:, pl.ds(at, LANES)], sems.at[k]))
         copies[-1].start()
     return copies
@@ -646,7 +647,7 @@
         direct_total_kernel, [((cols, LANES), BF16), ((8, LANES), F32)], [own, low, both, high]
     )
     gathered = {k: lax.ppermute(slab, axes, across(dates * k)) for k in (3, 2, 1)}
-    slabs = jnp.stack([slab] + [gathered[k] for k in (1, 2, 3)])
+    slabs = jnp.stack([slab] + [gathered[k] for k in TILE_ORDER[1:]])
     other_slabs = lax.ppermute(slabs, axes, across(1))
     outs = [
         jax.ShapeDtypeStruct((pixel_dev, dates_dev, model_d), BF16),

time: 43.1 us -> 42.5 us (0.986)
  waiting for transfers between devices: 18.9 us -> 18.4 us
    ppermute x3, waiting for transfers between devices: 3.75 us -> 3.2 us  [finish_direct(): lax.ppermute(slab, axes, across(dates * k))]
where the time goes in v13:
time: 42.5 us; the launch traced here: 42.4 us
  starting transfers between devices  18.4 us (43%)
  waiting for transfers between devices  18.4 us (43%)
  Pallas kernels  4.91 us (12%)
  between operations  0.71 us (2%)
    ppermute x3, waiting for transfers between devices, direct_series(): lax.ppermute(levels[k], axes, across(2 * k))  5.91 us
    ppermute x3, starting transfers between devices, direct_series(): lax.ppermute(levels[k], axes, across(2 * k))  5.59 us
    ppermute x3, waiting for transfers between devices, finish_direct(): lax.ppermute(levels[k - 1], axes, across(2 * k))  4.88 us
    ppermute x3, starting transfers between devices, finish_direct(): lax.ppermute(levels[k - 1], axes, across(2 * k))  4.47 us
    ppermute x3, starting transfers between devices, finish_direct(): lax.ppermute(slab, axes, across(dates * k))  3.55 us
    ppermute x3, waiting for transfers between devices, finish_direct(): lax.ppermute(slab, axes, across(dates * k))  3.2 us
    ppermute x3, starting transfers between devices, finish_direct(): lax.ppermute(sends[k], axes, across(dates * k + k % 2))  2.99 us
    ppermute x3, waiting for transfers between devices, finish_direct(): lax.ppermute(sends[k], axes, across(dates * k + k % 2))  2.14 us
  transfers between devices with their start and end apart: 15, of which 13 were waited for; matrix products, arithmetic and copies ran while one was open for 0% of the time, Pallas kernels for 3%

profile of v13, /device:TPU:0, one launch (start us, length us, event | category | flops | bytes accessed | tf_op | source)
XLA Modules:
  0.0 42.4 jit_solution(10902347859518514006)
XLA Ops:
  0.6 1.3 %shard_map.137 = (bf16[4,4,3200]{2,1,0:T(4,128)(2,1)S(1)}, bf16[4,4,3200]{2,1,0:T(4,128)(2,1)S(1)}, bf16[264,1024]{1,0:T(8,128)(2,1)S(1)}) custom-call(s32[1]{0:T(128)} %bitcast.pos, bf16[264,1024]{1,0:T(8,128)(2,1)} %bitcast.17, s32[4]{0:T(128)} %ids_in.1, s32[4,8]{1,0:T(4,128)} %bitcast.24, f32[2,1024]{1,0:T(2,128)} %table_in.1, f32[1,8]{1,0:T(1,128)} %bitcast.25, ...), custom_call_target="tpu_custom_call" | custom-call | tf_op jit(solution)/shard_map/pallas_call | solution.py:587
  2.0 0.5 %collective-permute-start = (bf16[4,4,3200]{2,1,0:T(4,128)(2,1)S(1)}, bf16[4,4,3200]{2,1,0:T(4,128)(2,1)S(1)}, u32[]{:S(2)}, u32[]{:S(2)}) collective-permute-start(bf16[4,4,3200]{2,1,0:T(4,128)(2,1)S(1)} %get-tuple-element.35), channel_id=1, source_target_pairs={{0,1},{1,0},{2,3},{3,2},{4,5},{5,4},{6,7},{7,6},{8,9},{9,8},{10,11... | collective-permute-start | bytes 307208 | tf_op jit(solution)/shard_map/ppermute | solution.py:602
  2.5 0.9 %collective-permute-done.got = bf16[4,4,3200]{2,1,0:T(4,128)(2,1)S(1)} collective-permute-done((bf16[4,4,3200]{2,1,0:T(4,128)(2,1)S(1)}, bf16[4,4,3200]{2,1,0:T(4,128)(2,1)S(1)}, u32[]{:S(2)}, u32[]{:S(2)}) %collective-permute-start) | collective-permute-done | bytes 102432 | tf_op jit(solution)/shard_map/ppermute | solution.py:602
  3.5 0.1 shard_map.138
  3.5 4.0 %collective-permute-start.1 = (bf16[8,3200]{1,0:T(8,128)(2,1)S(1)}, bf16[8,3200]{1,0:T(8,128)(2,1)S(1)}, u32[]{:S(2)}, u32[]{:S(2)}) collective-permute-start(bf16[8,3200]{1,0:T(8,128)(2,1)S(1)} %get-tuple-element.37), channel_id=1, source_target_pairs={{0,4},{1,5},{2,6},{3,7},{4,0},{5,1},{6,2},{7,3},{8,12},{9,13},{10,... | collective-permute-start | bytes 153608 | tf_op jit(solution)/shard_map/ppermute | solution.py:606
  7.5 1.6 %collective-permute-start.2 = (bf16[8,3200]{1,0:T(8,128)(2,1)S(1)}, bf16[8,3200]{1,0:T(8,128)(2,1)S(1)}, u32[]{:S(2)}, u32[]{:S(2)}) collective-permute-start(bf16[8,3200]{1,0:T(8,128)(2,1)S(1)} %get-tuple-element.38), channel_id=1, source_target_pairs={{0,2},{1,3},{2,0},{3,1},{4,6},{5,7},{6,4},{7,5},{8,10},{9,11},{10,... | collective-permute-start | bytes 153608 | tf_op jit(solution)/shard_map/ppermute | solution.py:606
  9.1 0.0 collective-permute-start.3
  9.1 0.5 %collective-permute-done.1.refs_1_ = bf16[8,3200]{1,0:T(8,128)(2,1)S(1)} collective-permute-done((bf16[8,3200]{1,0:T(8,128)(2,1)S(1)}, bf16[8,3200]{1,0:T(8,128)(2,1)S(1)}, u32[]{:S(2)}, u32[]{:S(2)}) %collective-permute-start.1) | collective-permute-done | bytes 51232 | tf_op jit(solution)/shard_map/ppermute | solution.py:606
  9.6 2.0 %collective-permute-done.2.refs_2_ = bf16[8,3200]{1,0:T(8,128)(2,1)S(1)} collective-permute-done((bf16[8,3200]{1,0:T(8,128)(2,1)S(1)}, bf16[8,3200]{1,0:T(8,128)(2,1)S(1)}, u32[]{:S(2)}, u32[]{:S(2)}) %collective-permute-start.2) | collective-permute-done | bytes 51232 | tf_op jit(solution)/shard_map/ppermute | solution.py:606
  11.6 3.4 %collective-permute-done.3.refs_3_ = bf16[8,3200]{1,0:T(8,128)(2,1)S(1)} collective-permute-done((bf16[8,3200]{1,0:T(8,128)(2,1)S(1)}, bf16[8,3200]{1,0:T(8,128)(2,1)S(1)}, u32[]{:S(2)}, u32[]{:S(2)}) %collective-permute-start.3) | collective-permute-done | bytes 51232 | tf_op jit(solution)/shard_map/ppermute | solution.py:606
  15.0 1.2 %shard_map.139 = (bf16[144,128]{1,0:T(8,128)(2,1)S(1)}, bf16[144,128]{1,0:T(8,128)(2,1)S(1)}, bf16[144,128]{1,0:T(8,128)(2,1)S(1)}, bf16[144,128]{1,0:T(8,128)(2...) custom-call(s32[1]{0:T(128)} %bitcast.pos, s32[1]{0:T(128)} %bitcast.1.tile, ...), custom_call_target="tpu_custom_call" | custom-call | tf_op jit(solution)/shard_map/pallas_call | solution.py:434
  16.2 0.6 %collective-permute-start.4 = (bf16[144,128]{1,0:T(8,128)(2,1)S(1)}, bf16[144,128]{1,0:T(8,128)(2,1)S(1)}, u32[]{:S(2)}, u32[]{:S(2)}) collective-permute-start(bf16[144,128]{1,0:T(8,128)(2,1)S(1)} %get-tuple-element.42), channel_id=1, source_target_pairs={{0,25},{1,24},{2,27},{3,26},{4,29},{5,28},{6,31},{7,30},{8,17},{9,... | collective-permute-start | bytes 110600 | tf_op jit(solution)/shard_map/ppermute | solution.py:631
  16.8 1.1 %collective-permute-start.5 = (bf16[144,128]{1,0:T(8,128)(2,1)S(1)}, bf16[144,128]{1,0:T(8,128)(2,1)S(1)}, u32[]{:S(2)}, u32[]{:S(2)}) collective-permute-start(bf16[144,128]{1,0:T(8,128)(2,1)S(1)} %get-tuple-element.43), channel_id=1, source_target_pairs={{0,16},{1,17},{2,18},{3,19},{4,20},{5,21},{6,22},{7,23},{8,24},{9,... | collective-permute-start | bytes 110600 | tf_op jit(solution)/shard_map/ppermute | solution.py:631
  17.9 1.3 %collective-permute-start.6 = (bf16[144,128]{1,0:T(8,128)(2,1)S(1)}, bf16[144,128]{1,0:T(8,128)(2,1)S(1)}, u32[]{:S(2)}, u32[]{:S(2)}) collective-permute-start(bf16[144,128]{1,0:T(8,128)(2,1)S(1)} %get-tuple-element.44), channel_id=1, source_target_pairs={{0,9},{1,8},{2,11},{3,10},{4,13},{5,12},{6,15},{7,14},{8,1},{9,0},... | collective-permute-start | bytes 110600 | tf_op jit(solution)/shard_map/ppermute | solution.py:631
  19.2 1.7 %collective-permute-done.4.refs_1_ = bf16[144,128]{1,0:T(8,128)(2,1)S(1)} collective-permute-done((bf16[144,128]{1,0:T(8,128)(2,1)S(1)}, bf16[144,128]{1,0:T(8,128)(2,1)S(1)}, u32[]{:S(2)}, u32[]{:S(2)}) %collective-permute-start.4) | collective-permute-done | bytes 36896 | tf_op jit(solution)/shard_map/ppermute | solution.py:631
  20.9 0.4 %collective-permute-done.5.refs_2_ = bf16[144,128]{1,0:T(8,128)(2,1)S(1)} collective-permute-done((bf16[144,128]{1,0:T(8,128)(2,1)S(1)}, bf16[144,128]{1,0:T(8,128)(2,1)S(1)}, u32[]{:S(2)}, u32[]{:S(2)}) %collective-permute-start.5) | collective-permute-done | bytes 36896 | tf_op jit(solution)/shard_map/ppermute | solution.py:631
  21.3 0.0 collective-permute-done.6.refs_3_
  21.3 0.2 shard_map.140
  21.6 1.2 %collective-permute-start.7 = (bf16[456,128]{1,0:T(8,128)(2,1)S(1)}, bf16[456,128]{1,0:T(8,128)(2,1)S(1)}, u32[]{:S(2)}, u32[]{:S(2)}) collective-permute-start(bf16[456,128]{1,0:T(8,128)(2,1)S(1)} %get-tuple-element.50), channel_id=1, source_target_pairs={{0,1},{1,0},{2,3},{3,2},{4,5},{5,4},{6,7},{7,6},{8,9},{9,8},{10,11... | collective-permute-start | bytes 350216 | tf_op jit(solution)/shard_map/ppermute | solution.py:638
  22.7 1.0 %collective-permute-done.7.got = bf16[456,128]{1,0:T(8,128)(2,1)S(1)} collective-permute-done((bf16[456,128]{1,0:T(8,128)(2,1)S(1)}, bf16[456,128]{1,0:T(8,128)(2,1)S(1)}, u32[]{:S(2)}, u32[]{:S(2)}) %collective-permute-start.7) | collective-permute-done | bytes 116768 | tf_op jit(solution)/shard_map/ppermute | solution.py:638
  23.7 0.1 shard_map.141
  23.8 0.7 %collective-permute-start.10 = (bf16[368,128]{1,0:T(8,128)(2,1)S(1)}, bf16[368,128]{1,0:T(8,128)(2,1)S(1)}, u32[]{:S(2)}, u32[]{:S(2)}) collective-permute-start(bf16[368,128]{1,0:T(8,128)(2,1)S(1)} %get-tuple-element.54), channel_id=1, source_target_pairs={{0,4},{1,5},{2,6},{3,7},{4,0},{5,1},{6,2},{7,3},{8,12},{9,13},{10,... | collective-permute-start | bytes 282632 | tf_op jit(solution)/shard_map/ppermute | solution.py:644
  24.5 0.6 %collective-permute-start.8 = (bf16[368,128]{1,0:T(8,128)(2,1)S(1)}, bf16[368,128]{1,0:T(8,128)(2,1)S(1)}, u32[]{:S(2)}, u32[]{:S(2)}) collective-permute-start(bf16[368,128]{1,0:T(8,128)(2,1)S(1)} %get-tuple-element.52), channel_id=1, source_target_pairs={{0,2},{1,3},{2,0},{3,1},{4,6},{5,7},{6,4},{7,5},{8,10},{9,11},{10,... | collective-permute-start | bytes 282632 | tf_op jit(solution)/shard_map/ppermute | solution.py:644
  25.1 3.1 %collective-permute-start.9 = (bf16[368,128]{1,0:T(8,128)(2,1)S(1)}, bf16[368,128]{1,0:T(8,128)(2,1)S(1)}, u32[]{:S(2)}, u32[]{:S(2)}) collective-permute-start(bf16[368,128]{1,0:T(8,128)(2,1)S(1)} %get-tuple-element.53), channel_id=1, source_target_pairs={{0,6},{1,7},{2,4},{3,5},{4,2},{5,3},{6,0},{7,1},{8,14},{9,15},{10,... | collective-permute-start | bytes 282632 | tf_op jit(solution)/shard_map/ppermute | solution.py:644
  28.2 2.4 %collective-permute-done.10.high = bf16[368,128]{1,0:T(8,128)(2,1)S(1)} collective-permute-done((bf16[368,128]{1,0:T(8,128)(2,1)S(1)}, bf16[368,128]{1,0:T(8,128)(2,1)S(1)}, u32[]{:S(2)}, u32[]{:S(2)}) %collective-permute-start.10) | collective-permute-done | bytes 94240 | tf_op jit(solution)/shard_map/ppermute | solution.py:644
  30.6 2.5 %collective-permute-done.8.low = bf16[368,128]{1,0:T(8,128)(2,1)S(1)} collective-permute-done((bf16[368,128]{1,0:T(8,128)(2,1)S(1)}, bf16[368,128]{1,0:T(8,128)(2,1)S(1)}, u32[]{:S(2)}, u32[]{:S(2)}) %collective-permute-start.8) | collective-permute-done | bytes 94240 | tf_op jit(solution)/shard_map/ppermute | solution.py:644
  33.1 0.0 collective-permute-done.9.both
  33.1 1.6 %collective-permute-start.11 = (bf16[264,128]{1,0:T(8,128)(2,1)S(1)}, bf16[264,128]{1,0:T(8,128)(2,1)S(1)}, u32[]{:S(2)}, u32[]{:S(2)}) collective-permute-start(bf16[264,128]{1,0:T(8,128)(2,1)S(1)} %get-tuple-element.55), channel_id=1, source_target_pairs={{0,24},{1,25},{2,26},{3,27},{4,28},{5,29},{6,30},{7,31},{8,16},{9,... | collective-permute-start | bytes 202760 | tf_op jit(solution)/shard_map/ppermute | solution.py:649
  34.7 0.9 %collective-permute-start.12 = (bf16[264,128]{1,0:T(8,128)(2,1)S(1)}, bf16[264,128]{1,0:T(8,128)(2,1)S(1)}, u32[]{:S(2)}, u32[]{:S(2)}) collective-permute-start(bf16[264,128]{1,0:T(8,128)(2,1)S(1)} %get-tuple-element.55), channel_id=1, source_target_pairs={{0,16},{1,17},{2,18},{3,19},{4,20},{5,21},{6,22},{7,23},{8,24},{9,... | collective-permute-start | bytes 202760 | tf_op jit(solution)/shard_map/ppermute | solution.py:649
  35.6 1.1 %collective-permute-start.13 = (bf16[264,128]{1,0:T(8,128)(2,1)S(1)}, bf16[264,128]{1,0:T(8,128)(2,1)S(1)}, u32[]{:S(2)}, u32[]{:S(2)}) collective-permute-start(bf16[264,128]{1,0:T(8,128)(2,1)S(1)} %get-tuple-element.55), channel_id=1, source_target_pairs={{0,8},{1,9},{2,10},{3,11},{4,12},{5,13},{6,14},{7,15},{8,0},{9,1},... | collective-permute-start | bytes 202760 | tf_op jit(solution)/shard_map/ppermute | solution.py:649
  36.7 2.1 %collective-permute-done.11 = bf16[264,128]{1,0:T(8,128)(2,1)S(1)} collective-permute-done((bf16[264,128]{1,0:T(8,128)(2,1)S(1)}, bf16[264,128]{1,0:T(8,128)(2,1)S(1)}, u32[]{:S(2)}, u32[]{:S(2)}) %collective-permute-start.11) | collective-permute-done | bytes 67616 | tf_op jit(solution)/shard_map/ppermute | solution.py:649
  38.8 0.6 %collective-permute-done.12 = bf16[264,128]{1,0:T(8,128)(2,1)S(1)} collective-permute-done((bf16[264,128]{1,0:T(8,128)(2,1)S(1)}, bf16[264,128]{1,0:T(8,128)(2,1)S(1)}, u32[]{:S(2)}, u32[]{:S(2)}) %collective-permute-start.12) | collective-permute-done | bytes 67616 | tf_op jit(solution)/shard_map/ppermute | solution.py:649
  39.4 0.5 %collective-permute-done.13 = bf16[264,128]{1,0:T(8,128)(2,1)S(1)} collective-permute-done((bf16[264,128]{1,0:T(8,128)(2,1)S(1)}, bf16[264,128]{1,0:T(8,128)(2,1)S(1)}, u32[]{:S(2)}, u32[]{:S(2)}) %collective-permute-start.13) | collective-permute-done | bytes 67616 | tf_op jit(solution)/shard_map/ppermute | solution.py:649
  39.9 0.1 collective-permute-start.14
  40.0 1.2 %shard_map.143 = (bf16[8,4,1024]{2,1,0:T(4,128)(2,1)}, bf16[8,4,1024]{2,1,0:T(4,128)(2,1)}, f32[2,1024]{1,0:T(2,128)}, f32[3,8]{1,0:T(4,128)}, f32[264,1024]{1,0:T(8,128)}) custom-call(s32[1]{0:T(128)} %bitcast.pos, s32[1]{0:T(128)} %bitcast.1.tile, bf16[4,264,128]{2,1,0:T(8,128)(2,1)S(1)} %pad_maximum_fusion.slabs, ...), custom_call_target="tpu_custom_call" | custom-call | tf_op jit(solution)/shard_map/pallas_call | solution.py:661
  41.2 0.3 collective-permute-done.14.slabs
  41.6 0.8 %shard_map.144 = f32[264,1024]{1,0:T(8,128)} custom-call(s32[1]{0:T(128)} %bitcast.pos, s32[1]{0:T(128)} %bitcast.1.tile, bf16[4,264,128]{2,1,0:T(8,128)(2,1)S(1)} %collective-permute-done.14.slabs, f32[264,1024]{1,0:T(8,128)} %get-tuple-element.60.weight_in), custom_call_target="tpu_custom_call", output_to_operand_aliasing={{}: (3, {})} | custom-call | tf_op jit(solution)/shard_map/pallas_call | solution.py:671
  (2 shorter events, 0.1 us)
Async XLA Ops:
  2.0 1.5 %collective-permute-start = (bf16[4,4,3200]{2,1,0:T(4,128)(2,1)S(1)}, bf16[4,4,3200]{2,1,0:T(4,128)(2,1)S(1)}, u32[]{:S(2)}, u32[]{:S(2)}) collective-permute-start(bf16[4,4,3200]{2,1,0:T(4,128)(2,1)S(1)} %get-tuple-element.35), channel_id=1, source_target_pairs={{0,1},{1,0},{2,3},{3,2},{4,5},{5,4},{6,7},{7,6},{8,9},{9,8},{10,11... | collective-permute-start | bytes 307208 | tf_op jit(solution)/shard_map/ppermute | solution.py:602
  3.5 6.1 %collective-permute-start.1 = (bf16[8,3200]{1,0:T(8,128)(2,1)S(1)}, bf16[8,3200]{1,0:T(8,128)(2,1)S(1)}, u32[]{:S(2)}, u32[]{:S(2)}) collective-permute-start(bf16[8,3200]{1,0:T(8,128)(2,1)S(1)} %get-tuple-element.37), channel_id=1, source_target_pairs={{0,4},{1,5},{2,6},{3,7},{4,0},{5,1},{6,2},{7,3},{8,12},{9,13},{10,... | collective-permute-start | bytes 153608 | tf_op jit(solution)/shard_map/ppermute | solution.py:606
  7.5 4.1 %collective-permute-start.2 = (bf16[8,3200]{1,0:T(8,128)(2,1)S(1)}, bf16[8,3200]{1,0:T(8,128)(2,1)S(1)}, u32[]{:S(2)}, u32[]{:S(2)}) collective-permute-start(bf16[8,3200]{1,0:T(8,128)(2,1)S(1)} %get-tuple-element.38), channel_id=1, source_target_pairs={{0,2},{1,3},{2,0},{3,1},{4,6},{5,7},{6,4},{7,5},{8,10},{9,11},{10,... | collective-permute-start | bytes 153608 | tf_op jit(solution)/shard_map/ppermute | solution.py:606
  9.1 5.9 %collective-permute-start.3 = (bf16[8,3200]{1,0:T(8,128)(2,1)S(1)}, bf16[8,3200]{1,0:T(8,128)(2,1)S(1)}, u32[]{:S(2)}, u32[]{:S(2)}) collective-permute-start(bf16[8,3200]{1,0:T(8,128)(2,1)S(1)} %get-tuple-element.39), channel_id=1, source_target_pairs={{0,6},{1,7},{2,4},{3,5},{4,2},{5,3},{6,0},{7,1},{8,14},{9,15},{10,... | collective-permute-start | bytes 153608 | tf_op jit(solution)/shard_map/ppermute | solution.py:606
  16.2 4.7 %collective-permute-start.4 = (bf16[144,128]{1,0:T(8,128)(2,1)S(1)}, bf16[144,128]{1,0:T(8,128)(2,1)S(1)}, u32[]{:S(2)}, u32[]{:S(2)}) collective-permute-start(bf16[144,128]{1,0:T(8,128)(2,1)S(1)} %get-tuple-element.42), channel_id=1, source_target_pairs={{0,25},{1,24},{2,27},{3,26},{4,29},{5,28},{6,31},{7,30},{8,17},{9,... | collective-permute-start | bytes 110600 | tf_op jit(solution)/shard_map/ppermute | solution.py:631
  16.8 4.6 %collective-permute-start.5 = (bf16[144,128]{1,0:T(8,128)(2,1)S(1)}, bf16[144,128]{1,0:T(8,128)(2,1)S(1)}, u32[]{:S(2)}, u32[]{:S(2)}) collective-permute-start(bf16[144,128]{1,0:T(8,128)(2,1)S(1)} %get-tuple-element.43), channel_id=1, source_target_pairs={{0,16},{1,17},{2,18},{3,19},{4,20},{5,21},{6,22},{7,23},{8,24},{9,... | collective-permute-start | bytes 110600 | tf_op jit(solution)/shard_map/ppermute | solution.py:631
  17.9 3.5 %collective-permute-start.6 = (bf16[144,128]{1,0:T(8,128)(2,1)S(1)}, bf16[144,128]{1,0:T(8,128)(2,1)S(1)}, u32[]{:S(2)}, u32[]{:S(2)}) collective-permute-start(bf16[144,128]{1,0:T(8,128)(2,1)S(1)} %get-tuple-element.44), channel_id=1, source_target_pairs={{0,9},{1,8},{2,11},{3,10},{4,13},{5,12},{6,15},{7,14},{8,1},{9,0},... | collective-permute-start | bytes 110600 | tf_op jit(solution)/shard_map/ppermute | solution.py:631
  21.6 2.1 %collective-permute-start.7 = (bf16[456,128]{1,0:T(8,128)(2,1)S(1)}, bf16[456,128]{1,0:T(8,128)(2,1)S(1)}, u32[]{:S(2)}, u32[]{:S(2)}) collective-permute-start(bf16[456,128]{1,0:T(8,128)(2,1)S(1)} %get-tuple-element.50), channel_id=1, source_target_pairs={{0,1},{1,0},{2,3},{3,2},{4,5},{5,4},{6,7},{7,6},{8,9},{9,8},{10,11... | collective-permute-start | bytes 350216 | tf_op jit(solution)/shard_map/ppermute | solution.py:638
  23.8 6.9 %collective-permute-start.10 = (bf16[368,128]{1,0:T(8,128)(2,1)S(1)}, bf16[368,128]{1,0:T(8,128)(2,1)S(1)}, u32[]{:S(2)}, u32[]{:S(2)}) collective-permute-start(bf16[368,128]{1,0:T(8,128)(2,1)S(1)} %get-tuple-element.54), channel_id=1, source_target_pairs={{0,4},{1,5},{2,6},{3,7},{4,0},{5,1},{6,2},{7,3},{8,12},{9,13},{10,... | collective-permute-start | bytes 282632 | tf_op jit(solution)/shard_map/ppermute | solution.py:644
  24.5 8.6 %collective-permute-start.8 = (bf16[368,128]{1,0:T(8,128)(2,1)S(1)}, bf16[368,128]{1,0:T(8,128)(2,1)S(1)}, u32[]{:S(2)}, u32[]{:S(2)}) collective-permute-start(bf16[368,128]{1,0:T(8,128)(2,1)S(1)} %get-tuple-element.52), channel_id=1, source_target_pairs={{0,2},{1,3},{2,0},{3,1},{4,6},{5,7},{6,4},{7,5},{8,10},{9,11},{10,... | collective-permute-start | bytes 282632 | tf_op jit(solution)/shard_map/ppermute | solution.py:644
  25.1 8.0 %collective-permute-start.9 = (bf16[368,128]{1,0:T(8,128)(2,1)S(1)}, bf16[368,128]{1,0:T(8,128)(2,1)S(1)}, u32[]{:S(2)}, u32[]{:S(2)}) collective-permute-start(bf16[368,128]{1,0:T(8,128)(2,1)S(1)} %get-tuple-element.53), channel_id=1, source_target_pairs={{0,6},{1,7},{2,4},{3,5},{4,2},{5,3},{6,0},{7,1},{8,14},{9,15},{10,... | collective-permute-start | bytes 282632 | tf_op jit(solution)/shard_map/ppermute | solution.py:644
  33.1 5.6 %collective-permute-start.11 = (bf16[264,128]{1,0:T(8,128)(2,1)S(1)}, bf16[264,128]{1,0:T(8,128)(2,1)S(1)}, u32[]{:S(2)}, u32[]{:S(2)}) collective-permute-start(bf16[264,128]{1,0:T(8,128)(2,1)S(1)} %get-tuple-element.55), channel_id=1, source_target_pairs={{0,24},{1,25},{2,26},{3,27},{4,28},{5,29},{6,30},{7,31},{8,16},{9,... | collective-permute-start | bytes 202760 | tf_op jit(solution)/shard_map/ppermute | solution.py:649
  34.7 4.7 %collective-permute-start.12 = (bf16[264,128]{1,0:T(8,128)(2,1)S(1)}, bf16[264,128]{1,0:T(8,128)(2,1)S(1)}, u32[]{:S(2)}, u32[]{:S(2)}) collective-permute-start(bf16[264,128]{1,0:T(8,128)(2,1)S(1)} %get-tuple-element.55), channel_id=1, source_target_pairs={{0,16},{1,17},{2,18},{3,19},{4,20},{5,21},{6,22},{7,23},{8,24},{9,... | collective-permute-start | bytes 202760 | tf_op jit(solution)/shard_map/ppermute | solution.py:649
  35.6 4.3 %collective-permute-start.13 = (bf16[264,128]{1,0:T(8,128)(2,1)S(1)}, bf16[264,128]{1,0:T(8,128)(2,1)S(1)}, u32[]{:S(2)}, u32[]{:S(2)}) collective-permute-start(bf16[264,128]{1,0:T(8,128)(2,1)S(1)} %get-tuple-element.55), channel_id=1, source_target_pairs={{0,8},{1,9},{2,10},{3,11},{4,12},{5,13},{6,14},{7,15},{8,0},{9,1},... | collective-permute-start | bytes 202760 | tf_op jit(solution)/shard_map/ppermute | solution.py:649
  39.9 1.6 %collective-permute-start.14 = (bf16[4,264,128]{2,1,0:T(8,128)(2,1)S(1)}, bf16[4,264,128]{2,1,0:T(8,128)(2,1)S(1)}, u32[]{:S(2)}, u32[]{:S(2)}) collective-permute-start(bf16[4,264,128]{2,1,0:T(8,128)(2,1)S(1)} %pad_maximum_fusion.slabs), channel_id=1, source_target_pairs={{0,1},{1,0},{2,3},{3,2},{4,5},{5,4},{6,7},{7,6},{8,9},{9,8},{10,11... | collective-permute-start | bytes 811016 | tf_op jit(solution)/shard_map/ppermute | solution.py:651
